TPU v7x, 512 devices: a whole 4x4x16 slice. The times are simulated.
512 devices in a mesh: section: 32 (over z, y_hi), tensor: 8 (over x, core), dp: 2 (over y_lo).
Axes of the slice: x: 4, y: 4 (y_hi: 2, y_lo: 2; y = y_hi * 2 + y_lo), z: 16, core: 2. Of those that a mesh axis runs over, the one named last changes fastest.
Arguments:
- weight: bfloat16 [32, 6144, 6144], P('section', 'tensor', 'dp'), may hold values from -0.078125 to 0.078125
- adapter_down_map: bfloat16 [32, 6144, 16], P('section', 'tensor'), may hold values from -0.078125 to 0.078125
- adapter_up_map: bfloat16 [32, 16, 6144], P('section', None, 'tensor'), may hold values from -1.5 to 1.5
- gain: float32 [32, 6144], P('section', 'tensor'), may hold values from 0.5 to 1.5
- prior_epoch_input: bfloat16 [32, 2, 2, 48, 6144], P('section', 'dp', None, None, 'tensor'), as said below
- prior_epoch_output: bfloat16 [32, 2, 2, 48, 6144], P('section', 'dp', None, None, 'tensor'), as said below
- initial_step_inputs: bfloat16 [32, 96, 6144], P('section', 'dp', 'tensor'), may hold values from -6 to 6
- initial_step_gradients: bfloat16 [32, 96, 6144], P('section', 'dp', 'tensor'), may hold values from -6 to 6
- sample_numbers: int32 [32, 2, 4], P('section', 'dp'), may hold values from 0 to 1
Outputs:
- grad_down: bfloat16 [32, 6144, 16], P('section', 'tensor')
- grad_up: bfloat16 [32, 16, 6144], P('section', None, 'tensor')
Inputs may be any that keep to these rules, and one draw needn't show every extreme that they name: prior_epoch_input[s] equals prior_epoch_output[s-1] for every section s >= 1. `prior_epoch_output`: stored activations of order one.
All inputs are finite; a program needn't handle non-finite values. Where the computation divides by a largest or mean magnitude, that divisor is 1e-20 or more.
Results may differ from a plain program's by a relative error of at most 0.03.
Values may be sent and summed in bfloat16 or wider, within the bound.
No kernel may reach another device: no remote copies, remote signals or barrier semaphores. Data moves between devices by JAX's collectives and lax.ppermute only.
A program may use at most 64 MiB of HBM per device.

v0:
```python
import jax
import jax.numpy as jnp
from jax import lax
from jax.sharding import PartitionSpec as P

MODEL_WIDTH = 6144
QBLOCK = 128
TICKS = 4


def from_behind(block, axis, distance):
    devices = range(lax.axis_size(axis))
    route = [(i - distance, i) for i in devices if i - distance in devices]
    return lax.ppermute(block, axis, route)


def on_device(
    weight,
    adapter_down_map,
    adapter_up_map,
    gain,
    prior_epoch_input,
    prior_epoch_output,
    initial_step_inputs,
    initial_step_gradients,
    sample_numbers,
):
    highest = lax.Precision.HIGHEST
    w_local = weight[0]
    local_down_matrix = adapter_down_map[0]
    down_wide = local_down_matrix.astype(jnp.float32)
    local_up_matrix = adapter_up_map[0]
    local_gain_vector = gain[0]
    cache_in = prior_epoch_input[0, 0]
    cache_out = prior_epoch_output[0, 0]
    order = sample_numbers[0, 0]
    layer_index = lax.axis_index("section")
    is_first = layer_index == 0
    is_last = layer_index == lax.axis_size("section") - 1
    w_full = lax.all_gather(w_local, "dp", axis=1, tiled=True)
    carry_state = initial_step_inputs[0].astype(jnp.float32)
    grad_in = initial_step_gradients[0]
    sample = order[0]
    rows = carry_state.shape[0]
    acc_a = jnp.zeros(local_down_matrix.shape, jnp.float32)
    acc_b = jnp.zeros(local_up_matrix.shape, jnp.float32)
    for tick in range(TICKS):
        sum_one = jnp.sum(carry_state, axis=1)
        sum_two = jnp.sum(carry_state * carry_state, axis=1)
        sum_one, sum_two = lax.psum((sum_one, sum_two), "tensor")
        average_value = sum_one / MODEL_WIDTH
        var_val = sum_two / MODEL_WIDTH - average_value * average_value
        inverse_deviation = lax.rsqrt(var_val + 1e-05)
        centered_scaled_input = (carry_state - average_value[:, None]) * inverse_deviation[:, None]
        normalized_rows = centered_scaled_input * local_gain_vector
        normed_b = normalized_rows.astype(jnp.bfloat16)
        low_full = lax.psum(jnp.dot(normalized_rows, down_wide, precision=highest), "tensor")
        low_b = low_full.astype(jnp.bfloat16)
        projected = jnp.dot(normed_b, w_full, preferred_element_type=jnp.float32)
        mixed = lax.psum_scatter(projected, "tensor", scatter_dimension=1, tiled=True)
        output = (
            carry_state
            + mixed
            + jnp.dot(low_b, local_up_matrix, preferred_element_type=jnp.float32)
        )
        bias_gradient = jnp.where(is_last, output.astype(jnp.bfloat16), grad_in)
        grad_full = lax.all_gather(bias_gradient, "tensor", axis=1, tiled=True)
        contract = (((1,), (1,)), ((), ()))
        du_main = lax.dot_general(grad_full, w_full, contract, preferred_element_type=jnp.float32)
        low_grad_part = lax.dot_general(
            bias_gradient, local_up_matrix, contract, preferred_element_type=jnp.float32
        )
        low_grad = lax.psum(low_grad_part, "tensor")
        grad_norm = du_main + jnp.dot(low_grad, down_wide.T, precision=highest)
        hidden_gradient_value = grad_norm * local_gain_vector
        first_average, second_average = lax.psum(
            (
                jnp.sum(hidden_gradient_value, axis=1),
                jnp.sum(hidden_gradient_value * centered_scaled_input, axis=1),
            ),
            "tensor",
        )
        first_average = first_average / MODEL_WIDTH
        second_average = second_average / MODEL_WIDTH
        grad_x = bias_gradient.astype(jnp.float32) + inverse_deviation[:, None] * (
            hidden_gradient_value
            - first_average[:, None]
            - centered_scaled_input * second_average[:, None]
        )
        acc_a = acc_a + jnp.dot(normalized_rows.T, low_grad, precision=highest)
        acc_b = acc_b + jnp.dot(low_b.T, bias_gradient, preferred_element_type=jnp.float32)
        if tick < TICKS - 1:
            base_now = lax.dynamic_index_in_dim(cache_out, sample, 0, keepdims=False)
            delta = output - base_now.astype(jnp.float32)
            blocks = delta.reshape(rows, -1, QBLOCK)
            scales = (jnp.max(jnp.abs(blocks), axis=-1) + 1e-06).astype(jnp.bfloat16)
            coded = (blocks / scales.astype(jnp.float32)[..., None]).astype(jnp.bfloat16)
            got_coded, got_scales, got_sample = from_behind(
                (coded, scales, sample[None]), "section", 1
            )
            next_sample = jnp.where(is_first, order[tick + 1], got_sample[0])
            base_next = lax.dynamic_index_in_dim(cache_in, next_sample, 0, keepdims=False).astype(
                jnp.float32
            )
            decoded = (
                got_coded.astype(jnp.float32) * got_scales.astype(jnp.float32)[..., None]
            ).reshape(rows, -1)
            carry_state = jnp.where(is_first, base_next, base_next + decoded)
            sample = next_sample
            grad_in = from_behind(grad_x.astype(jnp.bfloat16), "section", -1)
    total_a, total_b = (
        lax.psum(acc_a.astype(jnp.bfloat16), "dp").astype(jnp.float32),
        lax.psum(acc_b.astype(jnp.bfloat16), "dp").astype(jnp.float32),
    )
    denom = jnp.float32(rows * lax.axis_size("dp"))
    return (
        (total_a / denom).astype(jnp.bfloat16)[None],
        (total_b / denom).astype(jnp.bfloat16)[None],
    )


def solution(mesh):
    in_specs = (
        P("section", "tensor", "dp"),
        P("section", "tensor", None),
        P("section", None, "tensor"),
        P("section", "tensor"),
        P("section", "dp", None, None, "tensor"),
        P("section", "dp", None, None, "tensor"),
        P("section", "dp", "tensor"),
        P("section", "dp", "tensor"),
        P("section", "dp", None),
    )
    out_specs = (P("section", "tensor", None), P("section", None, "tensor"))
    return jax.shard_map(
        on_device, mesh=mesh, in_specs=in_specs, out_specs=out_specs, check_vma=False
    )
```

profile of v0, /device:TPU:112, one launch (start us, length us, event | category | flops | bytes accessed | tf_op | source)
XLA Modules:
  0.0 478.4 jit_solution(14974071390182323774)
XLA Ops:
  10.7 14.6 %all-reduce.6 = (f32[48]{0:T(128)S(1)}, f32[48]{0:T(128)S(1)}) all-reduce(f32[48]{0:T(128)S(1)} %fusion.46, f32[48]{0:T(128)S(1)} %convert_reduce_fusion), channel_id=1, replica_groups=mesh['section'=32,'tensor'=8,'dp'=2] {'tensor'}, use_global_device_ids=true, to_apply=%region_3.0 | all-reduce | flops 96 | bytes 768 | tf_op jit(solution)/shard_map/psum | solution.py:50
  25.4 115.9 %all-gather.3.cloned.1.call-done = bf16[1,768,6144]{2,1,0:T(8,128)(2,1)} async-done(((bf16[1,768,3072]{2,1,0:T(8,128)(2,1)}), bf16[1,768,6144]{2,1,0:T(8,128)(2,1)}) %all-gather.3.cloned.1.call-update) | async-done | bytes 9437200 | tf_op jit(solution)/shard_map/all_gather | solution.py:40
  141.3 6.6 %fusion.12 = f32[48,6144]{1,0:T(8,128)} fusion(bf16[1,768,6144]{2,1,0:T(8,128)(2,1)} %all-gather.3.cloned.1.call-done, bf16[1,48,768]{2,1,0:T(8,128)(2,1)} %param.15, f32[768]{0:T(1024)S(1)} %reduce.1, f32[48]{0:T(128)S(1)} %get-tuple-element.56, f32[48]{0:T(128)S(1)} %get-tuple-element.55), kind=kOutput, calls=%fused_computation.12 | convolution fusion | flops 453169152 | bytes 10694016 | tf_op jit(solution)/shard_map/dot_general | solution.py:59
  148.6 4.9 %collective-permute-start = (s32[1]{0:T(128)}, s32[1]{0:T(128)}, u32[]{:S(2)}, u32[]{:S(2)}) collective-permute-start(s32[1]{0:T(128)} %bitcast.7), channel_id=1, source_target_pairs={{0,16},{16,32},{32,48},{48,64},{64,80},{80,96},{96,112},{112,128},... | collective-permute-start | bytes 20 | tf_op jit(solution)/shard_map/ppermute | solution.py:14
  155.7 14.6 %psum.170 = bf16[48,16]{0,1:T(8,128)(2,1)S(1)} all-reduce(f32[48,16]{0,1:T(8,128)S(1)} %fusion.50), channel_id=1, replica_groups=mesh['section'=32,'tensor'=8,'dp'=2] {'tensor'}, use_global_device_ids=true, to_apply=%region_5.0 | all-reduce | flops 768 | bytes 4608 | tf_op jit(solution)/shard_map/psum | solution.py:57
  171.5 17.5 %reduce-scatter.5.cloned.1.call-done = f32[48,768]{1,0:T(8,128)} async-done(((f32[48,6144]{1,0:T(8,128)}), f32[48,768]{1,0:T(8,128)}) %reduce-scatter.5.cloned.1.call-update) | async-done | bytes 147472 | tf_op jit(solution)/shard_map/reduce_scatter | solution.py:60
  195.2 5.0 %collective-permute-start.2 = (bf16[48,6]{1,0:T(8,128)(2,1)S(1)}, bf16[48,6]{1,0:T(8,128)(2,1)S(1)}, u32[]{:S(2)}, u32[]{:S(2)}) collective-permute-start(bf16[48,6]{1,0:T(8,128)(2,1)S(1)} %get-tuple-element.44), channel_id=1, source_target_pairs={{0,16},{16,32},{32,48},{48,64},{64,80},{80,96},{96,112},{112,128},... | collective-permute-start | bytes 1736 | tf_op jit(solution)/shard_map/ppermute | solution.py:14
  202.6 12.9 %all-reduce.5 = (f32[48,16]{0,1:T(8,128)S(1)}, f32[48]{0:T(128)S(1)}, f32[48]{0:T(128)S(1)}) all-reduce(f32[48,16]{0,1:T(8,128)S(1)} %fusion.129, f32[48]{0:T(128)S(1)} %get-tuple-element.11, f32[48]{0:T(128)S(1)} %get-tuple-element.10), channel_id=1, replica_groups=mesh['section'=32,'tensor'=8,'dp'=2] {'tensor'}, use_global_device_ids=true, to_apply=%region_6.7 | all-reduce | flops 864 | bytes 6912 | tf_op jit(solution)/shard_map/psum | solution.py:73
  215.5 6.5 %fusion.10 = f32[48,6144]{1,0:T(8,128)} fusion(bf16[1,768,6144]{2,1,0:T(8,128)(2,1)} %all-gather.3.cloned.1.call-done, f32[48,768]{1,0:T(8,128)S(1)} %get-tuple-element.42, f32[48]{0:T(128)S(1)} %get-tuple-element.54, f32[48]{0:T(128)S(1)} %get-tuple-element.53, f32[768]{0:T(1024)S(1)} %reduce.1), kind=kOutput, calls=%fused_computation.10 | convolution fusion | flops 453132288 | bytes 10767744 | tf_op jit(solution)/shard_map/dot_general | solution.py:59
  222.0 8.4 %collective-permute-start.4 = (s32[1]{0:T(128)}, s32[1]{0:T(128)}, u32[]{:S(2)}, u32[]{:S(2)}) collective-permute-start(s32[1]{0:T(128)} %bitcast.14), channel_id=1, source_target_pairs={{0,16},{16,32},{32,48},{48,64},{64,80},{80,96},{96,112},{112,128},... | collective-permute-start | bytes 20 | tf_op jit(solution)/shard_map/ppermute | solution.py:14
  231.7 9.2 %collective-permute-start.8 = (s32[1]{0:T(128)}, s32[1]{0:T(128)}, u32[]{:S(2)}, u32[]{:S(2)}) collective-permute-start(s32[1]{0:T(128)} %bitcast.20), channel_id=1, source_target_pairs={{0,16},{16,32},{32,48},{48,64},{64,80},{80,96},{96,112},{112,128},... | collective-permute-start | bytes 20 | tf_op jit(solution)/shard_map/ppermute | solution.py:14
  242.2 13.5 %all_gather.13 = bf16[48,6144]{1,0:T(8,128)(2,1)S(1)} all-gather(bf16[48,768]{1,0:T(8,128)(2,1)S(1)} %get-tuple-element.57), channel_id=1, replica_groups=mesh['section'=32,'tensor'=8,'dp'=2] {'tensor'}, dimensions={1}, use_global_device_ids=true | all-gather | bytes 663552 | tf_op jit(solution)/shard_map/all_gather | solution.py:67
  255.7 6.7 %fusion.8 = f32[48,768]{1,0:T(8,128)S(1)} fusion(bf16[48,6144]{1,0:T(8,128)(2,1)S(1)} %all_gather.13, bf16[1,768,6144]{2,1,0:T(8,128)(2,1)} %all-gather.3.cloned.1.call-done), kind=kOutput, calls=%fused_computation.8 | convolution fusion | flops 452984832 | bytes 10174464 | tf_op jit(solution)/shard_map/dot_general | solution.py:69
  263.1 13.3 %all-reduce.4 = (f32[48]{0:T(128)S(1)}, f32[48]{0:T(128)S(1)}, bf16[48,16]{0,1:T(8,128)(2,1)S(1)}) all-reduce(f32[48]{0:T(128)S(1)} %get-tuple-element.13, f32[48]{0:T(128)S(1)} %get-tuple-element.12, f32[48,16]{0,1:T(8,128)S(1)} %fusion.56), channel_id=1, replica_groups=mesh['section'=32,'tensor'=8,'dp'=2] {'tensor'}, use_global_device_ids=true, to_apply=%region_17.18 | all-reduce | flops 864 | bytes 5376 | tf_op jit(solution)/shard_map/psum | solution.py:76
  278.6 7.9 %collective-permute-done.3 = bf16[48,768]{1,0:T(8,128)(2,1)S(1)} collective-permute-done((bf16[48,768]{1,0:T(8,128)(2,1)S(1)}, bf16[48,768]{1,0:T(8,128)(2,1)S(1)}, u32[]{:S(2)}, u32[]{:S(2)}) %collective-permute-start.3) | collective-permute-done | bytes 73760 | tf_op jit(solution)/shard_map/ppermute | solution.py:14
  288.0 5.4 %collective-permute-start.5 = (bf16[48,6,128]{2,1,0:T(8,128)(2,1)S(1)}, bf16[48,6,128]{2,1,0:T(8,128)(2,1)S(1)}, u32[]{:S(2)}, u32[]{:S(2)}) collective-permute-start(bf16[48,6,128]{2,1,0:T(8,128)(2,1)S(1)} %divide_convert_fusion.1), channel_id=1, source_target_pairs={{0,16},{16,32},{32,48},{48,64},{64,80},{80,96},{96,112},{112,128},... | collective-permute-start | bytes 221192 | tf_op jit(solution)/shard_map/ppermute | solution.py:14
  295.4 5.0 %collective-permute-done.6 = bf16[48,6]{1,0:T(8,128)(2,1)S(1)} collective-permute-done((bf16[48,6]{1,0:T(8,128)(2,1)S(1)}, bf16[48,6]{1,0:T(8,128)(2,1)S(1)}, u32[]{:S(2)}, u32[]{:S(2)}) %collective-permute-start.6) | collective-permute-done | bytes 608 | tf_op jit(solution)/shard_map/ppermute | solution.py:14
  300.8 12.9 %all-reduce.3 = (f32[48,16]{0,1:T(8,128)S(1)}, f32[48]{0:T(128)S(1)}, f32[48]{0:T(128)S(1)}) all-reduce(f32[48,16]{0,1:T(8,128)S(1)} %fusion.126, f32[48]{0:T(128)S(1)} %get-tuple-element.7, f32[48]{0:T(128)S(1)} %get-tuple-element.6), channel_id=1, replica_groups=mesh['section'=32,'tensor'=8,'dp'=2] {'tensor'}, use_global_device_ids=true, to_apply=%region_18.19 | all-reduce | flops 864 | bytes 6912 | tf_op jit(solution)/shard_map/psum | solution.py:73
  313.7 6.5 %fusion.6 = f32[48,6144]{1,0:T(8,128)} fusion(bf16[1,768,6144]{2,1,0:T(8,128)(2,1)} %all-gather.3.cloned.1.call-done, f32[48,768]{1,0:T(8,128)S(1)} %get-tuple-element.39, f32[48]{0:T(128)S(1)} %get-tuple-element.52, f32[48]{0:T(128)S(1)} %get-tuple-element.51, f32[768]{0:T(1024)S(1)} %reduce.1), kind=kOutput, calls=%fused_computation.6 | convolution fusion | flops 453132288 | bytes 10767744 | tf_op jit(solution)/shard_map/dot_general | solution.py:59
  320.7 13.3 %all_gather.14 = bf16[48,6144]{1,0:T(8,128)(2,1)S(1)} all-gather(bf16[48,768]{1,0:T(8,128)(2,1)S(1)} %get-tuple-element.60), channel_id=1, replica_groups=mesh['section'=32,'tensor'=8,'dp'=2] {'tensor'}, dimensions={1}, use_global_device_ids=true | all-gather | bytes 663552 | tf_op jit(solution)/shard_map/all_gather | solution.py:67
  334.5 6.8 %fusion.157 = (f32[48]{0:T(128)S(1)}, f32[48]{0:T(128)S(1)}, f32[48,768]{1,0:T(8,128)S(1)}) fusion(f32[48]{0:T(128)S(1)} %get-tuple-element.54, f32[48,768]{1,0:T(8,128)S(1)} %get-tuple-element.42, f32[48]{0:T(128)S(1)} %get-tuple-element.53, f32[768]{0:T(1024)S(1)} %reduce.1, f32[48,768]{1,0:T(8,128)S(1)} %fusion.135, ...), kind=kOutput, calls=%fused_computation.213 | convolution fusion | flops 453242752 | bytes 10473216 | tf_op jit(solution)/shard_map/dot_general | solution.py:69
  341.4 13.5 %all-reduce.2 = (f32[48]{0:T(128)S(1)}, f32[48]{0:T(128)S(1)}, bf16[48,16]{0,1:T(8,128)(2,1)S(1)}) all-reduce(f32[48]{0:T(128)S(1)} %get-tuple-element.9, f32[48]{0:T(128)S(1)} %get-tuple-element.8, f32[48,16]{0,1:T(8,128)S(1)} %fusion.62), channel_id=1, replica_groups=mesh['section'=32,'tensor'=8,'dp'=2] {'tensor'}, use_global_device_ids=true, to_apply=%region_29.30 | all-reduce | flops 864 | bytes 5376 | tf_op jit(solution)/shard_map/psum | solution.py:76
  359.3 6.6 %collective-permute-start.9 = (bf16[48,6,128]{2,1,0:T(8,128)(2,1)S(1)}, bf16[48,6,128]{2,1,0:T(8,128)(2,1)S(1)}, u32[]{:S(2)}, u32[]{:S(2)}) collective-permute-start(bf16[48,6,128]{2,1,0:T(8,128)(2,1)S(1)} %divide_convert_fusion), channel_id=1, source_target_pairs={{0,16},{16,32},{32,48},{48,64},{64,80},{80,96},{96,112},{112,128},... | collective-permute-start | bytes 221192 | tf_op jit(solution)/shard_map/ppermute | solution.py:14
  368.0 5.0 %collective-permute-done.10 = bf16[48,6]{1,0:T(8,128)(2,1)S(1)} collective-permute-done((bf16[48,6]{1,0:T(8,128)(2,1)S(1)}, bf16[48,6]{1,0:T(8,128)(2,1)S(1)}, u32[]{:S(2)}, u32[]{:S(2)}) %collective-permute-start.10) | collective-permute-done | bytes 608 | tf_op jit(solution)/shard_map/ppermute | solution.py:14
  373.3 12.9 %all-reduce.1 = (f32[48,16]{0,1:T(8,128)S(1)}, f32[48]{0:T(128)S(1)}, f32[48]{0:T(128)S(1)}) all-reduce(f32[48,16]{0,1:T(8,128)S(1)} %fusion.123, f32[48]{0:T(128)S(1)} %get-tuple-element.3, f32[48]{0:T(128)S(1)} %get-tuple-element.2), channel_id=1, replica_groups=mesh['section'=32,'tensor'=8,'dp'=2] {'tensor'}, use_global_device_ids=true, to_apply=%region_30.31 | all-reduce | flops 864 | bytes 6912 | tf_op jit(solution)/shard_map/psum | solution.py:73
  386.2 6.5 %fusion.2 = f32[48,6144]{1,0:T(8,128)} fusion(bf16[1,768,6144]{2,1,0:T(8,128)(2,1)} %all-gather.3.cloned.1.call-done, f32[48,768]{1,0:T(8,128)S(1)} %get-tuple-element.36, f32[48]{0:T(128)S(1)} %get-tuple-element.46, f32[48]{0:T(128)S(1)} %get-tuple-element.45, f32[768]{0:T(1024)S(1)} %reduce.1), kind=kOutput, calls=%fused_computation.2 | convolution fusion | flops 453132288 | bytes 10767744 | tf_op jit(solution)/shard_map/dot_general | solution.py:59
  393.0 13.2 %all_gather.15 = bf16[48,6144]{1,0:T(8,128)(2,1)S(1)} all-gather(bf16[48,768]{1,0:T(8,128)(2,1)S(1)} %convert_select_fusion.3), channel_id=1, replica_groups=mesh['section'=32,'tensor'=8,'dp'=2] {'tensor'}, dimensions={1}, use_global_device_ids=true | all-gather | bytes 663552 | tf_op jit(solution)/shard_map/all_gather | solution.py:67
  406.7 6.8 %fusion.155 = (f32[48]{0:T(128)S(1)}, f32[48]{0:T(128)S(1)}, f32[48,768]{1,0:T(8,128)S(1)}) fusion(f32[48]{0:T(128)S(1)} %get-tuple-element.52, f32[48,768]{1,0:T(8,128)S(1)} %get-tuple-element.39, f32[48]{0:T(128)S(1)} %get-tuple-element.51, f32[768]{0:T(1024)S(1)} %reduce.1, f32[48,768]{1,0:T(8,128)S(1)} %fusion.132, ...), kind=kOutput, calls=%fused_computation.211 | convolution fusion | flops 453242752 | bytes 10473216 | tf_op jit(solution)/shard_map/dot_general | solution.py:69
  413.6 13.3 %all-reduce = (f32[48]{0:T(128)S(1)}, f32[48]{0:T(128)S(1)}, bf16[48,16]{0,1:T(8,128)(2,1)S(1)}) all-reduce(f32[48]{0:T(128)S(1)} %get-tuple-element.5, f32[48]{0:T(128)S(1)} %get-tuple-element.4, f32[48,16]{0,1:T(8,128)S(1)} %fusion.68), channel_id=1, replica_groups=mesh['section'=32,'tensor'=8,'dp'=2] {'tensor'}, use_global_device_ids=true, to_apply=%region_41.42 | all-reduce | flops 864 | bytes 5376 | tf_op jit(solution)/shard_map/psum | solution.py:76
  429.3 7.6 %collective-permute-done.11 = bf16[48,768]{1,0:T(8,128)(2,1)S(1)} collective-permute-done((bf16[48,768]{1,0:T(8,128)(2,1)S(1)}, bf16[48,768]{1,0:T(8,128)(2,1)S(1)}, u32[]{:S(2)}, u32[]{:S(2)}) %collective-permute-start.11) | collective-permute-done | bytes 73760 | tf_op jit(solution)/shard_map/ppermute | solution.py:14
  438.3 23.6 %psum.189 = f32[48,16]{1,0:T(8,128)S(1)} all-reduce(f32[48,16]{1,0:T(8,128)S(1)} %fusion.120), channel_id=1, replica_groups=mesh['section'=32,'tensor'=8,'dp'=2] {'tensor'}, use_global_device_ids=true, to_apply=%region_42.43 | all-reduce | flops 768 | bytes 6144 | tf_op jit(solution)/shard_map/psum | solution.py:73
  462.3 8.3 %all-reduce.7 = (bf16[768,16]{0,1:T(8,128)(2,1)S(1)}, bf16[16,768]{1,0:T(8,128)(2,1)S(1)}) all-reduce(bf16[768,16]{0,1:T(8,128)(2,1)S(1)} %fusion.29, bf16[16,768]{1,0:T(8,128)(2,1)S(1)} %fusion.30), channel_id=1, replica_groups=mesh['section'=32,'tensor'=8,'dp'=2] {'dp'}, use_global_device_ids=true, to_apply=%region_43.44 | all-reduce | flops 24576 | bytes 98304 | tf_op jit(solution)/shard_map/psum | solution.py:112
  (109 shorter events, 33.4 us)
Async XLA Ops:
  7.2 181.9 %copy-start = (bf16[1,16,768]{2,1,0:T(8,128)(2,1)S(1)}, bf16[1,16,768]{2,1,0:T(8,128)(2,1)}, u32[]{:S(2)}) copy-start(bf16[1,16,768]{2,1,0:T(8,128)(2,1)} %param.11) | copy-start | bytes 73732
  7.2 134.1 %all-gather.3.cloned.1.call-start = ((), (), s32[]{:S(2)}) async-start(), calls=%async_computation.8 | async-start | bytes 14155776 | tf_op jit(solution)/shard_map/all_gather | solution.py:40
  7.9 140.0 %copy-start.6 = (s32[1,1,4]{2,1,0:T(1,128)S(1)}, s32[1,1,4]{2,1,0:T(1,128)}, u32[]{:S(2)}) copy-start(s32[1,1,4]{2,1,0:T(1,128)} %param.17) | copy-start | bytes 52
  7.9 147.5 %copy-start.1 = (bf16[1,48,768]{2,1,0:T(8,128)(2,1)S(1)}, bf16[1,48,768]{2,1,0:T(8,128)(2,1)}, u32[]{:S(2)}) copy-start(bf16[1,48,768]{2,1,0:T(8,128)(2,1)} %param.15) | copy-start | bytes 221188
  7.9 147.5 %copy-start.4 = (bf16[1,768,16]{1,2,0:T(8,128)(2,1)S(1)}, bf16[1,768,16]{1,2,0:T(8,128)(2,1)}, u32[]{:S(2)}) copy-start(bf16[1,768,16]{1,2,0:T(8,128)(2,1)} %param.10) | copy-start | bytes 73732
  7.9 181.1 %copy-start.5 = (bf16[1,48,768]{2,1,0:T(8,128)(2,1)S(1)}, bf16[1,48,768]{2,1,0:T(8,128)(2,1)}, u32[]{:S(2)}) copy-start(bf16[1,48,768]{2,1,0:T(8,128)(2,1)} %param.16) | copy-start | bytes 221188
  8.0 181.1 %reduce-scatter.5.cloned.1.call-start = ((), (), s32[]{:S(2)}) async-start(), calls=%async_computation.4 | async-start | bytes 1327104 | tf_op jit(solution)/shard_map/reduce_scatter | solution.py:60
  141.3 48.9 %copy-start.3 = (bf16[1,1,2,48,768]{4,3,2,1,0:T(8,128)(2,1)S(1)}, bf16[1,1,2,48,768]{4,3,2,1,0:T(8,128)(2,1)}, u32[]{:S(2)}) copy-start(bf16[1,1,2,48,768]{4,3,2,1,0:T(8,128)(2,1)} %param.14) | copy-start | bytes 442372
  141.3 61.1 %copy-start.2 = (bf16[1,1,2,48,768]{4,3,2,1,0:T(8,128)(2,1)S(1)}, bf16[1,1,2,48,768]{4,3,2,1,0:T(8,128)(2,1)}, u32[]{:S(2)}) copy-start(bf16[1,1,2,48,768]{4,3,2,1,0:T(8,128)(2,1)} %param.13) | copy-start | bytes 442372
  147.9 138.7 %reduce-scatter.7.cloned.1.call-start = ((), (), s32[]{:S(2)}) async-start(), calls=%async_computation.5 | async-start | bytes 1327104 | tf_op jit(solution)/shard_map/reduce_scatter | solution.py:60
  148.6 21.7 %collective-permute-start = (s32[1]{0:T(128)}, s32[1]{0:T(128)}, u32[]{:S(2)}, u32[]{:S(2)}) collective-permute-start(s32[1]{0:T(128)} %bitcast.7), channel_id=1, source_target_pairs={{0,16},{16,32},{32,48},{48,64},{64,80},{80,96},{96,112},{112,128},... | collective-permute-start | bytes 20 | tf_op jit(solution)/shard_map/ppermute | solution.py:14
  190.5 11.8 %collective-permute-start.1 = (bf16[48,6,128]{2,1,0:T(8,128)(2,1)S(1)}, bf16[48,6,128]{2,1,0:T(8,128)(2,1)S(1)}, u32[]{:S(2)}, u32[]{:S(2)}) collective-permute-start(bf16[48,6,128]{2,1,0:T(8,128)(2,1)S(1)} %divide_convert_fusion.2), channel_id=1, source_target_pairs={{0,16},{16,32},{32,48},{48,64},{64,80},{80,96},{96,112},{112,128},... | collective-permute-start | bytes 221192 | tf_op jit(solution)/shard_map/ppermute | solution.py:14
  195.2 7.1 %collective-permute-start.2 = (bf16[48,6]{1,0:T(8,128)(2,1)S(1)}, bf16[48,6]{1,0:T(8,128)(2,1)S(1)}, u32[]{:S(2)}, u32[]{:S(2)}) collective-permute-start(bf16[48,6]{1,0:T(8,128)(2,1)S(1)} %get-tuple-element.44), channel_id=1, source_target_pairs={{0,16},{16,32},{32,48},{48,64},{64,80},{80,96},{96,112},{112,128},... | collective-permute-start | bytes 1736 | tf_op jit(solution)/shard_map/ppermute | solution.py:14
  222.0 135.9 %reduce-scatter.9.cloned.1.call-start = ((), (), s32[]{:S(2)}) async-start(), calls=%async_computation.6 | async-start | bytes 1327104 | tf_op jit(solution)/shard_map/reduce_scatter | solution.py:60
  222.0 8.4 %collective-permute-start.4 = (s32[1]{0:T(128)}, s32[1]{0:T(128)}, u32[]{:S(2)}, u32[]{:S(2)}) collective-permute-start(s32[1]{0:T(128)} %bitcast.14), channel_id=1, source_target_pairs={{0,16},{16,32},{32,48},{48,64},{64,80},{80,96},{96,112},{112,128},... | collective-permute-start | bytes 20 | tf_op jit(solution)/shard_map/ppermute | solution.py:14
  231.7 9.2 %collective-permute-start.8 = (s32[1]{0:T(128)}, s32[1]{0:T(128)}, u32[]{:S(2)}, u32[]{:S(2)}) collective-permute-start(s32[1]{0:T(128)} %bitcast.20), channel_id=1, source_target_pairs={{0,16},{16,32},{32,48},{48,64},{64,80},{80,96},{96,112},{112,128},... | collective-permute-start | bytes 20 | tf_op jit(solution)/shard_map/ppermute | solution.py:14
  276.5 10.0 %collective-permute-start.3 = (bf16[48,768]{1,0:T(8,128)(2,1)S(1)}, bf16[48,768]{1,0:T(8,128)(2,1)S(1)}, u32[]{:S(2)}, u32[]{:S(2)}) collective-permute-start(bf16[48,768]{1,0:T(8,128)(2,1)S(1)} %fusion.45), channel_id=1, source_target_pairs={{16,0},{32,16},{48,32},{64,48},{80,64},{96,80},{112,96},{128,112},... | collective-permute-start | bytes 221192 | tf_op jit(solution)/shard_map/ppermute | solution.py:14
  288.0 12.5 %collective-permute-start.5 = (bf16[48,6,128]{2,1,0:T(8,128)(2,1)S(1)}, bf16[48,6,128]{2,1,0:T(8,128)(2,1)S(1)}, u32[]{:S(2)}, u32[]{:S(2)}) collective-permute-start(bf16[48,6,128]{2,1,0:T(8,128)(2,1)S(1)} %divide_convert_fusion.1), channel_id=1, source_target_pairs={{0,16},{16,32},{32,48},{48,64},{64,80},{80,96},{96,112},{112,128},... | collective-permute-start | bytes 221192 | tf_op jit(solution)/shard_map/ppermute | solution.py:14
  293.4 7.1 %collective-permute-start.6 = (bf16[48,6]{1,0:T(8,128)(2,1)S(1)}, bf16[48,6]{1,0:T(8,128)(2,1)S(1)}, u32[]{:S(2)}, u32[]{:S(2)}) collective-permute-start(bf16[48,6]{1,0:T(8,128)(2,1)S(1)} %get-tuple-element.41), channel_id=1, source_target_pairs={{0,16},{16,32},{32,48},{48,64},{64,80},{80,96},{96,112},{112,128},... | collective-permute-start | bytes 1736 | tf_op jit(solution)/shard_map/ppermute | solution.py:14
  320.2 116.7 %reduce-scatter.11.cloned.1.call-start = ((), (), s32[]{:S(2)}) async-start(), calls=%async_computation.7 | async-start | bytes 1327104 | tf_op jit(solution)/shard_map/reduce_scatter | solution.py:60
  355.0 12.9 %collective-permute-start.7 = (bf16[48,768]{1,0:T(8,128)(2,1)S(1)}, bf16[48,768]{1,0:T(8,128)(2,1)S(1)}, u32[]{:S(2)}, u32[]{:S(2)}) collective-permute-start(bf16[48,768]{1,0:T(8,128)(2,1)S(1)} %add_convert_fusion.1), channel_id=1, source_target_pairs={{16,0},{32,16},{48,32},{64,48},{80,64},{96,80},{112,96},{128,112},... | collective-permute-start | bytes 221192 | tf_op jit(solution)/shard_map/ppermute | solution.py:14
  359.3 13.8 %collective-permute-start.9 = (bf16[48,6,128]{2,1,0:T(8,128)(2,1)S(1)}, bf16[48,6,128]{2,1,0:T(8,128)(2,1)S(1)}, u32[]{:S(2)}, u32[]{:S(2)}) collective-permute-start(bf16[48,6,128]{2,1,0:T(8,128)(2,1)S(1)} %divide_convert_fusion), channel_id=1, source_target_pairs={{0,16},{16,32},{32,48},{48,64},{64,80},{80,96},{96,112},{112,128},... | collective-permute-start | bytes 221192 | tf_op jit(solution)/shard_map/ppermute | solution.py:14
  365.9 7.1 %collective-permute-start.10 = (bf16[48,6]{1,0:T(8,128)(2,1)S(1)}, bf16[48,6]{1,0:T(8,128)(2,1)S(1)}, u32[]{:S(2)}, u32[]{:S(2)}) collective-permute-start(bf16[48,6]{1,0:T(8,128)(2,1)S(1)} %get-tuple-element.38), channel_id=1, source_target_pairs={{0,16},{16,32},{32,48},{48,64},{64,80},{80,96},{96,112},{112,128},... | collective-permute-start | bytes 1736 | tf_op jit(solution)/shard_map/ppermute | solution.py:14
  427.0 9.9 %collective-permute-start.11 = (bf16[48,768]{1,0:T(8,128)(2,1)S(1)}, bf16[48,768]{1,0:T(8,128)(2,1)S(1)}, u32[]{:S(2)}, u32[]{:S(2)}) collective-permute-start(bf16[48,768]{1,0:T(8,128)(2,1)S(1)} %add_convert_fusion), channel_id=1, source_target_pairs={{16,0},{32,16},{48,32},{64,48},{80,64},{96,80},{112,96},{128,112},... | collective-permute-start | bytes 221192 | tf_op jit(solution)/shard_map/ppermute | solution.py:14
Sparse Core Ops, SparseCore 0:
  10.1 131.0 all-gather.2
  148.0 41.0 reduce-scatter.4
  222.1 39.0 reduce-scatter.6
  320.3 36.4 reduce-scatter.8
  392.8 36.3 reduce-scatter.10
where the time goes:
time: 480 us; the launch traced here: 478 us
  blocking collectives  180 us (38%)
  waiting for transfers between devices  162 us (34%)
  starting transfers between devices  54.9 us (11%)
  matrix products  54.8 us (11%)
  between operations  20.2 us (4%)
  other arithmetic  5.97 us (1%)
    all_gather x1, waiting for transfers between devices, on_device(): w_full = lax.all_gather(w_local, 'dp', axis=1, tiled=True)  116 us
    psum x4, blocking collectives, on_device(): low_grad = lax.psum(low_grad_part, 'tensor')  62.3 us
    ppermute x12, starting transfers between devices, from_behind(): return lax.ppermute(block, axis, route)  54.7 us
    psum x3, blocking collectives, on_device(): lax.psum((jnp.sum(hidden_gradient_value, axis=1), jnp.sum(hidden_gradient...  40.1 us
    all_gather x3, blocking collectives, on_device(): grad_full = lax.all_gather(bias_gradient, 'tensor', axis=1, tiled=True)  40 us
    ppermute x12, waiting for transfers between devices, from_behind(): return lax.ppermute(block, axis, route)  27.6 us
    dot_general x4, matrix products, on_device(): projected = jnp.dot(normed_b, w_full, preferred_element_type=jnp.float32)  26 us
    dot_general x3, matrix products, on_device(): lax.dot_general(grad_full, w_full, contract, preferred_element_type=jnp.f...  20.4 us
  transfers between devices with their start and end apart: 17, of which 7 were waited for; matrix products, arithmetic and copies ran while one was open for 6% of the time, Pallas kernels for 0%

commit v1 on v0

v1 whole, which is shorter than its diff:
```python
import jax
import jax.numpy as jnp
from jax import lax
from jax.sharding import PartitionSpec as P

TICKS = 4
CHIPS = 4
EPS = 1e-05
AXES = ("section", "tensor", "dp")
HIGHEST = lax.Precision.HIGHEST
BF = jnp.bfloat16
F32 = jnp.float32


def flat(section, tensor, dp):
    return (section * 2 * CHIPS + tensor) * 2 + dp


def owner(block, core):
    return 2 * (block % CHIPS) + core, block // CHIPS


def to_owner(array, sections, back):
    route = []
    for s in range(sections):
        for block in range(2 * CHIPS):
            for half in range(2):
                if s - back >= 0:
                    route.append((flat(s, block, half), flat(s - back, *owner(block, half))))
    return lax.ppermute(array, AXES, route)


def to_next(array, sections):
    route = []
    for s in range(sections - 1):
        for block in range(2 * CHIPS):
            for half in range(2):
                route.append((flat(s, *owner(block, half)), flat(s + 1, block, half)))
    return lax.ppermute(array, AXES, route)


def swap_cores(array):
    return lax.ppermute(array, "tensor", [(i, i ^ 1) for i in range(2 * CHIPS)])


def over_chips(array):
    groups = [[2 * i for i in range(CHIPS)], [2 * i + 1 for i in range(CHIPS)]]
    return lax.all_to_all(array, "tensor", 0, 0, axis_index_groups=groups)


def split(values, parts=3):
    out = []
    for _ in range(parts):
        high = lax.reduce_precision(values, 8, 7)
        out.append(high.astype(BF))
        values = values - high
    return jnp.concatenate(out, axis=-1)


def join(pieces, width, parts=3):
    total = pieces[..., :width].astype(F32)
    for i in range(1, parts):
        total = total + pieces[..., i * width : (i + 1) * width].astype(F32)
    return total


def pad_to(array, width):
    return jnp.pad(array, [(0, 0)] * (array.ndim - 1) + [(0, width - array.shape[-1])])


def dot(a, b, **kw):
    return jnp.dot(a, b, preferred_element_type=F32, **kw)


def dot_t(a, b, **kw):
    return lax.dot_general(a, b, (((1,), (1,)), ((), ())), preferred_element_type=F32, **kw)


def t_dot(a, b, **kw):
    return lax.dot_general(a, b, (((0,), (0,)), ((), ())), preferred_element_type=F32, **kw)


def on_device(
    weight,
    adapter_down_map,
    adapter_up_map,
    gain,
    prior_epoch_input,
    prior_epoch_output,
    initial_step_inputs,
    initial_step_gradients,
    sample_numbers,
):
    del prior_epoch_output
    w = weight[0]
    down = adapter_down_map[0].astype(F32)
    gains = gain[0]
    order = sample_numbers[0, 0]
    sections = lax.axis_size("section")
    section = lax.axis_index("section")
    tensor = lax.axis_index("tensor")
    half = lax.axis_index("dp")
    core = tensor % 2
    is_first = section == 0
    is_last = section == sections - 1
    toks, feats = initial_step_inputs.shape[1:]
    rank = down.shape[1]
    width = feats * 2 * CHIPS
    rows = 2 * toks

    def both_replicas(mine, theirs):
        return jnp.where(
            half == 0,
            jnp.concatenate([mine, theirs], axis=-2),
            jnp.concatenate([theirs, mine], axis=-2),
        )

    mine = initial_step_inputs[0]
    x = both_replicas(mine, lax.ppermute(mine, "dp", [(0, 1), (1, 0)]))
    given = to_owner(
        jnp.concatenate([initial_step_gradients[0], adapter_up_map[0]], axis=0), sections, 0
    )
    zeros = jnp.zeros((toks, feats), BF)
    grad_part = jnp.where(
        core == 0,
        jnp.concatenate([given[:toks], zeros]),
        jnp.concatenate([zeros, given[:toks]]),
    )
    up = given[toks:]
    chosen = jnp.take(prior_epoch_input[0, 0], order[1:], axis=0)
    theirs = lax.ppermute(
        chosen,
        AXES,
        [(flat(0, t, d), flat(0, t, 1 - d)) for t in range(2 * CHIPS) for d in range(2)],
    )
    first_x = both_replicas(chosen, theirs)

    n_small = rank + 2 + rank + 2
    small_width = 128
    acc_down = jnp.zeros((rank, feats), F32)
    acc_up = jnp.zeros((rank, feats), F32)
    before = None
    dots = None
    for tick in range(TICKS):
        wide = x.astype(F32)
        mid = jnp.mean(wide, axis=1, keepdims=True)
        centered = wide - mid
        square = jnp.sum(centered * centered, axis=1, keepdims=True)
        scaled = centered * gains
        low_part = dot(scaled, down, precision=HIGHEST)
        left = scaled.astype(BF)
        small = [mid, square, low_part]
        x_owned = to_owner(x, sections, 0)
        if tick == 0:
            gain_rows = split(gains[None, :]).reshape(3, feats)
            gain_low = dot(gains[None, :], down, precision=HIGHEST)
            product = dot(jnp.concatenate([left, pad_rows(gain_rows, 16)]), w)
            gain_w = jnp.sum(product[rows:], axis=0, keepdims=True)
            gain_w = split(gain_w.reshape(CHIPS, 1, feats)).reshape(CHIPS, 3, feats)
            gain_low = split(gain_low).reshape(3, rank)
            tail = jnp.concatenate(
                [gain_w, jnp.broadcast_to(pad_to(gain_low, small_width), (CHIPS, 3, small_width))],
                axis=2,
            )
            product = product[:rows]
        else:
            product = dot(left, w)
        product = product.astype(BF).reshape(rows, CHIPS, feats).transpose(1, 0, 2)
        if tick:
            small.append(dots)
            extra = [jnp.broadcast_to(grad_part, (CHIPS, rows, feats))]
        else:
            extra = []
        small = pad_to(split(jnp.concatenate(small, axis=1)), small_width)
        parcel = jnp.concatenate(
            [product] + extra + [jnp.broadcast_to(small, (CHIPS, rows, small_width))], axis=2
        )
        if tick == 0:
            parcel = jnp.concatenate([parcel, jnp.pad(tail, ((0, 0), (0, 13), (0, 0)))], axis=1)
        got = over_chips(parcel)
        if tick == 0:
            tail = got[:, rows : rows + 3].astype(F32).sum(1)
            got = got[:, :rows]
        summed = jnp.sum(got[:, :, :feats].astype(F32), axis=0).astype(BF)
        n_now = 2 + rank + (rank + 2 if tick else 0)
        values = join(got[:, :, -small_width:], n_now)
        packed = [values[:, :, 0].T, values[:, :, 1].T, jnp.sum(values[:, :, 2:], axis=0)]
        packed = jnp.concatenate(packed, axis=1)
        n_packed = packed.shape[1]
        parts = [summed, pad_to(split(packed), small_width)]
        if tick:
            parts.append(got[:, :, feats : 2 * feats].transpose(1, 0, 2).reshape(rows, CHIPS * feats))
        if tick == 0:
            extra_rows = jnp.concatenate(
                [
                    split(tail[:, :feats].reshape(1, -1)).reshape(3 * CHIPS, feats),
                    jnp.broadcast_to(
                        pad_to(split(tail[:, feats : feats + rank]), small_width)[None],
                        (3, CHIPS, small_width),
                    ).reshape(3 * CHIPS, small_width),
                ],
                axis=1,
            )
            parts = [jnp.concatenate([jnp.concatenate(parts, 1), pad_rows(extra_rows, 16)], 0)]
        other = swap_cores(jnp.concatenate(parts, axis=1))
        if tick == 0:
            tail_other = other[rows:]
            gain_w = jnp.concatenate(
                [
                    tail[:, :feats],
                    jnp.sum(
                        tail_other[: 3 * CHIPS, :feats].astype(F32).reshape(3, CHIPS, feats), axis=0
                    ),
                ]
            )
            gain_low = jnp.concatenate(
                [
                    tail[:, feats : feats + rank],
                    join(tail_other[:CHIPS, feats:], rank),
                ]
            )
            gain_w_all = jnp.sum(gain_w, axis=0, keepdims=True)
            gain_low_all = jnp.sum(gain_low, axis=0, keepdims=True)
            other = other[:rows]
        packed_other = join(other[:, feats : feats + small_width], n_packed)
        both = packed + packed_other
        mids = jnp.concatenate([packed[:, :CHIPS], packed_other[:, :CHIPS]], axis=1)
        mean = jnp.sum(mids, axis=1, keepdims=True) / (2 * CHIPS)
        off = mids - mean
        var = (
            jnp.sum(both[:, CHIPS : 2 * CHIPS], axis=1, keepdims=True)
            + feats * jnp.sum(off * off, axis=1, keepdims=True)
        ) / width
        inv = lax.rsqrt(var + EPS)
        mixed = inv * (
            summed.astype(F32)
            + other[:, :feats].astype(F32)
            + dot(off, gain_w, precision=HIGHEST)
        )
        low = inv * (
            both[:, 2 * CHIPS : 2 * CHIPS + rank] + dot(off, gain_low, precision=HIGHEST)
        )
        low_b = low.astype(BF)
        output = (x_owned.astype(F32) + mixed + dot(low_b, up)).astype(BF)
        if tick < TICKS - 1:
            arrived = to_next(output, sections)
        now = (x, mean, inv, low)
        if tick:
            x_was, mean_was, inv_was, low_was = before
            low_grad = both[:, 2 * CHIPS + rank : 2 * CHIPS + 2 * rank]
            first = both[:, 2 * CHIPS + 2 * rank : 2 * CHIPS + 2 * rank + 1]
            second = both[:, 2 * CHIPS + 2 * rank + 1 : 2 * CHIPS + 2 * rank + 2]
            first = (first + jnp.sum(low_grad * gain_low_all, axis=1, keepdims=True)) / width
            second = (second + jnp.sum(low_grad * low_was, axis=1, keepdims=True)) / width
            grads = (
                parts[2].astype(F32) + other[:, feats + small_width :].astype(F32)
            ).astype(BF)
            xhat = (x_was.astype(F32) - mean_was) * inv_was
            acc_down = acc_down + t_dot(low_grad, xhat * gains, precision=HIGHEST)
            grad_norm = dot_t(grads, w) + dot_t(low_grad, down, precision=HIGHEST)
            here = lax.dynamic_slice_in_dim(grads, (tensor % CHIPS) * feats, feats, axis=1)
            here = jnp.where(tensor // CHIPS == half, here.astype(F32), 0.0)
            grad_x = here + inv_was * (grad_norm * gains - first - xhat * second)
            grad_part = to_owner(grad_x.astype(BF), sections, 1)
        grad_part = jnp.where(
            is_last, jnp.where(core == 0, output, jnp.zeros_like(output)), grad_part
        )
        low_grad_part = dot_t(grad_part, up)
        acc_up = acc_up + t_dot(low_b, grad_part)
        if tick < TICKS - 1:
            wide_grad = grad_part.astype(F32)
            dots = jnp.concatenate(
                [
                    low_grad_part,
                    jnp.sum(wide_grad * gain_w_all, axis=1, keepdims=True),
                    jnp.sum(wide_grad * mixed, axis=1, keepdims=True),
                ],
                axis=1,
            )
            x = jnp.where(is_first, first_x[tick], arrived)
        before = now

    acc_other = lax.ppermute(acc_down, "dp", [(0, 1), (1, 0)])
    turned = pad_to(low_grad_part.T, 128)
    parcel = jnp.concatenate([acc_up.astype(BF), split(turned)], axis=1)
    got = lax.all_to_all(
        jnp.broadcast_to(parcel, (4 * CHIPS,) + parcel.shape), ("tensor", "dp"), 0, 0
    )
    low_grad = jnp.sum(join(got[:, :, feats:], 128), axis=0)[:, :rows]
    x_was, mean_was, inv_was, _ = before
    normed = (x_was.astype(F32) - mean_was) * inv_was * gains
    total_down = acc_down + acc_other + dot(low_grad, normed, precision=HIGHEST)
    block = 2 * (2 * (tensor % CHIPS)) + tensor // CHIPS
    total_up = lax.dynamic_index_in_dim(got, block, 0, False)[:, :feats].astype(F32)
    total_up = total_up + lax.dynamic_index_in_dim(got, block + 2, 0, False)[:, :feats].astype(F32)
    return ((total_down / rows).T.astype(BF)[None], (total_up / rows).astype(BF)[None])


def pad_rows(array, count):
    return jnp.pad(array, ((0, count - array.shape[0]), (0, 0)))


def solution(mesh):
    in_specs = (
        P("section", "tensor", "dp"),
        P("section", "tensor", None),
        P("section", None, "tensor"),
        P("section", "tensor"),
        P("section", "dp", None, None, "tensor"),
        P("section", "dp", None, None, "tensor"),
        P("section", "dp", "tensor"),
        P("section", "dp", "tensor"),
        P("section", "dp", None),
    )
    out_specs = (P("section", "tensor", None), P("section", None, "tensor"))
    return jax.shard_map(
        on_device, mesh=mesh, in_specs=in_specs, out_specs=out_specs, check_vma=False
    )
```

time: 480 us -> 276 us (0.57)
  the two profiles are of different devices: /device:TPU:112 before, /device:TPU:113 now
where the time goes in v1:
time: 276 us; the launch traced here: 274 us
  starting transfers between devices  79.2 us (29%)
  blocking collectives  63.8 us (23%)
  matrix products  44.4 us (16%)
  waiting for transfers between devices  34.2 us (12%)
  other arithmetic  26.1 us (9%)
  local copies, waits for them, and re-layouts  23.3 us (8%)
    all_to_all x3, blocking collectives, over_chips(): return lax.all_to_all(array, 'tensor', 0, 0, axis_index_groups=groups)  63.8 us
    dot_general x22, matrix products, dot(): return jnp.dot(a, b, preferred_element_type=F32, **kw)  23.5 us
    ppermute x4, starting transfers between devices, swap_cores(): return lax.ppermute(array, 'tensor', [(i, i ^ 1) for i in range(2 * CHIPS)])  20.2 us
    ppermute x3, starting transfers between devices, to_next(): return lax.ppermute(array, AXES, route)  20.1 us
    ppermute x8, starting transfers between devices, to_owner(): return lax.ppermute(array, AXES, route)  17.7 us
    ppermute x8, waiting for transfers between devices, to_owner(): return lax.ppermute(array, AXES, route)  17.5 us
    dot_general x10, matrix products, dot_t(): lax.dot_general(a, b, (((1,), (1,)), ((), ())), preferred_element_type=F3...  16.3 us
    unnamed x170, local copies, waits for them, and re-layouts  10.1 us
  transfers between devices with their start and end apart: 20, of which 10 were waited for; matrix products, arithmetic and copies ran while one was open for 23% of the time, Pallas kernels for 0%

profile of v1, /device:TPU:113, one launch (start us, length us, event | category | flops | bytes accessed | tf_op | source)
XLA Modules:
  0.0 273.7 jit_solution(12114450843416654727)
XLA Ops:
  1.7 2.9 %collective-permute-start.1 = (bf16[48,768]{0,1:T(8,128)(2,1)S(1)}, bf16[48,768]{0,1:T(8,128)(2,1)S(1)}, u32[]{:S(2)}, u32[]{:S(2)}) collective-permute-start(bf16[48,768]{0,1:T(8,128)(2,1)S(1)} %bitcast.290), channel_id=1, source_target_pairs={{0,1},{1,0},{2,3},{3,2},{4,5},{5,4},{6,7},{7,6},{8,9},{9,8},{10,11... | collective-permute-start | bytes 221192 | tf_op jit(solution)/shard_map/ppermute | solution.py:119
  6.7 2.7 collective-permute-done.1
  11.0 3.3 %fusion.12 = f32[112,3072]{1,0:T(8,128)S(1)} fusion(bf16[1,768,3072]{2,1,0:T(8,128)(2,1)} %param.9, bf16[3,768]{0,1:T(8,128)(2,1)S(1)} %copy.357, bf16[96,768]{0,1:T(8,128)(2,1)S(1)} %get-tuple-element.65), kind=kOutput, calls=%fused_computation.13 | convolution fusion | flops 528998400 | bytes 6246912 | tf_op jit(solution)/shard_map/dot_general | solution.py:72
  15.8 4.0 %all-to-all-start = ((bf16[4,112,896]{2,1,0:T(8,128)(2,1)}), bf16[4,112,896]{2,1,0:T(8,128)(2,1)S(1)}, u32[]{:S(2)}, u32[]{:S(2)}) async-start(bf16[4,112,896]{2,1,0:T(8,128)(2,1)} %fusion.97), calls=%async_computation | async-start | bytes 1605632 | tf_op jit(solution)/shard_map/all_to_all | solution.py:48
  23.6 6.5 %all-to-all-done = bf16[4,112,896]{2,1,0:T(8,128)(2,1)S(1)} async-done(((bf16[4,112,896]{2,1,0:T(8,128)(2,1)}), bf16[4,112,896]{2,1,0:T(8,128)(2,1)S(1)}, u32[]{:S(2)}, u32[]{:S(2)}) %all-to-all-start) | async-done | bytes 802848 | tf_op jit(solution)/shard_map/all_to_all | solution.py:48
  32.7 5.0 %collective-permute-start.3 = (bf16[112,896]{0,1:T(8,128)(2,1)S(1)}, bf16[112,896]{0,1:T(8,128)(2,1)S(1)}, u32[]{:S(2)}, u32[]{:S(2)}) collective-permute-start(bf16[112,896]{0,1:T(8,128)(2,1)S(1)} %fusion.156), channel_id=1, source_target_pairs={{0,2},{2,0},{4,6},{6,4},{8,10},{10,8},{12,14},{14,12},{1,3},{3,1},... | collective-permute-start | bytes 602120 | tf_op jit(solution)/shard_map/ppermute | solution.py:43
  38.5 2.1 collective-permute-start.4
  48.4 7.7 %collective-permute-start.5 = (bf16[96,768]{0,1:T(8,128)(2,1)S(1)}, bf16[96,768]{0,1:T(8,128)(2,1)S(1)}, u32[]{:S(2)}, u32[]{:S(2)}) collective-permute-start(bf16[96,768]{0,1:T(8,128)(2,1)S(1)} %get-tuple-element.147), channel_id=1, source_target_pairs={{0,16},{2,17},{4,18},{6,19},{8,20},{10,21},{12,22},{14,23},{1,24},... | collective-permute-start | bytes 442376 | tf_op jit(solution)/shard_map/ppermute | solution.py:39
  56.5 2.3 collective-permute-done.5
  59.4 3.3 %fusion.14 = bf16[96,3072]{1,0:T(8,128)(2,1)S(1)} fusion(bf16[1,768,3072]{2,1,0:T(8,128)(2,1)} %param.9, bf16[96,768]{0,1:T(8,128)(2,1)S(1)} %get-tuple-element.33, f32[96]{0:T(128)S(1)} %get-tuple-element.138, f32[768]{0:T(1024)S(1)} %get-tuple-element.130), kind=kOutput, calls=%fused_computation.15 | convolution fusion | flops 453574656 | bytes 5459328 | tf_op jit(solution)/shard_map/dot_general | solution.py:72
  63.8 24.7 %all_to_all.25 = bf16[4,96,1664]{2,1,0:T(8,128)(2,1)S(1)} all-to-all(bf16[4,96,1664]{2,1,0:T(8,128)(2,1)S(1)} %pad_maximum_fusion), channel_id=1, replica_groups={{0,4,8,12},{2,6,10,14},{1,5,9,13},{3,7,11,15},{16,20,24,28},{18,22,26,3..., dimensions={0} | all-to-all | bytes 2555904 | tf_op jit(solution)/shard_map/all_to_all | solution.py:48
  90.5 3.8 %collective-permute-start.6 = (bf16[96,3968]{1,0:T(8,128)(2,1)S(1)}, bf16[96,3968]{1,0:T(8,128)(2,1)S(1)}, u32[]{:S(2)}, u32[]{:S(2)}) collective-permute-start(bf16[96,3968]{1,0:T(8,128)(2,1)S(1)} %fusion.99), channel_id=1, source_target_pairs={{0,2},{2,0},{4,6},{6,4},{8,10},{10,8},{12,14},{14,12},{1,3},{3,1},... | collective-permute-start | bytes 2285576 | tf_op jit(solution)/shard_map/ppermute | solution.py:43
  94.8 2.3 collective-permute-start.7
  106.5 7.4 %collective-permute-start.8 = (bf16[96,768]{0,1:T(8,128)(2,1)S(1)}, bf16[96,768]{0,1:T(8,128)(2,1)S(1)}, u32[]{:S(2)}, u32[]{:S(2)}) collective-permute-start(bf16[96,768]{0,1:T(8,128)(2,1)S(1)} %add_convert_fusion.5), channel_id=1, source_target_pairs={{0,16},{2,17},{4,18},{6,19},{8,20},{10,21},{12,22},{14,23},{1,24},... | collective-permute-start | bytes 442376 | tf_op jit(solution)/shard_map/ppermute | solution.py:39
  115.8 3.9 %fusion.79 = bf16[96,768]{0,1:T(8,128)(2,1)S(1)} fusion(f32[96,768]{0,1:T(8,128)S(1)} %copy-done.14, bf16[96,3072]{0,1:T(8,128)(2,1)S(1)} %add_convert_fusion.2, bf16[1,768,3072]{2,1,0:T(8,128)(2,1)} %param.9, bf16[96,768]{0,1:T(8,128)(2,1)S(1)} %copy-done.12, f32[96]{0:T(128)S(1)} %get-tuple-element.90, f32[96]{0:T(128)S(1)} %get-tuple-element.89, ...), kind=kOutput, calls=%fused_computation.48 | convolution fusion | flops 453943296 | bytes 6445061 | tf_op jit(solution)/shard_map/dot_general | solution.py:76
  123.4 2.0 fusion.17
  127.7 3.4 %collective-permute-done.9 = bf16[96,768]{0,1:T(8,128)(2,1)S(1)} collective-permute-done((bf16[96,768]{0,1:T(8,128)(2,1)S(1)}, bf16[96,768]{0,1:T(8,128)(2,1)S(1)}, u32[]{:S(2)}, u32[]{:S(2)}) %collective-permute-start.9) | collective-permute-done | bytes 147488 | tf_op jit(solution)/shard_map/ppermute | solution.py:30
  132.9 19.0 %all_to_all.26 = bf16[4,96,1664]{2,1,0:T(8,128)(2,1)S(1)} all-to-all(bf16[4,96,1664]{2,1,0:T(8,128)(2,1)S(1)} %pad_maximum_fusion.1), channel_id=1, replica_groups={{0,4,8,12},{2,6,10,14},{1,5,9,13},{3,7,11,15},{16,20,24,28},{18,22,26,3..., dimensions={0} | all-to-all | bytes 2555904 | tf_op jit(solution)/shard_map/all_to_all | solution.py:48
  153.7 5.8 %collective-permute-start.10 = (bf16[96,3968]{1,0:T(8,128)(2,1)}, bf16[96,3968]{1,0:T(8,128)(2,1)S(1)}, u32[]{:S(2)}, u32[]{:S(2)}) collective-permute-start(bf16[96,3968]{1,0:T(8,128)(2,1)} %fusion.101), channel_id=1, source_target_pairs={{0,2},{2,0},{4,6},{6,4},{8,10},{10,8},{12,14},{14,12},{1,3},{3,1},... | collective-permute-start | bytes 2285576 | tf_op jit(solution)/shard_map/ppermute | solution.py:43
  159.5 2.1 collective-permute-start.11
  170.4 4.9 %collective-permute-start.12 = (bf16[96,768]{0,1:T(8,128)(2,1)S(1)}, bf16[96,768]{0,1:T(8,128)(2,1)S(1)}, u32[]{:S(2)}, u32[]{:S(2)}) collective-permute-start(bf16[96,768]{0,1:T(8,128)(2,1)S(1)} %add_convert_fusion.4), channel_id=1, source_target_pairs={{0,16},{2,17},{4,18},{6,19},{8,20},{10,21},{12,22},{14,23},{1,24},... | collective-permute-start | bytes 442376 | tf_op jit(solution)/shard_map/ppermute | solution.py:39
  176.4 3.9 %fusion.82 = bf16[96,768]{0,1:T(8,128)(2,1)S(1)} fusion(f32[96,768]{0,1:T(8,128)S(1)} %copy-done.15, bf16[96,3072]{0,1:T(8,128)(2,1)S(1)} %add_convert_fusion.1, bf16[1,768,3072]{2,1,0:T(8,128)(2,1)} %param.9, bf16[96,768]{0,1:T(8,128)(2,1)S(1)} %get-tuple-element.33, f32[96]{0:T(128)S(1)} %get-tuple-element.83, f32[96]{0:T(128)S(1)} %get-tuple-element.82, ...), kind=kOutput, calls=%fused_computation.49 | convolution fusion | flops 453943296 | bytes 6445061 | tf_op jit(solution)/shard_map/dot_general | solution.py:76
  180.4 3.4 %collective-permute-start.13 = (bf16[96,768]{0,1:T(8,128)(2,1)S(1)}, bf16[96,768]{0,1:T(8,128)(2,1)S(1)}, u32[]{:S(2)}, u32[]{:S(2)}) collective-permute-start(bf16[96,768]{0,1:T(8,128)(2,1)S(1)} %fusion.82), channel_id=1, source_target_pairs={{16,0},{17,2},{18,4},{19,6},{20,8},{21,10},{22,12},{23,14},{24,1},... | collective-permute-start | bytes 442376 | tf_op jit(solution)/shard_map/ppermute | solution.py:30
  186.3 5.6 %collective-permute-done.13 = bf16[96,768]{0,1:T(8,128)(2,1)S(1)} collective-permute-done((bf16[96,768]{0,1:T(8,128)(2,1)S(1)}, bf16[96,768]{0,1:T(8,128)(2,1)S(1)}, u32[]{:S(2)}, u32[]{:S(2)}) %collective-permute-start.13) | collective-permute-done | bytes 147488 | tf_op jit(solution)/shard_map/ppermute | solution.py:30
  193.7 20.1 %all_to_all.27 = bf16[4,96,1664]{2,1,0:T(8,128)(2,1)S(1)} all-to-all(bf16[4,96,1664]{2,1,0:T(8,128)(2,1)S(1)} %pad_maximum_fusion.2), channel_id=1, replica_groups={{0,4,8,12},{2,6,10,14},{1,5,9,13},{3,7,11,15},{16,20,24,28},{18,22,26,3..., dimensions={0} | all-to-all | bytes 2555904 | tf_op jit(solution)/shard_map/all_to_all | solution.py:48
  216.6 5.7 %collective-permute-start.14 = (bf16[96,3968]{1,0:T(8,128)(2,1)}, bf16[96,3968]{1,0:T(8,128)(2,1)S(1)}, u32[]{:S(2)}, u32[]{:S(2)}) collective-permute-start(bf16[96,3968]{1,0:T(8,128)(2,1)} %fusion.103), channel_id=1, source_target_pairs={{0,2},{2,0},{4,6},{6,4},{8,10},{10,8},{12,14},{14,12},{1,3},{3,1},... | collective-permute-start | bytes 2285576 | tf_op jit(solution)/shard_map/ppermute | solution.py:43
  222.6 2.1 collective-permute-start.16
  232.0 3.8 %fusion.85 = bf16[96,768]{0,1:T(8,128)(2,1)S(1)} fusion(f32[96,768]{0,1:T(8,128)S(1)} %copy-done.16, bf16[96,3072]{0,1:T(8,128)(2,1)S(1)} %add_convert_fusion, bf16[1,768,3072]{2,1,0:T(8,128)(2,1)} %param.9, bf16[96,768]{0,1:T(8,128)(2,1)} %get-tuple-element.28, f32[96]{0:T(128)S(1)} %get-tuple-element.76, f32[96]{0:T(128)S(1)} %get-tuple-element.75, ...), kind=kOutput, calls=%fused_computation.50 | convolution fusion | flops 453943296 | bytes 6395909 | tf_op jit(solution)/shard_map/dot_general | solution.py:76
  238.8 8.2 %collective-permute-done.17 = bf16[96,768]{0,1:T(8,128)(2,1)S(1)} collective-permute-done((bf16[96,768]{0,1:T(8,128)(2,1)S(1)}, bf16[96,768]{0,1:T(8,128)(2,1)S(1)}, u32[]{:S(2)}, u32[]{:S(2)}) %collective-permute-start.17) | collective-permute-done | bytes 147488 | tf_op jit(solution)/shard_map/ppermute | solution.py:30
  249.7 9.7 %all-to-all-start.4 = ((bf16[16,16,1152]{2,1,0:T(8,128)(2,1)}), bf16[16,16,1152]{2,1,0:T(8,128)(2,1)S(1)}, u32[]{:S(2)}, u32[]{:S(2)}) async-start(bf16[16,16,1152]{2,1,0:T(8,128)(2,1)} %broadcast_in_dim.150), calls=%async_computation.4 | async-start | bytes 1179648 | tf_op jit(solution)/shard_map/all_to_all | solution.py:286
  263.4 3.3 %collective-permute-start.15 = (f32[16,768]{1,0:T(8,128)S(1)}, f32[16,768]{1,0:T(8,128)S(1)}, u32[]{:S(2)}, u32[]{:S(2)}) collective-permute-start(f32[16,768]{1,0:T(8,128)S(1)} %convolution_add_fusion.2), channel_id=1, source_target_pairs={{0,1},{1,0},{2,3},{3,2},{4,5},{5,4},{6,7},{7,6},{8,9},{9,8},{10,11... | collective-permute-start | bytes 147464 | tf_op jit(solution)/shard_map/ppermute | solution.py:283
  266.7 4.7 %all-to-all-done.4 = bf16[16,16,1152]{2,1,0:T(8,128)(2,1)S(1)} async-done(((bf16[16,16,1152]{2,1,0:T(8,128)(2,1)}), bf16[16,16,1152]{2,1,0:T(8,128)(2,1)S(1)}, u32[]{:S(2)}, u32[]{:S(2)}) %all-to-all-start.4) | async-done | bytes 589856 | tf_op jit(solution)/shard_map/all_to_all | solution.py:286
  (406 shorter events, 81.5 us)
Async XLA Ops:
  0.6 19.2 %copy-start = (bf16[1,1,2,48,768]{4,3,2,1,0:T(8,128)(2,1)S(1)}, bf16[1,1,2,48,768]{4,3,2,1,0:T(8,128)(2,1)}, u32[]{:S(2)}) copy-start(bf16[1,1,2,48,768]{4,3,2,1,0:T(8,128)(2,1)} %param.13) | copy-start | bytes 442372
  1.7 7.7 %collective-permute-start.1 = (bf16[48,768]{0,1:T(8,128)(2,1)S(1)}, bf16[48,768]{0,1:T(8,128)(2,1)S(1)}, u32[]{:S(2)}, u32[]{:S(2)}) collective-permute-start(bf16[48,768]{0,1:T(8,128)(2,1)S(1)} %bitcast.290), channel_id=1, source_target_pairs={{0,1},{1,0},{2,3},{3,2},{4,5},{5,4},{6,7},{7,6},{8,9},{9,8},{10,11... | collective-permute-start | bytes 221192 | tf_op jit(solution)/shard_map/ppermute | solution.py:119
  5.4 54.0 %copy-start.23 = (f32[768]{0:T(1024)}, f32[768]{0:T(1024)S(1)}, u32[]{:S(2)}) copy-start(f32[768]{0:T(1024)S(1)} %get-tuple-element.130) | copy-start | bytes 9220
  9.7 31.0 %copy-start.11 = (bf16[96,768]{0,1:T(8,128)(2,1)}, bf16[96,768]{0,1:T(8,128)(2,1)S(1)}, u32[]{:S(2)}) copy-start(bf16[96,768]{0,1:T(8,128)(2,1)S(1)} %get-tuple-element.37) | copy-start | bytes 442372
  15.8 14.4 %all-to-all-start = ((bf16[4,112,896]{2,1,0:T(8,128)(2,1)}), bf16[4,112,896]{2,1,0:T(8,128)(2,1)S(1)}, u32[]{:S(2)}, u32[]{:S(2)}) async-start(bf16[4,112,896]{2,1,0:T(8,128)(2,1)} %fusion.97), calls=%async_computation | async-start | bytes 1605632 | tf_op jit(solution)/shard_map/all_to_all | solution.py:48
  21.9 20.7 %collective-permute-start = (bf16[3,48,768]{2,1,0:T(8,128)(2,1)}, bf16[3,48,768]{2,1,0:T(8,128)(2,1)}, u32[]{:S(2)}, u32[]{:S(2)}) collective-permute-start(bf16[3,48,768]{2,1,0:T(8,128)(2,1)} %copy.353), channel_id=1, source_target_pairs={{0,1},{1,0},{2,3},{3,2},{4,5},{5,4},{6,7},{7,6},{8,9},{9,8},{10,11... | collective-permute-start | bytes 663560 | tf_op jit(solution)/shard_map/ppermute | solution.py:131
  32.7 11.8 %collective-permute-start.3 = (bf16[112,896]{0,1:T(8,128)(2,1)S(1)}, bf16[112,896]{0,1:T(8,128)(2,1)S(1)}, u32[]{:S(2)}, u32[]{:S(2)}) collective-permute-start(bf16[112,896]{0,1:T(8,128)(2,1)S(1)} %fusion.156), channel_id=1, source_target_pairs={{0,2},{2,0},{4,6},{6,4},{8,10},{10,8},{12,14},{14,12},{1,3},{3,1},... | collective-permute-start | bytes 602120 | tf_op jit(solution)/shard_map/ppermute | solution.py:43
  38.5 9.0 %collective-permute-start.4 = (bf16[64,768]{0,1:T(8,128)(2,1)}, bf16[64,768]{0,1:T(8,128)(2,1)S(1)}, u32[]{:S(2)}, u32[]{:S(2)}) collective-permute-start(bf16[64,768]{0,1:T(8,128)(2,1)} %pad_maximum_fusion.3), channel_id=1, source_target_pairs={{0,0},{1,2},{2,4},{3,6},{4,8},{5,10},{6,12},{7,14},{8,1},{9,3},{10... | collective-permute-start | bytes 294920 | tf_op jit(solution)/shard_map/ppermute | solution.py:30
  40.6 7.2 %collective-permute-start.2 = (bf16[96,768]{0,1:T(8,128)(2,1)S(1)}, bf16[96,768]{0,1:T(8,128)(2,1)S(1)}, u32[]{:S(2)}, u32[]{:S(2)}) collective-permute-start(bf16[96,768]{0,1:T(8,128)(2,1)S(1)} %get-tuple-element.37), channel_id=1, source_target_pairs={{0,0},{1,2},{2,4},{3,6},{4,8},{5,10},{6,12},{7,14},{8,1},{9,3},{10... | collective-permute-start | bytes 442376 | tf_op jit(solution)/shard_map/ppermute | solution.py:30
  44.5 14.3 %copy-start.1 = (bf16[3,96,768]{1,2,0:T(8,128)(2,1)}, bf16[3,96,768]{1,2,0:T(8,128)(2,1)S(1)}, u32[]{:S(2)}) copy-start(bf16[3,96,768]{1,2,0:T(8,128)(2,1)S(1)} %maximum_select_fusion) | copy-start | bytes 1327108
  48.4 10.3 %collective-permute-start.5 = (bf16[96,768]{0,1:T(8,128)(2,1)S(1)}, bf16[96,768]{0,1:T(8,128)(2,1)S(1)}, u32[]{:S(2)}, u32[]{:S(2)}) collective-permute-start(bf16[96,768]{0,1:T(8,128)(2,1)S(1)} %get-tuple-element.147), channel_id=1, source_target_pairs={{0,16},{2,17},{4,18},{6,19},{8,20},{10,21},{12,22},{14,23},{1,24},... | collective-permute-start | bytes 442376 | tf_op jit(solution)/shard_map/ppermute | solution.py:39
  89.6 12.2 %copy-start.28 = (f32[96,4]{0,1:T(4,128)}, f32[96,4]{0,1:T(4,128)S(1)}, u32[]{:S(2)}) copy-start(f32[96,4]{0,1:T(4,128)S(1)} %get-tuple-element.74) | copy-start | bytes 4612
  90.5 7.8 %collective-permute-start.6 = (bf16[96,3968]{1,0:T(8,128)(2,1)S(1)}, bf16[96,3968]{1,0:T(8,128)(2,1)S(1)}, u32[]{:S(2)}, u32[]{:S(2)}) collective-permute-start(bf16[96,3968]{1,0:T(8,128)(2,1)S(1)} %fusion.99), channel_id=1, source_target_pairs={{0,2},{2,0},{4,6},{6,4},{8,10},{10,8},{12,14},{14,12},{1,3},{3,1},... | collective-permute-start | bytes 2285576 | tf_op jit(solution)/shard_map/ppermute | solution.py:43
  94.8 10.4 %collective-permute-start.7 = (bf16[96,768]{0,1:T(8,128)(2,1)S(1)}, bf16[96,768]{0,1:T(8,128)(2,1)}, u32[]{:S(2)}, u32[]{:S(2)}) collective-permute-start(bf16[96,768]{0,1:T(8,128)(2,1)S(1)} %get-tuple-element.33), channel_id=1, source_target_pairs={{0,0},{1,2},{2,4},{3,6},{4,8},{5,10},{6,12},{7,14},{8,1},{9,3},{10... | collective-permute-start | bytes 442376 | tf_op jit(solution)/shard_map/ppermute | solution.py:30
  104.3 26.7 %copy-start.38 = (f32[96]{0:T(128)}, f32[96]{0:T(128)S(1)}, u32[]{:S(2)}) copy-start(f32[96]{0:T(128)S(1)} %add_rsqrt_fusion.2) | copy-start | bytes 1156
  106.5 15.2 %collective-permute-start.8 = (bf16[96,768]{0,1:T(8,128)(2,1)S(1)}, bf16[96,768]{0,1:T(8,128)(2,1)S(1)}, u32[]{:S(2)}, u32[]{:S(2)}) collective-permute-start(bf16[96,768]{0,1:T(8,128)(2,1)S(1)} %add_convert_fusion.5), channel_id=1, source_target_pairs={{0,16},{2,17},{4,18},{6,19},{8,20},{10,21},{12,22},{14,23},{1,24},... | collective-permute-start | bytes 442376 | tf_op jit(solution)/shard_map/ppermute | solution.py:39
  119.7 11.4 %collective-permute-start.9 = (bf16[96,768]{0,1:T(8,128)(2,1)S(1)}, bf16[96,768]{0,1:T(8,128)(2,1)S(1)}, u32[]{:S(2)}, u32[]{:S(2)}) collective-permute-start(bf16[96,768]{0,1:T(8,128)(2,1)S(1)} %fusion.79), channel_id=1, source_target_pairs={{16,0},{17,2},{18,4},{19,6},{20,8},{21,10},{22,12},{23,14},{24,1},... | collective-permute-start | bytes 442376 | tf_op jit(solution)/shard_map/ppermute | solution.py:30
  153.7 8.4 %collective-permute-start.10 = (bf16[96,3968]{1,0:T(8,128)(2,1)}, bf16[96,3968]{1,0:T(8,128)(2,1)S(1)}, u32[]{:S(2)}, u32[]{:S(2)}) collective-permute-start(bf16[96,3968]{1,0:T(8,128)(2,1)} %fusion.101), channel_id=1, source_target_pairs={{0,2},{2,0},{4,6},{6,4},{8,10},{10,8},{12,14},{14,12},{1,3},{3,1},... | collective-permute-start | bytes 2285576 | tf_op jit(solution)/shard_map/ppermute | solution.py:43
  159.5 9.6 %collective-permute-start.11 = (bf16[96,768]{0,1:T(8,128)(2,1)}, bf16[96,768]{0,1:T(8,128)(2,1)}, u32[]{:S(2)}, u32[]{:S(2)}) collective-permute-start(bf16[96,768]{0,1:T(8,128)(2,1)} %get-tuple-element.28), channel_id=1, source_target_pairs={{0,0},{1,2},{2,4},{3,6},{4,8},{5,10},{6,12},{7,14},{8,1},{9,3},{10... | collective-permute-start | bytes 442376 | tf_op jit(solution)/shard_map/ppermute | solution.py:30
  170.4 13.3 %collective-permute-start.12 = (bf16[96,768]{0,1:T(8,128)(2,1)S(1)}, bf16[96,768]{0,1:T(8,128)(2,1)S(1)}, u32[]{:S(2)}, u32[]{:S(2)}) collective-permute-start(bf16[96,768]{0,1:T(8,128)(2,1)S(1)} %add_convert_fusion.4), channel_id=1, source_target_pairs={{0,16},{2,17},{4,18},{6,19},{8,20},{10,21},{12,22},{14,23},{1,24},... | collective-permute-start | bytes 442376 | tf_op jit(solution)/shard_map/ppermute | solution.py:39
  180.4 11.5 %collective-permute-start.13 = (bf16[96,768]{0,1:T(8,128)(2,1)S(1)}, bf16[96,768]{0,1:T(8,128)(2,1)S(1)}, u32[]{:S(2)}, u32[]{:S(2)}) collective-permute-start(bf16[96,768]{0,1:T(8,128)(2,1)S(1)} %fusion.82), channel_id=1, source_target_pairs={{16,0},{17,2},{18,4},{19,6},{20,8},{21,10},{22,12},{23,14},{24,1},... | collective-permute-start | bytes 442376 | tf_op jit(solution)/shard_map/ppermute | solution.py:30
  216.6 8.7 %collective-permute-start.14 = (bf16[96,3968]{1,0:T(8,128)(2,1)}, bf16[96,3968]{1,0:T(8,128)(2,1)S(1)}, u32[]{:S(2)}, u32[]{:S(2)}) collective-permute-start(bf16[96,3968]{1,0:T(8,128)(2,1)} %fusion.103), channel_id=1, source_target_pairs={{0,2},{2,0},{4,6},{6,4},{8,10},{10,8},{12,14},{14,12},{1,3},{3,1},... | collective-permute-start | bytes 2285576 | tf_op jit(solution)/shard_map/ppermute | solution.py:43
  222.6 16.2 %collective-permute-start.16 = (bf16[96,768]{0,1:T(8,128)(2,1)S(1)}, bf16[96,768]{0,1:T(8,128)(2,1)}, u32[]{:S(2)}, u32[]{:S(2)}) collective-permute-start(bf16[96,768]{0,1:T(8,128)(2,1)S(1)} %get-tuple-element.21), channel_id=1, source_target_pairs={{0,0},{1,2},{2,4},{3,6},{4,8},{5,10},{6,12},{7,14},{8,1},{9,3},{10... | collective-permute-start | bytes 442376 | tf_op jit(solution)/shard_map/ppermute | solution.py:30
  232.0 15.0 %copy-start.10 = (bf16[96,768]{0,1:T(8,128)(2,1)S(1)}, bf16[96,768]{0,1:T(8,128)(2,1)}, u32[]{:S(2)}) copy-start(bf16[96,768]{0,1:T(8,128)(2,1)} %copy.487) | copy-start | bytes 442372
  235.8 11.2 %collective-permute-start.17 = (bf16[96,768]{0,1:T(8,128)(2,1)S(1)}, bf16[96,768]{0,1:T(8,128)(2,1)S(1)}, u32[]{:S(2)}, u32[]{:S(2)}) collective-permute-start(bf16[96,768]{0,1:T(8,128)(2,1)S(1)} %fusion.85), channel_id=1, source_target_pairs={{16,0},{17,2},{18,4},{19,6},{20,8},{21,10},{22,12},{23,14},{24,1},... | collective-permute-start | bytes 442376 | tf_op jit(solution)/shard_map/ppermute | solution.py:30
  248.1 11.3 %copy-start.13 = (bf16[96,768]{0,1:T(8,128)(2,1)S(1)}, bf16[96,768]{0,1:T(8,128)(2,1)}, u32[]{:S(2)}) copy-start(bf16[96,768]{0,1:T(8,128)(2,1)} %copy-done.11) | copy-start | bytes 442372
  248.1 11.3 %copy-start.46 = (f32[96]{0:T(128)S(1)}, f32[96]{0:T(128)}, u32[]{:S(2)}) copy-start(f32[96]{0:T(128)} %copy-done.44) | copy-start | bytes 1156
  248.1 11.3 %copy-start.54 = (f32[96]{0:T(128)S(1)}, f32[96]{0:T(128)}, u32[]{:S(2)}) copy-start(f32[96]{0:T(128)} %copy-done.52) | copy-start | bytes 1156
  248.3 12.4 %copy-start.40 = (f32[96]{0:T(128)S(1)}, f32[96]{0:T(128)}, u32[]{:S(2)}) copy-start(f32[96]{0:T(128)} %copy-done.38) | copy-start | bytes 1156
  248.3 12.4 %copy-start.49 = (f32[96]{0:T(128)S(1)}, f32[96]{0:T(128)}, u32[]{:S(2)}) copy-start(f32[96]{0:T(128)} %copy-done.47) | copy-start | bytes 1156
  249.7 21.7 %all-to-all-start.4 = ((bf16[16,16,1152]{2,1,0:T(8,128)(2,1)}), bf16[16,16,1152]{2,1,0:T(8,128)(2,1)S(1)}, u32[]{:S(2)}, u32[]{:S(2)}) async-start(bf16[16,16,1152]{2,1,0:T(8,128)(2,1)} %broadcast_in_dim.150), calls=%async_computation.4 | async-start | bytes 1179648 | tf_op jit(solution)/shard_map/all_to_all | solution.py:286
  263.4 9.1 %collective-permute-start.15 = (f32[16,768]{1,0:T(8,128)S(1)}, f32[16,768]{1,0:T(8,128)S(1)}, u32[]{:S(2)}, u32[]{:S(2)}) collective-permute-start(f32[16,768]{1,0:T(8,128)S(1)} %convolution_add_fusion.2), channel_id=1, source_target_pairs={{0,1},{1,0},{2,3},{3,2},{4,5},{5,4},{6,7},{7,6},{8,9},{9,8},{10,11... | collective-permute-start | bytes 147464 | tf_op jit(solution)/shard_map/ppermute | solution.py:283
  (52 other events, 262.1 us)

commit v2 on v1

v2 whole, which is shorter than its diff:
```python
import functools

import jax
import jax.numpy as jnp
from jax import lax
from jax.experimental import pallas as pl
from jax.experimental.pallas import tpu as pltpu
from jax.sharding import PartitionSpec as P

TICKS = 4
CHIPS = 4
EPS = 1e-05
AXES = ("section", "tensor", "dp")
HIGHEST = lax.Precision.HIGHEST
BF = jnp.bfloat16
F32 = jnp.float32

LANES = 128
SQUARE = 8
LOW = 16
GRAD = 32
FIRST = 48
SECOND = 49


def flat(section, tensor, dp):
    return (section * 2 * CHIPS + tensor) * 2 + dp


def owner(block, core):
    return 2 * (block % CHIPS) + core, block // CHIPS


def to_owner(array, sections, back):
    route = []
    for s in range(sections):
        for block in range(2 * CHIPS):
            for half in range(2):
                if s - back >= 0:
                    route.append((flat(s, block, half), flat(s - back, *owner(block, half))))
    return lax.ppermute(array, AXES, route)


def to_next(array, sections):
    route = []
    for s in range(sections - 1):
        for block in range(2 * CHIPS):
            for half in range(2):
                route.append((flat(s, *owner(block, half)), flat(s + 1, block, half)))
    return lax.ppermute(array, AXES, route)


def swap_cores(array):
    return lax.ppermute(array, "tensor", [(i, i ^ 1) for i in range(2 * CHIPS)])


def over_chips(array):
    groups = [[2 * i for i in range(CHIPS)], [2 * i + 1 for i in range(CHIPS)]]
    return lax.all_to_all(array, "tensor", 0, 0, axis_index_groups=groups)


def dot(a, b, **kw):
    return jnp.dot(a, b, preferred_element_type=F32, **kw)


def dot_t(a, b, **kw):
    return lax.dot_general(a, b, (((1,), (1,)), ((), ())), preferred_element_type=F32, **kw)


def t_dot(a, b, **kw):
    return lax.dot_general(a, b, (((0,), (0,)), ((), ())), preferred_element_type=F32, **kw)


def lane(rows):
    return lax.broadcasted_iota(jnp.int32, (rows, LANES), 1)


def between(values, low, high):
    at = lane(values.shape[0])
    return jnp.where((at >= low) & (at < high), values, 0.0)


def pick(values, low, high):
    return jnp.sum(between(values, low, high), axis=1, keepdims=True)


def split(values):
    high = values.astype(BF).astype(F32)
    rest = pltpu.roll(values - high, LANES // 2, 1)
    return jnp.where(lane(values.shape[0]) < LANES // 2, high, rest).astype(BF)


def join(halves):
    wide = halves.astype(F32)
    return wide + pltpu.roll(wide, LANES // 2, 1)


def call(kernel, out, *args, scalars=(), vmem=24):
    return pl.pallas_call(
        kernel,
        out_shape=out,
        in_specs=[pl.BlockSpec(memory_space=pltpu.SMEM)] * len(scalars)
        + [pl.BlockSpec(memory_space=pltpu.VMEM)] * len(args),
        out_specs=jax.tree.map(lambda _: pl.BlockSpec(memory_space=pltpu.VMEM), out),
        compiler_params=pltpu.CompilerParams(vmem_limit_bytes=vmem * 2**20),
    )(*scalars, *args)


def shape(*dims, dtype=F32):
    return jax.ShapeDtypeStruct(dims, dtype)


def forward_kernel(start, flags, arrived, given, gains, w, down, x_out, product, small):
    place = flags[1]
    if start:
        x = given[...]
    else:
        x = jnp.where(flags[0] == 1, given[...], arrived[...])
    x_out[...] = x
    rows, feats = x.shape
    wide = x.astype(F32)
    mid = jnp.sum(wide, axis=1, keepdims=True) / feats
    centered = wide - mid
    square = jnp.sum(centered * centered, axis=1, keepdims=True)
    scaled = centered * gains[...]
    at = lane(rows)
    low = dot(scaled, down[...], precision=HIGHEST)
    low = jnp.where(at == place, mid, low)
    small[0:rows] = jnp.where(at == SQUARE + place, square, low)
    left = scaled.astype(BF)
    if start:
        row = lax.broadcasted_iota(jnp.int32, (2 * CHIPS, feats), 0)
        gain_rows = jnp.where(row == place, gains[...], 0.0)
        high = gain_rows.astype(BF).astype(F32)
        left = jnp.concatenate([left, jnp.concatenate([high, gain_rows - high]).astype(BF)])
        small[rows:] = jnp.concatenate(
            [dot(gain_rows, down[...], precision=HIGHEST), jnp.zeros((2 * CHIPS, LANES), F32)]
        )
    for j in range(CHIPS):
        part = dot(left, w[:, j * feats : (j + 1) * feats])
        if start:
            tail = part[rows : rows + 2 * CHIPS] + part[rows + 2 * CHIPS :]
            high = tail.astype(BF).astype(F32)
            part = jnp.concatenate([part[:rows], high, tail - high])
        product[j] = part.astype(BF)


def pack_kernel(start, flags, product, small, *refs):
    rows, feats = product.shape[1:]
    values = small[...]
    if start:
        parcel = refs[-1]
        columns = feats
    else:
        arrived, output, up, gain_w, mixed, grad_out, parcel = refs
        columns = 2 * feats
        kept = jnp.where(flags[1] == 0, output[...], jnp.zeros((rows, feats), BF))
        grad = jnp.where(flags[0] == 1, kept, arrived[...])
        grad_out[...] = grad
        wide = grad.astype(F32)
        first = jnp.sum(wide * jnp.sum(gain_w[...], axis=0, keepdims=True), axis=1, keepdims=True)
        second = jnp.sum(wide * mixed[...], axis=1, keepdims=True)
        at = lane(rows)
        values = values + pltpu.roll(dot_t(grad, up[...]), GRAD - LOW, 1)
        values = jnp.where(at == FIRST, first, values)
        values = jnp.where(at == SECOND, second, values)
        for j in range(CHIPS):
            parcel[j, :, feats : 2 * feats] = grad
    halves = split(values)
    for j in range(CHIPS):
        parcel[j, :, :feats] = product[j]
        parcel[j, :, columns:] = halves


def gather_kernel(start, got, out):
    feats = (got.shape[2] - LANES) // (1 if start else 2)
    total = got[0, :, :feats].astype(F32)
    values = join(got[0, :, -LANES:])
    for j in range(1, CHIPS):
        total = total + got[j, :, :feats].astype(F32)
        values = values + join(got[j, :, -LANES:])
    out[:, :feats] = total.astype(BF)
    out[:, feats : feats + LANES] = split(values)
    if not start:
        for j in range(CHIPS):
            at = feats + LANES + j * feats
            out[:, at : at + feats] = got[j, :, feats : 2 * feats]


def output_kernel(start, mine, theirs, x, up, *refs):
    rows, feats = x.shape
    if start:
        gain_w, gain_low, output, mixed, stats, sums = refs
        tail = mine[rows:, :feats].astype(F32) + theirs[rows:, :feats].astype(F32)
        gain_w[...] = tail[: 2 * CHIPS] + tail[2 * CHIPS :]
        tail = join(mine[rows:, feats:]) + join(theirs[rows:, feats:])
        gain_low[...] = between(tail[: 2 * CHIPS], LOW, GRAD)
    else:
        gain_w, gain_low, output, mixed, stats, sums = refs
    values = join(mine[:rows, feats : feats + LANES]) + join(theirs[:rows, feats : feats + LANES])
    values = between(values, 0, LANES // 2)
    sums[...] = values
    at = lane(rows)
    width = feats * 2 * CHIPS
    mean = pick(values, 0, SQUARE) / (2 * CHIPS)
    off = jnp.where(at < 2 * CHIPS, values - mean, 0.0)
    square = pick(values, SQUARE, LOW) + feats * jnp.sum(off * off, axis=1, keepdims=True)
    inv = lax.rsqrt(square / width + EPS)
    total = mine[:rows, :feats].astype(F32) + theirs[:rows, :feats].astype(F32)
    low = values
    for j in range(2 * CHIPS):
        total = total + off[:, j : j + 1] * gain_w[j : j + 1, :]
        low = low + off[:, j : j + 1] * gain_low[j : j + 1, :]
    total = inv * total
    low = between(inv * low, LOW, GRAD)
    mixed[...] = total
    stats[...] = jnp.where(at == 0, mean, jnp.where(at == 1, inv, low))
    output[...] = (x[...].astype(F32) + total + dot(low.astype(BF), up[...])).astype(BF)


def backward_kernel(flags, mine, theirs, sums, x, stats, gains, gain_low, w, down, grad_out):
    rows, feats = x.shape
    width = feats * 2 * CHIPS
    values = sums[...]
    low_grad = pltpu.roll(between(values, GRAD, FIRST), LANES - (GRAD - LOW), 1)
    low = between(stats[...], LOW, GRAD)
    low_all = jnp.sum(gain_low[...], axis=0, keepdims=True)
    first = pick(values, FIRST, FIRST + 1) + jnp.sum(low_grad * low_all, axis=1, keepdims=True)
    second = pick(values, SECOND, SECOND + 1) + jnp.sum(low_grad * low, axis=1, keepdims=True)
    mean, inv = pick(stats[...], 0, 1), pick(stats[...], 1, 2)
    xhat = (x[...].astype(F32) - mean) * inv
    grad_norm = dot_t(low_grad, down[...], precision=HIGHEST)
    here = jnp.zeros((rows, feats), F32)
    for j in range(CHIPS):
        at = feats + LANES + j * feats
        grad = mine[:, at : at + feats].astype(F32) + theirs[:, at : at + feats].astype(F32)
        grad = grad.astype(BF)
        grad_norm = grad_norm + dot_t(grad, w[:, j * feats : (j + 1) * feats])
        here = here + jnp.where(flags[0] == j, grad.astype(F32), 0.0)
    grad_x = here + inv * (grad_norm * gains[...] - first / width - xhat * (second / width))
    grad_out[...] = grad_x.astype(BF)


def on_device(
    weight,
    adapter_down_map,
    adapter_up_map,
    gain,
    prior_epoch_input,
    prior_epoch_output,
    initial_step_inputs,
    initial_step_gradients,
    sample_numbers,
):
    del prior_epoch_output
    w = weight[0]
    gains = gain
    order = sample_numbers[0, 0]
    sections = lax.axis_size("section")
    section = lax.axis_index("section")
    tensor = lax.axis_index("tensor")
    half = lax.axis_index("dp")
    core = tensor % 2
    is_first = section == 0
    is_last = section == sections - 1
    toks, feats = initial_step_inputs.shape[1:]
    rank = adapter_up_map.shape[1]
    rows = 2 * toks
    down = jnp.pad(adapter_down_map[0].astype(F32), ((0, 0), (LOW, LANES - LOW - rank)))
    flags_forward = jnp.stack([is_first, tensor]).astype(jnp.int32)
    flags_pack = jnp.stack([is_last, core]).astype(jnp.int32)
    flags_backward = jnp.where(tensor // CHIPS == half, tensor % CHIPS, -1).astype(jnp.int32)[None]

    def both_replicas(mine, theirs):
        return jnp.where(
            half == 0,
            jnp.concatenate([mine, theirs], axis=-2),
            jnp.concatenate([theirs, mine], axis=-2),
        )

    mine = initial_step_inputs[0]
    x = both_replicas(mine, lax.ppermute(mine, "dp", [(0, 1), (1, 0)]))
    given = to_owner(
        jnp.concatenate([initial_step_gradients[0], adapter_up_map[0]], axis=0), sections, 0
    )
    zeros = jnp.zeros((toks, feats), BF)
    grad_arrived = jnp.where(
        core == 0,
        jnp.concatenate([given[:toks], zeros]),
        jnp.concatenate([zeros, given[:toks]]),
    )
    up = jnp.pad(given[toks:], ((LOW, LANES - LOW - rank), (0, 0)))
    chosen = jnp.take(prior_epoch_input[0, 0], order[1:], axis=0)
    theirs = lax.ppermute(
        chosen,
        AXES,
        [(flat(0, t, d), flat(0, t, 1 - d)) for t in range(2 * CHIPS) for d in range(2)],
    )
    first_x = both_replicas(chosen, theirs)

    acc_down = jnp.zeros((LANES, feats), F32)
    acc_up = jnp.zeros((rank, feats), F32)
    block = shape(rows, feats, dtype=BF)
    values = shape(rows, LANES)
    arrived = x
    before = None
    for tick in range(TICKS):
        start = tick == 0
        more = 4 * CHIPS if start else 0
        x, product, small = call(
            functools.partial(forward_kernel, start),
            [block, shape(CHIPS, rows + more, feats, dtype=BF), shape(rows + more, LANES)],
            arrived,
            x if start else first_x[tick - 1],
            gains,
            w,
            down,
            scalars=(flags_forward,),
        )
        x_owned = to_owner(x, sections, 0)
        columns = (1 if start else 2) * feats + LANES
        parcel = shape(CHIPS, rows + more, columns, dtype=BF)
        if start:
            parcel = call(
                functools.partial(pack_kernel, start), parcel, product, small, scalars=(flags_pack,)
            )
        else:
            grad_part, parcel = call(
                functools.partial(pack_kernel, start),
                [block, parcel],
                product,
                small,
                grad_arrived,
                output,
                up,
                gain_w,
                mixed,
                scalars=(flags_pack,),
            )
            acc_up = acc_up + t_dot(low_b, grad_part)
        got = over_chips(parcel)
        own = call(
            functools.partial(gather_kernel, start),
            shape(rows + more, feats + LANES + (0 if start else CHIPS * feats), dtype=BF),
            got,
        )
        other = swap_cores(own)
        out = [block, shape(rows, feats), values, values]
        if start:
            gain_w, gain_low, output, mixed, stats, sums = call(
                functools.partial(output_kernel, start),
                [shape(2 * CHIPS, feats), shape(2 * CHIPS, LANES)] + out,
                own,
                other,
                x_owned,
                up,
            )
        else:
            output, mixed, stats, sums = call(
                functools.partial(output_kernel, start),
                out,
                own,
                other,
                x_owned,
                up,
                gain_w,
                gain_low,
            )
        if tick < TICKS - 1:
            arrived = to_next(output, sections)
        low_b = stats[:, LOW : LOW + rank].astype(BF)
        if not start:
            x_was, stats_was = before
            grad_x = call(
                backward_kernel,
                block,
                own,
                other,
                sums,
                x_was,
                stats_was,
                gains,
                gain_low,
                w,
                down,
                scalars=(flags_backward,),
            )
            grad_arrived = to_owner(grad_x, sections, 1)
            normed = (x_was.astype(F32) - stats_was[:, 0:1]) * stats_was[:, 1:2] * gains
            acc_down = acc_down + t_dot(sums, normed, precision=HIGHEST)
        before = (x, stats)

    acc_down = acc_down[GRAD : GRAD + rank]
    acc_other = lax.ppermute(acc_down, "dp", [(0, 1), (1, 0)])
    kept = jnp.where(core == 0, output, jnp.zeros_like(output))
    grad_part = jnp.where(is_last, kept, grad_arrived)
    acc_up = acc_up + t_dot(low_b, grad_part)
    turned = jnp.pad(dot_t(up[LOW : LOW + rank], grad_part), ((0, 0), (0, LANES - rows)))
    high = lax.reduce_precision(turned, 8, 7)
    parcel = jnp.concatenate([acc_up.astype(BF), high.astype(BF), (turned - high).astype(BF)], 1)
    got = lax.all_to_all(
        jnp.broadcast_to(parcel, (4 * CHIPS,) + parcel.shape), ("tensor", "dp"), 0, 0
    )
    turned = jnp.sum(got[:, :, feats:].astype(F32), axis=0)
    low_grad = (turned[:, :LANES] + turned[:, LANES:])[:, :rows]
    normed = (x.astype(F32) - stats[:, 0:1]) * stats[:, 1:2] * gains
    total_down = acc_down + acc_other + dot(low_grad, normed, precision=HIGHEST)
    at = 2 * (2 * (tensor % CHIPS)) + tensor // CHIPS
    total_up = lax.dynamic_index_in_dim(got, at, 0, False)[:, :feats].astype(F32)
    total_up = total_up + lax.dynamic_index_in_dim(got, at + 2, 0, False)[:, :feats].astype(F32)
    return ((total_down / rows).T.astype(BF)[None], (total_up / rows).astype(BF)[None])


def solution(mesh):
    in_specs = (
        P("section", "tensor", "dp"),
        P("section", "tensor", None),
        P("section", None, "tensor"),
        P("section", "tensor"),
        P("section", "dp", None, None, "tensor"),
        P("section", "dp", None, None, "tensor"),
        P("section", "dp", "tensor"),
        P("section", "dp", "tensor"),
        P("section", "dp", None),
    )
    out_specs = (P("section", "tensor", None), P("section", None, "tensor"))
    return jax.shard_map(
        on_device, mesh=mesh, in_specs=in_specs, out_specs=out_specs, check_vma=False
    )
```

time: 276 us -> 232 us (0.84)
  the two profiles are of different devices: /device:TPU:113 before, /device:TPU:241 now
where the time goes in v2:
time: 232 us; the launch traced here: 230 us
  starting transfers between devices  87.3 us (38%)
  waiting for transfers between devices  59.5 us (26%)
  blocking collectives  37.9 us (16%)
  Pallas kernels  22.9 us (10%)
  local copies, waits for them, and re-layouts  14.8 us (6%)
  matrix products  4.6 us (2%)
    all_to_all x2, blocking collectives, over_chips(): return lax.all_to_all(array, 'tensor', 0, 0, axis_index_groups=groups)  37.9 us
    ppermute x8, waiting for transfers between devices, to_owner(): return lax.ppermute(array, AXES, route)  31.5 us
    ppermute x8, starting transfers between devices, to_owner(): return lax.ppermute(array, AXES, route)  23.6 us
    pallas_call x19, Pallas kernels, call(): pl.pallas_call(kernel, out_shape=out, in_specs=[pl.BlockSpec(memory_space...  22.9 us
    ppermute x4, starting transfers between devices, swap_cores(): return lax.ppermute(array, 'tensor', [(i, i ^ 1) for i in range(2 * CHIPS)])  19.7 us
    ppermute x3, starting transfers between devices, to_next(): return lax.ppermute(array, AXES, route)  18.6 us
    all_to_all x2, waiting for transfers between devices, over_chips(): return lax.all_to_all(array, 'tensor', 0, 0, axis_index_groups=groups)  16.2 us
    unnamed x29, local copies, waits for them, and re-layouts  12.6 us
  transfers between devices with their start and end apart: 21, of which 12 were waited for; matrix products, arithmetic and copies ran while one was open for 3% of the time, Pallas kernels for 3%

profile of v2, /device:TPU:241, one launch (start us, length us, event | category | flops | bytes accessed | tf_op | source)
XLA Modules:
  0.0 230.3 jit_solution(5069770690697332721)
XLA Ops:
  0.7 3.0 %collective-permute-start = (bf16[48,768]{1,0:T(8,128)(2,1)}, bf16[48,768]{1,0:T(8,128)(2,1)S(1)}, u32[]{:S(2)}, u32[]{:S(2)}) collective-permute-start(bf16[48,768]{1,0:T(8,128)(2,1)} %bitcast.51), channel_id=1, source_target_pairs={{0,1},{1,0},{2,3},{3,2},{4,5},{5,4},{6,7},{7,6},{8,9},{9,8},{10,11... | collective-permute-start | bytes 221192 | tf_op jit(solution)/shard_map/ppermute | solution.py:282
  6.3 2.3 %copy-done.1 = bf16[1,768,3072]{2,1,0:T(8,128)(2,1)S(1)} copy-done((bf16[1,768,3072]{2,1,0:T(8,128)(2,1)S(1)}, bf16[1,768,3072]{2,1,0:T(8,128)(2,1)}, u32[]{:S(2)}) %copy-start.1) | copy-done | bytes 4718616
  12.1 4.1 %all-to-all-start = ((bf16[4,112,896]{2,1,0:T(8,128)(2,1)}), bf16[4,112,896]{2,1,0:T(8,128)(2,1)S(1)}, u32[]{:S(2)}, u32[]{:S(2)}) async-start(bf16[4,112,896]{2,1,0:T(8,128)(2,1)} %shard_map.96), calls=%async_computation | async-start | bytes 1605632 | tf_op jit(solution)/shard_map/all_to_all | solution.py:59
  17.1 5.5 %collective-permute-start.3 = (bf16[64,768]{1,0:T(8,128)(2,1)S(1)}, bf16[64,768]{1,0:T(8,128)(2,1)S(1)}, u32[]{:S(2)}, u32[]{:S(2)}) collective-permute-start(bf16[64,768]{1,0:T(8,128)(2,1)S(1)} %pad_maximum_fusion), channel_id=1, source_target_pairs={{0,0},{1,2},{2,4},{3,6},{4,8},{5,10},{6,12},{7,14},{8,1},{9,3},{10... | collective-permute-start | bytes 294920 | tf_op jit(solution)/shard_map/ppermute | solution.py:41
  22.6 3.4 %collective-permute-start.2 = (bf16[96,768]{1,0:T(8,128)(2,1)S(1)}, bf16[96,768]{1,0:T(8,128)(2,1)S(1)}, u32[]{:S(2)}, u32[]{:S(2)}) collective-permute-start(bf16[96,768]{1,0:T(8,128)(2,1)S(1)} %get-tuple-element.38.x), channel_id=1, source_target_pairs={{0,0},{1,2},{2,4},{3,6},{4,8},{5,10},{6,12},{7,14},{8,1},{9,3},{10... | collective-permute-start | bytes 442376 | tf_op jit(solution)/shard_map/ppermute | solution.py:41
  26.6 5.1 %collective-permute-start.1 = (bf16[112,896]{1,0:T(8,128)(2,1)S(1)}, bf16[112,896]{1,0:T(8,128)(2,1)S(1)}, u32[]{:S(2)}, u32[]{:S(2)}) collective-permute-start(bf16[112,896]{1,0:T(8,128)(2,1)S(1)} %shard_map.97.mine), channel_id=1, source_target_pairs={{0,2},{2,0},{4,6},{6,4},{8,10},{10,8},{12,14},{14,12},{1,3},{3,1},... | collective-permute-start | bytes 602120 | tf_op jit(solution)/shard_map/ppermute | solution.py:54
  33.9 6.1 %collective-permute-start.4 = (bf16[96,768]{1,0:T(8,128)(2,1)S(1)}, bf16[96,768]{1,0:T(8,128)(2,1)S(1)}, u32[]{:S(2)}, u32[]{:S(2)}) collective-permute-start(bf16[96,768]{1,0:T(8,128)(2,1)S(1)} %get-tuple-element.39.refs_1_), channel_id=1, source_target_pairs={{0,16},{2,17},{4,18},{6,19},{8,20},{10,21},{12,22},{14,23},{1,24},... | collective-permute-start | bytes 442376 | tf_op jit(solution)/shard_map/ppermute | solution.py:50
  40.1 3.8 %collective-permute-done.4.arrived = bf16[96,768]{1,0:T(8,128)(2,1)S(1)} collective-permute-done((bf16[96,768]{1,0:T(8,128)(2,1)S(1)}, bf16[96,768]{1,0:T(8,128)(2,1)S(1)}, u32[]{:S(2)}, u32[]{:S(2)}) %collective-permute-start.4) | collective-permute-done | bytes 147488 | tf_op jit(solution)/shard_map/ppermute | solution.py:50
  43.9 2.3 %copy-done.2 = bf16[1,768,3072]{2,1,0:T(8,128)(2,1)S(1)} copy-done((bf16[1,768,3072]{2,1,0:T(8,128)(2,1)S(1)}, bf16[1,768,3072]{2,1,0:T(8,128)(2,1)}, u32[]{:S(2)}) %copy-start.2) | copy-done | bytes 4718616
  48.9 20.2 %all_to_all.25.got = bf16[4,96,1664]{2,1,0:T(8,128)(2,1)S(1)} all-to-all(bf16[4,96,1664]{2,1,0:T(8,128)(2,1)S(1)} %get-tuple-element.44), channel_id=1, replica_groups={{0,4,8,12},{2,6,10,14},{1,5,9,13},{3,7,11,15},{16,20,24,28},{18,22,26,3..., dimensions={0} | all-to-all | bytes 2555904 | tf_op jit(solution)/shard_map/all_to_all | solution.py:59
  69.3 4.3 %collective-permute-start.6 = (bf16[96,3968]{1,0:T(8,128)(2,1)S(1)}, bf16[96,3968]{1,0:T(8,128)(2,1)S(1)}, u32[]{:S(2)}, u32[]{:S(2)}) collective-permute-start(bf16[96,3968]{1,0:T(8,128)(2,1)S(1)} %shard_map.101.mine), channel_id=1, source_target_pairs={{0,2},{2,0},{4,6},{6,4},{8,10},{10,8},{12,14},{14,12},{1,3},{3,1},... | collective-permute-start | bytes 2285576 | tf_op jit(solution)/shard_map/ppermute | solution.py:54
  75.8 4.9 %collective-permute-done.7.x = bf16[96,768]{1,0:T(8,128)(2,1)S(1)} collective-permute-done((bf16[96,768]{1,0:T(8,128)(2,1)S(1)}, bf16[96,768]{1,0:T(8,128)(2,1)S(1)}, u32[]{:S(2)}, u32[]{:S(2)}) %collective-permute-start.7) | collective-permute-done | bytes 147488 | tf_op jit(solution)/shard_map/ppermute | solution.py:41
  81.3 8.9 %collective-permute-start.8 = (bf16[96,768]{1,0:T(8,128)(2,1)S(1)}, bf16[96,768]{1,0:T(8,128)(2,1)S(1)}, u32[]{:S(2)}, u32[]{:S(2)}) collective-permute-start(bf16[96,768]{1,0:T(8,128)(2,1)S(1)} %get-tuple-element.49.refs_1_), channel_id=1, source_target_pairs={{0,16},{2,17},{4,18},{6,19},{8,20},{10,21},{12,22},{14,23},{1,24},... | collective-permute-start | bytes 442376 | tf_op jit(solution)/shard_map/ppermute | solution.py:50
  90.2 2.3 %copy-done.3 = bf16[1,768,3072]{2,1,0:T(8,128)(2,1)S(1)} copy-done((bf16[1,768,3072]{2,1,0:T(8,128)(2,1)S(1)}, bf16[1,768,3072]{2,1,0:T(8,128)(2,1)}, u32[]{:S(2)}) %copy-start.3) | copy-done | bytes 4718616
  96.5 2.3 %copy-done.4 = bf16[1,768,3072]{2,1,0:T(8,128)(2,1)S(1)} copy-done((bf16[1,768,3072]{2,1,0:T(8,128)(2,1)S(1)}, bf16[1,768,3072]{2,1,0:T(8,128)(2,1)}, u32[]{:S(2)}) %copy-start.4) | copy-done | bytes 4718616
  100.6 3.3 %collective-permute-done.9.refs_0_ = bf16[96,768]{1,0:T(8,128)(2,1)S(1)} collective-permute-done((bf16[96,768]{1,0:T(8,128)(2,1)S(1)}, bf16[96,768]{1,0:T(8,128)(2,1)S(1)}, u32[]{:S(2)}, u32[]{:S(2)}) %collective-permute-start.9) | collective-permute-done | bytes 147488 | tf_op jit(solution)/shard_map/ppermute | solution.py:41
  104.8 17.6 %all_to_all.26.got = bf16[4,96,1664]{2,1,0:T(8,128)(2,1)S(1)} all-to-all(bf16[4,96,1664]{2,1,0:T(8,128)(2,1)S(1)} %get-tuple-element.53), channel_id=1, replica_groups={{0,4,8,12},{2,6,10,14},{1,5,9,13},{3,7,11,15},{16,20,24,28},{18,22,26,3..., dimensions={0} | all-to-all | bytes 2555904 | tf_op jit(solution)/shard_map/all_to_all | solution.py:59
  122.6 5.8 %collective-permute-start.10 = (bf16[96,3968]{1,0:T(8,128)(2,1)S(1)}, bf16[96,3968]{1,0:T(8,128)(2,1)S(1)}, u32[]{:S(2)}, u32[]{:S(2)}) collective-permute-start(bf16[96,3968]{1,0:T(8,128)(2,1)S(1)} %shard_map.106.mine), channel_id=1, source_target_pairs={{0,2},{2,0},{4,6},{6,4},{8,10},{10,8},{12,14},{14,12},{1,3},{3,1},... | collective-permute-start | bytes 2285576 | tf_op jit(solution)/shard_map/ppermute | solution.py:54
  128.4 2.1 collective-permute-start.11
  130.5 6.5 %collective-permute-done.11.x = bf16[96,768]{1,0:T(8,128)(2,1)S(1)} collective-permute-done((bf16[96,768]{1,0:T(8,128)(2,1)S(1)}, bf16[96,768]{1,0:T(8,128)(2,1)S(1)}, u32[]{:S(2)}, u32[]{:S(2)}) %collective-permute-start.11) | collective-permute-done | bytes 147488 | tf_op jit(solution)/shard_map/ppermute | solution.py:41
  137.6 3.6 %collective-permute-start.12 = (bf16[96,768]{1,0:T(8,128)(2,1)S(1)}, bf16[96,768]{1,0:T(8,128)(2,1)S(1)}, u32[]{:S(2)}, u32[]{:S(2)}) collective-permute-start(bf16[96,768]{1,0:T(8,128)(2,1)S(1)} %get-tuple-element.57.refs_1_), channel_id=1, source_target_pairs={{0,16},{2,17},{4,18},{6,19},{8,20},{10,21},{12,22},{14,23},{1,24},... | collective-permute-start | bytes 442376 | tf_op jit(solution)/shard_map/ppermute | solution.py:50
  143.3 4.6 %collective-permute-start.13 = (bf16[96,768]{1,0:T(8,128)(2,1)S(1)}, bf16[96,768]{1,0:T(8,128)(2,1)S(1)}, u32[]{:S(2)}, u32[]{:S(2)}) collective-permute-start(bf16[96,768]{1,0:T(8,128)(2,1)S(1)} %shard_map.109), channel_id=1, source_target_pairs={{16,0},{17,2},{18,4},{19,6},{20,8},{21,10},{22,12},{23,14},{24,1},... | collective-permute-start | bytes 442376 | tf_op jit(solution)/shard_map/ppermute | solution.py:41
  149.8 2.8 %collective-permute-done.13.refs_0_ = bf16[96,768]{1,0:T(8,128)(2,1)S(1)} collective-permute-done((bf16[96,768]{1,0:T(8,128)(2,1)S(1)}, bf16[96,768]{1,0:T(8,128)(2,1)S(1)}, u32[]{:S(2)}, u32[]{:S(2)}) %collective-permute-start.13) | collective-permute-done | bytes 147488 | tf_op jit(solution)/shard_map/ppermute | solution.py:41
  154.5 4.4 %all-to-all-start.3 = ((bf16[4,96,1664]{2,1,0:T(8,128)(2,1)}), bf16[4,96,1664]{2,1,0:T(8,128)(2,1)S(1)}, u32[]{:S(2)}, u32[]{:S(2)}) async-start(bf16[4,96,1664]{2,1,0:T(8,128)(2,1)} %get-tuple-element.61), calls=%async_computation.3 | async-start | bytes 2555904 | tf_op jit(solution)/shard_map/all_to_all | solution.py:59
  159.1 15.8 %all-to-all-done.3.got = bf16[4,96,1664]{2,1,0:T(8,128)(2,1)S(1)} async-done(((bf16[4,96,1664]{2,1,0:T(8,128)(2,1)}), bf16[4,96,1664]{2,1,0:T(8,128)(2,1)S(1)}, u32[]{:S(2)}, u32[]{:S(2)}) %all-to-all-start.3) | async-done | bytes 1277984 | tf_op jit(solution)/shard_map/all_to_all | solution.py:59
  175.1 4.4 %collective-permute-start.14 = (bf16[96,3968]{1,0:T(8,128)(2,1)S(1)}, bf16[96,3968]{1,0:T(8,128)(2,1)S(1)}, u32[]{:S(2)}, u32[]{:S(2)}) collective-permute-start(bf16[96,3968]{1,0:T(8,128)(2,1)S(1)} %shard_map.111.mine), channel_id=1, source_target_pairs={{0,2},{2,0},{4,6},{6,4},{8,10},{10,8},{12,14},{14,12},{1,3},{3,1},... | collective-permute-start | bytes 2285576 | tf_op jit(solution)/shard_map/ppermute | solution.py:54
  182.9 6.8 %collective-permute-done.15.x = bf16[96,768]{1,0:T(8,128)(2,1)S(1)} collective-permute-done((bf16[96,768]{1,0:T(8,128)(2,1)S(1)}, bf16[96,768]{1,0:T(8,128)(2,1)S(1)}, u32[]{:S(2)}, u32[]{:S(2)}) %collective-permute-start.15) | collective-permute-done | bytes 147488 | tf_op jit(solution)/shard_map/ppermute | solution.py:41
  191.0 2.3 %copy-done.5 = bf16[1,768,3072]{2,1,0:T(8,128)(2,1)S(1)} copy-done((bf16[1,768,3072]{2,1,0:T(8,128)(2,1)S(1)}, bf16[1,768,3072]{2,1,0:T(8,128)(2,1)}, u32[]{:S(2)}) %copy-start.5) | copy-done | bytes 4718616
  198.1 7.3 %collective-permute-done.17 = bf16[96,768]{1,0:T(8,128)(2,1)S(1)} collective-permute-done((bf16[96,768]{1,0:T(8,128)(2,1)S(1)}, bf16[96,768]{1,0:T(8,128)(2,1)S(1)}, u32[]{:S(2)}, u32[]{:S(2)}) %collective-permute-start.17) | collective-permute-done | bytes 147488 | tf_op jit(solution)/shard_map/ppermute | solution.py:41
  207.7 9.9 %all-to-all-start.4 = ((bf16[16,16,1024]{2,1,0:T(8,128)(2,1)}), bf16[16,16,1024]{2,1,0:T(8,128)(2,1)S(1)}, u32[]{:S(2)}, u32[]{:S(2)}) async-start(bf16[16,16,1024]{2,1,0:T(8,128)(2,1)} %broadcast_in_dim.30), calls=%async_computation.4 | async-start | bytes 1048576 | tf_op jit(solution)/shard_map/all_to_all | solution.py:401
  218.3 3.3 %collective-permute-start.16 = (f32[16,768]{1,0:T(8,128)S(1)}, f32[16,768]{1,0:T(8,128)S(1)}, u32[]{:S(2)}, u32[]{:S(2)}) collective-permute-start(f32[16,768]{1,0:T(8,128)S(1)} %slice_add_fusion), channel_id=1, source_target_pairs={{0,1},{1,0},{2,3},{3,2},{4,5},{5,4},{6,7},{7,6},{8,9},{9,8},{10,11... | collective-permute-start | bytes 147464 | tf_op jit(solution)/shard_map/ppermute | solution.py:394
  221.7 6.9 %all-to-all-done.4 = bf16[16,16,1024]{2,1,0:T(8,128)(2,1)S(1)} async-done(((bf16[16,16,1024]{2,1,0:T(8,128)(2,1)}), bf16[16,16,1024]{2,1,0:T(8,128)(2,1)S(1)}, u32[]{:S(2)}, u32[]{:S(2)}) %all-to-all-start.4) | async-done | bytes 524320 | tf_op jit(solution)/shard_map/all_to_all | solution.py:401
  (99 shorter events, 42.9 us)
Async XLA Ops:
  0.6 5.0 %copy-start = (bf16[1,1,2,48,768]{4,3,2,1,0:T(8,128)(2,1)S(1)}, bf16[1,1,2,48,768]{4,3,2,1,0:T(8,128)(2,1)}, u32[]{:S(2)}) copy-start(bf16[1,1,2,48,768]{4,3,2,1,0:T(8,128)(2,1)} %param.13) | copy-start | bytes 442372
  0.6 5.6 %copy-start.9 = (bf16[1,48,768]{2,1,0:T(8,128)(2,1)S(1)}, bf16[1,48,768]{2,1,0:T(8,128)(2,1)}, u32[]{:S(2)}) copy-start(bf16[1,48,768]{2,1,0:T(8,128)(2,1)} %param.14) | copy-start | bytes 221188
  0.7 5.6 %copy-start.6 = (f32[1,768]{1,0:T(1,128)S(1)}, f32[1,768]{1,0:T(1,128)}, u32[]{:S(2)}) copy-start(f32[1,768]{1,0:T(1,128)} %gains.13) | copy-start | bytes 9220
  0.7 5.6 %collective-permute-start = (bf16[48,768]{1,0:T(8,128)(2,1)}, bf16[48,768]{1,0:T(8,128)(2,1)S(1)}, u32[]{:S(2)}, u32[]{:S(2)}) collective-permute-start(bf16[48,768]{1,0:T(8,128)(2,1)} %bitcast.51), channel_id=1, source_target_pairs={{0,1},{1,0},{2,3},{3,2},{4,5},{5,4},{6,7},{7,6},{8,9},{9,8},{10,11... | collective-permute-start | bytes 221192 | tf_op jit(solution)/shard_map/ppermute | solution.py:282
  6.3 2.3 %copy-start.1 = (bf16[1,768,3072]{2,1,0:T(8,128)(2,1)S(1)}, bf16[1,768,3072]{2,1,0:T(8,128)(2,1)}, u32[]{:S(2)}) copy-start(bf16[1,768,3072]{2,1,0:T(8,128)(2,1)} %param.9) | copy-start | bytes 14155780
  10.5 5.7 %copy-start.11 = (s32[1,1,4]{2,1,0:T(1,128)S(1)}, s32[1,1,4]{2,1,0:T(1,128)}, u32[]{:S(2)}) copy-start(s32[1,1,4]{2,1,0:T(1,128)} %param.16) | copy-start | bytes 52
  12.1 5.0 %copy-start.8 = (bf16[1,48,768]{2,1,0:T(8,128)(2,1)S(1)}, bf16[1,48,768]{2,1,0:T(8,128)(2,1)}, u32[]{:S(2)}) copy-start(bf16[1,48,768]{2,1,0:T(8,128)(2,1)} %param.15) | copy-start | bytes 221188
  12.1 5.0 %copy-start.10 = (bf16[1,16,768]{2,1,0:T(8,128)(2,1)S(1)}, bf16[1,16,768]{2,1,0:T(8,128)(2,1)}, u32[]{:S(2)}) copy-start(bf16[1,16,768]{2,1,0:T(8,128)(2,1)} %param.11) | copy-start | bytes 73732
  12.1 14.4 %all-to-all-start = ((bf16[4,112,896]{2,1,0:T(8,128)(2,1)}), bf16[4,112,896]{2,1,0:T(8,128)(2,1)S(1)}, u32[]{:S(2)}, u32[]{:S(2)}) async-start(bf16[4,112,896]{2,1,0:T(8,128)(2,1)} %shard_map.96), calls=%async_computation | async-start | bytes 1605632 | tf_op jit(solution)/shard_map/all_to_all | solution.py:59
  16.4 15.4 %collective-permute-start.5 = (bf16[3,48,768]{2,1,0:T(8,128)(2,1)S(1)}, bf16[3,48,768]{2,1,0:T(8,128)(2,1)S(1)}, u32[]{:S(2)}, u32[]{:S(2)}) collective-permute-start(bf16[3,48,768]{2,1,0:T(8,128)(2,1)S(1)} %broadcast_select_fusion), channel_id=1, source_target_pairs={{0,1},{1,0},{2,3},{3,2},{4,5},{5,4},{6,7},{7,6},{8,9},{9,8},{10,11... | collective-permute-start | bytes 663560 | tf_op jit(solution)/shard_map/ppermute | solution.py:294
  17.1 8.9 %collective-permute-start.3 = (bf16[64,768]{1,0:T(8,128)(2,1)S(1)}, bf16[64,768]{1,0:T(8,128)(2,1)S(1)}, u32[]{:S(2)}, u32[]{:S(2)}) collective-permute-start(bf16[64,768]{1,0:T(8,128)(2,1)S(1)} %pad_maximum_fusion), channel_id=1, source_target_pairs={{0,0},{1,2},{2,4},{3,6},{4,8},{5,10},{6,12},{7,14},{8,1},{9,3},{10... | collective-permute-start | bytes 294920 | tf_op jit(solution)/shard_map/ppermute | solution.py:41
  22.6 9.3 %collective-permute-start.2 = (bf16[96,768]{1,0:T(8,128)(2,1)S(1)}, bf16[96,768]{1,0:T(8,128)(2,1)S(1)}, u32[]{:S(2)}, u32[]{:S(2)}) collective-permute-start(bf16[96,768]{1,0:T(8,128)(2,1)S(1)} %get-tuple-element.38.x), channel_id=1, source_target_pairs={{0,0},{1,2},{2,4},{3,6},{4,8},{5,10},{6,12},{7,14},{8,1},{9,3},{10... | collective-permute-start | bytes 442376 | tf_op jit(solution)/shard_map/ppermute | solution.py:41
  26.0 7.9 %copy-start.7 = (bf16[64,768]{1,0:T(8,128)(2,1)}, bf16[64,768]{1,0:T(8,128)(2,1)S(1)}, u32[]{:S(2)}) copy-start(bf16[64,768]{1,0:T(8,128)(2,1)S(1)} %collective-permute-done.3) | copy-start | bytes 294916
  26.6 6.2 %collective-permute-start.1 = (bf16[112,896]{1,0:T(8,128)(2,1)S(1)}, bf16[112,896]{1,0:T(8,128)(2,1)S(1)}, u32[]{:S(2)}, u32[]{:S(2)}) collective-permute-start(bf16[112,896]{1,0:T(8,128)(2,1)S(1)} %shard_map.97.mine), channel_id=1, source_target_pairs={{0,2},{2,0},{4,6},{6,4},{8,10},{10,8},{12,14},{14,12},{1,3},{3,1},... | collective-permute-start | bytes 602120 | tf_op jit(solution)/shard_map/ppermute | solution.py:54
  33.9 10.0 %collective-permute-start.4 = (bf16[96,768]{1,0:T(8,128)(2,1)S(1)}, bf16[96,768]{1,0:T(8,128)(2,1)S(1)}, u32[]{:S(2)}, u32[]{:S(2)}) collective-permute-start(bf16[96,768]{1,0:T(8,128)(2,1)S(1)} %get-tuple-element.39.refs_1_), channel_id=1, source_target_pairs={{0,16},{2,17},{4,18},{6,19},{8,20},{10,21},{12,22},{14,23},{1,24},... | collective-permute-start | bytes 442376 | tf_op jit(solution)/shard_map/ppermute | solution.py:50
  69.3 11.4 %collective-permute-start.6 = (bf16[96,3968]{1,0:T(8,128)(2,1)S(1)}, bf16[96,3968]{1,0:T(8,128)(2,1)S(1)}, u32[]{:S(2)}, u32[]{:S(2)}) collective-permute-start(bf16[96,3968]{1,0:T(8,128)(2,1)S(1)} %shard_map.101.mine), channel_id=1, source_target_pairs={{0,2},{2,0},{4,6},{6,4},{8,10},{10,8},{12,14},{14,12},{1,3},{3,1},... | collective-permute-start | bytes 2285576 | tf_op jit(solution)/shard_map/ppermute | solution.py:54
  73.7 7.0 %collective-permute-start.7 = (bf16[96,768]{1,0:T(8,128)(2,1)S(1)}, bf16[96,768]{1,0:T(8,128)(2,1)S(1)}, u32[]{:S(2)}, u32[]{:S(2)}) collective-permute-start(bf16[96,768]{1,0:T(8,128)(2,1)S(1)} %get-tuple-element.45.x), channel_id=1, source_target_pairs={{0,0},{1,2},{2,4},{3,6},{4,8},{5,10},{6,12},{7,14},{8,1},{9,3},{10... | collective-permute-start | bytes 442376 | tf_op jit(solution)/shard_map/ppermute | solution.py:41
  81.3 15.2 %collective-permute-start.8 = (bf16[96,768]{1,0:T(8,128)(2,1)S(1)}, bf16[96,768]{1,0:T(8,128)(2,1)S(1)}, u32[]{:S(2)}, u32[]{:S(2)}) collective-permute-start(bf16[96,768]{1,0:T(8,128)(2,1)S(1)} %get-tuple-element.49.refs_1_), channel_id=1, source_target_pairs={{0,16},{2,17},{4,18},{6,19},{8,20},{10,21},{12,22},{14,23},{1,24},... | collective-permute-start | bytes 442376 | tf_op jit(solution)/shard_map/ppermute | solution.py:50
  90.2 2.3 %copy-start.3 = (bf16[1,768,3072]{2,1,0:T(8,128)(2,1)S(1)}, bf16[1,768,3072]{2,1,0:T(8,128)(2,1)}, u32[]{:S(2)}) copy-start(bf16[1,768,3072]{2,1,0:T(8,128)(2,1)} %param.9) | copy-start | bytes 14155780
  94.6 9.3 %collective-permute-start.9 = (bf16[96,768]{1,0:T(8,128)(2,1)S(1)}, bf16[96,768]{1,0:T(8,128)(2,1)S(1)}, u32[]{:S(2)}, u32[]{:S(2)}) collective-permute-start(bf16[96,768]{1,0:T(8,128)(2,1)S(1)} %shard_map.104), channel_id=1, source_target_pairs={{16,0},{17,2},{18,4},{19,6},{20,8},{21,10},{22,12},{23,14},{24,1},... | collective-permute-start | bytes 442376 | tf_op jit(solution)/shard_map/ppermute | solution.py:41
  98.9 42.4 %slice-start = ((s8[4718592]{0:T(1024)(128)(4,1)}), s8[4194304]{0:T(1024)(128)(4,1)S(1)}, s32[]{:S(2)}) async-start(s8[4718592]{0:T(1024)(128)(4,1)} %bitcast.44), calls=%async_computation.5 | async-start | bytes 8388608
  103.9 37.4 %slice-start.1 = ((s8[4718592]{0:T(1024)(128)(4,1)}), s8[524288]{0:T(1024)(128)(4,1)S(1)}, s32[]{:S(2)}) async-start(s8[4718592]{0:T(1024)(128)(4,1)} %bitcast.44), calls=%async_computation.6 | async-start | bytes 1048576
  122.6 14.4 %collective-permute-start.10 = (bf16[96,3968]{1,0:T(8,128)(2,1)S(1)}, bf16[96,3968]{1,0:T(8,128)(2,1)S(1)}, u32[]{:S(2)}, u32[]{:S(2)}) collective-permute-start(bf16[96,3968]{1,0:T(8,128)(2,1)S(1)} %shard_map.106.mine), channel_id=1, source_target_pairs={{0,2},{2,0},{4,6},{6,4},{8,10},{10,8},{12,14},{14,12},{1,3},{3,1},... | collective-permute-start | bytes 2285576 | tf_op jit(solution)/shard_map/ppermute | solution.py:54
  128.4 8.6 %collective-permute-start.11 = (bf16[96,768]{1,0:T(8,128)(2,1)S(1)}, bf16[96,768]{1,0:T(8,128)(2,1)S(1)}, u32[]{:S(2)}, u32[]{:S(2)}) collective-permute-start(bf16[96,768]{1,0:T(8,128)(2,1)S(1)} %get-tuple-element.54.x), channel_id=1, source_target_pairs={{0,0},{1,2},{2,4},{3,6},{4,8},{5,10},{6,12},{7,14},{8,1},{9,3},{10... | collective-permute-start | bytes 442376 | tf_op jit(solution)/shard_map/ppermute | solution.py:41
  137.6 10.4 %collective-permute-start.12 = (bf16[96,768]{1,0:T(8,128)(2,1)S(1)}, bf16[96,768]{1,0:T(8,128)(2,1)S(1)}, u32[]{:S(2)}, u32[]{:S(2)}) collective-permute-start(bf16[96,768]{1,0:T(8,128)(2,1)S(1)} %get-tuple-element.57.refs_1_), channel_id=1, source_target_pairs={{0,16},{2,17},{4,18},{6,19},{8,20},{10,21},{12,22},{14,23},{1,24},... | collective-permute-start | bytes 442376 | tf_op jit(solution)/shard_map/ppermute | solution.py:50
  143.3 9.3 %collective-permute-start.13 = (bf16[96,768]{1,0:T(8,128)(2,1)S(1)}, bf16[96,768]{1,0:T(8,128)(2,1)S(1)}, u32[]{:S(2)}, u32[]{:S(2)}) collective-permute-start(bf16[96,768]{1,0:T(8,128)(2,1)S(1)} %shard_map.109), channel_id=1, source_target_pairs={{16,0},{17,2},{18,4},{19,6},{20,8},{21,10},{22,12},{23,14},{24,1},... | collective-permute-start | bytes 442376 | tf_op jit(solution)/shard_map/ppermute | solution.py:41
  154.5 20.4 %all-to-all-start.3 = ((bf16[4,96,1664]{2,1,0:T(8,128)(2,1)}), bf16[4,96,1664]{2,1,0:T(8,128)(2,1)S(1)}, u32[]{:S(2)}, u32[]{:S(2)}) async-start(bf16[4,96,1664]{2,1,0:T(8,128)(2,1)} %get-tuple-element.61), calls=%async_computation.3 | async-start | bytes 2555904 | tf_op jit(solution)/shard_map/all_to_all | solution.py:59
  175.1 14.6 %collective-permute-start.14 = (bf16[96,3968]{1,0:T(8,128)(2,1)S(1)}, bf16[96,3968]{1,0:T(8,128)(2,1)S(1)}, u32[]{:S(2)}, u32[]{:S(2)}) collective-permute-start(bf16[96,3968]{1,0:T(8,128)(2,1)S(1)} %shard_map.111.mine), channel_id=1, source_target_pairs={{0,2},{2,0},{4,6},{6,4},{8,10},{10,8},{12,14},{14,12},{1,3},{3,1},... | collective-permute-start | bytes 2285576 | tf_op jit(solution)/shard_map/ppermute | solution.py:54
  180.6 9.1 %collective-permute-start.15 = (bf16[96,768]{1,0:T(8,128)(2,1)S(1)}, bf16[96,768]{1,0:T(8,128)(2,1)S(1)}, u32[]{:S(2)}, u32[]{:S(2)}) collective-permute-start(bf16[96,768]{1,0:T(8,128)(2,1)S(1)} %get-tuple-element.62), channel_id=1, source_target_pairs={{0,0},{1,2},{2,4},{3,6},{4,8},{5,10},{6,12},{7,14},{8,1},{9,3},{10... | collective-permute-start | bytes 442376 | tf_op jit(solution)/shard_map/ppermute | solution.py:41
  195.4 10.0 %collective-permute-start.17 = (bf16[96,768]{1,0:T(8,128)(2,1)S(1)}, bf16[96,768]{1,0:T(8,128)(2,1)S(1)}, u32[]{:S(2)}, u32[]{:S(2)}) collective-permute-start(bf16[96,768]{1,0:T(8,128)(2,1)S(1)} %shard_map.113), channel_id=1, source_target_pairs={{16,0},{17,2},{18,4},{19,6},{20,8},{21,10},{22,12},{23,14},{24,1},... | collective-permute-start | bytes 442376 | tf_op jit(solution)/shard_map/ppermute | solution.py:41
  207.7 20.9 %all-to-all-start.4 = ((bf16[16,16,1024]{2,1,0:T(8,128)(2,1)}), bf16[16,16,1024]{2,1,0:T(8,128)(2,1)S(1)}, u32[]{:S(2)}, u32[]{:S(2)}) async-start(bf16[16,16,1024]{2,1,0:T(8,128)(2,1)} %broadcast_in_dim.30), calls=%async_computation.4 | async-start | bytes 1048576 | tf_op jit(solution)/shard_map/all_to_all | solution.py:401
  218.3 11.1 %collective-permute-start.16 = (f32[16,768]{1,0:T(8,128)S(1)}, f32[16,768]{1,0:T(8,128)S(1)}, u32[]{:S(2)}, u32[]{:S(2)}) collective-permute-start(f32[16,768]{1,0:T(8,128)S(1)} %slice_add_fusion), channel_id=1, source_target_pairs={{0,1},{1,0},{2,3},{3,2},{4,5},{5,4},{6,7},{7,6},{8,9},{9,8},{10,11... | collective-permute-start | bytes 147464 | tf_op jit(solution)/shard_map/ppermute | solution.py:394
  (3 other events, 7.0 us)

commit v3 on v2

v3 whole, which is shorter than its diff:
```python
import functools

import jax
import jax.numpy as jnp
from jax import lax
from jax.experimental import pallas as pl
from jax.experimental.pallas import tpu as pltpu
from jax.sharding import PartitionSpec as P

TICKS = 4
CHIPS = 4
EPS = 1e-05
AXES = ("section", "tensor", "dp")
HIGHEST = lax.Precision.HIGHEST
BF = jnp.bfloat16
F32 = jnp.float32

LANES = 128
SQUARE = 8
LOW = 16
GRAD = 32
FIRST = 48
SECOND = 49


def flat(section, tensor, dp):
    return (section * 2 * CHIPS + tensor) * 2 + dp


def owner(block, core):
    return 2 * (block % CHIPS) + core, block // CHIPS


def to_owner(array, sections, back):
    route = []
    for s in range(sections):
        for block in range(2 * CHIPS):
            for half in range(2):
                if s - back >= 0:
                    route.append((flat(s, block, half), flat(s - back, *owner(block, half))))
    return lax.ppermute(array, AXES, route)


def to_next(array, sections):
    route = []
    for s in range(sections - 1):
        for block in range(2 * CHIPS):
            for half in range(2):
                route.append((flat(s, *owner(block, half)), flat(s + 1, block, half)))
    return lax.ppermute(array, AXES, route)


def swap_cores(array):
    return lax.ppermute(array, "tensor", [(i, i ^ 1) for i in range(2 * CHIPS)])


def over_chips(array):
    groups = [[2 * i for i in range(CHIPS)], [2 * i + 1 for i in range(CHIPS)]]
    return lax.all_to_all(array, "tensor", 0, 0, axis_index_groups=groups)


def dot(a, b, **kw):
    return jnp.dot(a, b, preferred_element_type=F32, **kw)


def dot_t(a, b, **kw):
    return lax.dot_general(a, b, (((1,), (1,)), ((), ())), preferred_element_type=F32, **kw)


def t_dot(a, b, **kw):
    return lax.dot_general(a, b, (((0,), (0,)), ((), ())), preferred_element_type=F32, **kw)


def lane(rows):
    return lax.broadcasted_iota(jnp.int32, (rows, LANES), 1)


def between(values, low, high):
    at = lane(values.shape[0])
    return jnp.where((at >= low) & (at < high), values, 0.0)


def pick(values, low, high):
    return jnp.sum(between(values, low, high), axis=1, keepdims=True)


def split(values):
    high = values.astype(BF).astype(F32)
    rest = pltpu.roll(values - high, LANES // 2, 1)
    return jnp.where(lane(values.shape[0]) < LANES // 2, high, rest).astype(BF)


def join(halves):
    wide = halves.astype(F32)
    return wide + pltpu.roll(wide, LANES // 2, 1)


def call(kernel, out, *args, scalars=(), vmem=16):
    return pl.pallas_call(
        kernel,
        out_shape=out,
        in_specs=[pl.BlockSpec(memory_space=pltpu.SMEM)] * len(scalars)
        + [pl.BlockSpec(memory_space=pltpu.VMEM)] * len(args),
        out_specs=jax.tree.map(lambda _: pl.BlockSpec(memory_space=pltpu.VMEM), out),
        compiler_params=pltpu.CompilerParams(vmem_limit_bytes=vmem * 2**20),
    )(*scalars, *args)


def shape(*dims, dtype=F32):
    return jax.ShapeDtypeStruct(dims, dtype)


FIRST_SECTION, TENSOR, LAST_SECTION, CORE, OWN_BLOCK, REPLICA, ORDER = range(7)


def replicas(flags, mine, theirs):
    half = flags[REPLICA] == 0
    return jnp.concatenate([jnp.where(half, mine, theirs), jnp.where(half, theirs, mine)])


def prepare_kernel(flags, grads, up, stored, packed, chosen):
    toks = grads.shape[0]
    packed[:toks] = grads[...]
    packed[toks:] = up[...]
    for j in range(TICKS - 1):
        chosen[j] = jnp.where(flags[ORDER + j] == 0, stored[0], stored[1])


def forward_kernel(start, flags, *refs):
    place = flags[TENSOR]
    if start:
        mine, theirs, gains, w, down_rows, x_out, product, small, down = refs
        x = replicas(flags, mine[...], theirs[...])
        rank, feats = down_rows.shape
        down[:LOW] = jnp.zeros((LOW, feats), F32)
        down[LOW : LOW + rank] = down_rows[...].astype(F32)
        down[LOW + rank :] = jnp.zeros((LANES - LOW - rank, feats), F32)
    else:
        tick, arrived, mine, theirs, gains, w, down, x_out, product, small = refs
        given = replicas(flags, mine[tick - 1], theirs[tick - 1])
        x = jnp.where(flags[FIRST_SECTION] == 1, given, arrived[...])
    x_out[...] = x
    rows, feats = x.shape
    wide = x.astype(F32)
    mid = jnp.sum(wide, axis=1, keepdims=True) / feats
    centered = wide - mid
    square = jnp.sum(centered * centered, axis=1, keepdims=True)
    scaled = centered * gains[...]
    at = lane(rows)
    low = dot_t(scaled, down[...], precision=HIGHEST)
    low = jnp.where(at == place, mid, low)
    small[0:rows] = jnp.where(at == SQUARE + place, square, low)
    left = scaled.astype(BF)
    if start:
        row = lax.broadcasted_iota(jnp.int32, (2 * CHIPS, feats), 0)
        gain_rows = jnp.where(row == place, gains[...], 0.0)
        high = gain_rows.astype(BF).astype(F32)
        left = jnp.concatenate([left, jnp.concatenate([high, gain_rows - high]).astype(BF)])
        small[rows:] = jnp.concatenate(
            [dot_t(gain_rows, down[...], precision=HIGHEST), jnp.zeros((2 * CHIPS, LANES), F32)]
        )
    for j in range(CHIPS):
        part = dot(left, w[:, j * feats : (j + 1) * feats])
        if start:
            tail = part[rows : rows + 2 * CHIPS] + part[rows + 2 * CHIPS :]
            high = tail.astype(BF).astype(F32)
            part = jnp.concatenate([part[:rows], high, tail - high])
        product[j] = part.astype(BF)


def chosen_grad(flags, arrived, output):
    kept = jnp.where(flags[CORE] == 0, output[...], jnp.zeros(output.shape, BF))
    return jnp.where(flags[LAST_SECTION] == 1, kept, arrived[...])


def pack_kernel(start, flags, product, small, x_owned, *refs):
    rows, feats = product.shape[1:]
    values = small[...]
    if start:
        given, theirs, parcel, up, grad_out = refs
        columns = feats
        toks = theirs.shape[1]
        rank = given.shape[0] - toks
        up[:LOW] = jnp.zeros((LOW, feats), BF)
        up[LOW : LOW + rank] = given[toks:]
        up[LOW + rank :] = jnp.zeros((LANES - LOW - rank, feats), BF)
        zeros = jnp.zeros((toks, feats), BF)
        grad_out[:toks] = jnp.where(flags[CORE] == 0, given[:toks], zeros)
        grad_out[toks:] = jnp.where(flags[CORE] == 0, zeros, given[:toks])
    else:
        arrived, output, up, gain_w, mixed, parcel, grad_out = refs
        columns = 2 * feats
        grad = chosen_grad(flags, arrived, output)
        grad_out[...] = grad
        wide = grad.astype(F32)
        first = jnp.sum(wide * jnp.sum(gain_w[...], axis=0, keepdims=True), axis=1, keepdims=True)
        second = jnp.sum(wide * mixed[...], axis=1, keepdims=True)
        at = lane(rows)
        values = values + pltpu.roll(dot_t(grad, up[...]), GRAD - LOW, 1)
        values = jnp.where(at == FIRST, first, values)
        values = jnp.where(at == SECOND, second, values)
        for j in range(CHIPS):
            parcel[j, :, feats : 2 * feats] = grad
    halves = split(values)
    for j in range(CHIPS):
        parcel[j, :, :feats] = product[j]
        parcel[j, :, columns:] = halves


def gather_kernel(start, got, out):
    feats = (got.shape[2] - LANES) // (1 if start else 2)
    total = got[0, :, :feats].astype(F32)
    values = join(got[0, :, -LANES:])
    for j in range(1, CHIPS):
        total = total + got[j, :, :feats].astype(F32)
        values = values + join(got[j, :, -LANES:])
    out[:, :feats] = total.astype(BF)
    out[:, feats : feats + LANES] = split(values)
    if not start:
        for j in range(CHIPS):
            at = feats + LANES + j * feats
            out[:, at : at + feats] = got[j, :, feats : 2 * feats]


def output_kernel(start, mine, theirs, x, up, gain_w, gain_low, output, mixed, stats, sums):
    rows, feats = x.shape
    if start:
        tail = mine[rows:, :feats].astype(F32) + theirs[rows:, :feats].astype(F32)
        gain_w[...] = tail[: 2 * CHIPS] + tail[2 * CHIPS :]
        tail = join(mine[rows:, feats:]) + join(theirs[rows:, feats:])
        gain_low[...] = between(tail[: 2 * CHIPS], LOW, GRAD)
    values = join(mine[:rows, feats : feats + LANES]) + join(theirs[:rows, feats : feats + LANES])
    values = between(values, 0, LANES // 2)
    sums[...] = values
    at = lane(rows)
    width = feats * 2 * CHIPS
    mean = pick(values, 0, SQUARE) / (2 * CHIPS)
    off = jnp.where(at < 2 * CHIPS, values - mean, 0.0)
    square = pick(values, SQUARE, LOW) + feats * jnp.sum(off * off, axis=1, keepdims=True)
    inv = lax.rsqrt(square / width + EPS)
    total = mine[:rows, :feats].astype(F32) + theirs[:rows, :feats].astype(F32)
    low = values
    for j in range(2 * CHIPS):
        total = total + off[:, j : j + 1] * gain_w[j : j + 1, :]
        low = low + off[:, j : j + 1] * gain_low[j : j + 1, :]
    total = inv * total
    low = between(inv * low, LOW, GRAD)
    mixed[...] = total
    stats[...] = jnp.where(at == 0, mean, jnp.where(at == 1, inv, low))
    output[...] = (x[...].astype(F32) + total + dot(low.astype(BF), up[...])).astype(BF)


def rank_grads(sums):
    return pltpu.roll(between(sums, GRAD, FIRST), LANES - (GRAD - LOW), 1)


def normed(x, stats):
    return (x.astype(F32) - pick(stats, 0, 1)) * pick(stats, 1, 2)


def backward_kernel(flags, mine, theirs, sums, x, stats, gains, gain_low, w, down, grad_out):
    rows, feats = x.shape
    width = feats * 2 * CHIPS
    values = sums[...]
    low_grad = rank_grads(values)
    low = between(stats[...], LOW, GRAD)
    low_all = jnp.sum(gain_low[...], axis=0, keepdims=True)
    first = pick(values, FIRST, FIRST + 1) + jnp.sum(low_grad * low_all, axis=1, keepdims=True)
    second = pick(values, SECOND, SECOND + 1) + jnp.sum(low_grad * low, axis=1, keepdims=True)
    xhat = normed(x[...], stats[...])
    grad_norm = dot(low_grad, down[...], precision=HIGHEST)
    here = jnp.zeros((rows, feats), F32)
    for j in range(CHIPS):
        at = feats + LANES + j * feats
        grad = mine[:, at : at + feats].astype(F32) + theirs[:, at : at + feats].astype(F32)
        grad = grad.astype(BF)
        grad_norm = grad_norm + dot_t(grad, w[:, j * feats : (j + 1) * feats])
        here = here + jnp.where(flags[OWN_BLOCK] == j, grad.astype(F32), 0.0)
    inv = pick(stats[...], 1, 2)
    grad_x = here + inv * (grad_norm * gains[...] - first / width - xhat * (second / width))
    grad_out[...] = grad_x.astype(BF)


def accumulate_kernel(gains, after, *refs):
    count = TICKS - 1
    xs, stats, sums, grads = (refs[i * count : (i + 1) * count] for i in range(4))
    acc_down, acc_up = refs[4 * count :]
    rank = acc_up.shape[0]
    down, up = 0.0, 0.0
    for j in range(count):
        u = normed(xs[j][...], stats[j][...]) * gains[...]
        down = down + t_dot(rank_grads(sums[j][...]), u, precision=HIGHEST)
        up = up + t_dot(stats[j][...].astype(BF), grads[j][...])
    acc_down[...] = down[LOW : LOW + rank]
    acc_up[...] = up[LOW : LOW + rank]


def last_kernel(flags, arrived, output, up, stats, acc_up, low_out, up_out):
    rows, feats = arrived.shape
    rank = acc_up.shape[0]
    grad = chosen_grad(flags, arrived, output)
    turned = dot_t(up[LOW : LOW + rank], grad)
    turned = jnp.concatenate([turned, jnp.zeros((rank, LANES - rows), F32)], axis=1)
    high = turned.astype(BF).astype(F32)
    halves = jnp.concatenate([high, turned - high], axis=1).astype(BF)
    for j in range(4 * CHIPS):
        low_out[j] = halves
    low = t_dot(stats[...].astype(BF), grad)
    up_out[...] = (acc_up[...] + low[LOW : LOW + rank]).astype(BF)


def finish_kernel(got, x, stats, gains, mine, theirs, up_a, up_b, down_out, up_out):
    rows = x.shape[0]
    turned = got[0].astype(F32)
    for j in range(1, 4 * CHIPS):
        turned = turned + got[j].astype(F32)
    low_grad = turned[:, :LANES] + turned[:, LANES:]
    u = normed(x[...], stats[...]) * gains[...]
    u = jnp.concatenate([u, jnp.zeros((LANES - rows, u.shape[1]), F32)])
    total = mine[...] + theirs[...] + dot(low_grad, u, precision=HIGHEST)
    down_out[...] = (total / rows).astype(BF)
    up_out[...] = ((up_a[...].astype(F32) + up_b[...].astype(F32)) / rows).astype(BF)


def back_home(array, sections, flip):
    route = []
    for s in range(sections):
        for block in range(2 * CHIPS):
            for half in range(2):
                route.append((flat(s, *owner(block, half ^ flip)), flat(s, block, half)))
    return lax.ppermute(array, AXES, route)


def on_device(
    weight,
    adapter_down_map,
    adapter_up_map,
    gain,
    prior_epoch_input,
    prior_epoch_output,
    initial_step_inputs,
    initial_step_gradients,
    sample_numbers,
):
    del prior_epoch_output
    w = weight[0]
    gains = gain
    sections = lax.axis_size("section")
    section = lax.axis_index("section")
    tensor = lax.axis_index("tensor")
    half = lax.axis_index("dp")
    toks, feats = initial_step_inputs.shape[1:]
    rank = adapter_up_map.shape[1]
    rows = 2 * toks
    flags = [
        section == 0,
        tensor,
        section == sections - 1,
        tensor % 2,
        jnp.where(tensor // CHIPS == half, tensor % CHIPS, -1),
        half,
    ]
    flags = jnp.stack([f.astype(jnp.int32) for f in flags])
    flags = (jnp.concatenate([flags, sample_numbers[0, 0, 1:]]),)

    mine = initial_step_inputs[0]
    theirs = lax.ppermute(mine, "dp", [(0, 1), (1, 0)])
    packed, chosen = call(
        prepare_kernel,
        [shape(toks + rank, feats, dtype=BF), shape(TICKS - 1, toks, feats, dtype=BF)],
        initial_step_gradients[0],
        adapter_up_map[0],
        prior_epoch_input[0, 0],
        scalars=flags,
    )
    given = to_owner(packed, sections, 0)
    chosen_theirs = lax.ppermute(
        chosen,
        AXES,
        [(flat(0, t, d), flat(0, t, 1 - d)) for t in range(2 * CHIPS) for d in range(2)],
    )

    block = shape(rows, feats, dtype=BF)
    values = shape(rows, LANES)
    xs, all_stats, all_sums, grads = [], [], [], []
    for tick in range(TICKS):
        start = tick == 0
        more = 4 * CHIPS if start else 0
        out = [block, shape(CHIPS, rows + more, feats, dtype=BF), shape(rows + more, LANES)]
        if start:
            x, product, small, down = call(
                functools.partial(forward_kernel, True),
                out + [shape(LANES, feats)],
                mine,
                theirs,
                gains,
                w,
                adapter_down_map[0].T,
                scalars=flags,
            )
        else:
            x, product, small = call(
                lambda flags, *refs, tick=tick: forward_kernel(False, flags, tick, *refs),
                out,
                arrived,
                chosen,
                chosen_theirs,
                gains,
                w,
                down,
                scalars=flags,
            )
        x_owned = to_owner(x, sections, 0)
        columns = (1 if start else 2) * feats + LANES
        parcel = shape(CHIPS, rows + more, columns, dtype=BF)
        if start:
            parcel, up, grad_arrived = call(
                functools.partial(pack_kernel, True),
                [parcel, shape(LANES, feats, dtype=BF), block],
                product,
                small,
                x_owned,
                given,
                chosen_theirs,
                scalars=flags,
            )
        else:
            parcel, grad = call(
                functools.partial(pack_kernel, False),
                [parcel, block],
                product,
                small,
                x_owned,
                grad_arrived,
                output,
                up,
                gain_w,
                mixed,
                scalars=flags,
            )
            grads.append(grad)
        got = over_chips(parcel)
        own = call(
            functools.partial(gather_kernel, start),
            shape(rows + more, feats + LANES + (0 if start else CHIPS * feats), dtype=BF),
            got,
        )
        other = swap_cores(own)
        out = [block, shape(rows, feats), values, values]
        ins = [own, other, x_owned, up]
        kernel = functools.partial(output_kernel, start)
        if start:
            gain_w, gain_low, output, mixed, stats, sums = call(
                kernel, [shape(2 * CHIPS, feats), shape(2 * CHIPS, LANES)] + out, *ins
            )
        else:
            output, mixed, stats, sums = call(kernel, out, *ins, gain_w, gain_low)
            all_sums.append(sums)
        if tick < TICKS - 1:
            arrived = to_next(output, sections)
        if not start:
            grad_x = call(
                backward_kernel,
                block,
                own,
                other,
                sums,
                xs[-1],
                all_stats[-1],
                gains,
                gain_low,
                w,
                down,
                scalars=flags,
            )
            grad_arrived = to_owner(grad_x, sections, 1)
        xs.append(x)
        all_stats.append(stats)

    acc_down, acc_up = call(
        accumulate_kernel,
        [shape(rank, feats), shape(rank, feats)],
        gains,
        grad_x,
        *xs[:-1],
        *all_stats[:-1],
        *all_sums,
        *grads,
    )
    acc_other = lax.ppermute(acc_down, "dp", [(0, 1), (1, 0)])
    turned, up_part = call(
        last_kernel,
        [shape(4 * CHIPS, rank, 2 * LANES, dtype=BF), shape(rank, feats, dtype=BF)],
        grad_arrived,
        output,
        up,
        stats,
        acc_up,
        scalars=flags,
    )
    got = lax.all_to_all(turned, ("tensor", "dp"), 0, 0)
    grad_down, grad_up = call(
        finish_kernel,
        [shape(rank, feats, dtype=BF), shape(rank, feats, dtype=BF)],
        got,
        x,
        stats,
        gains,
        acc_down,
        acc_other,
        back_home(up_part, sections, 0),
        back_home(up_part, sections, 1),
    )
    return grad_down.T[None], grad_up[None]


def solution(mesh):
    in_specs = (
        P("section", "tensor", "dp"),
        P("section", "tensor", None),
        P("section", None, "tensor"),
        P("section", "tensor"),
        P("section", "dp", None, None, "tensor"),
        P("section", "dp", None, None, "tensor"),
        P("section", "dp", "tensor"),
        P("section", "dp", "tensor"),
        P("section", "dp", None),
    )
    out_specs = (P("section", "tensor", None), P("section", None, "tensor"))
    return jax.shard_map(
        on_device, mesh=mesh, in_specs=in_specs, out_specs=out_specs, check_vma=False
    )
```

time: 232 us -> 233 us (level)
  the two profiles are of different devices: /device:TPU:241 before, /device:TPU:121 now
where the time goes in v3:
time: 233 us; the launch traced here: 232 us
  starting transfers between devices  77.1 us (33%)
  blocking collectives  73.8 us (32%)
  waiting for transfers between devices  45.1 us (19%)
  Pallas kernels  26.8 us (12%)
  local copies, waits for them, and re-layouts  7.99 us (3%)
    all_to_all x4, blocking collectives, over_chips(): return lax.all_to_all(array, 'tensor', 0, 0, axis_index_groups=groups)  73.8 us
    ppermute x8, waiting for transfers between devices, to_owner(): return lax.ppermute(array, AXES, route)  32.2 us
    pallas_call x23, Pallas kernels, call(): pl.pallas_call(kernel, out_shape=out, in_specs=[pl.BlockSpec(memory_space...  26.8 us
    ppermute x3, starting transfers between devices, to_next(): return lax.ppermute(array, AXES, route)  23.8 us
    ppermute x8, starting transfers between devices, to_owner(): return lax.ppermute(array, AXES, route)  22.9 us
    ppermute x4, starting transfers between devices, swap_cores(): return lax.ppermute(array, 'tensor', [(i, i ^ 1) for i in range(2 * CHIPS)])  13.5 us
    ppermute x2, starting transfers between devices, back_home(): return lax.ppermute(array, AXES, route)  8.38 us
    unnamed x18, local copies, waits for them, and re-layouts  7.18 us
  transfers between devices with their start and end apart: 21, of which 11 were waited for; matrix products, arithmetic and copies ran while one was open for 0% of the time, Pallas kernels for 5%

profile of v3, /device:TPU:121, one launch (start us, length us, event | category | flops | bytes accessed | tf_op | source)
XLA Modules:
  0.0 231.8 jit_solution(819679732014733602)
XLA Ops:
  0.6 2.4 %collective-permute-start = (bf16[48,768]{1,0:T(8,128)(2,1)}, bf16[48,768]{1,0:T(8,128)(2,1)S(1)}, u32[]{:S(2)}, u32[]{:S(2)}) collective-permute-start(bf16[48,768]{1,0:T(8,128)(2,1)} %bitcast.29), channel_id=1, source_target_pairs={{0,1},{1,0},{2,3},{3,2},{4,5},{5,4},{6,7},{7,6},{8,9},{9,8},{10,11... | collective-permute-start | bytes 221192 | tf_op jit(solution)/shard_map/ppermute | solution.py:367
  7.7 2.3 %copy-done = bf16[1,768,3072]{2,1,0:T(8,128)(2,1)S(1)} copy-done((bf16[1,768,3072]{2,1,0:T(8,128)(2,1)S(1)}, bf16[1,768,3072]{2,1,0:T(8,128)(2,1)}, u32[]{:S(2)}) %copy-start) | copy-done | bytes 4718616
  12.3 2.0 shard_map.95
  14.3 3.8 %collective-permute-start.1 = (bf16[96,768]{1,0:T(8,128)(2,1)S(1)}, bf16[96,768]{1,0:T(8,128)(2,1)S(1)}, u32[]{:S(2)}, u32[]{:S(2)}) collective-permute-start(bf16[96,768]{1,0:T(8,128)(2,1)S(1)} %get-tuple-element.50.x.refs_0_), channel_id=1, source_target_pairs={{0,0},{1,2},{2,4},{3,6},{4,8},{5,10},{6,12},{7,14},{8,1},{9,3},{10... | collective-permute-start | bytes 442376 | tf_op jit(solution)/shard_map/ppermute | solution.py:41
  18.2 4.6 %collective-permute-start.2 = (bf16[64,768]{1,0:T(8,128)(2,1)S(1)}, bf16[64,768]{1,0:T(8,128)(2,1)S(1)}, u32[]{:S(2)}, u32[]{:S(2)}) collective-permute-start(bf16[64,768]{1,0:T(8,128)(2,1)S(1)} %get-tuple-element.51), channel_id=1, source_target_pairs={{0,0},{1,2},{2,4},{3,6},{4,8},{5,10},{6,12},{7,14},{8,1},{9,3},{10... | collective-permute-start | bytes 294920 | tf_op jit(solution)/shard_map/ppermute | solution.py:41
  22.8 3.1 %collective-permute-done.2.refs_0_ = bf16[64,768]{1,0:T(8,128)(2,1)S(1)} collective-permute-done((bf16[64,768]{1,0:T(8,128)(2,1)S(1)}, bf16[64,768]{1,0:T(8,128)(2,1)S(1)}, u32[]{:S(2)}, u32[]{:S(2)}) %collective-permute-start.2) | collective-permute-done | bytes 98336 | tf_op jit(solution)/shard_map/ppermute | solution.py:41
  26.6 14.3 %all_to_all.25.got = bf16[4,112,896]{2,1,0:T(8,128)(2,1)S(1)} all-to-all(bf16[4,112,896]{2,1,0:T(8,128)(2,1)S(1)} %get-tuple-element.53), channel_id=1, replica_groups={{0,4,8,12},{2,6,10,14},{1,5,9,13},{3,7,11,15},{16,20,24,28},{18,22,26,3..., dimensions={0} | all-to-all | bytes 1605632 | tf_op jit(solution)/shard_map/all_to_all | solution.py:59
  41.1 3.4 %collective-permute-start.4 = (bf16[112,896]{1,0:T(8,128)(2,1)S(1)}, bf16[112,896]{1,0:T(8,128)(2,1)S(1)}, u32[]{:S(2)}, u32[]{:S(2)}) collective-permute-start(bf16[112,896]{1,0:T(8,128)(2,1)S(1)} %shard_map.98.mine), channel_id=1, source_target_pairs={{0,2},{2,0},{4,6},{6,4},{8,10},{10,8},{12,14},{14,12},{1,3},{3,1},... | collective-permute-start | bytes 602120 | tf_op jit(solution)/shard_map/ppermute | solution.py:54
  46.6 6.2 %collective-permute-start.5 = (bf16[96,768]{1,0:T(8,128)(2,1)S(1)}, bf16[96,768]{1,0:T(8,128)(2,1)S(1)}, u32[]{:S(2)}, u32[]{:S(2)}) collective-permute-start(bf16[96,768]{1,0:T(8,128)(2,1)S(1)} %get-tuple-element.55.refs_1_), channel_id=1, source_target_pairs={{0,16},{2,17},{4,18},{6,19},{8,20},{10,21},{12,22},{14,23},{1,24},... | collective-permute-start | bytes 442376 | tf_op jit(solution)/shard_map/ppermute | solution.py:50
  52.9 3.0 %collective-permute-done.5.refs_0_ = bf16[96,768]{1,0:T(8,128)(2,1)S(1)} collective-permute-done((bf16[96,768]{1,0:T(8,128)(2,1)S(1)}, bf16[96,768]{1,0:T(8,128)(2,1)S(1)}, u32[]{:S(2)}, u32[]{:S(2)}) %collective-permute-start.5) | collective-permute-done | bytes 147488 | tf_op jit(solution)/shard_map/ppermute | solution.py:50
  57.8 4.6 %collective-permute-start.6 = (bf16[96,768]{1,0:T(8,128)(2,1)S(1)}, bf16[96,768]{1,0:T(8,128)(2,1)S(1)}, u32[]{:S(2)}, u32[]{:S(2)}) collective-permute-start(bf16[96,768]{1,0:T(8,128)(2,1)S(1)} %get-tuple-element.59.x.refs_1_), channel_id=1, source_target_pairs={{0,0},{1,2},{2,4},{3,6},{4,8},{5,10},{6,12},{7,14},{8,1},{9,3},{10... | collective-permute-start | bytes 442376 | tf_op jit(solution)/shard_map/ppermute | solution.py:41
  62.4 3.4 %collective-permute-done.6.x_owned.x = bf16[96,768]{1,0:T(8,128)(2,1)S(1)} collective-permute-done((bf16[96,768]{1,0:T(8,128)(2,1)S(1)}, bf16[96,768]{1,0:T(8,128)(2,1)S(1)}, u32[]{:S(2)}, u32[]{:S(2)}) %collective-permute-start.6) | collective-permute-done | bytes 147488 | tf_op jit(solution)/shard_map/ppermute | solution.py:41
  66.7 19.7 %all_to_all.26.got = bf16[4,96,1664]{2,1,0:T(8,128)(2,1)S(1)} all-to-all(bf16[4,96,1664]{2,1,0:T(8,128)(2,1)S(1)} %get-tuple-element.63), channel_id=1, replica_groups={{0,4,8,12},{2,6,10,14},{1,5,9,13},{3,7,11,15},{16,20,24,28},{18,22,26,3..., dimensions={0} | all-to-all | bytes 2555904 | tf_op jit(solution)/shard_map/all_to_all | solution.py:59
  86.5 4.3 %collective-permute-start.7 = (bf16[96,3968]{1,0:T(8,128)(2,1)S(1)}, bf16[96,3968]{1,0:T(8,128)(2,1)S(1)}, u32[]{:S(2)}, u32[]{:S(2)}) collective-permute-start(bf16[96,3968]{1,0:T(8,128)(2,1)S(1)} %shard_map.102.mine), channel_id=1, source_target_pairs={{0,2},{2,0},{4,6},{6,4},{8,10},{10,8},{12,14},{14,12},{1,3},{3,1},... | collective-permute-start | bytes 2285576 | tf_op jit(solution)/shard_map/ppermute | solution.py:54
  93.3 8.7 %collective-permute-start.8 = (bf16[96,768]{1,0:T(8,128)(2,1)S(1)}, bf16[96,768]{1,0:T(8,128)(2,1)S(1)}, u32[]{:S(2)}, u32[]{:S(2)}) collective-permute-start(bf16[96,768]{1,0:T(8,128)(2,1)S(1)} %get-tuple-element.65.refs_1_), channel_id=1, source_target_pairs={{0,16},{2,17},{4,18},{6,19},{8,20},{10,21},{12,22},{14,23},{1,24},... | collective-permute-start | bytes 442376 | tf_op jit(solution)/shard_map/ppermute | solution.py:50
  101.9 2.3 %shard_map.105 = bf16[96,768]{1,0:T(8,128)(2,1)S(1)} custom-call(s32[9]{0:T(128)S(1)} %concatenate.3.flags, bf16[96,3968]{1,0:T(8,128)(2,1)S(1)} %shard_map.102.mine, bf16[96,3968]{1,0:T(8,128)(2,1)S(1)} %collective-permute-done.7.theirs, f32[96,128]{1,0:T(8,128)S(1)} %get-tuple-element.69.sums.refs_6_, bf16[96,768]{1,0:T(8,128)(2,1)S(1)} %get-tuple-element.50.x.refs_0_, ...), custom_call_target="tpu_custom_call" | custom-call | tf_op jit(solution)/shard_map/pallas_call | solution.py:99
  108.1 2.0 collective-permute-start.9
  110.2 7.5 %collective-permute-done.10.refs_0_ = bf16[96,768]{1,0:T(8,128)(2,1)S(1)} collective-permute-done((bf16[96,768]{1,0:T(8,128)(2,1)S(1)}, bf16[96,768]{1,0:T(8,128)(2,1)S(1)}, u32[]{:S(2)}, u32[]{:S(2)}) %collective-permute-start.10) | collective-permute-done | bytes 147488 | tf_op jit(solution)/shard_map/ppermute | solution.py:41
  118.5 19.9 %all_to_all.27.got = bf16[4,96,1664]{2,1,0:T(8,128)(2,1)S(1)} all-to-all(bf16[4,96,1664]{2,1,0:T(8,128)(2,1)S(1)} %get-tuple-element.72), channel_id=1, replica_groups={{0,4,8,12},{2,6,10,14},{1,5,9,13},{3,7,11,15},{16,20,24,28},{18,22,26,3..., dimensions={0} | all-to-all | bytes 2555904 | tf_op jit(solution)/shard_map/all_to_all | solution.py:59
  138.6 2.9 %collective-permute-start.11 = (bf16[96,3968]{1,0:T(8,128)(2,1)S(1)}, bf16[96,3968]{1,0:T(8,128)(2,1)S(1)}, u32[]{:S(2)}, u32[]{:S(2)}) collective-permute-start(bf16[96,3968]{1,0:T(8,128)(2,1)S(1)} %shard_map.107.mine), channel_id=1, source_target_pairs={{0,2},{2,0},{4,6},{6,4},{8,10},{10,8},{12,14},{14,12},{1,3},{3,1},... | collective-permute-start | bytes 2285576 | tf_op jit(solution)/shard_map/ppermute | solution.py:54
  144.1 8.9 %collective-permute-start.12 = (bf16[96,768]{1,0:T(8,128)(2,1)S(1)}, bf16[96,768]{1,0:T(8,128)(2,1)S(1)}, u32[]{:S(2)}, u32[]{:S(2)}) collective-permute-start(bf16[96,768]{1,0:T(8,128)(2,1)S(1)} %get-tuple-element.73.refs_1_), channel_id=1, source_target_pairs={{0,16},{2,17},{4,18},{6,19},{8,20},{10,21},{12,22},{14,23},{1,24},... | collective-permute-start | bytes 442376 | tf_op jit(solution)/shard_map/ppermute | solution.py:50
  152.9 2.3 %shard_map.110 = bf16[96,768]{1,0:T(8,128)(2,1)S(1)} custom-call(s32[9]{0:T(128)S(1)} %concatenate.3.flags, bf16[96,3968]{1,0:T(8,128)(2,1)S(1)} %shard_map.107.mine, bf16[96,3968]{1,0:T(8,128)(2,1)S(1)} %collective-permute-done.11.theirs, f32[96,128]{1,0:T(8,128)S(1)} %get-tuple-element.77.sums.refs_7_, bf16[96,768]{1,0:T(8,128)(2,1)S(1)} %get-tuple-element.59.x.refs_1_, ...), custom_call_target="tpu_custom_call" | custom-call | tf_op jit(solution)/shard_map/pallas_call | solution.py:99
  159.1 2.1 collective-permute-start.13
  161.2 7.5 %collective-permute-done.14.refs_0_ = bf16[96,768]{1,0:T(8,128)(2,1)S(1)} collective-permute-done((bf16[96,768]{1,0:T(8,128)(2,1)S(1)}, bf16[96,768]{1,0:T(8,128)(2,1)S(1)}, u32[]{:S(2)}, u32[]{:S(2)}) %collective-permute-start.14) | collective-permute-done | bytes 147488 | tf_op jit(solution)/shard_map/ppermute | solution.py:41
  169.6 19.9 %all_to_all.28.got = bf16[4,96,1664]{2,1,0:T(8,128)(2,1)S(1)} all-to-all(bf16[4,96,1664]{2,1,0:T(8,128)(2,1)S(1)} %get-tuple-element.80), channel_id=1, replica_groups={{0,4,8,12},{2,6,10,14},{1,5,9,13},{3,7,11,15},{16,20,24,28},{18,22,26,3..., dimensions={0} | all-to-all | bytes 2555904 | tf_op jit(solution)/shard_map/all_to_all | solution.py:59
  189.8 2.9 %collective-permute-start.15 = (bf16[96,3968]{1,0:T(8,128)(2,1)S(1)}, bf16[96,3968]{1,0:T(8,128)(2,1)S(1)}, u32[]{:S(2)}, u32[]{:S(2)}) collective-permute-start(bf16[96,3968]{1,0:T(8,128)(2,1)S(1)} %shard_map.112.mine), channel_id=1, source_target_pairs={{0,2},{2,0},{4,6},{6,4},{8,10},{10,8},{12,14},{14,12},{1,3},{3,1},... | collective-permute-start | bytes 2285576 | tf_op jit(solution)/shard_map/ppermute | solution.py:54
  195.9 2.3 %shard_map.114.after = bf16[96,768]{1,0:T(8,128)(2,1)S(1)} custom-call(s32[9]{0:T(128)S(1)} %concatenate.3.flags, bf16[96,3968]{1,0:T(8,128)(2,1)S(1)} %shard_map.112.mine, bf16[96,3968]{1,0:T(8,128)(2,1)S(1)} %collective-permute-done.15.theirs, f32[96,128]{1,0:T(8,128)S(1)} %get-tuple-element.81.sums.refs_8_, ...), custom_call_target="tpu_custom_call" | custom-call | tf_op jit(solution)/shard_map/pallas_call | solution.py:99
  201.6 10.8 %collective-permute-done.16.arrived = bf16[96,768]{1,0:T(8,128)(2,1)S(1)} collective-permute-done((bf16[96,768]{1,0:T(8,128)(2,1)S(1)}, bf16[96,768]{1,0:T(8,128)(2,1)S(1)}, u32[]{:S(2)}, u32[]{:S(2)}) %collective-permute-start.16) | collective-permute-done | bytes 147488 | tf_op jit(solution)/shard_map/ppermute | solution.py:41
  213.7 3.4 %all-to-all-start.4 = ((bf16[16,16,256]{2,1,0:T(8,128)(2,1)}), bf16[16,16,256]{2,1,0:T(8,128)(2,1)S(1)}, u32[]{:S(2)}, u32[]{:S(2)}) async-start(bf16[16,16,256]{2,1,0:T(8,128)(2,1)} %get-tuple-element.89), calls=%async_computation.4 | async-start | bytes 262144 | tf_op jit(solution)/shard_map/all_to_all | solution.py:501
  219.2 6.2 %collective-permute-start.19 = (bf16[16,768]{1,0:T(8,128)(2,1)S(1)}, bf16[16,768]{1,0:T(8,128)(2,1)S(1)}, u32[]{:S(2)}, u32[]{:S(2)}) collective-permute-start(bf16[16,768]{1,0:T(8,128)(2,1)S(1)} %get-tuple-element.91), channel_id=1, source_target_pairs={{2,0},{0,1},{6,2},{4,3},{10,4},{8,5},{14,6},{12,7},{3,8},{1,9},{7,... | collective-permute-start | bytes 73736 | tf_op jit(solution)/shard_map/ppermute | solution.py:331
  225.4 2.2 collective-permute-start.18
  227.6 3.3 %collective-permute-done.18.up_a = bf16[16,768]{1,0:T(8,128)(2,1)S(1)} collective-permute-done((bf16[16,768]{1,0:T(8,128)(2,1)S(1)}, bf16[16,768]{1,0:T(8,128)(2,1)S(1)}, u32[]{:S(2)}, u32[]{:S(2)}) %collective-permute-start.18) | collective-permute-done | bytes 24608 | tf_op jit(solution)/shard_map/ppermute | solution.py:331
  (57 shorter events, 38.5 us)
Async XLA Ops:
  0.6 7.0 %collective-permute-start = (bf16[48,768]{1,0:T(8,128)(2,1)}, bf16[48,768]{1,0:T(8,128)(2,1)S(1)}, u32[]{:S(2)}, u32[]{:S(2)}) collective-permute-start(bf16[48,768]{1,0:T(8,128)(2,1)} %bitcast.29), channel_id=1, source_target_pairs={{0,1},{1,0},{2,3},{3,2},{4,5},{5,4},{6,7},{7,6},{8,9},{9,8},{10,11... | collective-permute-start | bytes 221192 | tf_op jit(solution)/shard_map/ppermute | solution.py:367
  3.9 0.9 copy-start.4
  4.8 0.9 copy-start.5
  5.6 0.7 copy-start.8
  7.0 19.0 %collective-permute-start.3 = (bf16[3,48,768]{2,1,0:T(8,128)(2,1)S(1)}, bf16[3,48,768]{2,1,0:T(8,128)(2,1)S(1)}, u32[]{:S(2)}, u32[]{:S(2)}) collective-permute-start(bf16[3,48,768]{2,1,0:T(8,128)(2,1)S(1)} %get-tuple-element.52.refs_1_), channel_id=1, source_target_pairs={{0,1},{1,0},{2,3},{3,2},{4,5},{5,4},{6,7},{7,6},{8,9},{9,8},{10,11... | collective-permute-start | bytes 663560 | tf_op jit(solution)/shard_map/ppermute | solution.py:377
  7.7 2.3 %copy-start = (bf16[1,768,3072]{2,1,0:T(8,128)(2,1)S(1)}, bf16[1,768,3072]{2,1,0:T(8,128)(2,1)}, u32[]{:S(2)}) copy-start(bf16[1,768,3072]{2,1,0:T(8,128)(2,1)} %param.9) | copy-start | bytes 14155780
  10.0 0.7 copy-start.2
  10.7 0.9 copy-start.6
  11.6 0.7 copy-start.7
  12.3 43.6 %copy-start.1 = (bf16[1,768,3072]{2,1,0:T(8,128)(2,1)S(1)}, bf16[1,768,3072]{2,1,0:T(8,128)(2,1)}, u32[]{:S(2)}) copy-start(bf16[1,768,3072]{2,1,0:T(8,128)(2,1)} %param.9) | copy-start | bytes 14155780
  14.3 11.6 %collective-permute-start.1 = (bf16[96,768]{1,0:T(8,128)(2,1)S(1)}, bf16[96,768]{1,0:T(8,128)(2,1)S(1)}, u32[]{:S(2)}, u32[]{:S(2)}) collective-permute-start(bf16[96,768]{1,0:T(8,128)(2,1)S(1)} %get-tuple-element.50.x.refs_0_), channel_id=1, source_target_pairs={{0,0},{1,2},{2,4},{3,6},{4,8},{5,10},{6,12},{7,14},{8,1},{9,3},{10... | collective-permute-start | bytes 442376 | tf_op jit(solution)/shard_map/ppermute | solution.py:41
  18.2 7.7 %collective-permute-start.2 = (bf16[64,768]{1,0:T(8,128)(2,1)S(1)}, bf16[64,768]{1,0:T(8,128)(2,1)S(1)}, u32[]{:S(2)}, u32[]{:S(2)}) collective-permute-start(bf16[64,768]{1,0:T(8,128)(2,1)S(1)} %get-tuple-element.51), channel_id=1, source_target_pairs={{0,0},{1,2},{2,4},{3,6},{4,8},{5,10},{6,12},{7,14},{8,1},{9,3},{10... | collective-permute-start | bytes 294920 | tf_op jit(solution)/shard_map/ppermute | solution.py:41
  40.9 15.0 %copy-start.3 = (f32[1,768]{1,0:T(1,128)S(1)}, f32[1,768]{1,0:T(1,128)}, u32[]{:S(2)}) copy-start(f32[1,768]{1,0:T(1,128)} %gains.9) | copy-start | bytes 9220
  41.1 4.5 %collective-permute-start.4 = (bf16[112,896]{1,0:T(8,128)(2,1)S(1)}, bf16[112,896]{1,0:T(8,128)(2,1)S(1)}, u32[]{:S(2)}, u32[]{:S(2)}) collective-permute-start(bf16[112,896]{1,0:T(8,128)(2,1)S(1)} %shard_map.98.mine), channel_id=1, source_target_pairs={{0,2},{2,0},{4,6},{6,4},{8,10},{10,8},{12,14},{14,12},{1,3},{3,1},... | collective-permute-start | bytes 602120 | tf_op jit(solution)/shard_map/ppermute | solution.py:54
  46.6 9.3 %collective-permute-start.5 = (bf16[96,768]{1,0:T(8,128)(2,1)S(1)}, bf16[96,768]{1,0:T(8,128)(2,1)S(1)}, u32[]{:S(2)}, u32[]{:S(2)}) collective-permute-start(bf16[96,768]{1,0:T(8,128)(2,1)S(1)} %get-tuple-element.55.refs_1_), channel_id=1, source_target_pairs={{0,16},{2,17},{4,18},{6,19},{8,20},{10,21},{12,22},{14,23},{1,24},... | collective-permute-start | bytes 442376 | tf_op jit(solution)/shard_map/ppermute | solution.py:50
  57.8 8.0 %collective-permute-start.6 = (bf16[96,768]{1,0:T(8,128)(2,1)S(1)}, bf16[96,768]{1,0:T(8,128)(2,1)S(1)}, u32[]{:S(2)}, u32[]{:S(2)}) collective-permute-start(bf16[96,768]{1,0:T(8,128)(2,1)S(1)} %get-tuple-element.59.x.refs_1_), channel_id=1, source_target_pairs={{0,0},{1,2},{2,4},{3,6},{4,8},{5,10},{6,12},{7,14},{8,1},{9,3},{10... | collective-permute-start | bytes 442376 | tf_op jit(solution)/shard_map/ppermute | solution.py:41
  86.5 6.1 %collective-permute-start.7 = (bf16[96,3968]{1,0:T(8,128)(2,1)S(1)}, bf16[96,3968]{1,0:T(8,128)(2,1)S(1)}, u32[]{:S(2)}, u32[]{:S(2)}) collective-permute-start(bf16[96,3968]{1,0:T(8,128)(2,1)S(1)} %shard_map.102.mine), channel_id=1, source_target_pairs={{0,2},{2,0},{4,6},{6,4},{8,10},{10,8},{12,14},{14,12},{1,3},{3,1},... | collective-permute-start | bytes 2285576 | tf_op jit(solution)/shard_map/ppermute | solution.py:54
  93.3 13.0 %collective-permute-start.8 = (bf16[96,768]{1,0:T(8,128)(2,1)S(1)}, bf16[96,768]{1,0:T(8,128)(2,1)S(1)}, u32[]{:S(2)}, u32[]{:S(2)}) collective-permute-start(bf16[96,768]{1,0:T(8,128)(2,1)S(1)} %get-tuple-element.65.refs_1_), channel_id=1, source_target_pairs={{0,16},{2,17},{4,18},{6,19},{8,20},{10,21},{12,22},{14,23},{1,24},... | collective-permute-start | bytes 442376 | tf_op jit(solution)/shard_map/ppermute | solution.py:50
  104.3 13.3 %collective-permute-start.10 = (bf16[96,768]{1,0:T(8,128)(2,1)S(1)}, bf16[96,768]{1,0:T(8,128)(2,1)S(1)}, u32[]{:S(2)}, u32[]{:S(2)}) collective-permute-start(bf16[96,768]{1,0:T(8,128)(2,1)S(1)} %shard_map.105), channel_id=1, source_target_pairs={{16,0},{17,2},{18,4},{19,6},{20,8},{21,10},{22,12},{23,14},{24,1},... | collective-permute-start | bytes 442376 | tf_op jit(solution)/shard_map/ppermute | solution.py:41
  108.1 9.5 %collective-permute-start.9 = (bf16[96,768]{1,0:T(8,128)(2,1)S(1)}, bf16[96,768]{1,0:T(8,128)(2,1)S(1)}, u32[]{:S(2)}, u32[]{:S(2)}) collective-permute-start(bf16[96,768]{1,0:T(8,128)(2,1)S(1)} %get-tuple-element.68.x.refs_2_), channel_id=1, source_target_pairs={{0,0},{1,2},{2,4},{3,6},{4,8},{5,10},{6,12},{7,14},{8,1},{9,3},{10... | collective-permute-start | bytes 442376 | tf_op jit(solution)/shard_map/ppermute | solution.py:41
  138.6 4.8 %collective-permute-start.11 = (bf16[96,3968]{1,0:T(8,128)(2,1)S(1)}, bf16[96,3968]{1,0:T(8,128)(2,1)S(1)}, u32[]{:S(2)}, u32[]{:S(2)}) collective-permute-start(bf16[96,3968]{1,0:T(8,128)(2,1)S(1)} %shard_map.107.mine), channel_id=1, source_target_pairs={{0,2},{2,0},{4,6},{6,4},{8,10},{10,8},{12,14},{14,12},{1,3},{3,1},... | collective-permute-start | bytes 2285576 | tf_op jit(solution)/shard_map/ppermute | solution.py:54
  144.1 13.2 %collective-permute-start.12 = (bf16[96,768]{1,0:T(8,128)(2,1)S(1)}, bf16[96,768]{1,0:T(8,128)(2,1)S(1)}, u32[]{:S(2)}, u32[]{:S(2)}) collective-permute-start(bf16[96,768]{1,0:T(8,128)(2,1)S(1)} %get-tuple-element.73.refs_1_), channel_id=1, source_target_pairs={{0,16},{2,17},{4,18},{6,19},{8,20},{10,21},{12,22},{14,23},{1,24},... | collective-permute-start | bytes 442376 | tf_op jit(solution)/shard_map/ppermute | solution.py:50
  155.3 13.4 %collective-permute-start.14 = (bf16[96,768]{1,0:T(8,128)(2,1)S(1)}, bf16[96,768]{1,0:T(8,128)(2,1)S(1)}, u32[]{:S(2)}, u32[]{:S(2)}) collective-permute-start(bf16[96,768]{1,0:T(8,128)(2,1)S(1)} %shard_map.110), channel_id=1, source_target_pairs={{16,0},{17,2},{18,4},{19,6},{20,8},{21,10},{22,12},{23,14},{24,1},... | collective-permute-start | bytes 442376 | tf_op jit(solution)/shard_map/ppermute | solution.py:41
  159.1 9.6 %collective-permute-start.13 = (bf16[96,768]{1,0:T(8,128)(2,1)S(1)}, bf16[96,768]{1,0:T(8,128)(2,1)S(1)}, u32[]{:S(2)}, u32[]{:S(2)}) collective-permute-start(bf16[96,768]{1,0:T(8,128)(2,1)S(1)} %get-tuple-element.76.x), channel_id=1, source_target_pairs={{0,0},{1,2},{2,4},{3,6},{4,8},{5,10},{6,12},{7,14},{8,1},{9,3},{10... | collective-permute-start | bytes 442376 | tf_op jit(solution)/shard_map/ppermute | solution.py:41
  189.8 4.8 %collective-permute-start.15 = (bf16[96,3968]{1,0:T(8,128)(2,1)S(1)}, bf16[96,3968]{1,0:T(8,128)(2,1)S(1)}, u32[]{:S(2)}, u32[]{:S(2)}) collective-permute-start(bf16[96,3968]{1,0:T(8,128)(2,1)S(1)} %shard_map.112.mine), channel_id=1, source_target_pairs={{0,2},{2,0},{4,6},{6,4},{8,10},{10,8},{12,14},{14,12},{1,3},{3,1},... | collective-permute-start | bytes 2285576 | tf_op jit(solution)/shard_map/ppermute | solution.py:54
  198.2 14.1 %collective-permute-start.16 = (bf16[96,768]{1,0:T(8,128)(2,1)S(1)}, bf16[96,768]{1,0:T(8,128)(2,1)S(1)}, u32[]{:S(2)}, u32[]{:S(2)}) collective-permute-start(bf16[96,768]{1,0:T(8,128)(2,1)S(1)} %shard_map.114.after), channel_id=1, source_target_pairs={{16,0},{17,2},{18,4},{19,6},{20,8},{21,10},{22,12},{23,14},{24,1},... | collective-permute-start | bytes 442376 | tf_op jit(solution)/shard_map/ppermute | solution.py:41
  213.7 17.1 %all-to-all-start.4 = ((bf16[16,16,256]{2,1,0:T(8,128)(2,1)}), bf16[16,16,256]{2,1,0:T(8,128)(2,1)S(1)}, u32[]{:S(2)}, u32[]{:S(2)}) async-start(bf16[16,16,256]{2,1,0:T(8,128)(2,1)} %get-tuple-element.89), calls=%async_computation.4 | async-start | bytes 262144 | tf_op jit(solution)/shard_map/all_to_all | solution.py:501
  217.2 10.4 %collective-permute-start.17 = (f32[16,768]{1,0:T(8,128)S(1)}, f32[16,768]{1,0:T(8,128)S(1)}, u32[]{:S(2)}, u32[]{:S(2)}) collective-permute-start(f32[16,768]{1,0:T(8,128)S(1)} %get-tuple-element.90.mine), channel_id=1, source_target_pairs={{0,1},{1,0},{2,3},{3,2},{4,5},{5,4},{6,7},{7,6},{8,9},{9,8},{10,11... | collective-permute-start | bytes 147464 | tf_op jit(solution)/shard_map/ppermute | solution.py:490
  219.2 8.4 %collective-permute-start.19 = (bf16[16,768]{1,0:T(8,128)(2,1)S(1)}, bf16[16,768]{1,0:T(8,128)(2,1)S(1)}, u32[]{:S(2)}, u32[]{:S(2)}) collective-permute-start(bf16[16,768]{1,0:T(8,128)(2,1)S(1)} %get-tuple-element.91), channel_id=1, source_target_pairs={{2,0},{0,1},{6,2},{4,3},{10,4},{8,5},{14,6},{12,7},{3,8},{1,9},{7,... | collective-permute-start | bytes 73736 | tf_op jit(solution)/shard_map/ppermute | solution.py:331
  225.4 5.5 %collective-permute-start.18 = (bf16[16,768]{1,0:T(8,128)(2,1)S(1)}, bf16[16,768]{1,0:T(8,128)(2,1)S(1)}, u32[]{:S(2)}, u32[]{:S(2)}) collective-permute-start(bf16[16,768]{1,0:T(8,128)(2,1)S(1)} %get-tuple-element.91), channel_id=1, source_target_pairs={{0,0},{2,1},{4,2},{6,3},{8,4},{10,5},{12,6},{14,7},{1,8},{3,9},{5,... | collective-permute-start | bytes 73736 | tf_op jit(solution)/shard_map/ppermute | solution.py:331

commit v4 on v3

--- a/solution.py
+++ b/solution.py
@@ -110,35 +110,32 @@
     return jax.ShapeDtypeStruct(dims, dtype)
 
 
-FIRST_SECTION, TENSOR, LAST_SECTION, CORE, OWN_BLOCK, REPLICA, ORDER = range(7)
-
-
-def replicas(flags, mine, theirs):
-    half = flags[REPLICA] == 0
-    return jnp.concatenate([jnp.where(half, mine, theirs), jnp.where(half, theirs, mine)])
-
-
-def prepare_kernel(flags, grads, up, stored, packed, chosen):
-    toks = grads.shape[0]
-    packed[:toks] = grads[...]
-    packed[toks:] = up[...]
-    for j in range(TICKS - 1):
-        chosen[j] = jnp.where(flags[ORDER + j] == 0, stored[0], stored[1])
-
-
-def forward_kernel(start, flags, *refs):
-    place = flags[TENSOR]
+def own_block():
+    tensor = lax.axis_index("tensor")
+    return jnp.where(tensor // CHIPS == lax.axis_index("dp"), tensor % CHIPS, -1)
+
+
+def replicas(mine, theirs):
+    first = lax.axis_index("dp") == 0
+    return jnp.concatenate([jnp.where(first, mine, theirs), jnp.where(first, theirs, mine)])
+
+
+def forward_kernel(start, tick, *refs):
+    place = lax.axis_index("tensor")
     if start:
-        mine, theirs, gains, w, down_rows, x_out, product, small, down = refs
-        x = replicas(flags, mine[...], theirs[...])
+        _, _, _, _, mine, theirs, gains, w, down_rows, x_out, product, small, down = refs
+        x = replicas(mine[...], theirs[...])
         rank, feats = down_rows.shape
         down[:LOW] = jnp.zeros((LOW, feats), F32)
         down[LOW : LOW + rank] = down_rows[...].astype(F32)
         down[LOW + rank :] = jnp.zeros((LANES - LOW - rank, feats), F32)
     else:
-        tick, arrived, mine, theirs, gains, w, down, x_out, product, small = refs
-        given = replicas(flags, mine[tick - 1], theirs[tick - 1])
-        x = jnp.where(flags[FIRST_SECTION] == 1, given, arrived[...])
+        order, order_theirs, arrived, mine, theirs, gains, w, down, x_out, product, small = refs
+        given = replicas(
+            jnp.where(order[tick] == 0, mine[0], mine[1]),
+            jnp.where(order_theirs[tick] == 0, theirs[0], theirs[1]),
+        )
+        x = jnp.where(lax.axis_index("section") == 0, given, arrived[...])
     x_out[...] = x
     rows, feats = x.shape
     wide = x.astype(F32)
@@ -168,29 +165,33 @@
         product[j] = part.astype(BF)
 
 
-def chosen_grad(flags, arrived, output):
-    kept = jnp.where(flags[CORE] == 0, output[...], jnp.zeros(output.shape, BF))
-    return jnp.where(flags[LAST_SECTION] == 1, kept, arrived[...])
-
-
-def pack_kernel(start, flags, product, small, x_owned, *refs):
-    rows, feats = product.shape[1:]
+def first_core():
+    return lax.axis_index("tensor") % 2 == 0
+
+
+def chosen_grad(sections, arrived, output):
+    kept = jnp.where(first_core(), output[...], jnp.zeros(output.shape, BF))
+    return jnp.where(lax.axis_index("section") == sections - 1, kept, arrived[...])
+
+
+def pack_kernel(start, sections, product, small, x, *refs):
+    rows, feats = x.shape
     values = small[...]
     if start:
-        given, theirs, parcel, up, grad_out = refs
+        given, given_up, parcel, up, grad_out = refs
         columns = feats
-        toks = theirs.shape[1]
-        rank = given.shape[0] - toks
+        toks = given.shape[0]
+        rank = given_up.shape[0]
         up[:LOW] = jnp.zeros((LOW, feats), BF)
-        up[LOW : LOW + rank] = given[toks:]
+        up[LOW : LOW + rank] = given_up[...]
         up[LOW + rank :] = jnp.zeros((LANES - LOW - rank, feats), BF)
         zeros = jnp.zeros((toks, feats), BF)
-        grad_out[:toks] = jnp.where(flags[CORE] == 0, given[:toks], zeros)
-        grad_out[toks:] = jnp.where(flags[CORE] == 0, zeros, given[:toks])
+        grad_out[:toks] = jnp.where(first_core(), given[...], zeros)
+        grad_out[toks:] = jnp.where(first_core(), zeros, given[...])
     else:
         arrived, output, up, gain_w, mixed, parcel, grad_out = refs
         columns = 2 * feats
-        grad = chosen_grad(flags, arrived, output)
+        grad = chosen_grad(sections, arrived, output)
         grad_out[...] = grad
         wide = grad.astype(F32)
         first = jnp.sum(wide * jnp.sum(gain_w[...], axis=0, keepdims=True), axis=1, keepdims=True)
@@ -202,34 +203,44 @@
         for j in range(CHIPS):
             parcel[j, :, feats : 2 * feats] = grad
     halves = split(values)
+    block = own_block()
     for j in range(CHIPS):
         parcel[j, :, :feats] = product[j]
-        parcel[j, :, columns:] = halves
+        parcel[j, :rows, columns : columns + feats] = jnp.where(
+            block == j, x[...], jnp.zeros(x.shape, BF)
+        )
+        if start:
+            parcel[j, rows:, columns : columns + feats] = jnp.zeros((4 * CHIPS, feats), BF)
+        parcel[j, :, columns + feats :] = halves
 
 
 def gather_kernel(start, got, out):
-    feats = (got.shape[2] - LANES) // (1 if start else 2)
+    feats = (got.shape[2] - LANES) // (2 if start else 3)
     total = got[0, :, :feats].astype(F32)
+    x = got[0, :, -LANES - feats : -LANES]
     values = join(got[0, :, -LANES:])
     for j in range(1, CHIPS):
         total = total + got[j, :, :feats].astype(F32)
+        x = x + got[j, :, -LANES - feats : -LANES]
         values = values + join(got[j, :, -LANES:])
     out[:, :feats] = total.astype(BF)
-    out[:, feats : feats + LANES] = split(values)
+    out[:, feats : 2 * feats] = x
+    out[:, 2 * feats : 2 * feats + LANES] = split(values)
     if not start:
         for j in range(CHIPS):
-            at = feats + LANES + j * feats
+            at = 2 * feats + LANES + j * feats
             out[:, at : at + feats] = got[j, :, feats : 2 * feats]
 
 
-def output_kernel(start, mine, theirs, x, up, gain_w, gain_low, output, mixed, stats, sums):
-    rows, feats = x.shape
+def output_kernel(start, mine, theirs, up, gain_w, gain_low, output, mixed, stats, sums):
+    rows, feats = output.shape
+    ends = slice(2 * feats, 2 * feats + LANES)
     if start:
         tail = mine[rows:, :feats].astype(F32) + theirs[rows:, :feats].astype(F32)
         gain_w[...] = tail[: 2 * CHIPS] + tail[2 * CHIPS :]
-        tail = join(mine[rows:, feats:]) + join(theirs[rows:, feats:])
+        tail = join(mine[rows:, ends]) + join(theirs[rows:, ends])
         gain_low[...] = between(tail[: 2 * CHIPS], LOW, GRAD)
-    values = join(mine[:rows, feats : feats + LANES]) + join(theirs[:rows, feats : feats + LANES])
+    values = join(mine[:rows, ends]) + join(theirs[:rows, ends])
     values = between(values, 0, LANES // 2)
     sums[...] = values
     at = lane(rows)
@@ -247,7 +258,8 @@
     low = between(inv * low, LOW, GRAD)
     mixed[...] = total
     stats[...] = jnp.where(at == 0, mean, jnp.where(at == 1, inv, low))
-    output[...] = (x[...].astype(F32) + total + dot(low.astype(BF), up[...])).astype(BF)
+    x = mine[:rows, feats : 2 * feats].astype(F32) + theirs[:rows, feats : 2 * feats].astype(F32)
+    output[...] = (x + total + dot(low.astype(BF), up[...])).astype(BF)
 
 
 def rank_grads(sums):
@@ -258,7 +270,7 @@
     return (x.astype(F32) - pick(stats, 0, 1)) * pick(stats, 1, 2)
 
 
-def backward_kernel(flags, mine, theirs, sums, x, stats, gains, gain_low, w, down, grad_out):
+def backward_kernel(mine, theirs, sums, x, stats, gains, gain_low, w, down, grad_out):
     rows, feats = x.shape
     width = feats * 2 * CHIPS
     values = sums[...]
@@ -271,11 +283,11 @@
     grad_norm = dot(low_grad, down[...], precision=HIGHEST)
     here = jnp.zeros((rows, feats), F32)
     for j in range(CHIPS):
-        at = feats + LANES + j * feats
+        at = 2 * feats + LANES + j * feats
         grad = mine[:, at : at + feats].astype(F32) + theirs[:, at : at + feats].astype(F32)
         grad = grad.astype(BF)
         grad_norm = grad_norm + dot_t(grad, w[:, j * feats : (j + 1) * feats])
-        here = here + jnp.where(flags[OWN_BLOCK] == j, grad.astype(F32), 0.0)
+        here = here + jnp.where(own_block() == j, grad.astype(F32), 0.0)
     inv = pick(stats[...], 1, 2)
     grad_x = here + inv * (grad_norm * gains[...] - first / width - xhat * (second / width))
     grad_out[...] = grad_x.astype(BF)
@@ -295,10 +307,10 @@
     acc_up[...] = up[LOW : LOW + rank]
 
 
-def last_kernel(flags, arrived, output, up, stats, acc_up, low_out, up_out):
+def last_kernel(sections, arrived, output, up, stats, acc_up, after, low_out, up_out):
     rows, feats = arrived.shape
     rank = acc_up.shape[0]
-    grad = chosen_grad(flags, arrived, output)
+    grad = chosen_grad(sections, arrived, output)
     turned = dot_t(up[LOW : LOW + rank], grad)
     turned = jnp.concatenate([turned, jnp.zeros((rank, LANES - rows), F32)], axis=1)
     high = turned.astype(BF).astype(F32)
@@ -346,39 +358,19 @@
     w = weight[0]
     gains = gain
     sections = lax.axis_size("section")
-    section = lax.axis_index("section")
-    tensor = lax.axis_index("tensor")
-    half = lax.axis_index("dp")
     toks, feats = initial_step_inputs.shape[1:]
     rank = adapter_up_map.shape[1]
     rows = 2 * toks
-    flags = [
-        section == 0,
-        tensor,
-        section == sections - 1,
-        tensor % 2,
-        jnp.where(tensor // CHIPS == half, tensor % CHIPS, -1),
-        half,
-    ]
-    flags = jnp.stack([f.astype(jnp.int32) for f in flags])
-    flags = (jnp.concatenate([flags, sample_numbers[0, 0, 1:]]),)
 
     mine = initial_step_inputs[0]
     theirs = lax.ppermute(mine, "dp", [(0, 1), (1, 0)])
-    packed, chosen = call(
-        prepare_kernel,
-        [shape(toks + rank, feats, dtype=BF), shape(TICKS - 1, toks, feats, dtype=BF)],
-        initial_step_gradients[0],
-        adapter_up_map[0],
-        prior_epoch_input[0, 0],
-        scalars=flags,
-    )
-    given = to_owner(packed, sections, 0)
-    chosen_theirs = lax.ppermute(
-        chosen,
-        AXES,
-        [(flat(0, t, d), flat(0, t, 1 - d)) for t in range(2 * CHIPS) for d in range(2)],
-    )
+    given = to_owner(initial_step_gradients[0], sections, 0)
+    given_up = to_owner(adapter_up_map[0], sections, 0)
+    stored = prior_epoch_input[0, 0]
+    order = sample_numbers[0, 0]
+    to_partner = [(flat(0, t, d), flat(0, t, 1 - d)) for t in range(2 * CHIPS) for d in range(2)]
+    stored_theirs = lax.ppermute(stored, AXES, to_partner)
+    order_theirs = lax.ppermute(order, AXES, to_partner)
 
     block = shape(rows, feats, dtype=BF)
     values = shape(rows, LANES)
@@ -389,65 +381,65 @@
         out = [block, shape(CHIPS, rows + more, feats, dtype=BF), shape(rows + more, LANES)]
         if start:
             x, product, small, down = call(
-                functools.partial(forward_kernel, True),
+                functools.partial(forward_kernel, True, tick),
                 out + [shape(LANES, feats)],
+                given,
+                given_up,
+                stored_theirs,
                 mine,
                 theirs,
                 gains,
                 w,
                 adapter_down_map[0].T,
-                scalars=flags,
+                scalars=(order_theirs,),
             )
         else:
             x, product, small = call(
-                lambda flags, *refs, tick=tick: forward_kernel(False, flags, tick, *refs),
+                functools.partial(forward_kernel, False, tick),
                 out,
                 arrived,
-                chosen,
-                chosen_theirs,
+                stored,
+                stored_theirs,
                 gains,
                 w,
                 down,
-                scalars=flags,
+                scalars=(order, order_theirs),
             )
-        x_owned = to_owner(x, sections, 0)
-        columns = (1 if start else 2) * feats + LANES
+        columns = (2 if start else 3) * feats + LANES
         parcel = shape(CHIPS, rows + more, columns, dtype=BF)
         if start:
             parcel, up, grad_arrived = call(
-                functools.partial(pack_kernel, True),
+                functools.partial(pack_kernel, True, sections),
                 [parcel, shape(LANES, feats, dtype=BF), block],
                 product,
                 small,
-                x_owned,
+                x,
                 given,
-                chosen_theirs,
-                scalars=flags,
+                given_up,
             )
         else:
             parcel, grad = call(
-                functools.partial(pack_kernel, False),
+                functools.partial(pack_kernel, False, sections),
                 [parcel, block],
                 product,
                 small,
-                x_owned,
+                x,
                 grad_arrived,
                 output,
                 up,
                 gain_w,
                 mixed,
-                scalars=flags,
             )
             grads.append(grad)
         got = over_chips(parcel)
         own = call(
             functools.partial(gather_kernel, start),
-            shape(rows + more, feats + LANES + (0 if start else CHIPS * feats), dtype=BF),
+            shape(rows + more, 2 * feats + LANES + (0 if start else CHIPS * feats), dtype=BF),
             got,
         )
         other = swap_cores(own)
         out = [block, shape(rows, feats), values, values]
-        ins = [own, other, x_owned, up]
+        ins = [own, other, up]
         kernel = functools.partial(output_kernel, start)
         if start:
             gain_w, gain_low, output, mixed, stats, sums = call(
@@ -471,7 +463,6 @@
                 gain_low,
                 w,
                 down,
-                scalars=flags,
             )
             grad_arrived = to_owner(grad_x, sections, 1)
         xs.append(x)
@@ -489,14 +480,14 @@
     )
     acc_other = lax.ppermute(acc_down, "dp", [(0, 1), (1, 0)])
     turned, up_part = call(
-        last_kernel,
+        functools.partial(last_kernel, sections),
         [shape(4 * CHIPS, rank, 2 * LANES, dtype=BF), shape(rank, feats, dtype=BF)],
         grad_arrived,
         output,
         up,
         stats,
         acc_up,
-        scalars=flags,
+        acc_other,
     )
     got = lax.all_to_all(turned, ("tensor", "dp"), 0, 0)
     grad_down, grad_up = call(

time: 233 us -> 232 us (level)
  the two profiles are of different devices: /device:TPU:121 before, /device:TPU:116 now
where the time goes in v4:
time: 232 us; the launch traced here: 231 us
  blocking collectives  97 us (42%)
  starting transfers between devices  63.3 us (27%)
  waiting for transfers between devices  43 us (19%)
  Pallas kernels  22.5 us (10%)
  local copies, waits for them, and re-layouts  4.65 us (2%)
    all_to_all x4, blocking collectives, over_chips(): return lax.all_to_all(array, 'tensor', 0, 0, axis_index_groups=groups)  97 us
    pallas_call x22, Pallas kernels, call(): pl.pallas_call(kernel, out_shape=out, in_specs=[pl.BlockSpec(memory_space...  22.5 us
    ppermute x5, waiting for transfers between devices, to_owner(): return lax.ppermute(array, AXES, route)  21.7 us
    ppermute x3, starting transfers between devices, to_next(): return lax.ppermute(array, AXES, route)  20.4 us
    ppermute x5, starting transfers between devices, to_owner(): return lax.ppermute(array, AXES, route)  12.6 us
    ppermute x4, waiting for transfers between devices, swap_cores(): return lax.ppermute(array, 'tensor', [(i, i ^ 1) for i in range(2 * CHIPS)])  8.94 us
    all_to_all x1, starting transfers between devices, on_device(): got = lax.all_to_all(turned, ('tensor', 'dp'), 0, 0)  8.57 us
    ppermute x4, starting transfers between devices, swap_cores(): return lax.ppermute(array, 'tensor', [(i, i ^ 1) for i in range(2 * CHIPS)])  7.68 us
  transfers between devices with their start and end apart: 19, of which 12 were waited for; matrix products, arithmetic and copies ran while one was open for 0% of the time, Pallas kernels for 4%

profile of v4, /device:TPU:116, one launch (start us, length us, event | category | flops | bytes accessed | tf_op | source)
XLA Modules:
  0.0 231.3 jit_solution(5817644203104482397)
XLA Ops:
  1.3 3.2 %collective-permute-start.4 = (bf16[48,768]{1,0:T(8,128)(2,1)}, bf16[48,768]{1,0:T(8,128)(2,1)S(1)}, u32[]{:S(2)}, u32[]{:S(2)}) collective-permute-start(bf16[48,768]{1,0:T(8,128)(2,1)} %bitcast.24), channel_id=1, source_target_pairs={{0,1},{1,0},{2,3},{3,2},{4,5},{5,4},{6,7},{7,6},{8,9},{9,8},{10,11... | collective-permute-start | bytes 221192 | tf_op jit(solution)/shard_map/ppermute | solution.py:366
  4.5 2.6 %collective-permute-start.1 = (bf16[48,768]{1,0:T(8,128)(2,1)}, bf16[48,768]{1,0:T(8,128)(2,1)S(1)}, u32[]{:S(2)}, u32[]{:S(2)}) collective-permute-start(bf16[48,768]{1,0:T(8,128)(2,1)} %bitcast.31), channel_id=1, source_target_pairs={{0,0},{1,2},{2,4},{3,6},{4,8},{5,10},{6,12},{7,14},{8,1},{9,3},{10... | collective-permute-start | bytes 221192 | tf_op jit(solution)/shard_map/ppermute | solution.py:41
  7.1 2.4 %collective-permute-start.2 = (bf16[16,768]{1,0:T(8,128)(2,1)}, bf16[16,768]{1,0:T(8,128)(2,1)S(1)}, u32[]{:S(2)}, u32[]{:S(2)}) collective-permute-start(bf16[16,768]{1,0:T(8,128)(2,1)} %bitcast.32), channel_id=1, source_target_pairs={{0,0},{1,2},{2,4},{3,6},{4,8},{5,10},{6,12},{7,14},{8,1},{9,3},{10... | collective-permute-start | bytes 73736 | tf_op jit(solution)/shard_map/ppermute | solution.py:41
  10.1 2.9 %collective-permute-done.2.refs_2_.refs_1_ = bf16[16,768]{1,0:T(8,128)(2,1)S(1)} collective-permute-done((bf16[16,768]{1,0:T(8,128)(2,1)}, bf16[16,768]{1,0:T(8,128)(2,1)S(1)}, u32[]{:S(2)}, u32[]{:S(2)}) %collective-permute-start.2) | collective-permute-done | bytes 24608 | tf_op jit(solution)/shard_map/ppermute | solution.py:41
  13.1 2.3 %copy-done = bf16[1,768,3072]{2,1,0:T(8,128)(2,1)S(1)} copy-done((bf16[1,768,3072]{2,1,0:T(8,128)(2,1)S(1)}, bf16[1,768,3072]{2,1,0:T(8,128)(2,1)}, u32[]{:S(2)}) %copy-start) | copy-done | bytes 4718616
  17.7 2.0 shard_map.95
  19.9 23.5 %all_to_all.25.got = bf16[4,112,1664]{2,1,0:T(8,128)(2,1)S(1)} all-to-all(bf16[4,112,1664]{2,1,0:T(8,128)(2,1)S(1)} %get-tuple-element.49), channel_id=1, replica_groups={{0,4,8,12},{2,6,10,14},{1,5,9,13},{3,7,11,15},{16,20,24,28},{18,22,26,3..., dimensions={0} | all-to-all | bytes 2981888 | tf_op jit(solution)/shard_map/all_to_all | solution.py:59
  48.5 5.8 %collective-permute-start.6 = (bf16[96,768]{1,0:T(8,128)(2,1)S(1)}, bf16[96,768]{1,0:T(8,128)(2,1)S(1)}, u32[]{:S(2)}, u32[]{:S(2)}) collective-permute-start(bf16[96,768]{1,0:T(8,128)(2,1)S(1)} %get-tuple-element.51.refs_1_), channel_id=1, source_target_pairs={{0,16},{2,17},{4,18},{6,19},{8,20},{10,21},{12,22},{14,23},{1,24},... | collective-permute-start | bytes 442376 | tf_op jit(solution)/shard_map/ppermute | solution.py:50
  54.3 4.3 %collective-permute-done.6.refs_2_ = bf16[96,768]{1,0:T(8,128)(2,1)S(1)} collective-permute-done((bf16[96,768]{1,0:T(8,128)(2,1)S(1)}, bf16[96,768]{1,0:T(8,128)(2,1)S(1)}, u32[]{:S(2)}, u32[]{:S(2)}) %collective-permute-start.6) | collective-permute-done | bytes 147488 | tf_op jit(solution)/shard_map/ppermute | solution.py:50
  60.9 27.3 %all_to_all.26.got = bf16[4,96,2432]{2,1,0:T(8,128)(2,1)S(1)} all-to-all(bf16[4,96,2432]{2,1,0:T(8,128)(2,1)S(1)} %get-tuple-element.59), channel_id=1, replica_groups={{0,4,8,12},{2,6,10,14},{1,5,9,13},{3,7,11,15},{16,20,24,28},{18,22,26,3..., dimensions={0} | all-to-all | bytes 3735552 | tf_op jit(solution)/shard_map/all_to_all | solution.py:59
  88.5 1.9 collective-permute-start.7
  90.4 2.4 %collective-permute-done.7.theirs = bf16[96,4736]{1,0:T(8,128)(2,1)S(1)} collective-permute-done((bf16[96,4736]{1,0:T(8,128)(2,1)S(1)}, bf16[96,4736]{1,0:T(8,128)(2,1)S(1)}, u32[]{:S(2)}, u32[]{:S(2)}) %collective-permute-start.7) | collective-permute-done | bytes 909344 | tf_op jit(solution)/shard_map/ppermute | solution.py:54
  93.5 8.6 %collective-permute-start.8 = (bf16[96,768]{1,0:T(8,128)(2,1)S(1)}, bf16[96,768]{1,0:T(8,128)(2,1)S(1)}, u32[]{:S(2)}, u32[]{:S(2)}) collective-permute-start(bf16[96,768]{1,0:T(8,128)(2,1)S(1)} %get-tuple-element.61.refs_1_), channel_id=1, source_target_pairs={{0,16},{2,17},{4,18},{6,19},{8,20},{10,21},{12,22},{14,23},{1,24},... | collective-permute-start | bytes 442376 | tf_op jit(solution)/shard_map/ppermute | solution.py:50
  103.9 1.9 collective-permute-start.9
  107.8 8.7 %collective-permute-done.9.refs_0_ = bf16[96,768]{1,0:T(8,128)(2,1)S(1)} collective-permute-done((bf16[96,768]{1,0:T(8,128)(2,1)S(1)}, bf16[96,768]{1,0:T(8,128)(2,1)S(1)}, u32[]{:S(2)}, u32[]{:S(2)}) %collective-permute-start.9) | collective-permute-done | bytes 147488 | tf_op jit(solution)/shard_map/ppermute | solution.py:41
  116.8 22.7 %all_to_all.27.got = bf16[4,96,2432]{2,1,0:T(8,128)(2,1)S(1)} all-to-all(bf16[4,96,2432]{2,1,0:T(8,128)(2,1)S(1)} %get-tuple-element.68), channel_id=1, replica_groups={{0,4,8,12},{2,6,10,14},{1,5,9,13},{3,7,11,15},{16,20,24,28},{18,22,26,3..., dimensions={0} | all-to-all | bytes 3735552 | tf_op jit(solution)/shard_map/all_to_all | solution.py:59
  139.8 1.9 collective-permute-start.10
  141.7 2.4 %collective-permute-done.10.theirs = bf16[96,4736]{1,0:T(8,128)(2,1)S(1)} collective-permute-done((bf16[96,4736]{1,0:T(8,128)(2,1)S(1)}, bf16[96,4736]{1,0:T(8,128)(2,1)S(1)}, u32[]{:S(2)}, u32[]{:S(2)}) %collective-permute-start.10) | collective-permute-done | bytes 909344 | tf_op jit(solution)/shard_map/ppermute | solution.py:54
  144.8 6.0 %collective-permute-start.11 = (bf16[96,768]{1,0:T(8,128)(2,1)S(1)}, bf16[96,768]{1,0:T(8,128)(2,1)S(1)}, u32[]{:S(2)}, u32[]{:S(2)}) collective-permute-start(bf16[96,768]{1,0:T(8,128)(2,1)S(1)} %get-tuple-element.69.refs_1_), channel_id=1, source_target_pairs={{0,16},{2,17},{4,18},{6,19},{8,20},{10,21},{12,22},{14,23},{1,24},... | collective-permute-start | bytes 442376 | tf_op jit(solution)/shard_map/ppermute | solution.py:50
  152.6 2.5 %collective-permute-start.12 = (bf16[96,768]{1,0:T(8,128)(2,1)S(1)}, bf16[96,768]{1,0:T(8,128)(2,1)S(1)}, u32[]{:S(2)}, u32[]{:S(2)}) collective-permute-start(bf16[96,768]{1,0:T(8,128)(2,1)S(1)} %shard_map.109), channel_id=1, source_target_pairs={{16,0},{17,2},{18,4},{19,6},{20,8},{21,10},{22,12},{23,14},{24,1},... | collective-permute-start | bytes 442376 | tf_op jit(solution)/shard_map/ppermute | solution.py:41
  157.0 8.1 %collective-permute-done.12.refs_0_ = bf16[96,768]{1,0:T(8,128)(2,1)S(1)} collective-permute-done((bf16[96,768]{1,0:T(8,128)(2,1)S(1)}, bf16[96,768]{1,0:T(8,128)(2,1)S(1)}, u32[]{:S(2)}, u32[]{:S(2)}) %collective-permute-start.12) | collective-permute-done | bytes 147488 | tf_op jit(solution)/shard_map/ppermute | solution.py:41
  165.5 23.4 %all_to_all.28.got = bf16[4,96,2432]{2,1,0:T(8,128)(2,1)S(1)} all-to-all(bf16[4,96,2432]{2,1,0:T(8,128)(2,1)S(1)} %get-tuple-element.76), channel_id=1, replica_groups={{0,4,8,12},{2,6,10,14},{1,5,9,13},{3,7,11,15},{16,20,24,28},{18,22,26,3..., dimensions={0} | all-to-all | bytes 3735552 | tf_op jit(solution)/shard_map/all_to_all | solution.py:59
  191.1 2.4 %collective-permute-done.13.theirs = bf16[96,4736]{1,0:T(8,128)(2,1)S(1)} collective-permute-done((bf16[96,4736]{1,0:T(8,128)(2,1)S(1)}, bf16[96,4736]{1,0:T(8,128)(2,1)S(1)}, u32[]{:S(2)}, u32[]{:S(2)}) %collective-permute-start.13) | collective-permute-done | bytes 909344 | tf_op jit(solution)/shard_map/ppermute | solution.py:54
  196.6 3.3 %collective-permute-start.14 = (bf16[96,768]{1,0:T(8,128)(2,1)S(1)}, bf16[96,768]{1,0:T(8,128)(2,1)S(1)}, u32[]{:S(2)}, u32[]{:S(2)}) collective-permute-start(bf16[96,768]{1,0:T(8,128)(2,1)S(1)} %shard_map.113.after), channel_id=1, source_target_pairs={{16,0},{17,2},{18,4},{19,6},{20,8},{21,10},{22,12},{23,14},{24,1},... | collective-permute-start | bytes 442376 | tf_op jit(solution)/shard_map/ppermute | solution.py:41
  201.4 4.0 %collective-permute-start.15 = (f32[16,768]{1,0:T(8,128)S(1)}, f32[16,768]{1,0:T(8,128)S(1)}, u32[]{:S(2)}, u32[]{:S(2)}) collective-permute-start(f32[16,768]{1,0:T(8,128)S(1)} %get-tuple-element.85.mine), channel_id=1, source_target_pairs={{0,1},{1,0},{2,3},{3,2},{4,5},{5,4},{6,7},{7,6},{8,9},{9,8},{10,11... | collective-permute-start | bytes 147464 | tf_op jit(solution)/shard_map/ppermute | solution.py:481
  205.3 2.1 collective-permute-done.15.after.theirs
  207.4 2.1 collective-permute-done.14.arrived
  210.3 8.6 %all-to-all-start.4 = ((bf16[16,16,256]{2,1,0:T(8,128)(2,1)}), bf16[16,16,256]{2,1,0:T(8,128)(2,1)S(1)}, u32[]{:S(2)}, u32[]{:S(2)}) async-start(bf16[16,16,256]{2,1,0:T(8,128)(2,1)} %get-tuple-element.86), calls=%async_computation.4 | async-start | bytes 262144 | tf_op jit(solution)/shard_map/all_to_all | solution.py:492
  218.9 3.4 %collective-permute-start.17 = (bf16[16,768]{1,0:T(8,128)(2,1)S(1)}, bf16[16,768]{1,0:T(8,128)(2,1)S(1)}, u32[]{:S(2)}, u32[]{:S(2)}) collective-permute-start(bf16[16,768]{1,0:T(8,128)(2,1)S(1)} %get-tuple-element.87), channel_id=1, source_target_pairs={{2,0},{0,1},{6,2},{4,3},{10,4},{8,5},{14,6},{12,7},{3,8},{1,9},{7,... | collective-permute-start | bytes 73736 | tf_op jit(solution)/shard_map/ppermute | solution.py:343
  222.3 2.2 collective-permute-start.16
  224.5 1.9 collective-permute-done.17.up_b
  226.4 4.0 %collective-permute-done.16.up_a = bf16[16,768]{1,0:T(8,128)(2,1)S(1)} collective-permute-done((bf16[16,768]{1,0:T(8,128)(2,1)S(1)}, bf16[16,768]{1,0:T(8,128)(2,1)S(1)}, u32[]{:S(2)}, u32[]{:S(2)}) %collective-permute-start.16) | collective-permute-done | bytes 24608 | tf_op jit(solution)/shard_map/ppermute | solution.py:343
  (48 shorter events, 29.6 us)
Async XLA Ops:
  0.6 12.4 %collective-permute-start.3 = (bf16[2,48,768]{2,1,0:T(8,128)(2,1)}, bf16[2,48,768]{2,1,0:T(8,128)(2,1)S(1)}, u32[]{:S(2)}, u32[]{:S(2)}) collective-permute-start(bf16[2,48,768]{2,1,0:T(8,128)(2,1)} %bitcast.20), channel_id=1, source_target_pairs={{0,1},{1,0},{2,3},{3,2},{4,5},{5,4},{6,7},{7,6},{8,9},{9,8},{10,11... | collective-permute-start | bytes 442376 | tf_op jit(solution)/shard_map/ppermute | solution.py:372
  1.3 11.7 %collective-permute-start.4 = (bf16[48,768]{1,0:T(8,128)(2,1)}, bf16[48,768]{1,0:T(8,128)(2,1)S(1)}, u32[]{:S(2)}, u32[]{:S(2)}) collective-permute-start(bf16[48,768]{1,0:T(8,128)(2,1)} %bitcast.24), channel_id=1, source_target_pairs={{0,1},{1,0},{2,3},{3,2},{4,5},{5,4},{6,7},{7,6},{8,9},{9,8},{10,11... | collective-permute-start | bytes 221192 | tf_op jit(solution)/shard_map/ppermute | solution.py:366
  4.5 8.5 %collective-permute-start.1 = (bf16[48,768]{1,0:T(8,128)(2,1)}, bf16[48,768]{1,0:T(8,128)(2,1)S(1)}, u32[]{:S(2)}, u32[]{:S(2)}) collective-permute-start(bf16[48,768]{1,0:T(8,128)(2,1)} %bitcast.31), channel_id=1, source_target_pairs={{0,0},{1,2},{2,4},{3,6},{4,8},{5,10},{6,12},{7,14},{8,1},{9,3},{10... | collective-permute-start | bytes 221192 | tf_op jit(solution)/shard_map/ppermute | solution.py:41
  7.1 5.9 %collective-permute-start.2 = (bf16[16,768]{1,0:T(8,128)(2,1)}, bf16[16,768]{1,0:T(8,128)(2,1)S(1)}, u32[]{:S(2)}, u32[]{:S(2)}) collective-permute-start(bf16[16,768]{1,0:T(8,128)(2,1)} %bitcast.32), channel_id=1, source_target_pairs={{0,0},{1,2},{2,4},{3,6},{4,8},{5,10},{6,12},{7,14},{8,1},{9,3},{10... | collective-permute-start | bytes 73736 | tf_op jit(solution)/shard_map/ppermute | solution.py:41
  9.5 0.7 collective-permute-start
  13.1 2.3 %copy-start = (bf16[1,768,3072]{2,1,0:T(8,128)(2,1)S(1)}, bf16[1,768,3072]{2,1,0:T(8,128)(2,1)}, u32[]{:S(2)}) copy-start(bf16[1,768,3072]{2,1,0:T(8,128)(2,1)} %param.9) | copy-start | bytes 14155780
  15.4 0.7 copy-start.3
  16.1 0.9 copy-start.5
  17.0 0.7 copy-start.6
  19.9 38.7 %copy-start.1 = (bf16[1,768,3072]{2,1,0:T(8,128)(2,1)S(1)}, bf16[1,768,3072]{2,1,0:T(8,128)(2,1)}, u32[]{:S(2)}) copy-start(bf16[1,768,3072]{2,1,0:T(8,128)(2,1)} %param.9) | copy-start | bytes 14155780
  43.4 15.2 %copy-start.2 = (bf16[1,1,2,48,768]{4,3,2,1,0:T(8,128)(2,1)S(1)}, bf16[1,1,2,48,768]{4,3,2,1,0:T(8,128)(2,1)}, u32[]{:S(2)}) copy-start(bf16[1,1,2,48,768]{4,3,2,1,0:T(8,128)(2,1)} %param.13) | copy-start | bytes 442372
  43.4 15.2 %copy-start.4 = (f32[1,768]{1,0:T(1,128)S(1)}, f32[1,768]{1,0:T(1,128)}, u32[]{:S(2)}) copy-start(f32[1,768]{1,0:T(1,128)} %gains.9) | copy-start | bytes 9220
  43.4 15.2 %copy-start.7 = (s32[1,1,4]{2,1,0:T(1,128)S(1)}, s32[1,1,4]{2,1,0:T(1,128)}, u32[]{:S(2)}) copy-start(s32[1,1,4]{2,1,0:T(1,128)} %param.16) | copy-start | bytes 52
  43.7 3.6 %collective-permute-start.5 = (bf16[112,1664]{1,0:T(8,128)(2,1)S(1)}, bf16[112,1664]{1,0:T(8,128)(2,1)S(1)}, u32[]{:S(2)}, u32[]{:S(2)}) collective-permute-start(bf16[112,1664]{1,0:T(8,128)(2,1)S(1)} %shard_map.97.mine), channel_id=1, source_target_pairs={{0,2},{2,0},{4,6},{6,4},{8,10},{10,8},{12,14},{14,12},{1,3},{3,1},... | collective-permute-start | bytes 1118216 | tf_op jit(solution)/shard_map/ppermute | solution.py:54
  48.5 10.2 %collective-permute-start.6 = (bf16[96,768]{1,0:T(8,128)(2,1)S(1)}, bf16[96,768]{1,0:T(8,128)(2,1)S(1)}, u32[]{:S(2)}, u32[]{:S(2)}) collective-permute-start(bf16[96,768]{1,0:T(8,128)(2,1)S(1)} %get-tuple-element.51.refs_1_), channel_id=1, source_target_pairs={{0,16},{2,17},{4,18},{6,19},{8,20},{10,21},{12,22},{14,23},{1,24},... | collective-permute-start | bytes 442376 | tf_op jit(solution)/shard_map/ppermute | solution.py:50
  88.5 4.4 %collective-permute-start.7 = (bf16[96,4736]{1,0:T(8,128)(2,1)S(1)}, bf16[96,4736]{1,0:T(8,128)(2,1)S(1)}, u32[]{:S(2)}, u32[]{:S(2)}) collective-permute-start(bf16[96,4736]{1,0:T(8,128)(2,1)S(1)} %shard_map.101.mine), channel_id=1, source_target_pairs={{0,2},{2,0},{4,6},{6,4},{8,10},{10,8},{12,14},{14,12},{1,3},{3,1},... | collective-permute-start | bytes 2727944 | tf_op jit(solution)/shard_map/ppermute | solution.py:54
  93.5 12.3 %collective-permute-start.8 = (bf16[96,768]{1,0:T(8,128)(2,1)S(1)}, bf16[96,768]{1,0:T(8,128)(2,1)S(1)}, u32[]{:S(2)}, u32[]{:S(2)}) collective-permute-start(bf16[96,768]{1,0:T(8,128)(2,1)S(1)} %get-tuple-element.61.refs_1_), channel_id=1, source_target_pairs={{0,16},{2,17},{4,18},{6,19},{8,20},{10,21},{12,22},{14,23},{1,24},... | collective-permute-start | bytes 442376 | tf_op jit(solution)/shard_map/ppermute | solution.py:50
  103.9 12.5 %collective-permute-start.9 = (bf16[96,768]{1,0:T(8,128)(2,1)S(1)}, bf16[96,768]{1,0:T(8,128)(2,1)S(1)}, u32[]{:S(2)}, u32[]{:S(2)}) collective-permute-start(bf16[96,768]{1,0:T(8,128)(2,1)S(1)} %shard_map.104), channel_id=1, source_target_pairs={{16,0},{17,2},{18,4},{19,6},{20,8},{21,10},{22,12},{23,14},{24,1},... | collective-permute-start | bytes 442376 | tf_op jit(solution)/shard_map/ppermute | solution.py:41
  139.8 4.4 %collective-permute-start.10 = (bf16[96,4736]{1,0:T(8,128)(2,1)S(1)}, bf16[96,4736]{1,0:T(8,128)(2,1)S(1)}, u32[]{:S(2)}, u32[]{:S(2)}) collective-permute-start(bf16[96,4736]{1,0:T(8,128)(2,1)S(1)} %shard_map.106.mine), channel_id=1, source_target_pairs={{0,2},{2,0},{4,6},{6,4},{8,10},{10,8},{12,14},{14,12},{1,3},{3,1},... | collective-permute-start | bytes 2727944 | tf_op jit(solution)/shard_map/ppermute | solution.py:54
  144.8 10.3 %collective-permute-start.11 = (bf16[96,768]{1,0:T(8,128)(2,1)S(1)}, bf16[96,768]{1,0:T(8,128)(2,1)S(1)}, u32[]{:S(2)}, u32[]{:S(2)}) collective-permute-start(bf16[96,768]{1,0:T(8,128)(2,1)S(1)} %get-tuple-element.69.refs_1_), channel_id=1, source_target_pairs={{0,16},{2,17},{4,18},{6,19},{8,20},{10,21},{12,22},{14,23},{1,24},... | collective-permute-start | bytes 442376 | tf_op jit(solution)/shard_map/ppermute | solution.py:50
  152.6 12.5 %collective-permute-start.12 = (bf16[96,768]{1,0:T(8,128)(2,1)S(1)}, bf16[96,768]{1,0:T(8,128)(2,1)S(1)}, u32[]{:S(2)}, u32[]{:S(2)}) collective-permute-start(bf16[96,768]{1,0:T(8,128)(2,1)S(1)} %shard_map.109), channel_id=1, source_target_pairs={{16,0},{17,2},{18,4},{19,6},{20,8},{21,10},{22,12},{23,14},{24,1},... | collective-permute-start | bytes 442376 | tf_op jit(solution)/shard_map/ppermute | solution.py:41
  189.2 4.4 %collective-permute-start.13 = (bf16[96,4736]{1,0:T(8,128)(2,1)S(1)}, bf16[96,4736]{1,0:T(8,128)(2,1)S(1)}, u32[]{:S(2)}, u32[]{:S(2)}) collective-permute-start(bf16[96,4736]{1,0:T(8,128)(2,1)S(1)} %shard_map.111.mine), channel_id=1, source_target_pairs={{0,2},{2,0},{4,6},{6,4},{8,10},{10,8},{12,14},{14,12},{1,3},{3,1},... | collective-permute-start | bytes 2727944 | tf_op jit(solution)/shard_map/ppermute | solution.py:54
  196.6 12.8 %collective-permute-start.14 = (bf16[96,768]{1,0:T(8,128)(2,1)S(1)}, bf16[96,768]{1,0:T(8,128)(2,1)S(1)}, u32[]{:S(2)}, u32[]{:S(2)}) collective-permute-start(bf16[96,768]{1,0:T(8,128)(2,1)S(1)} %shard_map.113.after), channel_id=1, source_target_pairs={{16,0},{17,2},{18,4},{19,6},{20,8},{21,10},{22,12},{23,14},{24,1},... | collective-permute-start | bytes 442376 | tf_op jit(solution)/shard_map/ppermute | solution.py:41
  201.4 6.0 %collective-permute-start.15 = (f32[16,768]{1,0:T(8,128)S(1)}, f32[16,768]{1,0:T(8,128)S(1)}, u32[]{:S(2)}, u32[]{:S(2)}) collective-permute-start(f32[16,768]{1,0:T(8,128)S(1)} %get-tuple-element.85.mine), channel_id=1, source_target_pairs={{0,1},{1,0},{2,3},{3,2},{4,5},{5,4},{6,7},{7,6},{8,9},{9,8},{10,11... | collective-permute-start | bytes 147464 | tf_op jit(solution)/shard_map/ppermute | solution.py:481
  210.3 20.1 %all-to-all-start.4 = ((bf16[16,16,256]{2,1,0:T(8,128)(2,1)}), bf16[16,16,256]{2,1,0:T(8,128)(2,1)S(1)}, u32[]{:S(2)}, u32[]{:S(2)}) async-start(bf16[16,16,256]{2,1,0:T(8,128)(2,1)} %get-tuple-element.86), calls=%async_computation.4 | async-start | bytes 262144 | tf_op jit(solution)/shard_map/all_to_all | solution.py:492
  218.9 7.5 %collective-permute-start.17 = (bf16[16,768]{1,0:T(8,128)(2,1)S(1)}, bf16[16,768]{1,0:T(8,128)(2,1)S(1)}, u32[]{:S(2)}, u32[]{:S(2)}) collective-permute-start(bf16[16,768]{1,0:T(8,128)(2,1)S(1)} %get-tuple-element.87), channel_id=1, source_target_pairs={{2,0},{0,1},{6,2},{4,3},{10,4},{8,5},{14,6},{12,7},{3,8},{1,9},{7,... | collective-permute-start | bytes 73736 | tf_op jit(solution)/shard_map/ppermute | solution.py:343
  222.3 8.1 %collective-permute-start.16 = (bf16[16,768]{1,0:T(8,128)(2,1)S(1)}, bf16[16,768]{1,0:T(8,128)(2,1)S(1)}, u32[]{:S(2)}, u32[]{:S(2)}) collective-permute-start(bf16[16,768]{1,0:T(8,128)(2,1)S(1)} %get-tuple-element.87), channel_id=1, source_target_pairs={{0,0},{2,1},{4,2},{6,3},{8,4},{10,5},{12,6},{14,7},{1,8},{3,9},{5,... | collective-permute-start | bytes 73736 | tf_op jit(solution)/shard_map/ppermute | solution.py:343

commit v5 on v4

--- a/solution.py
+++ b/solution.py
@@ -174,12 +174,27 @@
     return jnp.where(lax.axis_index("section") == sections - 1, kept, arrived[...])
 
 
-def pack_kernel(start, sections, product, small, x, *refs):
+def own_half(array):
+    feats = array.shape[-1]
+    return jnp.where(first_core(), array[..., : feats // 2], array[..., feats // 2 :])
+
+
+def other_half(array):
+    feats = array.shape[-1]
+    return jnp.where(first_core(), array[..., feats // 2 :], array[..., : feats // 2])
+
+
+def both_halves(mine, theirs):
+    return jnp.concatenate(
+        [jnp.where(first_core(), mine, theirs), jnp.where(first_core(), theirs, mine)], axis=-1
+    )
+
+
+def deal_kernel(start, sections, product, small, x, *refs):
     rows, feats = x.shape
-    values = small[...]
-    if start:
-        given, given_up, parcel, up, grad_out = refs
-        columns = feats
+    width = feats // 2
+    if start:
+        given, given_up, out, up, grad_out = refs
         toks = given.shape[0]
         rank = given_up.shape[0]
         up[:LOW] = jnp.zeros((LOW, feats), BF)
@@ -189,67 +204,83 @@
         grad_out[:toks] = jnp.where(first_core(), given[...], zeros)
         grad_out[toks:] = jnp.where(first_core(), zeros, given[...])
     else:
-        arrived, output, up, gain_w, mixed, parcel, grad_out = refs
-        columns = 2 * feats
+        arrived, output, out, grad_out = refs
         grad = chosen_grad(sections, arrived, output)
+        grad_out[...] = grad
+        at = (CHIPS + 1) * width + LANES
+        out[:, at:] = other_half(grad)
+    for j in range(CHIPS):
+        out[:, j * width : (j + 1) * width] = other_half(product[j])
+    at = CHIPS * width
+    out[:rows, at : at + width] = other_half(x[...])
+    if start:
+        out[rows:, at : at + width] = jnp.zeros((4 * CHIPS, width), BF)
+    out[:, at + width : at + width + LANES] = split(small[...])
+
+
+def pack_kernel(start, product, small, x, theirs, *refs):
+    rows, feats = x.shape
+    width = feats // 2
+    at = CHIPS * width
+    mine_x = own_half(x[...])
+    theirs_x = theirs[:rows, at : at + width]
+    at = at + width
+    values = join(split(small[...])) + join(theirs[:, at : at + LANES])
+    values = between(values, 0, LANES // 2)
+    if start:
+        (parcel,) = refs
+    else:
+        grad_part, up, gain_w, mixed, parcel, grad_out = refs
+        grad = own_half(grad_part[...]).astype(F32) + theirs[:, at + LANES :].astype(F32)
+        grad = grad.astype(BF)
         grad_out[...] = grad
         wide = grad.astype(F32)
         first = jnp.sum(wide * jnp.sum(gain_w[...], axis=0, keepdims=True), axis=1, keepdims=True)
         second = jnp.sum(wide * mixed[...], axis=1, keepdims=True)
-        at = lane(rows)
-        values = values + pltpu.roll(dot_t(grad, up[...]), GRAD - LOW, 1)
-        values = jnp.where(at == FIRST, first, values)
-        values = jnp.where(at == SECOND, second, values)
+        lanes = lane(rows)
+        values = values + pltpu.roll(dot_t(grad, own_half(up[...])), GRAD - LOW, 1)
+        values = jnp.where(lanes == FIRST, first, values)
+        values = jnp.where(lanes == SECOND, second, values)
         for j in range(CHIPS):
-            parcel[j, :, feats : 2 * feats] = grad
+            parcel[j, :, 2 * width + LANES :] = grad
     halves = split(values)
     block = own_block()
     for j in range(CHIPS):
-        parcel[j, :, :feats] = product[j]
-        parcel[j, :rows, columns : columns + feats] = jnp.where(
-            block == j, x[...], jnp.zeros(x.shape, BF)
-        )
+        total = own_half(product[j]).astype(F32)
+        total = total + theirs[:, j * width : (j + 1) * width].astype(F32)
+        parcel[j, :, :width] = total.astype(BF)
+        held = jnp.where(block == j, mine_x, jnp.where(block == (j ^ 1), theirs_x, 0.0).astype(BF))
+        parcel[j, :rows, width : 2 * width] = held
         if start:
-            parcel[j, rows:, columns : columns + feats] = jnp.zeros((4 * CHIPS, feats), BF)
-        parcel[j, :, columns + feats :] = halves
-
-
-def gather_kernel(start, got, out):
-    feats = (got.shape[2] - LANES) // (2 if start else 3)
-    total = got[0, :, :feats].astype(F32)
-    x = got[0, :, -LANES - feats : -LANES]
-    values = join(got[0, :, -LANES:])
+            parcel[j, rows:, width : 2 * width] = jnp.zeros((4 * CHIPS, width), BF)
+        parcel[j, :, 2 * width : 2 * width + LANES] = halves
+
+
+def output_kernel(start, got, up, *refs):
+    if start:
+        gain_w, gain_low, out, mixed, stats = refs
+    else:
+        gain_w, gain_low, out, mixed, stats = refs
+    rows, width = mixed.shape
+    feats = 2 * width
+    total = got[0, :, :width].astype(F32)
+    x = got[0, :rows, width:feats].astype(F32)
+    values = join(got[0, :, feats : feats + LANES])
     for j in range(1, CHIPS):
-        total = total + got[j, :, :feats].astype(F32)
-        x = x + got[j, :, -LANES - feats : -LANES]
-        values = values + join(got[j, :, -LANES:])
-    out[:, :feats] = total.astype(BF)
-    out[:, feats : 2 * feats] = x
-    out[:, 2 * feats : 2 * feats + LANES] = split(values)
-    if not start:
-        for j in range(CHIPS):
-            at = 2 * feats + LANES + j * feats
-            out[:, at : at + feats] = got[j, :, feats : 2 * feats]
-
-
-def output_kernel(start, mine, theirs, up, gain_w, gain_low, output, mixed, stats, sums):
-    rows, feats = output.shape
-    ends = slice(2 * feats, 2 * feats + LANES)
-    if start:
-        tail = mine[rows:, :feats].astype(F32) + theirs[rows:, :feats].astype(F32)
-        gain_w[...] = tail[: 2 * CHIPS] + tail[2 * CHIPS :]
-        tail = join(mine[rows:, ends]) + join(theirs[rows:, ends])
-        gain_low[...] = between(tail[: 2 * CHIPS], LOW, GRAD)
-    values = join(mine[:rows, ends]) + join(theirs[:rows, ends])
+        total = total + got[j, :, :width].astype(F32)
+        x = x + got[j, :rows, width:feats].astype(F32)
+        values = values + join(got[j, :, feats : feats + LANES])
     values = between(values, 0, LANES // 2)
-    sums[...] = values
+    if start:
+        gain_w[...] = total[rows : rows + 2 * CHIPS] + total[rows + 2 * CHIPS :]
+        gain_low[...] = between(values[rows : rows + 2 * CHIPS], LOW, GRAD)
+        total = total[:rows]
+        values = values[:rows]
     at = lane(rows)
-    width = feats * 2 * CHIPS
     mean = pick(values, 0, SQUARE) / (2 * CHIPS)
     off = jnp.where(at < 2 * CHIPS, values - mean, 0.0)
     square = pick(values, SQUARE, LOW) + feats * jnp.sum(off * off, axis=1, keepdims=True)
-    inv = lax.rsqrt(square / width + EPS)
-    total = mine[:rows, :feats].astype(F32) + theirs[:rows, :feats].astype(F32)
+    inv = lax.rsqrt(square / (feats * 2 * CHIPS) + EPS)
     low = values
     for j in range(2 * CHIPS):
         total = total + off[:, j : j + 1] * gain_w[j : j + 1, :]
@@ -258,8 +289,17 @@
     low = between(inv * low, LOW, GRAD)
     mixed[...] = total
     stats[...] = jnp.where(at == 0, mean, jnp.where(at == 1, inv, low))
-    x = mine[:rows, feats : 2 * feats].astype(F32) + theirs[:rows, feats : 2 * feats].astype(F32)
-    output[...] = (x + total + dot(low.astype(BF), up[...])).astype(BF)
+    out[:, :width] = (x + total + dot(low.astype(BF), own_half(up[...]))).astype(BF)
+    if not start:
+        out[:, width : width + LANES] = split(values)
+        for j in range(CHIPS):
+            at = width + LANES + j * width
+            out[:, at : at + width] = got[j, :, feats + LANES :]
+
+
+def whole_kernel(mine, theirs, output):
+    width = output.shape[1] // 2
+    output[...] = both_halves(mine[:, :width], theirs[:, :width])
 
 
 def rank_grads(sums):
@@ -270,10 +310,13 @@
     return (x.astype(F32) - pick(stats, 0, 1)) * pick(stats, 1, 2)
 
 
-def backward_kernel(mine, theirs, sums, x, stats, gains, gain_low, w, down, grad_out):
+def backward_kernel(mine, theirs, x, stats, gains, gain_low, w, down, grad_out, sums):
     rows, feats = x.shape
     width = feats * 2 * CHIPS
-    values = sums[...]
+    half = feats // 2
+    ends = slice(half, half + LANES)
+    values = join(mine[:, ends]) + join(theirs[:, ends])
+    sums[...] = values
     low_grad = rank_grads(values)
     low = between(stats[...], LOW, GRAD)
     low_all = jnp.sum(gain_low[...], axis=0, keepdims=True)
@@ -283,9 +326,8 @@
     grad_norm = dot(low_grad, down[...], precision=HIGHEST)
     here = jnp.zeros((rows, feats), F32)
     for j in range(CHIPS):
-        at = 2 * feats + LANES + j * feats
-        grad = mine[:, at : at + feats].astype(F32) + theirs[:, at : at + feats].astype(F32)
-        grad = grad.astype(BF)
+        at = half + LANES + j * half
+        grad = both_halves(mine[:, at : at + half], theirs[:, at : at + half])
         grad_norm = grad_norm + dot_t(grad, w[:, j * feats : (j + 1) * feats])
         here = here + jnp.where(own_block() == j, grad.astype(F32), 0.0)
     inv = pick(stats[...], 1, 2)
@@ -318,7 +360,12 @@
     for j in range(4 * CHIPS):
         low_out[j] = halves
     low = t_dot(stats[...].astype(BF), grad)
-    up_out[...] = (acc_up[...] + low[LOW : LOW + rank]).astype(BF)
+    zeros = jnp.zeros(acc_up.shape, F32)
+    acc = jnp.concatenate(
+        [jnp.where(first_core(), acc_up[...], zeros), jnp.where(first_core(), zeros, acc_up[...])],
+        axis=1,
+    )
+    up_out[...] = (acc + low[LOW : LOW + rank]).astype(BF)
 
 
 def finish_kernel(got, x, stats, gains, mine, theirs, up_a, up_b, down_out, up_out):
@@ -405,58 +452,62 @@
                 down,
                 scalars=(order, order_theirs),
             )
-        columns = (2 if start else 3) * feats + LANES
+        width = feats // 2
+        ins = [product, small, x]
+        columns = (CHIPS + (1 if start else 2)) * width + LANES
+        dealt = shape(rows + more, columns, dtype=BF)
+        if start:
+            dealt, up, grad_arrived = call(
+                functools.partial(deal_kernel, True, sections),
+                [dealt, shape(LANES, feats, dtype=BF), block],
+                *ins,
+                given,
+                given_up,
+            )
+        else:
+            dealt, grad_part = call(
+                functools.partial(deal_kernel, False, sections),
+                [dealt, block],
+                *ins,
+                grad_arrived,
+                output,
+            )
+        ins.append(swap_cores(dealt))
+        columns = (2 if start else 3) * width + LANES
         parcel = shape(CHIPS, rows + more, columns, dtype=BF)
         if start:
-            parcel, up, grad_arrived = call(
-                functools.partial(pack_kernel, True, sections),
-                [parcel, shape(LANES, feats, dtype=BF), block],
-                product,
-                small,
-                x,
-                given,
-                given_up,
-            )
+            parcel = call(functools.partial(pack_kernel, True), parcel, *ins)
         else:
             parcel, grad = call(
-                functools.partial(pack_kernel, False, sections),
-                [parcel, block],
-                product,
-                small,
-                x,
-                grad_arrived,
-                output,
+                functools.partial(pack_kernel, False),
+                [parcel, shape(rows, width, dtype=BF)],
+                *ins,
+                grad_part,
                 up,
                 gain_w,
                 mixed,
             )
             grads.append(grad)
         got = over_chips(parcel)
-        own = call(
-            functools.partial(gather_kernel, start),
-            shape(rows + more, 2 * feats + LANES + (0 if start else CHIPS * feats), dtype=BF),
-            got,
-        )
-        other = swap_cores(own)
-        out = [block, shape(rows, feats), values, values]
-        ins = [own, other, up]
+        columns = width + (0 if start else LANES + CHIPS * width)
+        out = [shape(rows, columns, dtype=BF), shape(rows, width), values]
         kernel = functools.partial(output_kernel, start)
         if start:
-            gain_w, gain_low, output, mixed, stats, sums = call(
-                kernel, [shape(2 * CHIPS, feats), shape(2 * CHIPS, LANES)] + out, *ins
+            gain_w, gain_low, own, mixed, stats = call(
+                kernel, [shape(2 * CHIPS, width), shape(2 * CHIPS, LANES)] + out, got, up
             )
         else:
-            output, mixed, stats, sums = call(kernel, out, *ins, gain_w, gain_low)
-            all_sums.append(sums)
+            own, mixed, stats = call(kernel, out, got, up, gain_w, gain_low)
+        other = swap_cores(own)
+        output = call(whole_kernel, block, own, other)
         if tick < TICKS - 1:
             arrived = to_next(output, sections)
         if not start:
-            grad_x = call(
+            grad_x, sums = call(
                 backward_kernel,
-                block,
+                [block, values],
                 own,
                 other,
-                sums,
                 xs[-1],
                 all_stats[-1],
                 gains,
@@ -464,13 +515,14 @@
                 w,
                 down,
             )
+            all_sums.append(sums)
             grad_arrived = to_owner(grad_x, sections, 1)
         xs.append(x)
         all_stats.append(stats)
 
     acc_down, acc_up = call(
         accumulate_kernel,
-        [shape(rank, feats), shape(rank, feats)],
+        [shape(rank, feats), shape(rank, feats // 2)],
         gains,
         grad_x,
         *xs[:-1],

time: 232 us -> 213 us (0.918)
  blocking collectives: 97 us -> 69.5 us
  starting transfers between devices: 63.3 us -> 71.7 us
    all_to_all x4, blocking collectives: 97 us -> 69.5 us  [over_chips(): return lax.all_to_all(array, 'tensor', 0, 0, axis_index_groups=groups)]
    ppermute x4 -> x8, starting transfers between devices: 7.68 us -> 16.9 us  [swap_cores(): return lax.ppermute(array, 'tensor', [(i, i ^ 1) for i in range(2 * CHIPS)])]
    ppermute x5, waiting for transfers between devices: 21.7 us -> 17.7 us  [to_owner(): return lax.ppermute(array, AXES, route)]
    ppermute x4 -> x8, waiting for transfers between devices: 8.94 us -> 12.7 us  [swap_cores(): return lax.ppermute(array, 'tensor', [(i, i ^ 1) for i in range(2 * CHIPS)])]
    ppermute x5, starting transfers between devices: 12.6 us -> 16.1 us  [to_owner(): return lax.ppermute(array, AXES, route)]
    ppermute x3, starting transfers between devices: 20.4 us -> 17.8 us  [to_next(): return lax.ppermute(array, AXES, route)]
    pallas_call x22 -> x26, Pallas kernels: 22.5 us -> 21.7 us  [call(): pl.pallas_call(kernel, out_shape=out, in_specs=[pl.BlockSpec(memory_space...]
  transfers between devices with their start and end apart: 19 -> 23, of which waited for: 12 -> 17; matrix products, arithmetic and copies ran while one was open for 0% -> 0% of each run, Pallas kernels for 4% -> 4%
where the time goes in v5:
time: 213 us; the launch traced here: 212 us
  starting transfers between devices  71.7 us (34%)
  blocking collectives  69.5 us (33%)
  waiting for transfers between devices  43.8 us (21%)
  Pallas kernels  21.7 us (10%)
  local copies, waits for them, and re-layouts  4.65 us (2%)
    all_to_all x4, blocking collectives, over_chips(): return lax.all_to_all(array, 'tensor', 0, 0, axis_index_groups=groups)  69.5 us
    pallas_call x26, Pallas kernels, call(): pl.pallas_call(kernel, out_shape=out, in_specs=[pl.BlockSpec(memory_space...  21.7 us
    ppermute x3, starting transfers between devices, to_next(): return lax.ppermute(array, AXES, route)  17.8 us
    ppermute x5, waiting for transfers between devices, to_owner(): return lax.ppermute(array, AXES, route)  17.7 us
    ppermute x8, starting transfers between devices, swap_cores(): return lax.ppermute(array, 'tensor', [(i, i ^ 1) for i in range(2 * CHIPS)])  16.9 us
    ppermute x5, starting transfers between devices, to_owner(): return lax.ppermute(array, AXES, route)  16.1 us
    ppermute x8, waiting for transfers between devices, swap_cores(): return lax.ppermute(array, 'tensor', [(i, i ^ 1) for i in range(2 * CHIPS)])  12.7 us
    all_to_all x1, starting transfers between devices, on_device(): got = lax.all_to_all(turned, ('tensor', 'dp'), 0, 0)  7.08 us
  transfers between devices with their start and end apart: 23, of which 17 were waited for; matrix products, arithmetic and copies ran while one was open for 0% of the time, Pallas kernels for 4%

profile of v5, /device:TPU:116, one launch (start us, length us, event | category | flops | bytes accessed | tf_op | source)
XLA Modules:
  0.0 212.3 jit_solution(17513082008149618147)
XLA Ops:
  1.3 3.2 %collective-permute-start.4 = (bf16[48,768]{1,0:T(8,128)(2,1)}, bf16[48,768]{1,0:T(8,128)(2,1)S(1)}, u32[]{:S(2)}, u32[]{:S(2)}) collective-permute-start(bf16[48,768]{1,0:T(8,128)(2,1)} %bitcast.24), channel_id=1, source_target_pairs={{0,1},{1,0},{2,3},{3,2},{4,5},{5,4},{6,7},{7,6},{8,9},{9,8},{10,11... | collective-permute-start | bytes 221192 | tf_op jit(solution)/shard_map/ppermute | solution.py:413
  4.5 2.6 %collective-permute-start.1 = (bf16[48,768]{1,0:T(8,128)(2,1)}, bf16[48,768]{1,0:T(8,128)(2,1)S(1)}, u32[]{:S(2)}, u32[]{:S(2)}) collective-permute-start(bf16[48,768]{1,0:T(8,128)(2,1)} %bitcast.31), channel_id=1, source_target_pairs={{0,0},{1,2},{2,4},{3,6},{4,8},{5,10},{6,12},{7,14},{8,1},{9,3},{10... | collective-permute-start | bytes 221192 | tf_op jit(solution)/shard_map/ppermute | solution.py:41
  7.1 2.4 %collective-permute-start.2 = (bf16[16,768]{1,0:T(8,128)(2,1)}, bf16[16,768]{1,0:T(8,128)(2,1)S(1)}, u32[]{:S(2)}, u32[]{:S(2)}) collective-permute-start(bf16[16,768]{1,0:T(8,128)(2,1)} %bitcast.32), channel_id=1, source_target_pairs={{0,0},{1,2},{2,4},{3,6},{4,8},{5,10},{6,12},{7,14},{8,1},{9,3},{10... | collective-permute-start | bytes 73736 | tf_op jit(solution)/shard_map/ppermute | solution.py:41
  10.1 2.9 %collective-permute-done.2.refs_2_.refs_1_ = bf16[16,768]{1,0:T(8,128)(2,1)S(1)} collective-permute-done((bf16[16,768]{1,0:T(8,128)(2,1)}, bf16[16,768]{1,0:T(8,128)(2,1)S(1)}, u32[]{:S(2)}, u32[]{:S(2)}) %collective-permute-start.2) | collective-permute-done | bytes 24608 | tf_op jit(solution)/shard_map/ppermute | solution.py:41
  13.1 2.3 %copy-done = bf16[1,768,3072]{2,1,0:T(8,128)(2,1)S(1)} copy-done((bf16[1,768,3072]{2,1,0:T(8,128)(2,1)S(1)}, bf16[1,768,3072]{2,1,0:T(8,128)(2,1)}, u32[]{:S(2)}) %copy-start) | copy-done | bytes 4718616
  17.7 2.0 shard_map.95
  19.9 2.4 %collective-permute-start.5 = (bf16[112,2048]{1,0:T(8,128)(2,1)S(1)}, bf16[112,2048]{1,0:T(8,128)(2,1)S(1)}, u32[]{:S(2)}, u32[]{:S(2)}) collective-permute-start(bf16[112,2048]{1,0:T(8,128)(2,1)S(1)} %get-tuple-element.58), channel_id=1, source_target_pairs={{0,2},{2,0},{4,6},{6,4},{8,10},{10,8},{12,14},{14,12},{1,3},{3,1},... | collective-permute-start | bytes 1376264 | tf_op jit(solution)/shard_map/ppermute | solution.py:54
  24.0 15.9 %all_to_all.25.got = bf16[4,112,896]{2,1,0:T(8,128)(2,1)S(1)} all-to-all(bf16[4,112,896]{2,1,0:T(8,128)(2,1)S(1)} %shard_map.97), channel_id=1, replica_groups={{0,4,8,12},{2,6,10,14},{1,5,9,13},{3,7,11,15},{16,20,24,28},{18,22,26,3..., dimensions={0} | all-to-all | bytes 1605632 | tf_op jit(solution)/shard_map/all_to_all | solution.py:59
  40.5 1.9 collective-permute-start.6
  43.7 5.8 %collective-permute-start.7 = (bf16[96,768]{1,0:T(8,128)(2,1)S(1)}, bf16[96,768]{1,0:T(8,128)(2,1)S(1)}, u32[]{:S(2)}, u32[]{:S(2)}) collective-permute-start(bf16[96,768]{1,0:T(8,128)(2,1)S(1)} %shard_map.99.refs_1_), channel_id=1, source_target_pairs={{0,16},{2,17},{4,18},{6,19},{8,20},{10,21},{12,22},{14,23},{1,24},... | collective-permute-start | bytes 442376 | tf_op jit(solution)/shard_map/ppermute | solution.py:50
  49.5 4.7 %collective-permute-done.7.refs_2_ = bf16[96,768]{1,0:T(8,128)(2,1)S(1)} collective-permute-done((bf16[96,768]{1,0:T(8,128)(2,1)S(1)}, bf16[96,768]{1,0:T(8,128)(2,1)S(1)}, u32[]{:S(2)}, u32[]{:S(2)}) %collective-permute-start.7) | collective-permute-done | bytes 147488 | tf_op jit(solution)/shard_map/ppermute | solution.py:50
  56.2 3.0 %collective-permute-start.8 = (bf16[96,2432]{1,0:T(8,128)(2,1)S(1)}, bf16[96,2432]{1,0:T(8,128)(2,1)S(1)}, u32[]{:S(2)}, u32[]{:S(2)}) collective-permute-start(bf16[96,2432]{1,0:T(8,128)(2,1)S(1)} %get-tuple-element.66), channel_id=1, source_target_pairs={{0,2},{2,0},{4,6},{6,4},{8,10},{10,8},{12,14},{14,12},{1,3},{3,1},... | collective-permute-start | bytes 1400840 | tf_op jit(solution)/shard_map/ppermute | solution.py:54
  61.2 17.6 %all_to_all.26.got = bf16[4,96,1280]{2,1,0:T(8,128)(2,1)S(1)} all-to-all(bf16[4,96,1280]{2,1,0:T(8,128)(2,1)S(1)} %get-tuple-element.70), channel_id=1, replica_groups={{0,4,8,12},{2,6,10,14},{1,5,9,13},{3,7,11,15},{16,20,24,28},{18,22,26,3..., dimensions={0} | all-to-all | bytes 1966080 | tf_op jit(solution)/shard_map/all_to_all | solution.py:59
  83.0 9.2 %collective-permute-start.10 = (bf16[96,768]{1,0:T(8,128)(2,1)S(1)}, bf16[96,768]{1,0:T(8,128)(2,1)S(1)}, u32[]{:S(2)}, u32[]{:S(2)}) collective-permute-start(bf16[96,768]{1,0:T(8,128)(2,1)S(1)} %shard_map.104.refs_1_), channel_id=1, source_target_pairs={{0,16},{2,17},{4,18},{6,19},{8,20},{10,21},{12,22},{14,23},{1,24},... | collective-permute-start | bytes 442376 | tf_op jit(solution)/shard_map/ppermute | solution.py:50
  94.0 1.9 collective-permute-start.11
  97.9 8.7 %collective-permute-done.11.refs_0_ = bf16[96,768]{1,0:T(8,128)(2,1)S(1)} collective-permute-done((bf16[96,768]{1,0:T(8,128)(2,1)S(1)}, bf16[96,768]{1,0:T(8,128)(2,1)S(1)}, u32[]{:S(2)}, u32[]{:S(2)}) %collective-permute-start.11) | collective-permute-done | bytes 147488 | tf_op jit(solution)/shard_map/ppermute | solution.py:41
  106.6 1.9 collective-permute-start.12
  110.9 18.0 %all_to_all.27.got = bf16[4,96,1280]{2,1,0:T(8,128)(2,1)S(1)} all-to-all(bf16[4,96,1280]{2,1,0:T(8,128)(2,1)S(1)} %get-tuple-element.81), channel_id=1, replica_groups={{0,4,8,12},{2,6,10,14},{1,5,9,13},{3,7,11,15},{16,20,24,28},{18,22,26,3..., dimensions={0} | all-to-all | bytes 1966080 | tf_op jit(solution)/shard_map/all_to_all | solution.py:59
  129.5 1.9 collective-permute-start.13
  133.1 2.8 %collective-permute-start.14 = (bf16[96,768]{1,0:T(8,128)(2,1)S(1)}, bf16[96,768]{1,0:T(8,128)(2,1)S(1)}, u32[]{:S(2)}, u32[]{:S(2)}) collective-permute-start(bf16[96,768]{1,0:T(8,128)(2,1)S(1)} %shard_map.110.refs_1_), channel_id=1, source_target_pairs={{0,16},{2,17},{4,18},{6,19},{8,20},{10,21},{12,22},{14,23},{1,24},... | collective-permute-start | bytes 442376 | tf_op jit(solution)/shard_map/ppermute | solution.py:50
  137.8 5.6 %collective-permute-start.15 = (bf16[96,768]{1,0:T(8,128)(2,1)S(1)}, bf16[96,768]{1,0:T(8,128)(2,1)S(1)}, u32[]{:S(2)}, u32[]{:S(2)}) collective-permute-start(bf16[96,768]{1,0:T(8,128)(2,1)S(1)} %get-tuple-element.87), channel_id=1, source_target_pairs={{16,0},{17,2},{18,4},{19,6},{20,8},{21,10},{22,12},{23,14},{24,1},... | collective-permute-start | bytes 442376 | tf_op jit(solution)/shard_map/ppermute | solution.py:41
  145.8 4.5 %collective-permute-done.15.refs_0_ = bf16[96,768]{1,0:T(8,128)(2,1)S(1)} collective-permute-done((bf16[96,768]{1,0:T(8,128)(2,1)S(1)}, bf16[96,768]{1,0:T(8,128)(2,1)S(1)}, u32[]{:S(2)}, u32[]{:S(2)}) %collective-permute-start.15) | collective-permute-done | bytes 147488 | tf_op jit(solution)/shard_map/ppermute | solution.py:41
  150.4 1.9 collective-permute-start.16
  154.6 18.0 %all_to_all.28.got = bf16[4,96,1280]{2,1,0:T(8,128)(2,1)S(1)} all-to-all(bf16[4,96,1280]{2,1,0:T(8,128)(2,1)S(1)} %get-tuple-element.91), channel_id=1, replica_groups={{0,4,8,12},{2,6,10,14},{1,5,9,13},{3,7,11,15},{16,20,24,28},{18,22,26,3..., dimensions={0} | all-to-all | bytes 1966080 | tf_op jit(solution)/shard_map/all_to_all | solution.py:59
  179.2 3.6 %collective-permute-start.18 = (bf16[96,768]{1,0:T(8,128)(2,1)S(1)}, bf16[96,768]{1,0:T(8,128)(2,1)S(1)}, u32[]{:S(2)}, u32[]{:S(2)}) collective-permute-start(bf16[96,768]{1,0:T(8,128)(2,1)S(1)} %get-tuple-element.94.after), channel_id=1, source_target_pairs={{16,0},{17,2},{18,4},{19,6},{20,8},{21,10},{22,12},{23,14},{24,1},... | collective-permute-start | bytes 442376 | tf_op jit(solution)/shard_map/ppermute | solution.py:41
  184.2 3.7 %collective-permute-start.19 = (f32[16,768]{1,0:T(8,128)S(1)}, f32[16,768]{1,0:T(8,128)S(1)}, u32[]{:S(2)}, u32[]{:S(2)}) collective-permute-start(f32[16,768]{1,0:T(8,128)S(1)} %get-tuple-element.103.mine), channel_id=1, source_target_pairs={{0,1},{1,0},{2,3},{3,2},{4,5},{5,4},{6,7},{7,6},{8,9},{9,8},{10,11... | collective-permute-start | bytes 147464 | tf_op jit(solution)/shard_map/ppermute | solution.py:533
  187.9 2.2 %collective-permute-done.19.after.theirs = f32[16,768]{1,0:T(8,128)S(1)} collective-permute-done((f32[16,768]{1,0:T(8,128)S(1)}, f32[16,768]{1,0:T(8,128)S(1)}, u32[]{:S(2)}, u32[]{:S(2)}) %collective-permute-start.19) | collective-permute-done | bytes 49184 | tf_op jit(solution)/shard_map/ppermute | solution.py:533
  192.7 7.1 %all-to-all-start.4 = ((bf16[16,16,256]{2,1,0:T(8,128)(2,1)}), bf16[16,16,256]{2,1,0:T(8,128)(2,1)S(1)}, u32[]{:S(2)}, u32[]{:S(2)}) async-start(bf16[16,16,256]{2,1,0:T(8,128)(2,1)} %get-tuple-element.104), calls=%async_computation.4 | async-start | bytes 262144 | tf_op jit(solution)/shard_map/all_to_all | solution.py:544
  199.8 3.4 %collective-permute-start.21 = (bf16[16,768]{1,0:T(8,128)(2,1)S(1)}, bf16[16,768]{1,0:T(8,128)(2,1)S(1)}, u32[]{:S(2)}, u32[]{:S(2)}) collective-permute-start(bf16[16,768]{1,0:T(8,128)(2,1)S(1)} %get-tuple-element.105), channel_id=1, source_target_pairs={{2,0},{0,1},{6,2},{4,3},{10,4},{8,5},{14,6},{12,7},{3,8},{1,9},{7,... | collective-permute-start | bytes 73736 | tf_op jit(solution)/shard_map/ppermute | solution.py:390
  203.2 2.2 %collective-permute-start.20 = (bf16[16,768]{1,0:T(8,128)(2,1)S(1)}, bf16[16,768]{1,0:T(8,128)(2,1)S(1)}, u32[]{:S(2)}, u32[]{:S(2)}) collective-permute-start(bf16[16,768]{1,0:T(8,128)(2,1)S(1)} %get-tuple-element.105), channel_id=1, source_target_pairs={{0,0},{2,1},{4,2},{6,3},{8,4},{10,5},{12,6},{14,7},{1,8},{3,9},{5,... | collective-permute-start | bytes 73736 | tf_op jit(solution)/shard_map/ppermute | solution.py:390
  205.4 1.9 collective-permute-done.21.up_b
  207.4 4.0 %collective-permute-done.20.up_a = bf16[16,768]{1,0:T(8,128)(2,1)S(1)} collective-permute-done((bf16[16,768]{1,0:T(8,128)(2,1)S(1)}, bf16[16,768]{1,0:T(8,128)(2,1)S(1)}, u32[]{:S(2)}, u32[]{:S(2)}) %collective-permute-start.20) | collective-permute-done | bytes 24608 | tf_op jit(solution)/shard_map/ppermute | solution.py:390
  (60 shorter events, 42.1 us)
Async XLA Ops:
  0.6 12.4 %collective-permute-start.3 = (bf16[2,48,768]{2,1,0:T(8,128)(2,1)}, bf16[2,48,768]{2,1,0:T(8,128)(2,1)S(1)}, u32[]{:S(2)}, u32[]{:S(2)}) collective-permute-start(bf16[2,48,768]{2,1,0:T(8,128)(2,1)} %bitcast.20), channel_id=1, source_target_pairs={{0,1},{1,0},{2,3},{3,2},{4,5},{5,4},{6,7},{7,6},{8,9},{9,8},{10,11... | collective-permute-start | bytes 442376 | tf_op jit(solution)/shard_map/ppermute | solution.py:419
  1.3 11.7 %collective-permute-start.4 = (bf16[48,768]{1,0:T(8,128)(2,1)}, bf16[48,768]{1,0:T(8,128)(2,1)S(1)}, u32[]{:S(2)}, u32[]{:S(2)}) collective-permute-start(bf16[48,768]{1,0:T(8,128)(2,1)} %bitcast.24), channel_id=1, source_target_pairs={{0,1},{1,0},{2,3},{3,2},{4,5},{5,4},{6,7},{7,6},{8,9},{9,8},{10,11... | collective-permute-start | bytes 221192 | tf_op jit(solution)/shard_map/ppermute | solution.py:413
  4.5 8.5 %collective-permute-start.1 = (bf16[48,768]{1,0:T(8,128)(2,1)}, bf16[48,768]{1,0:T(8,128)(2,1)S(1)}, u32[]{:S(2)}, u32[]{:S(2)}) collective-permute-start(bf16[48,768]{1,0:T(8,128)(2,1)} %bitcast.31), channel_id=1, source_target_pairs={{0,0},{1,2},{2,4},{3,6},{4,8},{5,10},{6,12},{7,14},{8,1},{9,3},{10... | collective-permute-start | bytes 221192 | tf_op jit(solution)/shard_map/ppermute | solution.py:41
  7.1 5.9 %collective-permute-start.2 = (bf16[16,768]{1,0:T(8,128)(2,1)}, bf16[16,768]{1,0:T(8,128)(2,1)S(1)}, u32[]{:S(2)}, u32[]{:S(2)}) collective-permute-start(bf16[16,768]{1,0:T(8,128)(2,1)} %bitcast.32), channel_id=1, source_target_pairs={{0,0},{1,2},{2,4},{3,6},{4,8},{5,10},{6,12},{7,14},{8,1},{9,3},{10... | collective-permute-start | bytes 73736 | tf_op jit(solution)/shard_map/ppermute | solution.py:41
  9.5 0.7 collective-permute-start
  13.1 2.3 %copy-start = (bf16[1,768,3072]{2,1,0:T(8,128)(2,1)S(1)}, bf16[1,768,3072]{2,1,0:T(8,128)(2,1)}, u32[]{:S(2)}) copy-start(bf16[1,768,3072]{2,1,0:T(8,128)(2,1)} %param.9) | copy-start | bytes 14155780
  15.4 0.7 copy-start.3
  16.1 0.9 copy-start.5
  17.0 0.7 copy-start.6
  17.7 36.4 %copy-start.1 = (bf16[1,768,3072]{2,1,0:T(8,128)(2,1)S(1)}, bf16[1,768,3072]{2,1,0:T(8,128)(2,1)}, u32[]{:S(2)}) copy-start(bf16[1,768,3072]{2,1,0:T(8,128)(2,1)} %param.9) | copy-start | bytes 14155780
  17.7 36.4 %copy-start.2 = (bf16[1,1,2,48,768]{4,3,2,1,0:T(8,128)(2,1)S(1)}, bf16[1,1,2,48,768]{4,3,2,1,0:T(8,128)(2,1)}, u32[]{:S(2)}) copy-start(bf16[1,1,2,48,768]{4,3,2,1,0:T(8,128)(2,1)} %param.13) | copy-start | bytes 442372
  17.7 36.4 %copy-start.4 = (f32[1,768]{1,0:T(1,128)S(1)}, f32[1,768]{1,0:T(1,128)}, u32[]{:S(2)}) copy-start(f32[1,768]{1,0:T(1,128)} %gains.9) | copy-start | bytes 9220
  17.7 36.5 %copy-start.7 = (s32[1,1,4]{2,1,0:T(1,128)S(1)}, s32[1,1,4]{2,1,0:T(1,128)}, u32[]{:S(2)}) copy-start(s32[1,1,4]{2,1,0:T(1,128)} %param.16) | copy-start | bytes 52
  19.9 3.8 %collective-permute-start.5 = (bf16[112,2048]{1,0:T(8,128)(2,1)S(1)}, bf16[112,2048]{1,0:T(8,128)(2,1)S(1)}, u32[]{:S(2)}, u32[]{:S(2)}) collective-permute-start(bf16[112,2048]{1,0:T(8,128)(2,1)S(1)} %get-tuple-element.58), channel_id=1, source_target_pairs={{0,2},{2,0},{4,6},{6,4},{8,10},{10,8},{12,14},{14,12},{1,3},{3,1},... | collective-permute-start | bytes 1376264 | tf_op jit(solution)/shard_map/ppermute | solution.py:54
  40.5 3.2 %collective-permute-start.6 = (bf16[96,384]{1,0:T(8,128)(2,1)S(1)}, bf16[96,384]{1,0:T(8,128)(2,1)S(1)}, u32[]{:S(2)}, u32[]{:S(2)}) collective-permute-start(bf16[96,384]{1,0:T(8,128)(2,1)S(1)} %get-tuple-element.60.mine), channel_id=1, source_target_pairs={{0,2},{2,0},{4,6},{6,4},{8,10},{10,8},{12,14},{14,12},{1,3},{3,1},... | collective-permute-start | bytes 221192 | tf_op jit(solution)/shard_map/ppermute | solution.py:54
  43.7 10.4 %collective-permute-start.7 = (bf16[96,768]{1,0:T(8,128)(2,1)S(1)}, bf16[96,768]{1,0:T(8,128)(2,1)S(1)}, u32[]{:S(2)}, u32[]{:S(2)}) collective-permute-start(bf16[96,768]{1,0:T(8,128)(2,1)S(1)} %shard_map.99.refs_1_), channel_id=1, source_target_pairs={{0,16},{2,17},{4,18},{6,19},{8,20},{10,21},{12,22},{14,23},{1,24},... | collective-permute-start | bytes 442376 | tf_op jit(solution)/shard_map/ppermute | solution.py:50
  56.2 4.5 %collective-permute-start.8 = (bf16[96,2432]{1,0:T(8,128)(2,1)S(1)}, bf16[96,2432]{1,0:T(8,128)(2,1)S(1)}, u32[]{:S(2)}, u32[]{:S(2)}) collective-permute-start(bf16[96,2432]{1,0:T(8,128)(2,1)S(1)} %get-tuple-element.66), channel_id=1, source_target_pairs={{0,2},{2,0},{4,6},{6,4},{8,10},{10,8},{12,14},{14,12},{1,3},{3,1},... | collective-permute-start | bytes 1400840 | tf_op jit(solution)/shard_map/ppermute | solution.py:54
  79.4 3.6 %collective-permute-start.9 = (bf16[96,2048]{1,0:T(8,128)(2,1)S(1)}, bf16[96,2048]{1,0:T(8,128)(2,1)S(1)}, u32[]{:S(2)}, u32[]{:S(2)}) collective-permute-start(bf16[96,2048]{1,0:T(8,128)(2,1)S(1)} %get-tuple-element.72.mine), channel_id=1, source_target_pairs={{0,2},{2,0},{4,6},{6,4},{8,10},{10,8},{12,14},{14,12},{1,3},{3,1},... | collective-permute-start | bytes 1179656 | tf_op jit(solution)/shard_map/ppermute | solution.py:54
  83.0 13.0 %collective-permute-start.10 = (bf16[96,768]{1,0:T(8,128)(2,1)S(1)}, bf16[96,768]{1,0:T(8,128)(2,1)S(1)}, u32[]{:S(2)}, u32[]{:S(2)}) collective-permute-start(bf16[96,768]{1,0:T(8,128)(2,1)S(1)} %shard_map.104.refs_1_), channel_id=1, source_target_pairs={{0,16},{2,17},{4,18},{6,19},{8,20},{10,21},{12,22},{14,23},{1,24},... | collective-permute-start | bytes 442376 | tf_op jit(solution)/shard_map/ppermute | solution.py:50
  94.0 12.5 %collective-permute-start.11 = (bf16[96,768]{1,0:T(8,128)(2,1)S(1)}, bf16[96,768]{1,0:T(8,128)(2,1)S(1)}, u32[]{:S(2)}, u32[]{:S(2)}) collective-permute-start(bf16[96,768]{1,0:T(8,128)(2,1)S(1)} %get-tuple-element.77), channel_id=1, source_target_pairs={{16,0},{17,2},{18,4},{19,6},{20,8},{21,10},{22,12},{23,14},{24,1},... | collective-permute-start | bytes 442376 | tf_op jit(solution)/shard_map/ppermute | solution.py:41
  106.6 3.7 %collective-permute-start.12 = (bf16[96,2432]{1,0:T(8,128)(2,1)S(1)}, bf16[96,2432]{1,0:T(8,128)(2,1)S(1)}, u32[]{:S(2)}, u32[]{:S(2)}) collective-permute-start(bf16[96,2432]{1,0:T(8,128)(2,1)S(1)} %get-tuple-element.78), channel_id=1, source_target_pairs={{0,2},{2,0},{4,6},{6,4},{8,10},{10,8},{12,14},{14,12},{1,3},{3,1},... | collective-permute-start | bytes 1400840 | tf_op jit(solution)/shard_map/ppermute | solution.py:54
  129.5 3.6 %collective-permute-start.13 = (bf16[96,2048]{1,0:T(8,128)(2,1)S(1)}, bf16[96,2048]{1,0:T(8,128)(2,1)S(1)}, u32[]{:S(2)}, u32[]{:S(2)}) collective-permute-start(bf16[96,2048]{1,0:T(8,128)(2,1)S(1)} %get-tuple-element.82.mine), channel_id=1, source_target_pairs={{0,2},{2,0},{4,6},{6,4},{8,10},{10,8},{12,14},{14,12},{1,3},{3,1},... | collective-permute-start | bytes 1179656 | tf_op jit(solution)/shard_map/ppermute | solution.py:54
  133.1 10.8 %collective-permute-start.14 = (bf16[96,768]{1,0:T(8,128)(2,1)S(1)}, bf16[96,768]{1,0:T(8,128)(2,1)S(1)}, u32[]{:S(2)}, u32[]{:S(2)}) collective-permute-start(bf16[96,768]{1,0:T(8,128)(2,1)S(1)} %shard_map.110.refs_1_), channel_id=1, source_target_pairs={{0,16},{2,17},{4,18},{6,19},{8,20},{10,21},{12,22},{14,23},{1,24},... | collective-permute-start | bytes 442376 | tf_op jit(solution)/shard_map/ppermute | solution.py:50
  137.8 12.5 %collective-permute-start.15 = (bf16[96,768]{1,0:T(8,128)(2,1)S(1)}, bf16[96,768]{1,0:T(8,128)(2,1)S(1)}, u32[]{:S(2)}, u32[]{:S(2)}) collective-permute-start(bf16[96,768]{1,0:T(8,128)(2,1)S(1)} %get-tuple-element.87), channel_id=1, source_target_pairs={{16,0},{17,2},{18,4},{19,6},{20,8},{21,10},{22,12},{23,14},{24,1},... | collective-permute-start | bytes 442376 | tf_op jit(solution)/shard_map/ppermute | solution.py:41
  150.4 3.7 %collective-permute-start.16 = (bf16[96,2432]{1,0:T(8,128)(2,1)S(1)}, bf16[96,2432]{1,0:T(8,128)(2,1)S(1)}, u32[]{:S(2)}, u32[]{:S(2)}) collective-permute-start(bf16[96,2432]{1,0:T(8,128)(2,1)S(1)} %get-tuple-element.88), channel_id=1, source_target_pairs={{0,2},{2,0},{4,6},{6,4},{8,10},{10,8},{12,14},{14,12},{1,3},{3,1},... | collective-permute-start | bytes 1400840 | tf_op jit(solution)/shard_map/ppermute | solution.py:54
  173.8 3.6 %collective-permute-start.17 = (bf16[96,2048]{1,0:T(8,128)(2,1)S(1)}, bf16[96,2048]{1,0:T(8,128)(2,1)S(1)}, u32[]{:S(2)}, u32[]{:S(2)}) collective-permute-start(bf16[96,2048]{1,0:T(8,128)(2,1)S(1)} %get-tuple-element.92.mine), channel_id=1, source_target_pairs={{0,2},{2,0},{4,6},{6,4},{8,10},{10,8},{12,14},{14,12},{1,3},{3,1},... | collective-permute-start | bytes 1179656 | tf_op jit(solution)/shard_map/ppermute | solution.py:54
  179.2 12.7 %collective-permute-start.18 = (bf16[96,768]{1,0:T(8,128)(2,1)S(1)}, bf16[96,768]{1,0:T(8,128)(2,1)S(1)}, u32[]{:S(2)}, u32[]{:S(2)}) collective-permute-start(bf16[96,768]{1,0:T(8,128)(2,1)S(1)} %get-tuple-element.94.after), channel_id=1, source_target_pairs={{16,0},{17,2},{18,4},{19,6},{20,8},{21,10},{22,12},{23,14},{24,1},... | collective-permute-start | bytes 442376 | tf_op jit(solution)/shard_map/ppermute | solution.py:41
  184.2 6.0 %collective-permute-start.19 = (f32[16,768]{1,0:T(8,128)S(1)}, f32[16,768]{1,0:T(8,128)S(1)}, u32[]{:S(2)}, u32[]{:S(2)}) collective-permute-start(f32[16,768]{1,0:T(8,128)S(1)} %get-tuple-element.103.mine), channel_id=1, source_target_pairs={{0,1},{1,0},{2,3},{3,2},{4,5},{5,4},{6,7},{7,6},{8,9},{9,8},{10,11... | collective-permute-start | bytes 147464 | tf_op jit(solution)/shard_map/ppermute | solution.py:533
  192.7 18.6 %all-to-all-start.4 = ((bf16[16,16,256]{2,1,0:T(8,128)(2,1)}), bf16[16,16,256]{2,1,0:T(8,128)(2,1)S(1)}, u32[]{:S(2)}, u32[]{:S(2)}) async-start(bf16[16,16,256]{2,1,0:T(8,128)(2,1)} %get-tuple-element.104), calls=%async_computation.4 | async-start | bytes 262144 | tf_op jit(solution)/shard_map/all_to_all | solution.py:544
  199.8 7.5 %collective-permute-start.21 = (bf16[16,768]{1,0:T(8,128)(2,1)S(1)}, bf16[16,768]{1,0:T(8,128)(2,1)S(1)}, u32[]{:S(2)}, u32[]{:S(2)}) collective-permute-start(bf16[16,768]{1,0:T(8,128)(2,1)S(1)} %get-tuple-element.105), channel_id=1, source_target_pairs={{2,0},{0,1},{6,2},{4,3},{10,4},{8,5},{14,6},{12,7},{3,8},{1,9},{7,... | collective-permute-start | bytes 73736 | tf_op jit(solution)/shard_map/ppermute | solution.py:390
  203.2 8.1 %collective-permute-start.20 = (bf16[16,768]{1,0:T(8,128)(2,1)S(1)}, bf16[16,768]{1,0:T(8,128)(2,1)S(1)}, u32[]{:S(2)}, u32[]{:S(2)}) collective-permute-start(bf16[16,768]{1,0:T(8,128)(2,1)S(1)} %get-tuple-element.105), channel_id=1, source_target_pairs={{0,0},{2,1},{4,2},{6,3},{8,4},{10,5},{12,6},{14,7},{1,8},{3,9},{5,... | collective-permute-start | bytes 73736 | tf_op jit(solution)/shard_map/ppermute | solution.py:390

commit v6 on v5

--- a/solution.py
+++ b/solution.py
@@ -120,21 +120,27 @@
     return jnp.concatenate([jnp.where(first, mine, theirs), jnp.where(first, theirs, mine)])
 
 
+def warm_kernel(w, gains, mine, down_rows, down):
+    rank, feats = down_rows.shape
+    down[:LOW] = jnp.zeros((LOW, feats), F32)
+    down[LOW : LOW + rank] = down_rows[...].astype(F32)
+    down[LOW + rank :] = jnp.zeros((LANES - LOW - rank, feats), F32)
+
+
+def prepare_kernel(order, stored, grads, after, chosen, grads_out):
+    for j in range(TICKS - 1):
+        chosen[j] = jnp.where(order[j + 1] == 0, stored[0], stored[1])
+    grads_out[...] = grads[...]
+
+
 def forward_kernel(start, tick, *refs):
     place = lax.axis_index("tensor")
     if start:
-        _, _, _, _, mine, theirs, gains, w, down_rows, x_out, product, small, down = refs
+        mine, theirs, gains, w, down, x_out, product, small = refs
         x = replicas(mine[...], theirs[...])
-        rank, feats = down_rows.shape
-        down[:LOW] = jnp.zeros((LOW, feats), F32)
-        down[LOW : LOW + rank] = down_rows[...].astype(F32)
-        down[LOW + rank :] = jnp.zeros((LANES - LOW - rank, feats), F32)
     else:
-        order, order_theirs, arrived, mine, theirs, gains, w, down, x_out, product, small = refs
-        given = replicas(
-            jnp.where(order[tick] == 0, mine[0], mine[1]),
-            jnp.where(order_theirs[tick] == 0, theirs[0], theirs[1]),
-        )
+        arrived, mine, theirs, gains, w, down, x_out, product, small = refs
+        given = replicas(mine[tick - 1], theirs[tick - 1])
         x = jnp.where(lax.axis_index("section") == 0, given, arrived[...])
     x_out[...] = x
     rows, feats = x.shape
@@ -169,11 +175,6 @@
     return lax.axis_index("tensor") % 2 == 0
 
 
-def chosen_grad(sections, arrived, output):
-    kept = jnp.where(first_core(), output[...], jnp.zeros(output.shape, BF))
-    return jnp.where(lax.axis_index("section") == sections - 1, kept, arrived[...])
-
-
 def own_half(array):
     feats = array.shape[-1]
     return jnp.where(first_core(), array[..., : feats // 2], array[..., feats // 2 :])
@@ -190,31 +191,30 @@
     )
 
 
-def deal_kernel(start, sections, product, small, x, *refs):
+def deal_kernel(tick, sections, product, small, x, *refs):
     rows, feats = x.shape
     width = feats // 2
-    if start:
-        given, given_up, out, up, grad_out = refs
-        toks = given.shape[0]
-        rank = given_up.shape[0]
-        up[:LOW] = jnp.zeros((LOW, feats), BF)
-        up[LOW : LOW + rank] = given_up[...]
-        up[LOW + rank :] = jnp.zeros((LANES - LOW - rank, feats), BF)
-        zeros = jnp.zeros((toks, feats), BF)
-        grad_out[:toks] = jnp.where(first_core(), given[...], zeros)
-        grad_out[toks:] = jnp.where(first_core(), zeros, given[...])
+    at = CHIPS * width
+    if tick == 0:
+        up, out = refs
+        out[rows:, at : at + width] = other_half(up[...])
     else:
         arrived, output, out, grad_out = refs
-        grad = chosen_grad(sections, arrived, output)
+        if tick == 1:
+            given = arrived[...]
+            zeros = jnp.zeros(given.shape, BF)
+            given = jnp.concatenate(
+                [jnp.where(first_core(), given, zeros), jnp.where(first_core(), zeros, given)]
+            )
+        else:
+            given = arrived[...]
+        kept = jnp.where(first_core(), output[...], jnp.zeros(output.shape, BF))
+        grad = jnp.where(lax.axis_index("section") == sections - 1, kept, given)
         grad_out[...] = grad
-        at = (CHIPS + 1) * width + LANES
-        out[:, at:] = other_half(grad)
+        out[:, at + width + LANES :] = other_half(grad)
     for j in range(CHIPS):
         out[:, j * width : (j + 1) * width] = other_half(product[j])
-    at = CHIPS * width
     out[:rows, at : at + width] = other_half(x[...])
-    if start:
-        out[rows:, at : at + width] = jnp.zeros((4 * CHIPS, width), BF)
     out[:, at + width : at + width + LANES] = split(small[...])
 
 
@@ -228,7 +228,9 @@
     values = join(split(small[...])) + join(theirs[:, at : at + LANES])
     values = between(values, 0, LANES // 2)
     if start:
-        (parcel,) = refs
+        up, parcel = refs
+        mine_x = jnp.concatenate([mine_x, own_half(up[...])])
+        theirs_x = theirs[:, at - width : at]
     else:
         grad_part, up, gain_w, mixed, parcel, grad_out = refs
         grad = own_half(grad_part[...]).astype(F32) + theirs[:, at + LANES :].astype(F32)
@@ -238,7 +240,7 @@
         first = jnp.sum(wide * jnp.sum(gain_w[...], axis=0, keepdims=True), axis=1, keepdims=True)
         second = jnp.sum(wide * mixed[...], axis=1, keepdims=True)
         lanes = lane(rows)
-        values = values + pltpu.roll(dot_t(grad, own_half(up[...])), GRAD - LOW, 1)
+        values = values + pltpu.roll(dot_t(grad, up[...]), GRAD - LOW, 1)
         values = jnp.where(lanes == FIRST, first, values)
         values = jnp.where(lanes == SECOND, second, values)
         for j in range(CHIPS):
@@ -250,32 +252,30 @@
         total = total + theirs[:, j * width : (j + 1) * width].astype(F32)
         parcel[j, :, :width] = total.astype(BF)
         held = jnp.where(block == j, mine_x, jnp.where(block == (j ^ 1), theirs_x, 0.0).astype(BF))
-        parcel[j, :rows, width : 2 * width] = held
-        if start:
-            parcel[j, rows:, width : 2 * width] = jnp.zeros((4 * CHIPS, width), BF)
+        parcel[j, :, width : 2 * width] = held
         parcel[j, :, 2 * width : 2 * width + LANES] = halves
 
 
-def output_kernel(start, got, up, *refs):
-    if start:
-        gain_w, gain_low, out, mixed, stats = refs
-    else:
-        gain_w, gain_low, out, mixed, stats = refs
+def output_kernel(start, got, up, gain_w, gain_low, out, mixed, stats):
     rows, width = mixed.shape
     feats = 2 * width
     total = got[0, :, :width].astype(F32)
-    x = got[0, :rows, width:feats].astype(F32)
+    x = got[0, :, width:feats].astype(F32)
     values = join(got[0, :, feats : feats + LANES])
     for j in range(1, CHIPS):
         total = total + got[j, :, :width].astype(F32)
-        x = x + got[j, :rows, width:feats].astype(F32)
+        x = x + got[j, :, width:feats].astype(F32)
         values = values + join(got[j, :, feats : feats + LANES])
     values = between(values, 0, LANES // 2)
     if start:
         gain_w[...] = total[rows : rows + 2 * CHIPS] + total[rows + 2 * CHIPS :]
         gain_low[...] = between(values[rows : rows + 2 * CHIPS], LOW, GRAD)
+        up[:LOW] = jnp.zeros((LOW, width), BF)
+        up[LOW:GRAD] = x[rows:].astype(BF)
+        up[GRAD:] = jnp.zeros((LANES - GRAD, width), BF)
         total = total[:rows]
         values = values[:rows]
+        x = x[:rows]
     at = lane(rows)
     mean = pick(values, 0, SQUARE) / (2 * CHIPS)
     off = jnp.where(at < 2 * CHIPS, values - mean, 0.0)
@@ -289,7 +289,7 @@
     low = between(inv * low, LOW, GRAD)
     mixed[...] = total
     stats[...] = jnp.where(at == 0, mean, jnp.where(at == 1, inv, low))
-    out[:, :width] = (x + total + dot(low.astype(BF), own_half(up[...]))).astype(BF)
+    out[:, :width] = (x + total + dot(low.astype(BF), up[...])).astype(BF)
     if not start:
         out[:, width : width + LANES] = split(values)
         for j in range(CHIPS):
@@ -349,44 +349,45 @@
     acc_up[...] = up[LOW : LOW + rank]
 
 
-def last_kernel(sections, arrived, output, up, stats, acc_up, after, low_out, up_out):
+def last_kernel(sections, arrived, output, up, stats, acc_up, after, out, up_out):
     rows, feats = arrived.shape
-    rank = acc_up.shape[0]
-    grad = chosen_grad(sections, arrived, output)
-    turned = dot_t(up[LOW : LOW + rank], grad)
+    rank = up.shape[0]
+    kept = jnp.where(lax.axis_index("dp") == 0, output[...], jnp.zeros(output.shape, BF))
+    grad = jnp.where(lax.axis_index("section") == sections - 1, kept, arrived[...])
+    turned = dot_t(up[...], grad)
     turned = jnp.concatenate([turned, jnp.zeros((rank, LANES - rows), F32)], axis=1)
     high = turned.astype(BF).astype(F32)
-    halves = jnp.concatenate([high, turned - high], axis=1).astype(BF)
+    parcel = jnp.concatenate([high, turned - high, acc_up[...]], axis=1).astype(BF)
     for j in range(4 * CHIPS):
-        low_out[j] = halves
+        out[j] = parcel
     low = t_dot(stats[...].astype(BF), grad)
-    zeros = jnp.zeros(acc_up.shape, F32)
-    acc = jnp.concatenate(
-        [jnp.where(first_core(), acc_up[...], zeros), jnp.where(first_core(), zeros, acc_up[...])],
-        axis=1,
-    )
-    up_out[...] = (acc + low[LOW : LOW + rank]).astype(BF)
-
-
-def finish_kernel(got, x, stats, gains, mine, theirs, up_a, up_b, down_out, up_out):
+    up_out[...] = low[LOW : LOW + rank].astype(BF)
+
+
+def finish_kernel(got, x, stats, gains, mine, theirs, up_mine, up_theirs, down_out, up_out):
     rows = x.shape[0]
-    turned = got[0].astype(F32)
+    turned = got[0, :, : 2 * LANES].astype(F32)
     for j in range(1, 4 * CHIPS):
-        turned = turned + got[j].astype(F32)
+        turned = turned + got[j, :, : 2 * LANES].astype(F32)
     low_grad = turned[:, :LANES] + turned[:, LANES:]
     u = normed(x[...], stats[...]) * gains[...]
     u = jnp.concatenate([u, jnp.zeros((LANES - rows, u.shape[1]), F32)])
     total = mine[...] + theirs[...] + dot(low_grad, u, precision=HIGHEST)
     down_out[...] = (total / rows).astype(BF)
-    up_out[...] = ((up_a[...].astype(F32) + up_b[...].astype(F32)) / rows).astype(BF)
-
-
-def back_home(array, sections, flip):
-    route = []
-    for s in range(sections):
-        for block in range(2 * CHIPS):
-            for half in range(2):
-                route.append((flat(s, *owner(block, half ^ flip)), flat(s, block, half)))
+    tensor = lax.axis_index("tensor")
+    at = 4 * (tensor % CHIPS) + tensor // CHIPS
+    total = jnp.concatenate([got[at, :, 2 * LANES :], got[at + 2, :, 2 * LANES :]], axis=1)
+    total = total.astype(F32) + up_mine[...].astype(F32) + up_theirs[...].astype(F32)
+    up_out[...] = (total / rows).astype(BF)
+
+
+def to_same(array, sections):
+    return lax.ppermute(array, "section", [(s, s - 1) for s in range(1, sections)])
+
+
+def last_home(array, sections):
+    s = sections - 1
+    route = [(flat(s, *owner(block, 0)), flat(s, block, 0)) for block in range(2 * CHIPS)]
     return lax.ppermute(array, AXES, route)
 
 
@@ -411,13 +412,7 @@
 
     mine = initial_step_inputs[0]
     theirs = lax.ppermute(mine, "dp", [(0, 1), (1, 0)])
-    given = to_owner(initial_step_gradients[0], sections, 0)
-    given_up = to_owner(adapter_up_map[0], sections, 0)
-    stored = prior_epoch_input[0, 0]
-    order = sample_numbers[0, 0]
-    to_partner = [(flat(0, t, d), flat(0, t, 1 - d)) for t in range(2 * CHIPS) for d in range(2)]
-    stored_theirs = lax.ppermute(stored, AXES, to_partner)
-    order_theirs = lax.ppermute(order, AXES, to_partner)
+    down = call(warm_kernel, shape(LANES, feats), w, gains, mine, adapter_down_map[0].T)
 
     block = shape(rows, feats, dtype=BF)
     values = shape(rows, LANES)
@@ -427,46 +422,37 @@
         more = 4 * CHIPS if start else 0
         out = [block, shape(CHIPS, rows + more, feats, dtype=BF), shape(rows + more, LANES)]
         if start:
-            x, product, small, down = call(
+            x, product, small = call(
                 functools.partial(forward_kernel, True, tick),
-                out + [shape(LANES, feats)],
-                given,
-                given_up,
-                stored_theirs,
+                out,
                 mine,
                 theirs,
                 gains,
                 w,
-                adapter_down_map[0].T,
-                scalars=(order_theirs,),
+                down,
             )
         else:
             x, product, small = call(
                 functools.partial(forward_kernel, False, tick),
                 out,
                 arrived,
-                stored,
-                stored_theirs,
+                chosen,
+                chosen_theirs,
                 gains,
                 w,
                 down,
-                scalars=(order, order_theirs),
             )
         width = feats // 2
         ins = [product, small, x]
         columns = (CHIPS + (1 if start else 2)) * width + LANES
         dealt = shape(rows + more, columns, dtype=BF)
         if start:
-            dealt, up, grad_arrived = call(
-                functools.partial(deal_kernel, True, sections),
-                [dealt, shape(LANES, feats, dtype=BF), block],
-                *ins,
-                given,
-                given_up,
+            dealt = call(
+                functools.partial(deal_kernel, tick, sections), dealt, *ins, adapter_up_map[0]
             )
         else:
             dealt, grad_part = call(
-                functools.partial(deal_kernel, False, sections),
+                functools.partial(deal_kernel, tick, sections),
                 [dealt, block],
                 *ins,
                 grad_arrived,
@@ -476,7 +462,7 @@
         columns = (2 if start else 3) * width + LANES
         parcel = shape(CHIPS, rows + more, columns, dtype=BF)
         if start:
-            parcel = call(functools.partial(pack_kernel, True), parcel, *ins)
+            parcel = call(functools.partial(pack_kernel, True), parcel, *ins, adapter_up_map[0])
         else:
             parcel, grad = call(
                 functools.partial(pack_kernel, False),
@@ -493,8 +479,9 @@
         out = [shape(rows, columns, dtype=BF), shape(rows, width), values]
         kernel = functools.partial(output_kernel, start)
         if start:
-            gain_w, gain_low, own, mixed, stats = call(
-                kernel, [shape(2 * CHIPS, width), shape(2 * CHIPS, LANES)] + out, got, up
+            up = shape(LANES, width, dtype=BF)
+            up, gain_w, gain_low, own, mixed, stats = call(
+                kernel, [up, shape(2 * CHIPS, width), shape(2 * CHIPS, LANES)] + out, got
             )
         else:
             own, mixed, stats = call(kernel, out, got, up, gain_w, gain_low)
@@ -502,7 +489,22 @@
         output = call(whole_kernel, block, own, other)
         if tick < TICKS - 1:
             arrived = to_next(output, sections)
-        if not start:
+        if start:
+            chosen, grads_out = call(
+                prepare_kernel,
+                [shape(TICKS - 1, toks, feats, dtype=BF), shape(toks, feats, dtype=BF)],
+                prior_epoch_input[0, 0],
+                initial_step_gradients[0],
+                output,
+                scalars=(sample_numbers[0, 0],),
+            )
+            grad_arrived = to_owner(grads_out, sections, 0)
+            chosen_theirs = lax.ppermute(
+                chosen,
+                AXES,
+                [(flat(0, t, d), flat(0, t, 1 - d)) for t in range(2 * CHIPS) for d in range(2)],
+            )
+        else:
             grad_x, sums = call(
                 backward_kernel,
                 [block, values],
@@ -516,7 +518,10 @@
                 down,
             )
             all_sums.append(sums)
-            grad_arrived = to_owner(grad_x, sections, 1)
+            if tick < TICKS - 1:
+                grad_arrived = to_owner(grad_x, sections, 1)
+            else:
+                grad_arrived = to_same(grad_x, sections)
         xs.append(x)
         all_stats.append(stats)
 
@@ -531,17 +536,20 @@
         *grads,
     )
     acc_other = lax.ppermute(acc_down, "dp", [(0, 1), (1, 0)])
-    turned, up_part = call(
+    parcel, up_part = call(
         functools.partial(last_kernel, sections),
-        [shape(4 * CHIPS, rank, 2 * LANES, dtype=BF), shape(rank, feats, dtype=BF)],
+        [
+            shape(4 * CHIPS, rank, 2 * LANES + feats // 2, dtype=BF),
+            shape(rank, feats, dtype=BF),
+        ],
         grad_arrived,
-        output,
-        up,
+        last_home(output, sections),
+        adapter_up_map[0],
         stats,
         acc_up,
         acc_other,
     )
-    got = lax.all_to_all(turned, ("tensor", "dp"), 0, 0)
+    got = lax.all_to_all(parcel, ("tensor", "dp"), 0, 0)
     grad_down, grad_up = call(
         finish_kernel,
         [shape(rank, feats, dtype=BF), shape(rank, feats, dtype=BF)],
@@ -551,8 +559,8 @@
         gains,
         acc_down,
         acc_other,
-        back_home(up_part, sections, 0),
-        back_home(up_part, sections, 1),
+        up_part,
+        lax.ppermute(up_part, "dp", [(0, 1), (1, 0)]),
     )
     return grad_down.T[None], grad_up[None]
 

time: 213 us -> 200 us (0.939)
  the two profiles are of different devices: /device:TPU:116 before, /device:TPU:225 now
where the time goes in v6:
time: 200 us; the launch traced here: 199 us
  blocking collectives  70.7 us (35%)
  starting transfers between devices  65.9 us (33%)
  waiting for transfers between devices  36.6 us (18%)
  Pallas kernels  20.2 us (10%)
  local copies, waits for them, and re-layouts  4.67 us (2%)
    all_to_all x4, blocking collectives, over_chips(): return lax.all_to_all(array, 'tensor', 0, 0, axis_index_groups=groups)  70.7 us
    ppermute x8, starting transfers between devices, swap_cores(): return lax.ppermute(array, 'tensor', [(i, i ^ 1) for i in range(2 * CHIPS)])  22.5 us
    pallas_call x28, Pallas kernels, call(): pl.pallas_call(kernel, out_shape=out, in_specs=[pl.BlockSpec(memory_space...  20.2 us
    ppermute x3, starting transfers between devices, to_next(): return lax.ppermute(array, AXES, route)  17.1 us
    ppermute x8, waiting for transfers between devices, swap_cores(): return lax.ppermute(array, 'tensor', [(i, i ^ 1) for i in range(2 * CHIPS)])  11.7 us
    ppermute x3, waiting for transfers between devices, to_owner(): return lax.ppermute(array, AXES, route)  11 us
    ppermute x3, starting transfers between devices, to_owner(): return lax.ppermute(array, AXES, route)  10.9 us
    ppermute x1, waiting for transfers between devices, on_device(): acc_other = lax.ppermute(acc_down, 'dp', [(0, 1), (1, 0)])  5.8 us
  transfers between devices with their start and end apart: 21, of which 14 were waited for; matrix products, arithmetic and copies ran while one was open for 0% of the time, Pallas kernels for 5%

profile of v6, /device:TPU:225, one launch (start us, length us, event | category | flops | bytes accessed | tf_op | source)
XLA Modules:
  0.0 199.1 jit_solution(2650299545329770777)
XLA Ops:
  0.6 3.2 %collective-permute-start = (bf16[48,768]{1,0:T(8,128)(2,1)}, bf16[48,768]{1,0:T(8,128)(2,1)S(1)}, u32[]{:S(2)}, u32[]{:S(2)}) collective-permute-start(bf16[48,768]{1,0:T(8,128)(2,1)} %bitcast.23), channel_id=1, source_target_pairs={{0,1},{1,0},{2,3},{3,2},{4,5},{5,4},{6,7},{7,6},{8,9},{9,8},{10,11... | collective-permute-start | bytes 221192 | tf_op jit(solution)/shard_map/ppermute | solution.py:414
  3.9 2.3 %copy-done = bf16[1,768,3072]{2,1,0:T(8,128)(2,1)S(1)} copy-done((bf16[1,768,3072]{2,1,0:T(8,128)(2,1)S(1)}, bf16[1,768,3072]{2,1,0:T(8,128)(2,1)}, u32[]{:S(2)}) %copy-start) | copy-done | bytes 4718616
  10.2 2.9 %collective-permute-start.1 = (bf16[112,2048]{1,0:T(8,128)(2,1)S(1)}, bf16[112,2048]{1,0:T(8,128)(2,1)S(1)}, u32[]{:S(2)}, u32[]{:S(2)}) collective-permute-start(bf16[112,2048]{1,0:T(8,128)(2,1)S(1)} %shard_map.97), channel_id=1, source_target_pairs={{0,2},{2,0},{4,6},{6,4},{8,10},{10,8},{12,14},{14,12},{1,3},{3,1},... | collective-permute-start | bytes 1376264 | tf_op jit(solution)/shard_map/ppermute | solution.py:54
  14.9 15.7 %all_to_all.25.got = bf16[4,112,896]{2,1,0:T(8,128)(2,1)S(1)} all-to-all(bf16[4,112,896]{2,1,0:T(8,128)(2,1)S(1)} %shard_map.98), channel_id=1, replica_groups={{0,4,8,12},{2,6,10,14},{1,5,9,13},{3,7,11,15},{16,20,24,28},{18,22,26,3..., dimensions={0} | all-to-all | bytes 1605632 | tf_op jit(solution)/shard_map/all_to_all | solution.py:59
  31.2 3.4 %collective-permute-start.2 = (bf16[96,384]{1,0:T(8,128)(2,1)S(1)}, bf16[96,384]{1,0:T(8,128)(2,1)S(1)}, u32[]{:S(2)}, u32[]{:S(2)}) collective-permute-start(bf16[96,384]{1,0:T(8,128)(2,1)S(1)} %get-tuple-element.57.mine), channel_id=1, source_target_pairs={{0,2},{2,0},{4,6},{6,4},{8,10},{10,8},{12,14},{14,12},{1,3},{3,1},... | collective-permute-start | bytes 221192 | tf_op jit(solution)/shard_map/ppermute | solution.py:54
  36.8 4.1 %collective-permute-start.3 = (bf16[96,768]{1,0:T(8,128)(2,1)S(1)}, bf16[96,768]{1,0:T(8,128)(2,1)S(1)}, u32[]{:S(2)}, u32[]{:S(2)}) collective-permute-start(bf16[96,768]{1,0:T(8,128)(2,1)S(1)} %shard_map.100.after.refs_1_), channel_id=1, source_target_pairs={{0,16},{2,17},{4,18},{6,19},{8,20},{10,21},{12,22},{14,23},{1,24},... | collective-permute-start | bytes 442376 | tf_op jit(solution)/shard_map/ppermute | solution.py:50
  40.9 3.8 %collective-permute-start.5 = (bf16[48,768]{1,0:T(8,128)(2,1)S(1)}, bf16[48,768]{1,0:T(8,128)(2,1)S(1)}, u32[]{:S(2)}, u32[]{:S(2)}) collective-permute-start(bf16[48,768]{1,0:T(8,128)(2,1)S(1)} %get-tuple-element.62), channel_id=1, source_target_pairs={{0,0},{1,2},{2,4},{3,6},{4,8},{5,10},{6,12},{7,14},{8,1},{9,3},{10... | collective-permute-start | bytes 221192 | tf_op jit(solution)/shard_map/ppermute | solution.py:41
  44.7 2.8 %collective-permute-done.3.refs_0_ = bf16[96,768]{1,0:T(8,128)(2,1)S(1)} collective-permute-done((bf16[96,768]{1,0:T(8,128)(2,1)S(1)}, bf16[96,768]{1,0:T(8,128)(2,1)S(1)}, u32[]{:S(2)}, u32[]{:S(2)}) %collective-permute-start.3) | collective-permute-done | bytes 147488 | tf_op jit(solution)/shard_map/ppermute | solution.py:50
  49.0 1.9 collective-permute-start.6
  53.2 19.0 %all_to_all.26.got = bf16[4,96,1280]{2,1,0:T(8,128)(2,1)S(1)} all-to-all(bf16[4,96,1280]{2,1,0:T(8,128)(2,1)S(1)} %get-tuple-element.68), channel_id=1, replica_groups={{0,4,8,12},{2,6,10,14},{1,5,9,13},{3,7,11,15},{16,20,24,28},{18,22,26,3..., dimensions={0} | all-to-all | bytes 1966080 | tf_op jit(solution)/shard_map/all_to_all | solution.py:59
  72.8 3.4 %collective-permute-start.7 = (bf16[96,2048]{1,0:T(8,128)(2,1)S(1)}, bf16[96,2048]{1,0:T(8,128)(2,1)S(1)}, u32[]{:S(2)}, u32[]{:S(2)}) collective-permute-start(bf16[96,2048]{1,0:T(8,128)(2,1)S(1)} %get-tuple-element.70.mine), channel_id=1, source_target_pairs={{0,2},{2,0},{4,6},{6,4},{8,10},{10,8},{12,14},{14,12},{1,3},{3,1},... | collective-permute-start | bytes 1179656 | tf_op jit(solution)/shard_map/ppermute | solution.py:54
  77.6 3.9 %collective-permute-start.8 = (bf16[96,768]{1,0:T(8,128)(2,1)S(1)}, bf16[96,768]{1,0:T(8,128)(2,1)S(1)}, u32[]{:S(2)}, u32[]{:S(2)}) collective-permute-start(bf16[96,768]{1,0:T(8,128)(2,1)S(1)} %shard_map.106.refs_1_), channel_id=1, source_target_pairs={{0,16},{2,17},{4,18},{6,19},{8,20},{10,21},{12,22},{14,23},{1,24},... | collective-permute-start | bytes 442376 | tf_op jit(solution)/shard_map/ppermute | solution.py:50
  81.6 1.8 shard_map.108
  83.4 4.9 %collective-permute-start.9 = (bf16[96,768]{1,0:T(8,128)(2,1)S(1)}, bf16[96,768]{1,0:T(8,128)(2,1)S(1)}, u32[]{:S(2)}, u32[]{:S(2)}) collective-permute-start(bf16[96,768]{1,0:T(8,128)(2,1)S(1)} %get-tuple-element.75), channel_id=1, source_target_pairs={{16,0},{17,2},{18,4},{19,6},{20,8},{21,10},{22,12},{23,14},{24,1},... | collective-permute-start | bytes 442376 | tf_op jit(solution)/shard_map/ppermute | solution.py:41
  89.7 5.3 %collective-permute-done.9.refs_0_ = bf16[96,768]{1,0:T(8,128)(2,1)S(1)} collective-permute-done((bf16[96,768]{1,0:T(8,128)(2,1)S(1)}, bf16[96,768]{1,0:T(8,128)(2,1)S(1)}, u32[]{:S(2)}, u32[]{:S(2)}) %collective-permute-start.9) | collective-permute-done | bytes 147488 | tf_op jit(solution)/shard_map/ppermute | solution.py:41
  95.0 1.9 collective-permute-start.10
  99.2 16.9 %all_to_all.27.got = bf16[4,96,1280]{2,1,0:T(8,128)(2,1)S(1)} all-to-all(bf16[4,96,1280]{2,1,0:T(8,128)(2,1)S(1)} %get-tuple-element.79), channel_id=1, replica_groups={{0,4,8,12},{2,6,10,14},{1,5,9,13},{3,7,11,15},{16,20,24,28},{18,22,26,3..., dimensions={0} | all-to-all | bytes 1966080 | tf_op jit(solution)/shard_map/all_to_all | solution.py:59
  116.7 3.4 %collective-permute-start.11 = (bf16[96,2048]{1,0:T(8,128)(2,1)S(1)}, bf16[96,2048]{1,0:T(8,128)(2,1)S(1)}, u32[]{:S(2)}, u32[]{:S(2)}) collective-permute-start(bf16[96,2048]{1,0:T(8,128)(2,1)S(1)} %get-tuple-element.80.mine), channel_id=1, source_target_pairs={{0,2},{2,0},{4,6},{6,4},{8,10},{10,8},{12,14},{14,12},{1,3},{3,1},... | collective-permute-start | bytes 1179656 | tf_op jit(solution)/shard_map/ppermute | solution.py:54
  121.5 9.1 %collective-permute-start.12 = (bf16[96,768]{1,0:T(8,128)(2,1)S(1)}, bf16[96,768]{1,0:T(8,128)(2,1)S(1)}, u32[]{:S(2)}, u32[]{:S(2)}) collective-permute-start(bf16[96,768]{1,0:T(8,128)(2,1)S(1)} %shard_map.112.refs_1_), channel_id=1, source_target_pairs={{0,16},{2,17},{4,18},{6,19},{8,20},{10,21},{12,22},{14,23},{1,24},... | collective-permute-start | bytes 442376 | tf_op jit(solution)/shard_map/ppermute | solution.py:50
  130.6 1.8 shard_map.114
  132.4 2.1 %collective-permute-start.13 = (bf16[96,768]{1,0:T(8,128)(2,1)S(1)}, bf16[96,768]{1,0:T(8,128)(2,1)S(1)}, u32[]{:S(2)}, u32[]{:S(2)}) collective-permute-start(bf16[96,768]{1,0:T(8,128)(2,1)S(1)} %get-tuple-element.85), channel_id=1, source_target_pairs={{16,0},{17,2},{18,4},{19,6},{20,8},{21,10},{22,12},{23,14},{24,1},... | collective-permute-start | bytes 442376 | tf_op jit(solution)/shard_map/ppermute | solution.py:41
  135.9 5.8 %collective-permute-done.13.refs_0_ = bf16[96,768]{1,0:T(8,128)(2,1)S(1)} collective-permute-done((bf16[96,768]{1,0:T(8,128)(2,1)S(1)}, bf16[96,768]{1,0:T(8,128)(2,1)S(1)}, u32[]{:S(2)}, u32[]{:S(2)}) %collective-permute-start.13) | collective-permute-done | bytes 147488 | tf_op jit(solution)/shard_map/ppermute | solution.py:41
  141.8 1.9 collective-permute-start.14
  146.0 19.2 %all_to_all.28.got = bf16[4,96,1280]{2,1,0:T(8,128)(2,1)S(1)} all-to-all(bf16[4,96,1280]{2,1,0:T(8,128)(2,1)S(1)} %get-tuple-element.89), channel_id=1, replica_groups={{0,4,8,12},{2,6,10,14},{1,5,9,13},{3,7,11,15},{16,20,24,28},{18,22,26,3..., dimensions={0} | all-to-all | bytes 1966080 | tf_op jit(solution)/shard_map/all_to_all | solution.py:59
  166.3 3.6 %collective-permute-start.15 = (bf16[96,2048]{1,0:T(8,128)(2,1)S(1)}, bf16[96,2048]{1,0:T(8,128)(2,1)S(1)}, u32[]{:S(2)}, u32[]{:S(2)}) collective-permute-start(bf16[96,2048]{1,0:T(8,128)(2,1)S(1)} %get-tuple-element.90.mine), channel_id=1, source_target_pairs={{0,2},{2,0},{4,6},{6,4},{8,10},{10,8},{12,14},{14,12},{1,3},{3,1},... | collective-permute-start | bytes 1179656 | tf_op jit(solution)/shard_map/ppermute | solution.py:54
  171.2 1.8 shard_map.118
  173.0 1.9 collective-permute-start.16
  177.0 1.9 collective-permute-start.18
  179.0 5.8 %collective-permute-done.18.after.theirs = f32[16,768]{1,0:T(8,128)S(1)} collective-permute-done((f32[16,768]{1,0:T(8,128)S(1)}, f32[16,768]{1,0:T(8,128)S(1)}, u32[]{:S(2)}, u32[]{:S(2)}) %collective-permute-start.18) | collective-permute-done | bytes 49184 | tf_op jit(solution)/shard_map/ppermute | solution.py:538
  185.7 3.8 %all-to-all-start.4 = ((bf16[16,16,640]{2,1,0:T(8,128)(2,1)}), bf16[16,16,640]{2,1,0:T(8,128)(2,1)S(1)}, u32[]{:S(2)}, u32[]{:S(2)}) async-start(bf16[16,16,640]{2,1,0:T(8,128)(2,1)} %get-tuple-element.102), calls=%async_computation.4 | async-start | bytes 655360 | tf_op jit(solution)/shard_map/all_to_all | solution.py:552
  189.5 3.3 %collective-permute-start.19 = (bf16[16,768]{1,0:T(8,128)(2,1)S(1)}, bf16[16,768]{1,0:T(8,128)(2,1)S(1)}, u32[]{:S(2)}, u32[]{:S(2)}) collective-permute-start(bf16[16,768]{1,0:T(8,128)(2,1)S(1)} %get-tuple-element.103.up_mine), channel_id=1, source_target_pairs={{0,1},{1,0},{2,3},{3,2},{4,5},{5,4},{6,7},{7,6},{8,9},{9,8},{10,11... | collective-permute-start | bytes 73736 | tf_op jit(solution)/shard_map/ppermute | solution.py:563
  194.4 3.7 %all-to-all-done.4.got = bf16[16,16,640]{2,1,0:T(8,128)(2,1)S(1)} async-done(((bf16[16,16,640]{2,1,0:T(8,128)(2,1)}), bf16[16,16,640]{2,1,0:T(8,128)(2,1)S(1)}, u32[]{:S(2)}, u32[]{:S(2)}) %all-to-all-start.4) | async-done | bytes 327712 | tf_op jit(solution)/shard_map/all_to_all | solution.py:552
  (65 shorter events, 31.7 us)
Async XLA Ops:
  0.6 7.9 %collective-permute-start = (bf16[48,768]{1,0:T(8,128)(2,1)}, bf16[48,768]{1,0:T(8,128)(2,1)S(1)}, u32[]{:S(2)}, u32[]{:S(2)}) collective-permute-start(bf16[48,768]{1,0:T(8,128)(2,1)} %bitcast.23), channel_id=1, source_target_pairs={{0,1},{1,0},{2,3},{3,2},{4,5},{5,4},{6,7},{7,6},{8,9},{9,8},{10,11... | collective-permute-start | bytes 221192 | tf_op jit(solution)/shard_map/ppermute | solution.py:414
  3.8 2.3 %copy-start = (bf16[1,768,3072]{2,1,0:T(8,128)(2,1)S(1)}, bf16[1,768,3072]{2,1,0:T(8,128)(2,1)}, u32[]{:S(2)}) copy-start(bf16[1,768,3072]{2,1,0:T(8,128)(2,1)} %param.9) | copy-start | bytes 14155780
  6.2 0.7 copy-start.1
  6.9 0.9 copy-start.3
  7.8 0.7 copy-start.7
  8.5 1.6 copy-start.4
  8.5 39.0 %slice-start = ((s8[4718592]{0:T(1024)(128)(4,1)}), s8[4194304]{0:T(1024)(128)(4,1)S(1)}, s32[]{:S(2)}) async-start(s8[4718592]{0:T(1024)(128)(4,1)} %bitcast.15), calls=%async_computation.5 | async-start | bytes 8388608
  8.5 27.0 %copy-start.5 = (bf16[1,1,2,48,768]{4,3,2,1,0:T(8,128)(2,1)S(1)}, bf16[1,1,2,48,768]{4,3,2,1,0:T(8,128)(2,1)}, u32[]{:S(2)}) copy-start(bf16[1,1,2,48,768]{4,3,2,1,0:T(8,128)(2,1)} %param.13) | copy-start | bytes 442372
  8.5 27.0 %copy-start.6 = (bf16[1,48,768]{2,1,0:T(8,128)(2,1)S(1)}, bf16[1,48,768]{2,1,0:T(8,128)(2,1)}, u32[]{:S(2)}) copy-start(bf16[1,48,768]{2,1,0:T(8,128)(2,1)} %param.15) | copy-start | bytes 221188
  8.5 27.0 %copy-start.8 = (s32[1,1,4]{2,1,0:T(1,128)S(1)}, s32[1,1,4]{2,1,0:T(1,128)}, u32[]{:S(2)}) copy-start(s32[1,1,4]{2,1,0:T(1,128)} %param.16) | copy-start | bytes 52
  8.6 38.9 %slice-start.1 = ((s8[4718592]{0:T(1024)(128)(4,1)}), s8[524288]{0:T(1024)(128)(4,1)S(1)}, s32[]{:S(2)}) async-start(s8[4718592]{0:T(1024)(128)(4,1)} %bitcast.15), calls=%async_computation.6 | async-start | bytes 1048576
  10.2 4.3 %collective-permute-start.1 = (bf16[112,2048]{1,0:T(8,128)(2,1)S(1)}, bf16[112,2048]{1,0:T(8,128)(2,1)S(1)}, u32[]{:S(2)}, u32[]{:S(2)}) collective-permute-start(bf16[112,2048]{1,0:T(8,128)(2,1)S(1)} %shard_map.97), channel_id=1, source_target_pairs={{0,2},{2,0},{4,6},{6,4},{8,10},{10,8},{12,14},{14,12},{1,3},{3,1},... | collective-permute-start | bytes 1376264 | tf_op jit(solution)/shard_map/ppermute | solution.py:54
  31.2 4.3 %collective-permute-start.2 = (bf16[96,384]{1,0:T(8,128)(2,1)S(1)}, bf16[96,384]{1,0:T(8,128)(2,1)S(1)}, u32[]{:S(2)}, u32[]{:S(2)}) collective-permute-start(bf16[96,384]{1,0:T(8,128)(2,1)S(1)} %get-tuple-element.57.mine), channel_id=1, source_target_pairs={{0,2},{2,0},{4,6},{6,4},{8,10},{10,8},{12,14},{14,12},{1,3},{3,1},... | collective-permute-start | bytes 221192 | tf_op jit(solution)/shard_map/ppermute | solution.py:54
  36.1 11.4 %collective-permute-start.4 = (bf16[3,48,768]{2,1,0:T(8,128)(2,1)S(1)}, bf16[3,48,768]{2,1,0:T(8,128)(2,1)S(1)}, u32[]{:S(2)}, u32[]{:S(2)}) collective-permute-start(bf16[3,48,768]{2,1,0:T(8,128)(2,1)S(1)} %get-tuple-element.58.refs_1_), channel_id=1, source_target_pairs={{0,1},{1,0},{2,3},{3,2},{4,5},{5,4},{6,7},{7,6},{8,9},{9,8},{10,11... | collective-permute-start | bytes 663560 | tf_op jit(solution)/shard_map/ppermute | solution.py:502
  36.8 10.7 %collective-permute-start.3 = (bf16[96,768]{1,0:T(8,128)(2,1)S(1)}, bf16[96,768]{1,0:T(8,128)(2,1)S(1)}, u32[]{:S(2)}, u32[]{:S(2)}) collective-permute-start(bf16[96,768]{1,0:T(8,128)(2,1)S(1)} %shard_map.100.after.refs_1_), channel_id=1, source_target_pairs={{0,16},{2,17},{4,18},{6,19},{8,20},{10,21},{12,22},{14,23},{1,24},... | collective-permute-start | bytes 442376 | tf_op jit(solution)/shard_map/ppermute | solution.py:50
  40.9 8.0 %collective-permute-start.5 = (bf16[48,768]{1,0:T(8,128)(2,1)S(1)}, bf16[48,768]{1,0:T(8,128)(2,1)S(1)}, u32[]{:S(2)}, u32[]{:S(2)}) collective-permute-start(bf16[48,768]{1,0:T(8,128)(2,1)S(1)} %get-tuple-element.62), channel_id=1, source_target_pairs={{0,0},{1,2},{2,4},{3,6},{4,8},{5,10},{6,12},{7,14},{8,1},{9,3},{10... | collective-permute-start | bytes 221192 | tf_op jit(solution)/shard_map/ppermute | solution.py:41
  49.0 3.7 %collective-permute-start.6 = (bf16[96,2432]{1,0:T(8,128)(2,1)S(1)}, bf16[96,2432]{1,0:T(8,128)(2,1)S(1)}, u32[]{:S(2)}, u32[]{:S(2)}) collective-permute-start(bf16[96,2432]{1,0:T(8,128)(2,1)S(1)} %get-tuple-element.63), channel_id=1, source_target_pairs={{0,2},{2,0},{4,6},{6,4},{8,10},{10,8},{12,14},{14,12},{1,3},{3,1},... | collective-permute-start | bytes 1400840 | tf_op jit(solution)/shard_map/ppermute | solution.py:54
  72.8 4.8 %collective-permute-start.7 = (bf16[96,2048]{1,0:T(8,128)(2,1)S(1)}, bf16[96,2048]{1,0:T(8,128)(2,1)S(1)}, u32[]{:S(2)}, u32[]{:S(2)}) collective-permute-start(bf16[96,2048]{1,0:T(8,128)(2,1)S(1)} %get-tuple-element.70.mine), channel_id=1, source_target_pairs={{0,2},{2,0},{4,6},{6,4},{8,10},{10,8},{12,14},{14,12},{1,3},{3,1},... | collective-permute-start | bytes 1179656 | tf_op jit(solution)/shard_map/ppermute | solution.py:54
  77.6 10.7 %collective-permute-start.8 = (bf16[96,768]{1,0:T(8,128)(2,1)S(1)}, bf16[96,768]{1,0:T(8,128)(2,1)S(1)}, u32[]{:S(2)}, u32[]{:S(2)}) collective-permute-start(bf16[96,768]{1,0:T(8,128)(2,1)S(1)} %shard_map.106.refs_1_), channel_id=1, source_target_pairs={{0,16},{2,17},{4,18},{6,19},{8,20},{10,21},{12,22},{14,23},{1,24},... | collective-permute-start | bytes 442376 | tf_op jit(solution)/shard_map/ppermute | solution.py:50
  83.4 11.6 %collective-permute-start.9 = (bf16[96,768]{1,0:T(8,128)(2,1)S(1)}, bf16[96,768]{1,0:T(8,128)(2,1)S(1)}, u32[]{:S(2)}, u32[]{:S(2)}) collective-permute-start(bf16[96,768]{1,0:T(8,128)(2,1)S(1)} %get-tuple-element.75), channel_id=1, source_target_pairs={{16,0},{17,2},{18,4},{19,6},{20,8},{21,10},{22,12},{23,14},{24,1},... | collective-permute-start | bytes 442376 | tf_op jit(solution)/shard_map/ppermute | solution.py:41
  95.0 3.7 %collective-permute-start.10 = (bf16[96,2432]{1,0:T(8,128)(2,1)S(1)}, bf16[96,2432]{1,0:T(8,128)(2,1)S(1)}, u32[]{:S(2)}, u32[]{:S(2)}) collective-permute-start(bf16[96,2432]{1,0:T(8,128)(2,1)S(1)} %get-tuple-element.76), channel_id=1, source_target_pairs={{0,2},{2,0},{4,6},{6,4},{8,10},{10,8},{12,14},{14,12},{1,3},{3,1},... | collective-permute-start | bytes 1400840 | tf_op jit(solution)/shard_map/ppermute | solution.py:54
  116.7 4.8 %collective-permute-start.11 = (bf16[96,2048]{1,0:T(8,128)(2,1)S(1)}, bf16[96,2048]{1,0:T(8,128)(2,1)S(1)}, u32[]{:S(2)}, u32[]{:S(2)}) collective-permute-start(bf16[96,2048]{1,0:T(8,128)(2,1)S(1)} %get-tuple-element.80.mine), channel_id=1, source_target_pairs={{0,2},{2,0},{4,6},{6,4},{8,10},{10,8},{12,14},{14,12},{1,3},{3,1},... | collective-permute-start | bytes 1179656 | tf_op jit(solution)/shard_map/ppermute | solution.py:54
  121.5 13.0 %collective-permute-start.12 = (bf16[96,768]{1,0:T(8,128)(2,1)S(1)}, bf16[96,768]{1,0:T(8,128)(2,1)S(1)}, u32[]{:S(2)}, u32[]{:S(2)}) collective-permute-start(bf16[96,768]{1,0:T(8,128)(2,1)S(1)} %shard_map.112.refs_1_), channel_id=1, source_target_pairs={{0,16},{2,17},{4,18},{6,19},{8,20},{10,21},{12,22},{14,23},{1,24},... | collective-permute-start | bytes 442376 | tf_op jit(solution)/shard_map/ppermute | solution.py:50
  132.4 9.3 %collective-permute-start.13 = (bf16[96,768]{1,0:T(8,128)(2,1)S(1)}, bf16[96,768]{1,0:T(8,128)(2,1)S(1)}, u32[]{:S(2)}, u32[]{:S(2)}) collective-permute-start(bf16[96,768]{1,0:T(8,128)(2,1)S(1)} %get-tuple-element.85), channel_id=1, source_target_pairs={{16,0},{17,2},{18,4},{19,6},{20,8},{21,10},{22,12},{23,14},{24,1},... | collective-permute-start | bytes 442376 | tf_op jit(solution)/shard_map/ppermute | solution.py:41
  141.8 3.7 %collective-permute-start.14 = (bf16[96,2432]{1,0:T(8,128)(2,1)S(1)}, bf16[96,2432]{1,0:T(8,128)(2,1)S(1)}, u32[]{:S(2)}, u32[]{:S(2)}) collective-permute-start(bf16[96,2432]{1,0:T(8,128)(2,1)S(1)} %get-tuple-element.86), channel_id=1, source_target_pairs={{0,2},{2,0},{4,6},{6,4},{8,10},{10,8},{12,14},{14,12},{1,3},{3,1},... | collective-permute-start | bytes 1400840 | tf_op jit(solution)/shard_map/ppermute | solution.py:54
  166.3 31.8 %copy-start.2 = (f32[1,768]{1,0:T(1,128)S(1)}, f32[1,768]{1,0:T(1,128)}, u32[]{:S(2)}) copy-start(f32[1,768]{1,0:T(1,128)} %gains.11) | copy-start | bytes 9220
  166.3 4.9 %collective-permute-start.15 = (bf16[96,2048]{1,0:T(8,128)(2,1)S(1)}, bf16[96,2048]{1,0:T(8,128)(2,1)S(1)}, u32[]{:S(2)}, u32[]{:S(2)}) collective-permute-start(bf16[96,2048]{1,0:T(8,128)(2,1)S(1)} %get-tuple-element.90.mine), channel_id=1, source_target_pairs={{0,2},{2,0},{4,6},{6,4},{8,10},{10,8},{12,14},{14,12},{1,3},{3,1},... | collective-permute-start | bytes 1179656 | tf_op jit(solution)/shard_map/ppermute | solution.py:54
  173.0 11.7 %collective-permute-start.16 = (bf16[96,768]{1,0:T(8,128)(2,1)S(1)}, bf16[96,768]{1,0:T(8,128)(2,1)S(1)}, u32[]{:S(2)}, u32[]{:S(2)}) collective-permute-start(bf16[96,768]{1,0:T(8,128)(2,1)S(1)} %get-tuple-element.92.after), channel_id=1, source_target_pairs={{16,0},{32,16},{48,32},{64,48},{80,64},{96,80},{112,96},{128,112},... | collective-permute-start | bytes 442376 | tf_op jit(solution)/shard_map/ppermute | solution.py:385
  175.0 9.8 %collective-permute-start.17 = (bf16[96,768]{1,0:T(8,128)(2,1)S(1)}, bf16[96,768]{1,0:T(8,128)(2,1)S(1)}, u32[]{:S(2)}, u32[]{:S(2)}) collective-permute-start(bf16[96,768]{1,0:T(8,128)(2,1)S(1)} %shard_map.119), channel_id=1, source_target_pairs={{496,496},{500,498},{504,500},{508,502},{497,504},{501,506},{505,5... | collective-permute-start | bytes 442376 | tf_op jit(solution)/shard_map/ppermute | solution.py:391
  177.0 7.7 %collective-permute-start.18 = (f32[16,768]{1,0:T(8,128)S(1)}, f32[16,768]{1,0:T(8,128)S(1)}, u32[]{:S(2)}, u32[]{:S(2)}) collective-permute-start(f32[16,768]{1,0:T(8,128)S(1)} %get-tuple-element.101.mine), channel_id=1, source_target_pairs={{0,1},{1,0},{2,3},{3,2},{4,5},{5,4},{6,7},{7,6},{8,9},{9,8},{10,11... | collective-permute-start | bytes 147464 | tf_op jit(solution)/shard_map/ppermute | solution.py:538
  185.7 12.4 %all-to-all-start.4 = ((bf16[16,16,640]{2,1,0:T(8,128)(2,1)}), bf16[16,16,640]{2,1,0:T(8,128)(2,1)S(1)}, u32[]{:S(2)}, u32[]{:S(2)}) async-start(bf16[16,16,640]{2,1,0:T(8,128)(2,1)} %get-tuple-element.102), calls=%async_computation.4 | async-start | bytes 655360 | tf_op jit(solution)/shard_map/all_to_all | solution.py:552
  189.5 4.9 %collective-permute-start.19 = (bf16[16,768]{1,0:T(8,128)(2,1)S(1)}, bf16[16,768]{1,0:T(8,128)(2,1)S(1)}, u32[]{:S(2)}, u32[]{:S(2)}) collective-permute-start(bf16[16,768]{1,0:T(8,128)(2,1)S(1)} %get-tuple-element.103.up_mine), channel_id=1, source_target_pairs={{0,1},{1,0},{2,3},{3,2},{4,5},{5,4},{6,7},{7,6},{8,9},{9,8},{10,11... | collective-permute-start | bytes 73736 | tf_op jit(solution)/shard_map/ppermute | solution.py:563

commit v7 on v6

--- a/solution.py
+++ b/solution.py
@@ -41,12 +41,12 @@
     return lax.ppermute(array, AXES, route)
 
 
-def to_next(array, sections):
+def to_next(array, sections, flip):
     route = []
     for s in range(sections - 1):
         for block in range(2 * CHIPS):
             for half in range(2):
-                route.append((flat(s, *owner(block, half)), flat(s + 1, block, half)))
+                route.append((flat(s, *owner(block, half ^ flip)), flat(s + 1, block, half)))
     return lax.ppermute(array, AXES, route)
 
 
@@ -139,9 +139,13 @@
         mine, theirs, gains, w, down, x_out, product, small = refs
         x = replicas(mine[...], theirs[...])
     else:
-        arrived, mine, theirs, gains, w, down, x_out, product, small = refs
+        near, far, mine, theirs, gains, w, down, x_out, product, small = refs
         given = replicas(mine[tick - 1], theirs[tick - 1])
-        x = jnp.where(lax.axis_index("section") == 0, given, arrived[...])
+        first = lax.axis_index("dp") == 0
+        arrived = jnp.concatenate(
+            [jnp.where(first, near[...], far[...]), jnp.where(first, far[...], near[...])], axis=1
+        )
+        x = jnp.where(lax.axis_index("section") == 0, given, arrived)
     x_out[...] = x
     rows, feats = x.shape
     wide = x.astype(F32)
@@ -208,7 +212,11 @@
             )
         else:
             given = arrived[...]
-        kept = jnp.where(first_core(), output[...], jnp.zeros(output.shape, BF))
+        zeros = jnp.zeros(output.shape, BF)
+        kept = jnp.concatenate(
+            [jnp.where(first_core(), output[...], zeros), jnp.where(first_core(), zeros, output[...])],
+            axis=1,
+        )
         grad = jnp.where(lax.axis_index("section") == sections - 1, kept, given)
         grad_out[...] = grad
         out[:, at + width + LANES :] = other_half(grad)
@@ -256,7 +264,7 @@
         parcel[j, :, 2 * width : 2 * width + LANES] = halves
 
 
-def output_kernel(start, got, up, gain_w, gain_low, out, mixed, stats):
+def output_kernel(start, got, up, gain_w, gain_low, out, mixed, stats, *rest):
     rows, width = mixed.shape
     feats = 2 * width
     total = got[0, :, :width].astype(F32)
@@ -289,17 +297,13 @@
     low = between(inv * low, LOW, GRAD)
     mixed[...] = total
     stats[...] = jnp.where(at == 0, mean, jnp.where(at == 1, inv, low))
-    out[:, :width] = (x + total + dot(low.astype(BF), up[...])).astype(BF)
+    out[...] = (x + total + dot(low.astype(BF), up[...])).astype(BF)
     if not start:
-        out[:, width : width + LANES] = split(values)
+        (out,) = rest
+        out[:, :LANES] = split(values)
         for j in range(CHIPS):
-            at = width + LANES + j * width
+            at = LANES + j * width
             out[:, at : at + width] = got[j, :, feats + LANES :]
-
-
-def whole_kernel(mine, theirs, output):
-    width = output.shape[1] // 2
-    output[...] = both_halves(mine[:, :width], theirs[:, :width])
 
 
 def rank_grads(sums):
@@ -314,8 +318,7 @@
     rows, feats = x.shape
     width = feats * 2 * CHIPS
     half = feats // 2
-    ends = slice(half, half + LANES)
-    values = join(mine[:, ends]) + join(theirs[:, ends])
+    values = join(mine[:, :LANES]) + join(theirs[:, :LANES])
     sums[...] = values
     low_grad = rank_grads(values)
     low = between(stats[...], LOW, GRAD)
@@ -326,7 +329,7 @@
     grad_norm = dot(low_grad, down[...], precision=HIGHEST)
     here = jnp.zeros((rows, feats), F32)
     for j in range(CHIPS):
-        at = half + LANES + j * half
+        at = LANES + j * half
         grad = both_halves(mine[:, at : at + half], theirs[:, at : at + half])
         grad_norm = grad_norm + dot_t(grad, w[:, j * feats : (j + 1) * feats])
         here = here + jnp.where(own_block() == j, grad.astype(F32), 0.0)
@@ -349,10 +352,14 @@
     acc_up[...] = up[LOW : LOW + rank]
 
 
-def last_kernel(sections, arrived, output, up, stats, acc_up, after, out, up_out):
+def last_kernel(sections, arrived, output, up, stats, acc_up, acc_down, out, part):
     rows, feats = arrived.shape
     rank = up.shape[0]
-    kept = jnp.where(lax.axis_index("dp") == 0, output[...], jnp.zeros(output.shape, BF))
+    first = lax.axis_index("dp") == 0
+    zeros = jnp.zeros(output.shape, BF)
+    kept = jnp.concatenate(
+        [jnp.where(first, output[...], zeros), jnp.where(first, zeros, output[...])], axis=1
+    )
     grad = jnp.where(lax.axis_index("section") == sections - 1, kept, arrived[...])
     turned = dot_t(up[...], grad)
     turned = jnp.concatenate([turned, jnp.zeros((rank, LANES - rows), F32)], axis=1)
@@ -361,10 +368,13 @@
     for j in range(4 * CHIPS):
         out[j] = parcel
     low = t_dot(stats[...].astype(BF), grad)
-    up_out[...] = low[LOW : LOW + rank].astype(BF)
-
-
-def finish_kernel(got, x, stats, gains, mine, theirs, up_mine, up_theirs, down_out, up_out):
+    part[:rank] = low[LOW : LOW + rank].astype(BF)
+    high = acc_down[...].astype(BF)
+    part[rank : 2 * rank] = high
+    part[2 * rank :] = (acc_down[...] - high.astype(F32)).astype(BF)
+
+
+def finish_kernel(got, x, stats, gains, mine, theirs, down_out, up_out):
     rows = x.shape[0]
     turned = got[0, :, : 2 * LANES].astype(F32)
     for j in range(1, 4 * CHIPS):
@@ -372,12 +382,15 @@
     low_grad = turned[:, :LANES] + turned[:, LANES:]
     u = normed(x[...], stats[...]) * gains[...]
     u = jnp.concatenate([u, jnp.zeros((LANES - rows, u.shape[1]), F32)])
-    total = mine[...] + theirs[...] + dot(low_grad, u, precision=HIGHEST)
+    rank = up_out.shape[0]
+    total = dot(low_grad, u, precision=HIGHEST)
+    for part in (mine, theirs):
+        total = total + part[rank : 2 * rank].astype(F32) + part[2 * rank :].astype(F32)
     down_out[...] = (total / rows).astype(BF)
     tensor = lax.axis_index("tensor")
     at = 4 * (tensor % CHIPS) + tensor // CHIPS
     total = jnp.concatenate([got[at, :, 2 * LANES :], got[at + 2, :, 2 * LANES :]], axis=1)
-    total = total.astype(F32) + up_mine[...].astype(F32) + up_theirs[...].astype(F32)
+    total = total.astype(F32) + mine[:rank].astype(F32) + theirs[:rank].astype(F32)
     up_out[...] = (total / rows).astype(BF)
 
 
@@ -387,7 +400,11 @@
 
 def last_home(array, sections):
     s = sections - 1
-    route = [(flat(s, *owner(block, 0)), flat(s, block, 0)) for block in range(2 * CHIPS)]
+    route = [
+        (flat(s, *owner(block, half)), flat(s, block, half))
+        for block in range(2 * CHIPS)
+        for half in range(2)
+    ]
     return lax.ppermute(array, AXES, route)
 
 
@@ -435,7 +452,7 @@
             x, product, small = call(
                 functools.partial(forward_kernel, False, tick),
                 out,
-                arrived,
+                *arrived,
                 chosen,
                 chosen_theirs,
                 gains,
@@ -475,20 +492,19 @@
             )
             grads.append(grad)
         got = over_chips(parcel)
-        columns = width + (0 if start else LANES + CHIPS * width)
-        out = [shape(rows, columns, dtype=BF), shape(rows, width), values]
+        out = [shape(rows, width, dtype=BF), shape(rows, width), values]
         kernel = functools.partial(output_kernel, start)
         if start:
             up = shape(LANES, width, dtype=BF)
-            up, gain_w, gain_low, own, mixed, stats = call(
+            up, gain_w, gain_low, output, mixed, stats = call(
                 kernel, [up, shape(2 * CHIPS, width), shape(2 * CHIPS, LANES)] + out, got
             )
         else:
-            own, mixed, stats = call(kernel, out, got, up, gain_w, gain_low)
-        other = swap_cores(own)
-        output = call(whole_kernel, block, own, other)
+            out.append(shape(rows, LANES + CHIPS * width, dtype=BF))
+            output, mixed, stats, own = call(kernel, out, got, up, gain_w, gain_low)
+            other = swap_cores(own)
         if tick < TICKS - 1:
-            arrived = to_next(output, sections)
+            arrived = [to_next(output, sections, flip) for flip in range(2)]
         if start:
             chosen, grads_out = call(
                 prepare_kernel,
@@ -535,19 +551,18 @@
         *all_sums,
         *grads,
     )
-    acc_other = lax.ppermute(acc_down, "dp", [(0, 1), (1, 0)])
-    parcel, up_part = call(
+    parcel, part = call(
         functools.partial(last_kernel, sections),
         [
             shape(4 * CHIPS, rank, 2 * LANES + feats // 2, dtype=BF),
-            shape(rank, feats, dtype=BF),
+            shape(3 * rank, feats, dtype=BF),
         ],
         grad_arrived,
         last_home(output, sections),
         adapter_up_map[0],
         stats,
         acc_up,
-        acc_other,
+        acc_down,
     )
     got = lax.all_to_all(parcel, ("tensor", "dp"), 0, 0)
     grad_down, grad_up = call(
@@ -557,10 +572,8 @@
         x,
         stats,
         gains,
-        acc_down,
-        acc_other,
-        up_part,
-        lax.ppermute(up_part, "dp", [(0, 1), (1, 0)]),
+        part,
+        lax.ppermute(part, "dp", [(0, 1), (1, 0)]),
     )
     return grad_down.T[None], grad_up[None]
 

time: 200 us -> 204 us (1.020)
  the two profiles are of different devices: /device:TPU:225 before, /device:TPU:120 now
where the time goes in v7:
time: 204 us; the launch traced here: 203 us
  blocking collectives  69 us (34%)
  starting transfers between devices  66 us (32%)
  waiting for transfers between devices  42 us (21%)
  Pallas kernels  20.1 us (10%)
  local copies, waits for them, and re-layouts  4.67 us (2%)
    all_to_all x4, blocking collectives, over_chips(): return lax.all_to_all(array, 'tensor', 0, 0, axis_index_groups=groups)  69 us
    ppermute x6, starting transfers between devices, to_next(): return lax.ppermute(array, AXES, route)  35 us
    pallas_call x24, Pallas kernels, call(): pl.pallas_call(kernel, out_shape=out, in_specs=[pl.BlockSpec(memory_space...  20.1 us
    ppermute x7, starting transfers between devices, swap_cores(): return lax.ppermute(array, 'tensor', [(i, i ^ 1) for i in range(2 * CHIPS)])  13.4 us
    ppermute x7, waiting for transfers between devices, swap_cores(): return lax.ppermute(array, 'tensor', [(i, i ^ 1) for i in range(2 * CHIPS)])  11.9 us
    ppermute x6, waiting for transfers between devices, to_next(): return lax.ppermute(array, AXES, route)  11.3 us
    ppermute x1, waiting for transfers between devices, to_same(): lax.ppermute(array, 'section', [(s, s - 1) for s in range(1, sections)])  7.43 us
    ppermute x1, waiting for transfers between devices, on_device(): lax.ppermute(part, 'dp', [(0, 1), (1, 0)])  6.5 us
  transfers between devices with their start and end apart: 22, of which 14 were waited for; matrix products, arithmetic and copies ran while one was open for 0% of the time, Pallas kernels for 3%

profile of v7, /device:TPU:120, one launch (start us, length us, event | category | flops | bytes accessed | tf_op | source)
XLA Modules:
  0.0 202.8 jit_solution(14905005789174055915)
XLA Ops:
  0.6 2.7 %collective-permute-start = (bf16[48,768]{1,0:T(8,128)(2,1)}, bf16[48,768]{1,0:T(8,128)(2,1)S(1)}, u32[]{:S(2)}, u32[]{:S(2)}) collective-permute-start(bf16[48,768]{1,0:T(8,128)(2,1)} %bitcast.23), channel_id=1, source_target_pairs={{0,1},{1,0},{2,3},{3,2},{4,5},{5,4},{6,7},{7,6},{8,9},{9,8},{10,11... | collective-permute-start | bytes 221192 | tf_op jit(solution)/shard_map/ppermute | solution.py:431
  3.3 2.3 %copy-done = bf16[1,768,3072]{2,1,0:T(8,128)(2,1)S(1)} copy-done((bf16[1,768,3072]{2,1,0:T(8,128)(2,1)S(1)}, bf16[1,768,3072]{2,1,0:T(8,128)(2,1)}, u32[]{:S(2)}) %copy-start) | copy-done | bytes 4718616
  9.6 1.9 collective-permute-start.1
  13.7 16.9 %all_to_all.25.got = bf16[4,112,896]{2,1,0:T(8,128)(2,1)S(1)} all-to-all(bf16[4,112,896]{2,1,0:T(8,128)(2,1)S(1)} %shard_map.98), channel_id=1, replica_groups={{0,4,8,12},{2,6,10,14},{1,5,9,13},{3,7,11,15},{16,20,24,28},{18,22,26,3..., dimensions={0} | all-to-all | bytes 1605632 | tf_op jit(solution)/shard_map/all_to_all | solution.py:59
  32.5 6.0 %collective-permute-start.3 = (bf16[96,384]{1,0:T(8,128)(2,1)S(1)}, bf16[96,384]{1,0:T(8,128)(2,1)S(1)}, u32[]{:S(2)}, u32[]{:S(2)}) collective-permute-start(bf16[96,384]{1,0:T(8,128)(2,1)S(1)} %get-tuple-element.60.after.refs_1_), channel_id=1, source_target_pairs={{2,16},{0,17},{6,18},{4,19},{10,20},{8,21},{14,22},{12,23},{3,24},... | collective-permute-start | bytes 221192 | tf_op jit(solution)/shard_map/ppermute | solution.py:50
  38.5 5.2 %collective-permute-start.2 = (bf16[96,384]{1,0:T(8,128)(2,1)S(1)}, bf16[96,384]{1,0:T(8,128)(2,1)S(1)}, u32[]{:S(2)}, u32[]{:S(2)}) collective-permute-start(bf16[96,384]{1,0:T(8,128)(2,1)S(1)} %get-tuple-element.60.after.refs_1_), channel_id=1, source_target_pairs={{0,16},{2,17},{4,18},{6,19},{8,20},{10,21},{12,22},{14,23},{1,24},... | collective-permute-start | bytes 221192 | tf_op jit(solution)/shard_map/ppermute | solution.py:50
  43.6 1.9 collective-permute-start.5
  47.3 4.9 %collective-permute-done.5.refs_0_ = bf16[48,768]{1,0:T(8,128)(2,1)S(1)} collective-permute-done((bf16[48,768]{1,0:T(8,128)(2,1)S(1)}, bf16[48,768]{1,0:T(8,128)(2,1)S(1)}, u32[]{:S(2)}, u32[]{:S(2)}) %collective-permute-start.5) | collective-permute-done | bytes 73760 | tf_op jit(solution)/shard_map/ppermute | solution.py:41
  52.4 1.9 collective-permute-start.6
  56.6 17.4 %all_to_all.26.got = bf16[4,96,1280]{2,1,0:T(8,128)(2,1)S(1)} all-to-all(bf16[4,96,1280]{2,1,0:T(8,128)(2,1)S(1)} %get-tuple-element.71), channel_id=1, replica_groups={{0,4,8,12},{2,6,10,14},{1,5,9,13},{3,7,11,15},{16,20,24,28},{18,22,26,3..., dimensions={0} | all-to-all | bytes 1966080 | tf_op jit(solution)/shard_map/all_to_all | solution.py:59
  74.6 1.9 collective-permute-start.9
  78.1 1.8 shard_map.106
  79.9 1.9 collective-permute-start.10
  81.9 9.7 %collective-permute-start.8 = (bf16[96,384]{1,0:T(8,128)(2,1)S(1)}, bf16[96,384]{1,0:T(8,128)(2,1)S(1)}, u32[]{:S(2)}, u32[]{:S(2)}) collective-permute-start(bf16[96,384]{1,0:T(8,128)(2,1)S(1)} %get-tuple-element.73.refs_1_), channel_id=1, source_target_pairs={{2,16},{0,17},{6,18},{4,19},{10,20},{8,21},{14,22},{12,23},{3,24},... | collective-permute-start | bytes 221192 | tf_op jit(solution)/shard_map/ppermute | solution.py:50
  91.5 1.9 collective-permute-start.7
  93.6 5.6 %collective-permute-done.7.refs_0_ = bf16[96,384]{1,0:T(8,128)(2,1)S(1)} collective-permute-done((bf16[96,384]{1,0:T(8,128)(2,1)S(1)}, bf16[96,384]{1,0:T(8,128)(2,1)S(1)}, u32[]{:S(2)}, u32[]{:S(2)}) %collective-permute-start.7) | collective-permute-done | bytes 73760 | tf_op jit(solution)/shard_map/ppermute | solution.py:50
  100.7 1.9 collective-permute-start.11
  104.9 17.4 %all_to_all.27.got = bf16[4,96,1280]{2,1,0:T(8,128)(2,1)S(1)} all-to-all(bf16[4,96,1280]{2,1,0:T(8,128)(2,1)S(1)} %get-tuple-element.83), channel_id=1, replica_groups={{0,4,8,12},{2,6,10,14},{1,5,9,13},{3,7,11,15},{16,20,24,28},{18,22,26,3..., dimensions={0} | all-to-all | bytes 1966080 | tf_op jit(solution)/shard_map/all_to_all | solution.py:59
  122.9 1.9 collective-permute-start.14
  128.2 1.9 collective-permute-start.15
  130.1 9.7 %collective-permute-start.13 = (bf16[96,384]{1,0:T(8,128)(2,1)S(1)}, bf16[96,384]{1,0:T(8,128)(2,1)S(1)}, u32[]{:S(2)}, u32[]{:S(2)}) collective-permute-start(bf16[96,384]{1,0:T(8,128)(2,1)S(1)} %get-tuple-element.84.refs_1_), channel_id=1, source_target_pairs={{2,16},{0,17},{6,18},{4,19},{10,20},{8,21},{14,22},{12,23},{3,24},... | collective-permute-start | bytes 221192 | tf_op jit(solution)/shard_map/ppermute | solution.py:50
  139.8 2.6 %collective-permute-start.12 = (bf16[96,384]{1,0:T(8,128)(2,1)S(1)}, bf16[96,384]{1,0:T(8,128)(2,1)S(1)}, u32[]{:S(2)}, u32[]{:S(2)}) collective-permute-start(bf16[96,384]{1,0:T(8,128)(2,1)S(1)} %get-tuple-element.84.refs_1_), channel_id=1, source_target_pairs={{0,16},{2,17},{4,18},{6,19},{8,20},{10,21},{12,22},{14,23},{1,24},... | collective-permute-start | bytes 221192 | tf_op jit(solution)/shard_map/ppermute | solution.py:50
  142.4 5.1 %collective-permute-done.12.refs_0_ = bf16[96,384]{1,0:T(8,128)(2,1)S(1)} collective-permute-done((bf16[96,384]{1,0:T(8,128)(2,1)S(1)}, bf16[96,384]{1,0:T(8,128)(2,1)S(1)}, u32[]{:S(2)}, u32[]{:S(2)}) %collective-permute-start.12) | collective-permute-done | bytes 73760 | tf_op jit(solution)/shard_map/ppermute | solution.py:50
  149.0 1.9 collective-permute-start.16
  153.2 17.4 %all_to_all.28.got = bf16[4,96,1280]{2,1,0:T(8,128)(2,1)S(1)} all-to-all(bf16[4,96,1280]{2,1,0:T(8,128)(2,1)S(1)} %get-tuple-element.94), channel_id=1, replica_groups={{0,4,8,12},{2,6,10,14},{1,5,9,13},{3,7,11,15},{16,20,24,28},{18,22,26,3..., dimensions={0} | all-to-all | bytes 1966080 | tf_op jit(solution)/shard_map/all_to_all | solution.py:59
  171.7 1.9 collective-permute-start.17
  175.2 1.8 shard_map.115
  177.0 1.9 collective-permute-start.18
  181.0 7.4 %collective-permute-done.18.arrived = bf16[96,768]{1,0:T(8,128)(2,1)S(1)} collective-permute-done((bf16[96,768]{1,0:T(8,128)(2,1)S(1)}, bf16[96,768]{1,0:T(8,128)(2,1)S(1)}, u32[]{:S(2)}, u32[]{:S(2)}) %collective-permute-start.18) | collective-permute-done | bytes 147488 | tf_op jit(solution)/shard_map/ppermute | solution.py:398
  189.4 3.9 %all-to-all-start.4 = ((bf16[16,16,640]{2,1,0:T(8,128)(2,1)}), bf16[16,16,640]{2,1,0:T(8,128)(2,1)S(1)}, u32[]{:S(2)}, u32[]{:S(2)}) async-start(bf16[16,16,640]{2,1,0:T(8,128)(2,1)} %get-tuple-element.108), calls=%async_computation.4 | async-start | bytes 655360 | tf_op jit(solution)/shard_map/all_to_all | solution.py:567
  193.3 2.0 collective-permute-start.20
  195.3 6.5 %collective-permute-done.20.theirs = bf16[48,768]{1,0:T(8,128)(2,1)S(1)} collective-permute-done((bf16[48,768]{1,0:T(8,128)(2,1)S(1)}, bf16[48,768]{1,0:T(8,128)(2,1)S(1)}, u32[]{:S(2)}, u32[]{:S(2)}) %collective-permute-start.20) | collective-permute-done | bytes 73760 | tf_op jit(solution)/shard_map/ppermute | solution.py:576
  (63 shorter events, 32.6 us)
Async XLA Ops:
  0.6 7.4 %collective-permute-start = (bf16[48,768]{1,0:T(8,128)(2,1)}, bf16[48,768]{1,0:T(8,128)(2,1)S(1)}, u32[]{:S(2)}, u32[]{:S(2)}) collective-permute-start(bf16[48,768]{1,0:T(8,128)(2,1)} %bitcast.23), channel_id=1, source_target_pairs={{0,1},{1,0},{2,3},{3,2},{4,5},{5,4},{6,7},{7,6},{8,9},{9,8},{10,11... | collective-permute-start | bytes 221192 | tf_op jit(solution)/shard_map/ppermute | solution.py:431
  3.3 2.3 %copy-start = (bf16[1,768,3072]{2,1,0:T(8,128)(2,1)S(1)}, bf16[1,768,3072]{2,1,0:T(8,128)(2,1)}, u32[]{:S(2)}) copy-start(bf16[1,768,3072]{2,1,0:T(8,128)(2,1)} %param.9) | copy-start | bytes 14155780
  6.3 0.9 copy-start.3
  7.2 0.7 copy-start.7
  7.9 1.6 copy-start.4
  7.9 38.0 %slice-start = ((s8[4718592]{0:T(1024)(128)(4,1)}), s8[4194304]{0:T(1024)(128)(4,1)S(1)}, s32[]{:S(2)}) async-start(s8[4718592]{0:T(1024)(128)(4,1)} %bitcast.15), calls=%async_computation.5 | async-start | bytes 8388608
  8.0 23.2 %copy-start.5 = (bf16[1,1,2,48,768]{4,3,2,1,0:T(8,128)(2,1)S(1)}, bf16[1,1,2,48,768]{4,3,2,1,0:T(8,128)(2,1)}, u32[]{:S(2)}) copy-start(bf16[1,1,2,48,768]{4,3,2,1,0:T(8,128)(2,1)} %param.13) | copy-start | bytes 442372
  8.0 23.2 %copy-start.6 = (bf16[1,48,768]{2,1,0:T(8,128)(2,1)S(1)}, bf16[1,48,768]{2,1,0:T(8,128)(2,1)}, u32[]{:S(2)}) copy-start(bf16[1,48,768]{2,1,0:T(8,128)(2,1)} %param.15) | copy-start | bytes 221188
  8.0 23.2 %copy-start.8 = (s32[1,1,4]{2,1,0:T(1,128)S(1)}, s32[1,1,4]{2,1,0:T(1,128)}, u32[]{:S(2)}) copy-start(s32[1,1,4]{2,1,0:T(1,128)} %param.16) | copy-start | bytes 52
  8.0 38.0 %slice-start.1 = ((s8[4718592]{0:T(1024)(128)(4,1)}), s8[524288]{0:T(1024)(128)(4,1)S(1)}, s32[]{:S(2)}) async-start(s8[4718592]{0:T(1024)(128)(4,1)} %bitcast.15), calls=%async_computation.6 | async-start | bytes 1048576
  9.6 3.7 %collective-permute-start.1 = (bf16[112,2048]{1,0:T(8,128)(2,1)S(1)}, bf16[112,2048]{1,0:T(8,128)(2,1)S(1)}, u32[]{:S(2)}, u32[]{:S(2)}) collective-permute-start(bf16[112,2048]{1,0:T(8,128)(2,1)S(1)} %shard_map.97), channel_id=1, source_target_pairs={{0,2},{2,0},{4,6},{6,4},{8,10},{10,8},{12,14},{14,12},{1,3},{3,1},... | collective-permute-start | bytes 1376264 | tf_op jit(solution)/shard_map/ppermute | solution.py:54
  31.8 14.2 %collective-permute-start.4 = (bf16[3,48,768]{2,1,0:T(8,128)(2,1)S(1)}, bf16[3,48,768]{2,1,0:T(8,128)(2,1)S(1)}, u32[]{:S(2)}, u32[]{:S(2)}) collective-permute-start(bf16[3,48,768]{2,1,0:T(8,128)(2,1)S(1)} %get-tuple-element.61.refs_2_), channel_id=1, source_target_pairs={{0,1},{1,0},{2,3},{3,2},{4,5},{5,4},{6,7},{7,6},{8,9},{9,8},{10,11... | collective-permute-start | bytes 663560 | tf_op jit(solution)/shard_map/ppermute | solution.py:518
  32.5 13.1 %collective-permute-start.3 = (bf16[96,384]{1,0:T(8,128)(2,1)S(1)}, bf16[96,384]{1,0:T(8,128)(2,1)S(1)}, u32[]{:S(2)}, u32[]{:S(2)}) collective-permute-start(bf16[96,384]{1,0:T(8,128)(2,1)S(1)} %get-tuple-element.60.after.refs_1_), channel_id=1, source_target_pairs={{2,16},{0,17},{6,18},{4,19},{10,20},{8,21},{14,22},{12,23},{3,24},... | collective-permute-start | bytes 221192 | tf_op jit(solution)/shard_map/ppermute | solution.py:50
  38.5 7.5 %collective-permute-start.2 = (bf16[96,384]{1,0:T(8,128)(2,1)S(1)}, bf16[96,384]{1,0:T(8,128)(2,1)S(1)}, u32[]{:S(2)}, u32[]{:S(2)}) collective-permute-start(bf16[96,384]{1,0:T(8,128)(2,1)S(1)} %get-tuple-element.60.after.refs_1_), channel_id=1, source_target_pairs={{0,16},{2,17},{4,18},{6,19},{8,20},{10,21},{12,22},{14,23},{1,24},... | collective-permute-start | bytes 221192 | tf_op jit(solution)/shard_map/ppermute | solution.py:50
  43.6 8.7 %collective-permute-start.5 = (bf16[48,768]{1,0:T(8,128)(2,1)S(1)}, bf16[48,768]{1,0:T(8,128)(2,1)S(1)}, u32[]{:S(2)}, u32[]{:S(2)}) collective-permute-start(bf16[48,768]{1,0:T(8,128)(2,1)S(1)} %get-tuple-element.65), channel_id=1, source_target_pairs={{0,0},{1,2},{2,4},{3,6},{4,8},{5,10},{6,12},{7,14},{8,1},{9,3},{10... | collective-permute-start | bytes 221192 | tf_op jit(solution)/shard_map/ppermute | solution.py:41
  52.4 3.7 %collective-permute-start.6 = (bf16[96,2432]{1,0:T(8,128)(2,1)S(1)}, bf16[96,2432]{1,0:T(8,128)(2,1)S(1)}, u32[]{:S(2)}, u32[]{:S(2)}) collective-permute-start(bf16[96,2432]{1,0:T(8,128)(2,1)S(1)} %get-tuple-element.66), channel_id=1, source_target_pairs={{0,2},{2,0},{4,6},{6,4},{8,10},{10,8},{12,14},{14,12},{1,3},{3,1},... | collective-permute-start | bytes 1400840 | tf_op jit(solution)/shard_map/ppermute | solution.py:54
  74.6 3.5 %collective-permute-start.9 = (bf16[96,1664]{1,0:T(8,128)(2,1)S(1)}, bf16[96,1664]{1,0:T(8,128)(2,1)S(1)}, u32[]{:S(2)}, u32[]{:S(2)}) collective-permute-start(bf16[96,1664]{1,0:T(8,128)(2,1)S(1)} %get-tuple-element.77.mine), channel_id=1, source_target_pairs={{0,2},{2,0},{4,6},{6,4},{8,10},{10,8},{12,14},{14,12},{1,3},{3,1},... | collective-permute-start | bytes 958472 | tf_op jit(solution)/shard_map/ppermute | solution.py:54
  79.9 20.6 %collective-permute-start.10 = (bf16[96,768]{1,0:T(8,128)(2,1)S(1)}, bf16[96,768]{1,0:T(8,128)(2,1)S(1)}, u32[]{:S(2)}, u32[]{:S(2)}) collective-permute-start(bf16[96,768]{1,0:T(8,128)(2,1)S(1)} %get-tuple-element.79), channel_id=1, source_target_pairs={{16,0},{17,2},{18,4},{19,6},{20,8},{21,10},{22,12},{23,14},{24,1},... | collective-permute-start | bytes 442376 | tf_op jit(solution)/shard_map/ppermute | solution.py:41
  81.9 11.7 %collective-permute-start.8 = (bf16[96,384]{1,0:T(8,128)(2,1)S(1)}, bf16[96,384]{1,0:T(8,128)(2,1)S(1)}, u32[]{:S(2)}, u32[]{:S(2)}) collective-permute-start(bf16[96,384]{1,0:T(8,128)(2,1)S(1)} %get-tuple-element.73.refs_1_), channel_id=1, source_target_pairs={{2,16},{0,17},{6,18},{4,19},{10,20},{8,21},{14,22},{12,23},{3,24},... | collective-permute-start | bytes 221192 | tf_op jit(solution)/shard_map/ppermute | solution.py:50
  91.5 7.7 %collective-permute-start.7 = (bf16[96,384]{1,0:T(8,128)(2,1)S(1)}, bf16[96,384]{1,0:T(8,128)(2,1)S(1)}, u32[]{:S(2)}, u32[]{:S(2)}) collective-permute-start(bf16[96,384]{1,0:T(8,128)(2,1)S(1)} %get-tuple-element.73.refs_1_), channel_id=1, source_target_pairs={{0,16},{2,17},{4,18},{6,19},{8,20},{10,21},{12,22},{14,23},{1,24},... | collective-permute-start | bytes 221192 | tf_op jit(solution)/shard_map/ppermute | solution.py:50
  100.7 3.7 %collective-permute-start.11 = (bf16[96,2432]{1,0:T(8,128)(2,1)S(1)}, bf16[96,2432]{1,0:T(8,128)(2,1)S(1)}, u32[]{:S(2)}, u32[]{:S(2)}) collective-permute-start(bf16[96,2432]{1,0:T(8,128)(2,1)S(1)} %get-tuple-element.80), channel_id=1, source_target_pairs={{0,2},{2,0},{4,6},{6,4},{8,10},{10,8},{12,14},{14,12},{1,3},{3,1},... | collective-permute-start | bytes 1400840 | tf_op jit(solution)/shard_map/ppermute | solution.py:54
  122.9 3.5 %collective-permute-start.14 = (bf16[96,1664]{1,0:T(8,128)(2,1)S(1)}, bf16[96,1664]{1,0:T(8,128)(2,1)S(1)}, u32[]{:S(2)}, u32[]{:S(2)}) collective-permute-start(bf16[96,1664]{1,0:T(8,128)(2,1)S(1)} %get-tuple-element.88.mine), channel_id=1, source_target_pairs={{0,2},{2,0},{4,6},{6,4},{8,10},{10,8},{12,14},{14,12},{1,3},{3,1},... | collective-permute-start | bytes 958472 | tf_op jit(solution)/shard_map/ppermute | solution.py:54
  128.2 20.6 %collective-permute-start.15 = (bf16[96,768]{1,0:T(8,128)(2,1)S(1)}, bf16[96,768]{1,0:T(8,128)(2,1)S(1)}, u32[]{:S(2)}, u32[]{:S(2)}) collective-permute-start(bf16[96,768]{1,0:T(8,128)(2,1)S(1)} %get-tuple-element.90), channel_id=1, source_target_pairs={{16,0},{17,2},{18,4},{19,6},{20,8},{21,10},{22,12},{23,14},{24,1},... | collective-permute-start | bytes 442376 | tf_op jit(solution)/shard_map/ppermute | solution.py:41
  130.1 12.3 %collective-permute-start.13 = (bf16[96,384]{1,0:T(8,128)(2,1)S(1)}, bf16[96,384]{1,0:T(8,128)(2,1)S(1)}, u32[]{:S(2)}, u32[]{:S(2)}) collective-permute-start(bf16[96,384]{1,0:T(8,128)(2,1)S(1)} %get-tuple-element.84.refs_1_), channel_id=1, source_target_pairs={{2,16},{0,17},{6,18},{4,19},{10,20},{8,21},{14,22},{12,23},{3,24},... | collective-permute-start | bytes 221192 | tf_op jit(solution)/shard_map/ppermute | solution.py:50
  139.8 7.7 %collective-permute-start.12 = (bf16[96,384]{1,0:T(8,128)(2,1)S(1)}, bf16[96,384]{1,0:T(8,128)(2,1)S(1)}, u32[]{:S(2)}, u32[]{:S(2)}) collective-permute-start(bf16[96,384]{1,0:T(8,128)(2,1)S(1)} %get-tuple-element.84.refs_1_), channel_id=1, source_target_pairs={{0,16},{2,17},{4,18},{6,19},{8,20},{10,21},{12,22},{14,23},{1,24},... | collective-permute-start | bytes 221192 | tf_op jit(solution)/shard_map/ppermute | solution.py:50
  149.0 3.7 %collective-permute-start.16 = (bf16[96,2432]{1,0:T(8,128)(2,1)S(1)}, bf16[96,2432]{1,0:T(8,128)(2,1)S(1)}, u32[]{:S(2)}, u32[]{:S(2)}) collective-permute-start(bf16[96,2432]{1,0:T(8,128)(2,1)S(1)} %get-tuple-element.91), channel_id=1, source_target_pairs={{0,2},{2,0},{4,6},{6,4},{8,10},{10,8},{12,14},{14,12},{1,3},{3,1},... | collective-permute-start | bytes 1400840 | tf_op jit(solution)/shard_map/ppermute | solution.py:54
  170.6 31.3 %copy-start.2 = (f32[1,768]{1,0:T(1,128)S(1)}, f32[1,768]{1,0:T(1,128)}, u32[]{:S(2)}) copy-start(f32[1,768]{1,0:T(1,128)} %gains.11) | copy-start | bytes 9220
  171.7 3.5 %collective-permute-start.17 = (bf16[96,1664]{1,0:T(8,128)(2,1)S(1)}, bf16[96,1664]{1,0:T(8,128)(2,1)S(1)}, u32[]{:S(2)}, u32[]{:S(2)}) collective-permute-start(bf16[96,1664]{1,0:T(8,128)(2,1)S(1)} %get-tuple-element.95.mine), channel_id=1, source_target_pairs={{0,2},{2,0},{4,6},{6,4},{8,10},{10,8},{12,14},{14,12},{1,3},{3,1},... | collective-permute-start | bytes 958472 | tf_op jit(solution)/shard_map/ppermute | solution.py:54
  177.0 11.4 %collective-permute-start.18 = (bf16[96,768]{1,0:T(8,128)(2,1)S(1)}, bf16[96,768]{1,0:T(8,128)(2,1)S(1)}, u32[]{:S(2)}, u32[]{:S(2)}) collective-permute-start(bf16[96,768]{1,0:T(8,128)(2,1)S(1)} %get-tuple-element.97.after), channel_id=1, source_target_pairs={{16,0},{32,16},{48,32},{64,48},{80,64},{96,80},{112,96},{128,112},... | collective-permute-start | bytes 442376 | tf_op jit(solution)/shard_map/ppermute | solution.py:398
  179.0 2.0 %collective-permute-start.19 = (bf16[96,384]{1,0:T(8,128)(2,1)S(1)}, bf16[96,384]{1,0:T(8,128)(2,1)S(1)}, u32[]{:S(2)}, u32[]{:S(2)}) collective-permute-start(bf16[96,384]{1,0:T(8,128)(2,1)S(1)} %get-tuple-element.98), channel_id=1, source_target_pairs={{496,496},{498,497},{500,498},{502,499},{504,500},{506,501},{508,5... | collective-permute-start | bytes 221192 | tf_op jit(solution)/shard_map/ppermute | solution.py:408
  189.4 12.4 %all-to-all-start.4 = ((bf16[16,16,640]{2,1,0:T(8,128)(2,1)}), bf16[16,16,640]{2,1,0:T(8,128)(2,1)S(1)}, u32[]{:S(2)}, u32[]{:S(2)}) async-start(bf16[16,16,640]{2,1,0:T(8,128)(2,1)} %get-tuple-element.108), calls=%async_computation.4 | async-start | bytes 655360 | tf_op jit(solution)/shard_map/all_to_all | solution.py:567
  193.3 8.5 %collective-permute-start.20 = (bf16[48,768]{1,0:T(8,128)(2,1)S(1)}, bf16[48,768]{1,0:T(8,128)(2,1)S(1)}, u32[]{:S(2)}, u32[]{:S(2)}) collective-permute-start(bf16[48,768]{1,0:T(8,128)(2,1)S(1)} %get-tuple-element.109.mine), channel_id=1, source_target_pairs={{0,1},{1,0},{2,3},{3,2},{4,5},{5,4},{6,7},{7,6},{8,9},{9,8},{10,11... | collective-permute-start | bytes 221192 | tf_op jit(solution)/shard_map/ppermute | solution.py:576
  (1 other events, 0.7 us)

commit v8 on v6

--- a/solution.py
+++ b/solution.py
@@ -27,8 +27,25 @@
     return (section * 2 * CHIPS + tensor) * 2 + dp
 
 
+OWNER = (0, 3, 1, 2, 2, 1, 3, 0)
+
+
 def owner(block, core):
-    return 2 * (block % CHIPS) + core, block // CHIPS
+    return 2 * OWNER[block] + core, block // CHIPS
+
+
+def look_up(table, at):
+    return sum(jnp.where(at == i, value, 0) for i, value in enumerate(table))
+
+
+def owner_chip(block):
+    mine = block // CHIPS == lax.axis_index("dp")
+    return jnp.where(mine, look_up(OWNER, block), -1)
+
+
+def block_of(chip):
+    half = lax.axis_index("dp")
+    return jnp.where(half == 0, OWNER[:CHIPS].index(chip), OWNER[CHIPS:].index(chip))
 
 
 def to_owner(array, sections, back):
@@ -108,11 +125,6 @@
 
 def shape(*dims, dtype=F32):
     return jax.ShapeDtypeStruct(dims, dtype)
-
-
-def own_block():
-    tensor = lax.axis_index("tensor")
-    return jnp.where(tensor // CHIPS == lax.axis_index("dp"), tensor % CHIPS, -1)
 
 
 def replicas(mine, theirs):
@@ -168,7 +180,8 @@
             tail = part[rows : rows + 2 * CHIPS] + part[rows + 2 * CHIPS :]
             high = tail.astype(BF).astype(F32)
             part = jnp.concatenate([part[:rows], high, tail - high])
-        product[j] = part.astype(BF)
+        slot = jnp.where(lax.axis_index("dp") == 0, OWNER[j], OWNER[CHIPS + j])
+        product[slot] = part.astype(BF)
 
 
 def first_core():
@@ -246,18 +259,21 @@
         for j in range(CHIPS):
             parcel[j, :, 2 * width + LANES :] = grad
     halves = split(values)
-    block = own_block()
+    tensor = lax.axis_index("tensor")
+    mine_at, theirs_at = owner_chip(tensor), owner_chip(tensor ^ 1)
     for j in range(CHIPS):
         total = own_half(product[j]).astype(F32)
         total = total + theirs[:, j * width : (j + 1) * width].astype(F32)
         parcel[j, :, :width] = total.astype(BF)
-        held = jnp.where(block == j, mine_x, jnp.where(block == (j ^ 1), theirs_x, 0.0).astype(BF))
+        held = jnp.where(theirs_at == j, theirs_x, jnp.zeros(theirs_x.shape, BF))
+        held = jnp.where(mine_at == j, mine_x, held)
         parcel[j, :, width : 2 * width] = held
         parcel[j, :, 2 * width : 2 * width + LANES] = halves
 
 
-def output_kernel(start, got, up, gain_w, gain_low, out, mixed, stats):
-    rows, width = mixed.shape
+def output_kernel(start, got, up, gain_w, gain_low, out, stats, *mixed):
+    rows = stats.shape[0]
+    width = gain_w.shape[1]
     feats = 2 * width
     total = got[0, :, :width].astype(F32)
     x = got[0, :, width:feats].astype(F32)
@@ -287,7 +303,8 @@
         low = low + off[:, j : j + 1] * gain_low[j : j + 1, :]
     total = inv * total
     low = between(inv * low, LOW, GRAD)
-    mixed[...] = total
+    for ref in mixed:
+        ref[...] = total
     stats[...] = jnp.where(at == 0, mean, jnp.where(at == 1, inv, low))
     out[:, :width] = (x + total + dot(low.astype(BF), up[...])).astype(BF)
     if not start:
@@ -325,11 +342,13 @@
     xhat = normed(x[...], stats[...])
     grad_norm = dot(low_grad, down[...], precision=HIGHEST)
     here = jnp.zeros((rows, feats), F32)
+    own_chip = owner_chip(lax.axis_index("tensor"))
     for j in range(CHIPS):
         at = half + LANES + j * half
         grad = both_halves(mine[:, at : at + half], theirs[:, at : at + half])
-        grad_norm = grad_norm + dot_t(grad, w[:, j * feats : (j + 1) * feats])
-        here = here + jnp.where(own_block() == j, grad.astype(F32), 0.0)
+        at = pl.multiple_of(block_of(j) * feats, LANES)
+        grad_norm = grad_norm + dot_t(grad, w[:, pl.ds(at, feats)])
+        here = here + jnp.where(own_chip == j, grad.astype(F32), 0.0)
     inv = pick(stats[...], 1, 2)
     grad_x = here + inv * (grad_norm * gains[...] - first / width - xhat * (second / width))
     grad_out[...] = grad_x.astype(BF)
@@ -375,7 +394,7 @@
     total = mine[...] + theirs[...] + dot(low_grad, u, precision=HIGHEST)
     down_out[...] = (total / rows).astype(BF)
     tensor = lax.axis_index("tensor")
-    at = 4 * (tensor % CHIPS) + tensor // CHIPS
+    at = 4 * look_up(OWNER, tensor) + tensor // CHIPS
     total = jnp.concatenate([got[at, :, 2 * LANES :], got[at + 2, :, 2 * LANES :]], axis=1)
     total = total.astype(F32) + up_mine[...].astype(F32) + up_theirs[...].astype(F32)
     up_out[...] = (total / rows).astype(BF)
@@ -476,15 +495,18 @@
             grads.append(grad)
         got = over_chips(parcel)
         columns = width + (0 if start else LANES + CHIPS * width)
-        out = [shape(rows, columns, dtype=BF), shape(rows, width), values]
+        out = [shape(rows, columns, dtype=BF), values]
+        if tick < TICKS - 1:
+            out.append(shape(rows, width))
         kernel = functools.partial(output_kernel, start)
         if start:
             up = shape(LANES, width, dtype=BF)
-            up, gain_w, gain_low, own, mixed, stats = call(
+            up, gain_w, gain_low, own, stats, mixed = call(
                 kernel, [up, shape(2 * CHIPS, width), shape(2 * CHIPS, LANES)] + out, got
             )
         else:
-            own, mixed, stats = call(kernel, out, got, up, gain_w, gain_low)
+            own, stats, *mixed = call(kernel, out, got, up, gain_w, gain_low)
+            mixed = mixed[0] if mixed else None
         other = swap_cores(own)
         output = call(whole_kernel, block, own, other)
         if tick < TICKS - 1:
@@ -495,7 +517,7 @@
                 [shape(TICKS - 1, toks, feats, dtype=BF), shape(toks, feats, dtype=BF)],
                 prior_epoch_input[0, 0],
                 initial_step_gradients[0],
-                output,
+                own,
                 scalars=(sample_numbers[0, 0],),
             )
             grad_arrived = to_owner(grads_out, sections, 0)

time: 200 us -> 195 us (0.975)
  waiting for transfers between devices: 36.6 us -> 32.5 us
  blocking collectives: 70.7 us -> 68.7 us
    ppermute x3, starting transfers between devices: 10.9 us -> 13 us  [to_owner(): return lax.ppermute(array, AXES, route)]
    all_to_all x4, blocking collectives: 70.7 us -> 68.7 us  [over_chips(): return lax.all_to_all(array, 'tensor', 0, 0, axis_index_groups=groups)]
  transfers between devices with their start and end apart: 21 -> 21, of which waited for: 14 -> 13; matrix products, arithmetic and copies ran while one was open for 0% -> 0% of each run, Pallas kernels for 5% -> 5%
where the time goes in v8:
time: 195 us; the launch traced here: 194 us
  blocking collectives  68.7 us (35%)
  starting transfers between devices  67.3 us (35%)
  waiting for transfers between devices  32.5 us (17%)
  Pallas kernels  19.6 us (10%)
  local copies, waits for them, and re-layouts  4.68 us (2%)
    all_to_all x4, blocking collectives, over_chips(): return lax.all_to_all(array, 'tensor', 0, 0, axis_index_groups=groups)  68.7 us
    ppermute x8, starting transfers between devices, swap_cores(): return lax.ppermute(array, 'tensor', [(i, i ^ 1) for i in range(2 * CHIPS)])  22.3 us
    pallas_call x28, Pallas kernels, call(): pl.pallas_call(kernel, out_shape=out, in_specs=[pl.BlockSpec(memory_space...  19.6 us
    ppermute x3, starting transfers between devices, to_next(): return lax.ppermute(array, AXES, route)  16.4 us
    ppermute x3, starting transfers between devices, to_owner(): return lax.ppermute(array, AXES, route)  13 us
    ppermute x8, waiting for transfers between devices, swap_cores(): return lax.ppermute(array, 'tensor', [(i, i ^ 1) for i in range(2 * CHIPS)])  10.8 us
    ppermute x3, waiting for transfers between devices, to_owner(): return lax.ppermute(array, AXES, route)  9.25 us
    ppermute x1, waiting for transfers between devices, on_device(): acc_other = lax.ppermute(acc_down, 'dp', [(0, 1), (1, 0)])  5.31 us
  transfers between devices with their start and end apart: 21, of which 13 were waited for; matrix products, arithmetic and copies ran while one was open for 0% of the time, Pallas kernels for 5%

profile of v8, /device:TPU:225, one launch (start us, length us, event | category | flops | bytes accessed | tf_op | source)
XLA Modules:
  0.0 193.8 jit_solution(7532932648478968765)
XLA Ops:
  0.6 3.2 %collective-permute-start = (bf16[48,768]{1,0:T(8,128)(2,1)}, bf16[48,768]{1,0:T(8,128)(2,1)S(1)}, u32[]{:S(2)}, u32[]{:S(2)}) collective-permute-start(bf16[48,768]{1,0:T(8,128)(2,1)} %bitcast.23), channel_id=1, source_target_pairs={{0,1},{1,0},{2,3},{3,2},{4,5},{5,4},{6,7},{7,6},{8,9},{9,8},{10,11... | collective-permute-start | bytes 221192 | tf_op jit(solution)/shard_map/ppermute | solution.py:433
  3.9 2.3 %copy-done = bf16[1,768,3072]{2,1,0:T(8,128)(2,1)S(1)} copy-done((bf16[1,768,3072]{2,1,0:T(8,128)(2,1)S(1)}, bf16[1,768,3072]{2,1,0:T(8,128)(2,1)}, u32[]{:S(2)}) %copy-start) | copy-done | bytes 4718616
  10.2 2.9 %collective-permute-start.1 = (bf16[112,2048]{1,0:T(8,128)(2,1)S(1)}, bf16[112,2048]{1,0:T(8,128)(2,1)S(1)}, u32[]{:S(2)}, u32[]{:S(2)}) collective-permute-start(bf16[112,2048]{1,0:T(8,128)(2,1)S(1)} %shard_map.97), channel_id=1, source_target_pairs={{0,2},{2,0},{4,6},{6,4},{8,10},{10,8},{12,14},{14,12},{1,3},{3,1},... | collective-permute-start | bytes 1376264 | tf_op jit(solution)/shard_map/ppermute | solution.py:71
  14.9 15.7 %all_to_all.25.got = bf16[4,112,896]{2,1,0:T(8,128)(2,1)S(1)} all-to-all(bf16[4,112,896]{2,1,0:T(8,128)(2,1)S(1)} %shard_map.98), channel_id=1, replica_groups={{0,4,8,12},{2,6,10,14},{1,5,9,13},{3,7,11,15},{16,20,24,28},{18,22,26,3..., dimensions={0} | all-to-all | bytes 1605632 | tf_op jit(solution)/shard_map/all_to_all | solution.py:76
  31.2 3.4 %collective-permute-start.2 = (bf16[96,384]{1,0:T(8,128)(2,1)S(1)}, bf16[96,384]{1,0:T(8,128)(2,1)S(1)}, u32[]{:S(2)}, u32[]{:S(2)}) collective-permute-start(bf16[96,384]{1,0:T(8,128)(2,1)S(1)} %get-tuple-element.57.mine.after), channel_id=1, source_target_pairs={{0,2},{2,0},{4,6},{6,4},{8,10},{10,8},{12,14},{14,12},{1,3},{3,1},... | collective-permute-start | bytes 221192 | tf_op jit(solution)/shard_map/ppermute | solution.py:71
  36.0 3.7 %collective-permute-start.3 = (bf16[96,768]{1,0:T(8,128)(2,1)S(1)}, bf16[96,768]{1,0:T(8,128)(2,1)S(1)}, u32[]{:S(2)}, u32[]{:S(2)}) collective-permute-start(bf16[96,768]{1,0:T(8,128)(2,1)S(1)} %shard_map.100.refs_1_), channel_id=1, source_target_pairs={{0,16},{2,17},{12,18},{14,19},{4,20},{6,21},{8,22},{10,23},{9,24},... | collective-permute-start | bytes 442376 | tf_op jit(solution)/shard_map/ppermute | solution.py:67
  39.7 5.4 %collective-permute-start.5 = (bf16[48,768]{1,0:T(8,128)(2,1)S(1)}, bf16[48,768]{1,0:T(8,128)(2,1)S(1)}, u32[]{:S(2)}, u32[]{:S(2)}) collective-permute-start(bf16[48,768]{1,0:T(8,128)(2,1)S(1)} %get-tuple-element.62), channel_id=1, source_target_pairs={{0,0},{1,2},{2,12},{3,14},{4,4},{5,6},{6,8},{7,10},{8,9},{9,11},{1... | collective-permute-start | bytes 221192 | tf_op jit(solution)/shard_map/ppermute | solution.py:58
  45.1 1.9 collective-permute-done.3.refs_0_
  48.4 1.9 collective-permute-start.6
  52.6 16.4 %all_to_all.26.got = bf16[4,96,1280]{2,1,0:T(8,128)(2,1)S(1)} all-to-all(bf16[4,96,1280]{2,1,0:T(8,128)(2,1)S(1)} %get-tuple-element.68), channel_id=1, replica_groups={{0,4,8,12},{2,6,10,14},{1,5,9,13},{3,7,11,15},{16,20,24,28},{18,22,26,3..., dimensions={0} | all-to-all | bytes 1966080 | tf_op jit(solution)/shard_map/all_to_all | solution.py:76
  69.7 3.4 %collective-permute-start.7 = (bf16[96,2048]{1,0:T(8,128)(2,1)S(1)}, bf16[96,2048]{1,0:T(8,128)(2,1)S(1)}, u32[]{:S(2)}, u32[]{:S(2)}) collective-permute-start(bf16[96,2048]{1,0:T(8,128)(2,1)S(1)} %get-tuple-element.70.mine), channel_id=1, source_target_pairs={{0,2},{2,0},{4,6},{6,4},{8,10},{10,8},{12,14},{14,12},{1,3},{3,1},... | collective-permute-start | bytes 1179656 | tf_op jit(solution)/shard_map/ppermute | solution.py:71
  74.4 5.2 %collective-permute-start.8 = (bf16[96,768]{1,0:T(8,128)(2,1)S(1)}, bf16[96,768]{1,0:T(8,128)(2,1)S(1)}, u32[]{:S(2)}, u32[]{:S(2)}) collective-permute-start(bf16[96,768]{1,0:T(8,128)(2,1)S(1)} %shard_map.106.refs_1_), channel_id=1, source_target_pairs={{0,16},{2,17},{12,18},{14,19},{4,20},{6,21},{8,22},{10,23},{9,24},... | collective-permute-start | bytes 442376 | tf_op jit(solution)/shard_map/ppermute | solution.py:67
  79.6 1.8 shard_map.108
  81.5 4.9 %collective-permute-start.9 = (bf16[96,768]{1,0:T(8,128)(2,1)S(1)}, bf16[96,768]{1,0:T(8,128)(2,1)S(1)}, u32[]{:S(2)}, u32[]{:S(2)}) collective-permute-start(bf16[96,768]{1,0:T(8,128)(2,1)S(1)} %get-tuple-element.75), channel_id=1, source_target_pairs={{16,0},{17,2},{18,12},{19,14},{20,4},{21,6},{22,8},{23,10},{24,9},... | collective-permute-start | bytes 442376 | tf_op jit(solution)/shard_map/ppermute | solution.py:58
  87.7 4.1 %collective-permute-done.9.refs_0_ = bf16[96,768]{1,0:T(8,128)(2,1)S(1)} collective-permute-done((bf16[96,768]{1,0:T(8,128)(2,1)S(1)}, bf16[96,768]{1,0:T(8,128)(2,1)S(1)}, u32[]{:S(2)}, u32[]{:S(2)}) %collective-permute-start.9) | collective-permute-done | bytes 147488 | tf_op jit(solution)/shard_map/ppermute | solution.py:58
  91.9 1.9 collective-permute-start.10
  96.2 17.7 %all_to_all.27.got = bf16[4,96,1280]{2,1,0:T(8,128)(2,1)S(1)} all-to-all(bf16[4,96,1280]{2,1,0:T(8,128)(2,1)S(1)} %get-tuple-element.79), channel_id=1, replica_groups={{0,4,8,12},{2,6,10,14},{1,5,9,13},{3,7,11,15},{16,20,24,28},{18,22,26,3..., dimensions={0} | all-to-all | bytes 1966080 | tf_op jit(solution)/shard_map/all_to_all | solution.py:76
  114.5 3.4 %collective-permute-start.11 = (bf16[96,2048]{1,0:T(8,128)(2,1)S(1)}, bf16[96,2048]{1,0:T(8,128)(2,1)S(1)}, u32[]{:S(2)}, u32[]{:S(2)}) collective-permute-start(bf16[96,2048]{1,0:T(8,128)(2,1)S(1)} %get-tuple-element.80.mine), channel_id=1, source_target_pairs={{0,2},{2,0},{4,6},{6,4},{8,10},{10,8},{12,14},{14,12},{1,3},{3,1},... | collective-permute-start | bytes 1179656 | tf_op jit(solution)/shard_map/ppermute | solution.py:71
  119.3 7.5 %collective-permute-start.12 = (bf16[96,768]{1,0:T(8,128)(2,1)S(1)}, bf16[96,768]{1,0:T(8,128)(2,1)S(1)}, u32[]{:S(2)}, u32[]{:S(2)}) collective-permute-start(bf16[96,768]{1,0:T(8,128)(2,1)S(1)} %shard_map.112.refs_1_), channel_id=1, source_target_pairs={{0,16},{2,17},{12,18},{14,19},{4,20},{6,21},{8,22},{10,23},{9,24},... | collective-permute-start | bytes 442376 | tf_op jit(solution)/shard_map/ppermute | solution.py:67
  126.8 1.8 shard_map.114
  128.6 2.8 %collective-permute-start.13 = (bf16[96,768]{1,0:T(8,128)(2,1)S(1)}, bf16[96,768]{1,0:T(8,128)(2,1)S(1)}, u32[]{:S(2)}, u32[]{:S(2)}) collective-permute-start(bf16[96,768]{1,0:T(8,128)(2,1)S(1)} %get-tuple-element.85), channel_id=1, source_target_pairs={{16,0},{17,2},{18,12},{19,14},{20,4},{21,6},{22,8},{23,10},{24,9},... | collective-permute-start | bytes 442376 | tf_op jit(solution)/shard_map/ppermute | solution.py:58
  132.8 5.1 %collective-permute-done.13.refs_0_ = bf16[96,768]{1,0:T(8,128)(2,1)S(1)} collective-permute-done((bf16[96,768]{1,0:T(8,128)(2,1)S(1)}, bf16[96,768]{1,0:T(8,128)(2,1)S(1)}, u32[]{:S(2)}, u32[]{:S(2)}) %collective-permute-start.13) | collective-permute-done | bytes 147488 | tf_op jit(solution)/shard_map/ppermute | solution.py:58
  138.0 1.9 collective-permute-start.14
  142.2 18.9 %all_to_all.28.got = bf16[4,96,1280]{2,1,0:T(8,128)(2,1)S(1)} all-to-all(bf16[4,96,1280]{2,1,0:T(8,128)(2,1)S(1)} %get-tuple-element.89), channel_id=1, replica_groups={{0,4,8,12},{2,6,10,14},{1,5,9,13},{3,7,11,15},{16,20,24,28},{18,22,26,3..., dimensions={0} | all-to-all | bytes 1966080 | tf_op jit(solution)/shard_map/all_to_all | solution.py:76
  161.7 3.4 %collective-permute-start.15 = (bf16[96,2048]{1,0:T(8,128)(2,1)S(1)}, bf16[96,2048]{1,0:T(8,128)(2,1)S(1)}, u32[]{:S(2)}, u32[]{:S(2)}) collective-permute-start(bf16[96,2048]{1,0:T(8,128)(2,1)S(1)} %get-tuple-element.90.mine), channel_id=1, source_target_pairs={{0,2},{2,0},{4,6},{6,4},{8,10},{10,8},{12,14},{14,12},{1,3},{3,1},... | collective-permute-start | bytes 1179656 | tf_op jit(solution)/shard_map/ppermute | solution.py:71
  166.4 1.8 shard_map.118
  168.3 1.9 collective-permute-start.16
  172.3 1.9 collective-permute-start.18
  174.2 5.3 %collective-permute-done.18.after.theirs = f32[16,768]{1,0:T(8,128)S(1)} collective-permute-done((f32[16,768]{1,0:T(8,128)S(1)}, f32[16,768]{1,0:T(8,128)S(1)}, u32[]{:S(2)}, u32[]{:S(2)}) %collective-permute-start.18) | collective-permute-done | bytes 49184 | tf_op jit(solution)/shard_map/ppermute | solution.py:560
  180.5 3.8 %all-to-all-start.4 = ((bf16[16,16,640]{2,1,0:T(8,128)(2,1)}), bf16[16,16,640]{2,1,0:T(8,128)(2,1)S(1)}, u32[]{:S(2)}, u32[]{:S(2)}) async-start(bf16[16,16,640]{2,1,0:T(8,128)(2,1)} %get-tuple-element.102), calls=%async_computation.4 | async-start | bytes 655360 | tf_op jit(solution)/shard_map/all_to_all | solution.py:574
  184.3 3.3 %collective-permute-start.19 = (bf16[16,768]{1,0:T(8,128)(2,1)S(1)}, bf16[16,768]{1,0:T(8,128)(2,1)S(1)}, u32[]{:S(2)}, u32[]{:S(2)}) collective-permute-start(bf16[16,768]{1,0:T(8,128)(2,1)S(1)} %get-tuple-element.103.up_mine), channel_id=1, source_target_pairs={{0,1},{1,0},{2,3},{3,2},{4,5},{5,4},{6,7},{7,6},{8,9},{9,8},{10,11... | collective-permute-start | bytes 73736 | tf_op jit(solution)/shard_map/ppermute | solution.py:585
  189.1 3.7 %all-to-all-done.4.got = bf16[16,16,640]{2,1,0:T(8,128)(2,1)S(1)} async-done(((bf16[16,16,640]{2,1,0:T(8,128)(2,1)}), bf16[16,16,640]{2,1,0:T(8,128)(2,1)S(1)}, u32[]{:S(2)}, u32[]{:S(2)}) %all-to-all-start.4) | async-done | bytes 327712 | tf_op jit(solution)/shard_map/all_to_all | solution.py:574
  (65 shorter events, 30.3 us)
Async XLA Ops:
  0.6 7.9 %collective-permute-start = (bf16[48,768]{1,0:T(8,128)(2,1)}, bf16[48,768]{1,0:T(8,128)(2,1)S(1)}, u32[]{:S(2)}, u32[]{:S(2)}) collective-permute-start(bf16[48,768]{1,0:T(8,128)(2,1)} %bitcast.23), channel_id=1, source_target_pairs={{0,1},{1,0},{2,3},{3,2},{4,5},{5,4},{6,7},{7,6},{8,9},{9,8},{10,11... | collective-permute-start | bytes 221192 | tf_op jit(solution)/shard_map/ppermute | solution.py:433
  3.8 2.3 %copy-start = (bf16[1,768,3072]{2,1,0:T(8,128)(2,1)S(1)}, bf16[1,768,3072]{2,1,0:T(8,128)(2,1)}, u32[]{:S(2)}) copy-start(bf16[1,768,3072]{2,1,0:T(8,128)(2,1)} %param.9) | copy-start | bytes 14155780
  6.2 0.7 copy-start.1
  6.9 0.9 copy-start.3
  7.8 0.7 copy-start.7
  8.5 1.6 copy-start.4
  8.5 38.5 %slice-start = ((s8[4718592]{0:T(1024)(128)(4,1)}), s8[4194304]{0:T(1024)(128)(4,1)S(1)}, s32[]{:S(2)}) async-start(s8[4718592]{0:T(1024)(128)(4,1)} %bitcast.15), calls=%async_computation.5 | async-start | bytes 8388608
  8.5 26.1 %copy-start.5 = (bf16[1,1,2,48,768]{4,3,2,1,0:T(8,128)(2,1)S(1)}, bf16[1,1,2,48,768]{4,3,2,1,0:T(8,128)(2,1)}, u32[]{:S(2)}) copy-start(bf16[1,1,2,48,768]{4,3,2,1,0:T(8,128)(2,1)} %param.13) | copy-start | bytes 442372
  8.5 26.1 %copy-start.6 = (bf16[1,48,768]{2,1,0:T(8,128)(2,1)S(1)}, bf16[1,48,768]{2,1,0:T(8,128)(2,1)}, u32[]{:S(2)}) copy-start(bf16[1,48,768]{2,1,0:T(8,128)(2,1)} %param.15) | copy-start | bytes 221188
  8.5 26.1 %copy-start.8 = (s32[1,1,4]{2,1,0:T(1,128)S(1)}, s32[1,1,4]{2,1,0:T(1,128)}, u32[]{:S(2)}) copy-start(s32[1,1,4]{2,1,0:T(1,128)} %param.16) | copy-start | bytes 52
  8.6 38.4 %slice-start.1 = ((s8[4718592]{0:T(1024)(128)(4,1)}), s8[524288]{0:T(1024)(128)(4,1)S(1)}, s32[]{:S(2)}) async-start(s8[4718592]{0:T(1024)(128)(4,1)} %bitcast.15), calls=%async_computation.6 | async-start | bytes 1048576
  10.2 4.3 %collective-permute-start.1 = (bf16[112,2048]{1,0:T(8,128)(2,1)S(1)}, bf16[112,2048]{1,0:T(8,128)(2,1)S(1)}, u32[]{:S(2)}, u32[]{:S(2)}) collective-permute-start(bf16[112,2048]{1,0:T(8,128)(2,1)S(1)} %shard_map.97), channel_id=1, source_target_pairs={{0,2},{2,0},{4,6},{6,4},{8,10},{10,8},{12,14},{14,12},{1,3},{3,1},... | collective-permute-start | bytes 1376264 | tf_op jit(solution)/shard_map/ppermute | solution.py:71
  31.2 4.7 %collective-permute-start.2 = (bf16[96,384]{1,0:T(8,128)(2,1)S(1)}, bf16[96,384]{1,0:T(8,128)(2,1)S(1)}, u32[]{:S(2)}, u32[]{:S(2)}) collective-permute-start(bf16[96,384]{1,0:T(8,128)(2,1)S(1)} %get-tuple-element.57.mine.after), channel_id=1, source_target_pairs={{0,2},{2,0},{4,6},{6,4},{8,10},{10,8},{12,14},{14,12},{1,3},{3,1},... | collective-permute-start | bytes 221192 | tf_op jit(solution)/shard_map/ppermute | solution.py:71
  35.2 11.7 %collective-permute-start.4 = (bf16[3,48,768]{2,1,0:T(8,128)(2,1)S(1)}, bf16[3,48,768]{2,1,0:T(8,128)(2,1)S(1)}, u32[]{:S(2)}, u32[]{:S(2)}) collective-permute-start(bf16[3,48,768]{2,1,0:T(8,128)(2,1)S(1)} %get-tuple-element.58.refs_1_), channel_id=1, source_target_pairs={{0,1},{1,0},{2,3},{3,2},{4,5},{5,4},{6,7},{7,6},{8,9},{9,8},{10,11... | collective-permute-start | bytes 663560 | tf_op jit(solution)/shard_map/ppermute | solution.py:524
  36.0 11.0 %collective-permute-start.3 = (bf16[96,768]{1,0:T(8,128)(2,1)S(1)}, bf16[96,768]{1,0:T(8,128)(2,1)S(1)}, u32[]{:S(2)}, u32[]{:S(2)}) collective-permute-start(bf16[96,768]{1,0:T(8,128)(2,1)S(1)} %shard_map.100.refs_1_), channel_id=1, source_target_pairs={{0,16},{2,17},{12,18},{14,19},{4,20},{6,21},{8,22},{10,23},{9,24},... | collective-permute-start | bytes 442376 | tf_op jit(solution)/shard_map/ppermute | solution.py:67
  39.7 8.6 %collective-permute-start.5 = (bf16[48,768]{1,0:T(8,128)(2,1)S(1)}, bf16[48,768]{1,0:T(8,128)(2,1)S(1)}, u32[]{:S(2)}, u32[]{:S(2)}) collective-permute-start(bf16[48,768]{1,0:T(8,128)(2,1)S(1)} %get-tuple-element.62), channel_id=1, source_target_pairs={{0,0},{1,2},{2,12},{3,14},{4,4},{5,6},{6,8},{7,10},{8,9},{9,11},{1... | collective-permute-start | bytes 221192 | tf_op jit(solution)/shard_map/ppermute | solution.py:58
  48.4 3.7 %collective-permute-start.6 = (bf16[96,2432]{1,0:T(8,128)(2,1)S(1)}, bf16[96,2432]{1,0:T(8,128)(2,1)S(1)}, u32[]{:S(2)}, u32[]{:S(2)}) collective-permute-start(bf16[96,2432]{1,0:T(8,128)(2,1)S(1)} %get-tuple-element.63), channel_id=1, source_target_pairs={{0,2},{2,0},{4,6},{6,4},{8,10},{10,8},{12,14},{14,12},{1,3},{3,1},... | collective-permute-start | bytes 1400840 | tf_op jit(solution)/shard_map/ppermute | solution.py:71
  69.7 4.7 %collective-permute-start.7 = (bf16[96,2048]{1,0:T(8,128)(2,1)S(1)}, bf16[96,2048]{1,0:T(8,128)(2,1)S(1)}, u32[]{:S(2)}, u32[]{:S(2)}) collective-permute-start(bf16[96,2048]{1,0:T(8,128)(2,1)S(1)} %get-tuple-element.70.mine), channel_id=1, source_target_pairs={{0,2},{2,0},{4,6},{6,4},{8,10},{10,8},{12,14},{14,12},{1,3},{3,1},... | collective-permute-start | bytes 1179656 | tf_op jit(solution)/shard_map/ppermute | solution.py:71
  74.4 11.9 %collective-permute-start.8 = (bf16[96,768]{1,0:T(8,128)(2,1)S(1)}, bf16[96,768]{1,0:T(8,128)(2,1)S(1)}, u32[]{:S(2)}, u32[]{:S(2)}) collective-permute-start(bf16[96,768]{1,0:T(8,128)(2,1)S(1)} %shard_map.106.refs_1_), channel_id=1, source_target_pairs={{0,16},{2,17},{12,18},{14,19},{4,20},{6,21},{8,22},{10,23},{9,24},... | collective-permute-start | bytes 442376 | tf_op jit(solution)/shard_map/ppermute | solution.py:67
  81.5 10.4 %collective-permute-start.9 = (bf16[96,768]{1,0:T(8,128)(2,1)S(1)}, bf16[96,768]{1,0:T(8,128)(2,1)S(1)}, u32[]{:S(2)}, u32[]{:S(2)}) collective-permute-start(bf16[96,768]{1,0:T(8,128)(2,1)S(1)} %get-tuple-element.75), channel_id=1, source_target_pairs={{16,0},{17,2},{18,12},{19,14},{20,4},{21,6},{22,8},{23,10},{24,9},... | collective-permute-start | bytes 442376 | tf_op jit(solution)/shard_map/ppermute | solution.py:58
  91.9 3.7 %collective-permute-start.10 = (bf16[96,2432]{1,0:T(8,128)(2,1)S(1)}, bf16[96,2432]{1,0:T(8,128)(2,1)S(1)}, u32[]{:S(2)}, u32[]{:S(2)}) collective-permute-start(bf16[96,2432]{1,0:T(8,128)(2,1)S(1)} %get-tuple-element.76), channel_id=1, source_target_pairs={{0,2},{2,0},{4,6},{6,4},{8,10},{10,8},{12,14},{14,12},{1,3},{3,1},... | collective-permute-start | bytes 1400840 | tf_op jit(solution)/shard_map/ppermute | solution.py:71
  114.5 4.8 %collective-permute-start.11 = (bf16[96,2048]{1,0:T(8,128)(2,1)S(1)}, bf16[96,2048]{1,0:T(8,128)(2,1)S(1)}, u32[]{:S(2)}, u32[]{:S(2)}) collective-permute-start(bf16[96,2048]{1,0:T(8,128)(2,1)S(1)} %get-tuple-element.80.mine), channel_id=1, source_target_pairs={{0,2},{2,0},{4,6},{6,4},{8,10},{10,8},{12,14},{14,12},{1,3},{3,1},... | collective-permute-start | bytes 1179656 | tf_op jit(solution)/shard_map/ppermute | solution.py:71
  119.3 12.1 %collective-permute-start.12 = (bf16[96,768]{1,0:T(8,128)(2,1)S(1)}, bf16[96,768]{1,0:T(8,128)(2,1)S(1)}, u32[]{:S(2)}, u32[]{:S(2)}) collective-permute-start(bf16[96,768]{1,0:T(8,128)(2,1)S(1)} %shard_map.112.refs_1_), channel_id=1, source_target_pairs={{0,16},{2,17},{12,18},{14,19},{4,20},{6,21},{8,22},{10,23},{9,24},... | collective-permute-start | bytes 442376 | tf_op jit(solution)/shard_map/ppermute | solution.py:67
  128.6 9.3 %collective-permute-start.13 = (bf16[96,768]{1,0:T(8,128)(2,1)S(1)}, bf16[96,768]{1,0:T(8,128)(2,1)S(1)}, u32[]{:S(2)}, u32[]{:S(2)}) collective-permute-start(bf16[96,768]{1,0:T(8,128)(2,1)S(1)} %get-tuple-element.85), channel_id=1, source_target_pairs={{16,0},{17,2},{18,12},{19,14},{20,4},{21,6},{22,8},{23,10},{24,9},... | collective-permute-start | bytes 442376 | tf_op jit(solution)/shard_map/ppermute | solution.py:58
  138.0 3.7 %collective-permute-start.14 = (bf16[96,2432]{1,0:T(8,128)(2,1)S(1)}, bf16[96,2432]{1,0:T(8,128)(2,1)S(1)}, u32[]{:S(2)}, u32[]{:S(2)}) collective-permute-start(bf16[96,2432]{1,0:T(8,128)(2,1)S(1)} %get-tuple-element.86), channel_id=1, source_target_pairs={{0,2},{2,0},{4,6},{6,4},{8,10},{10,8},{12,14},{14,12},{1,3},{3,1},... | collective-permute-start | bytes 1400840 | tf_op jit(solution)/shard_map/ppermute | solution.py:71
  161.7 31.2 %copy-start.2 = (f32[1,768]{1,0:T(1,128)S(1)}, f32[1,768]{1,0:T(1,128)}, u32[]{:S(2)}) copy-start(f32[1,768]{1,0:T(1,128)} %gains.11) | copy-start | bytes 9220
  161.7 4.8 %collective-permute-start.15 = (bf16[96,2048]{1,0:T(8,128)(2,1)S(1)}, bf16[96,2048]{1,0:T(8,128)(2,1)S(1)}, u32[]{:S(2)}, u32[]{:S(2)}) collective-permute-start(bf16[96,2048]{1,0:T(8,128)(2,1)S(1)} %get-tuple-element.90.mine), channel_id=1, source_target_pairs={{0,2},{2,0},{4,6},{6,4},{8,10},{10,8},{12,14},{14,12},{1,3},{3,1},... | collective-permute-start | bytes 1179656 | tf_op jit(solution)/shard_map/ppermute | solution.py:71
  168.3 11.3 %collective-permute-start.16 = (bf16[96,768]{1,0:T(8,128)(2,1)S(1)}, bf16[96,768]{1,0:T(8,128)(2,1)S(1)}, u32[]{:S(2)}, u32[]{:S(2)}) collective-permute-start(bf16[96,768]{1,0:T(8,128)(2,1)S(1)} %get-tuple-element.92.after), channel_id=1, source_target_pairs={{16,0},{32,16},{48,32},{64,48},{80,64},{96,80},{112,96},{128,112},... | collective-permute-start | bytes 442376 | tf_op jit(solution)/shard_map/ppermute | solution.py:404
  170.2 9.3 %collective-permute-start.17 = (bf16[96,768]{1,0:T(8,128)(2,1)S(1)}, bf16[96,768]{1,0:T(8,128)(2,1)S(1)}, u32[]{:S(2)}, u32[]{:S(2)}) collective-permute-start(bf16[96,768]{1,0:T(8,128)(2,1)S(1)} %shard_map.119), channel_id=1, source_target_pairs={{496,496},{508,498},{500,500},{504,502},{505,504},{501,506},{509,5... | collective-permute-start | bytes 442376 | tf_op jit(solution)/shard_map/ppermute | solution.py:410
  172.3 7.2 %collective-permute-start.18 = (f32[16,768]{1,0:T(8,128)S(1)}, f32[16,768]{1,0:T(8,128)S(1)}, u32[]{:S(2)}, u32[]{:S(2)}) collective-permute-start(f32[16,768]{1,0:T(8,128)S(1)} %get-tuple-element.101.mine), channel_id=1, source_target_pairs={{0,1},{1,0},{2,3},{3,2},{4,5},{5,4},{6,7},{7,6},{8,9},{9,8},{10,11... | collective-permute-start | bytes 147464 | tf_op jit(solution)/shard_map/ppermute | solution.py:560
  180.5 12.4 %all-to-all-start.4 = ((bf16[16,16,640]{2,1,0:T(8,128)(2,1)}), bf16[16,16,640]{2,1,0:T(8,128)(2,1)S(1)}, u32[]{:S(2)}, u32[]{:S(2)}) async-start(bf16[16,16,640]{2,1,0:T(8,128)(2,1)} %get-tuple-element.102), calls=%async_computation.4 | async-start | bytes 655360 | tf_op jit(solution)/shard_map/all_to_all | solution.py:574
  184.3 4.9 %collective-permute-start.19 = (bf16[16,768]{1,0:T(8,128)(2,1)S(1)}, bf16[16,768]{1,0:T(8,128)(2,1)S(1)}, u32[]{:S(2)}, u32[]{:S(2)}) collective-permute-start(bf16[16,768]{1,0:T(8,128)(2,1)S(1)} %get-tuple-element.103.up_mine), channel_id=1, source_target_pairs={{0,1},{1,0},{2,3},{3,2},{4,5},{5,4},{6,7},{7,6},{8,9},{9,8},{10,11... | collective-permute-start | bytes 73736 | tf_op jit(solution)/shard_map/ppermute | solution.py:585

commit v9 on v8

--- a/solution.py
+++ b/solution.py
@@ -132,7 +132,7 @@
     return jnp.concatenate([jnp.where(first, mine, theirs), jnp.where(first, theirs, mine)])
 
 
-def warm_kernel(w, gains, mine, down_rows, down):
+def warm_kernel(w, down_rows, down):
     rank, feats = down_rows.shape
     down[:LOW] = jnp.zeros((LOW, feats), F32)
     down[LOW : LOW + rank] = down_rows[...].astype(F32)
@@ -431,7 +431,7 @@
 
     mine = initial_step_inputs[0]
     theirs = lax.ppermute(mine, "dp", [(0, 1), (1, 0)])
-    down = call(warm_kernel, shape(LANES, feats), w, gains, mine, adapter_down_map[0].T)
+    down = call(warm_kernel, shape(LANES, feats), w, adapter_down_map[0].T)
 
     block = shape(rows, feats, dtype=BF)
     values = shape(rows, LANES)

time: 195 us -> 194 us (level)
    unnamed x22 -> x20, local copies, waits for them, and re-layouts: 4.68 us -> 3.89 us
where the time goes in v9:
time: 194 us; the launch traced here: 193 us
  blocking collectives  68.6 us (35%)
  starting transfers between devices  67.4 us (35%)
  waiting for transfers between devices  32.8 us (17%)
  Pallas kernels  19.6 us (10%)
  local copies, waits for them, and re-layouts  3.89 us (2%)
    all_to_all x4, blocking collectives, over_chips(): return lax.all_to_all(array, 'tensor', 0, 0, axis_index_groups=groups)  68.6 us
    ppermute x8, starting transfers between devices, swap_cores(): return lax.ppermute(array, 'tensor', [(i, i ^ 1) for i in range(2 * CHIPS)])  22.4 us
    pallas_call x28, Pallas kernels, call(): pl.pallas_call(kernel, out_shape=out, in_specs=[pl.BlockSpec(memory_space...  19.6 us
    ppermute x3, starting transfers between devices, to_next(): return lax.ppermute(array, AXES, route)  16.5 us
    ppermute x3, starting transfers between devices, to_owner(): return lax.ppermute(array, AXES, route)  13 us
    ppermute x8, waiting for transfers between devices, swap_cores(): return lax.ppermute(array, 'tensor', [(i, i ^ 1) for i in range(2 * CHIPS)])  10.8 us
    ppermute x3, waiting for transfers between devices, to_owner(): return lax.ppermute(array, AXES, route)  9.46 us
    ppermute x1, waiting for transfers between devices, on_device(): acc_other = lax.ppermute(acc_down, 'dp', [(0, 1), (1, 0)])  5.22 us
  transfers between devices with their start and end apart: 21, of which 13 were waited for; matrix products, arithmetic and copies ran while one was open for 0% of the time, Pallas kernels for 5%

profile of v9, /device:TPU:225, one launch (start us, length us, event | category | flops | bytes accessed | tf_op | source)
XLA Modules:
  0.0 193.3 jit_solution(15319739642969672248)
XLA Ops:
  0.6 3.2 %collective-permute-start = (bf16[48,768]{1,0:T(8,128)(2,1)}, bf16[48,768]{1,0:T(8,128)(2,1)S(1)}, u32[]{:S(2)}, u32[]{:S(2)}) collective-permute-start(bf16[48,768]{1,0:T(8,128)(2,1)} %bitcast.28), channel_id=1, source_target_pairs={{0,1},{1,0},{2,3},{3,2},{4,5},{5,4},{6,7},{7,6},{8,9},{9,8},{10,11... | collective-permute-start | bytes 221192 | tf_op jit(solution)/shard_map/ppermute | solution.py:433
  3.9 2.3 %copy-done = bf16[1,768,3072]{2,1,0:T(8,128)(2,1)S(1)} copy-done((bf16[1,768,3072]{2,1,0:T(8,128)(2,1)S(1)}, bf16[1,768,3072]{2,1,0:T(8,128)(2,1)}, u32[]{:S(2)}) %copy-start) | copy-done | bytes 4718616
  9.4 2.9 %collective-permute-start.1 = (bf16[112,2048]{1,0:T(8,128)(2,1)S(1)}, bf16[112,2048]{1,0:T(8,128)(2,1)S(1)}, u32[]{:S(2)}, u32[]{:S(2)}) collective-permute-start(bf16[112,2048]{1,0:T(8,128)(2,1)S(1)} %shard_map.97), channel_id=1, source_target_pairs={{0,2},{2,0},{4,6},{6,4},{8,10},{10,8},{12,14},{14,12},{1,3},{3,1},... | collective-permute-start | bytes 1376264 | tf_op jit(solution)/shard_map/ppermute | solution.py:71
  14.1 15.7 %all_to_all.25.got = bf16[4,112,896]{2,1,0:T(8,128)(2,1)S(1)} all-to-all(bf16[4,112,896]{2,1,0:T(8,128)(2,1)S(1)} %shard_map.98), channel_id=1, replica_groups={{0,4,8,12},{2,6,10,14},{1,5,9,13},{3,7,11,15},{16,20,24,28},{18,22,26,3..., dimensions={0} | all-to-all | bytes 1605632 | tf_op jit(solution)/shard_map/all_to_all | solution.py:76
  30.4 3.4 %collective-permute-start.2 = (bf16[96,384]{1,0:T(8,128)(2,1)S(1)}, bf16[96,384]{1,0:T(8,128)(2,1)S(1)}, u32[]{:S(2)}, u32[]{:S(2)}) collective-permute-start(bf16[96,384]{1,0:T(8,128)(2,1)S(1)} %get-tuple-element.57.mine.after), channel_id=1, source_target_pairs={{0,2},{2,0},{4,6},{6,4},{8,10},{10,8},{12,14},{14,12},{1,3},{3,1},... | collective-permute-start | bytes 221192 | tf_op jit(solution)/shard_map/ppermute | solution.py:71
  35.2 3.7 %collective-permute-start.3 = (bf16[96,768]{1,0:T(8,128)(2,1)S(1)}, bf16[96,768]{1,0:T(8,128)(2,1)S(1)}, u32[]{:S(2)}, u32[]{:S(2)}) collective-permute-start(bf16[96,768]{1,0:T(8,128)(2,1)S(1)} %shard_map.100.refs_1_), channel_id=1, source_target_pairs={{0,16},{2,17},{12,18},{14,19},{4,20},{6,21},{8,22},{10,23},{9,24},... | collective-permute-start | bytes 442376 | tf_op jit(solution)/shard_map/ppermute | solution.py:67
  38.9 5.4 %collective-permute-start.5 = (bf16[48,768]{1,0:T(8,128)(2,1)S(1)}, bf16[48,768]{1,0:T(8,128)(2,1)S(1)}, u32[]{:S(2)}, u32[]{:S(2)}) collective-permute-start(bf16[48,768]{1,0:T(8,128)(2,1)S(1)} %get-tuple-element.62), channel_id=1, source_target_pairs={{0,0},{1,2},{2,12},{3,14},{4,4},{5,6},{6,8},{7,10},{8,9},{9,11},{1... | collective-permute-start | bytes 221192 | tf_op jit(solution)/shard_map/ppermute | solution.py:58
  44.3 2.0 %collective-permute-done.3.refs_0_ = bf16[96,768]{1,0:T(8,128)(2,1)S(1)} collective-permute-done((bf16[96,768]{1,0:T(8,128)(2,1)S(1)}, bf16[96,768]{1,0:T(8,128)(2,1)S(1)}, u32[]{:S(2)}, u32[]{:S(2)}) %collective-permute-start.3) | collective-permute-done | bytes 147488 | tf_op jit(solution)/shard_map/ppermute | solution.py:67
  47.8 1.9 collective-permute-start.6
  52.0 16.4 %all_to_all.26.got = bf16[4,96,1280]{2,1,0:T(8,128)(2,1)S(1)} all-to-all(bf16[4,96,1280]{2,1,0:T(8,128)(2,1)S(1)} %get-tuple-element.68), channel_id=1, replica_groups={{0,4,8,12},{2,6,10,14},{1,5,9,13},{3,7,11,15},{16,20,24,28},{18,22,26,3..., dimensions={0} | all-to-all | bytes 1966080 | tf_op jit(solution)/shard_map/all_to_all | solution.py:76
  69.0 3.5 %collective-permute-start.7 = (bf16[96,2048]{1,0:T(8,128)(2,1)S(1)}, bf16[96,2048]{1,0:T(8,128)(2,1)S(1)}, u32[]{:S(2)}, u32[]{:S(2)}) collective-permute-start(bf16[96,2048]{1,0:T(8,128)(2,1)S(1)} %get-tuple-element.70.mine), channel_id=1, source_target_pairs={{0,2},{2,0},{4,6},{6,4},{8,10},{10,8},{12,14},{14,12},{1,3},{3,1},... | collective-permute-start | bytes 1179656 | tf_op jit(solution)/shard_map/ppermute | solution.py:71
  73.8 5.1 %collective-permute-start.8 = (bf16[96,768]{1,0:T(8,128)(2,1)S(1)}, bf16[96,768]{1,0:T(8,128)(2,1)S(1)}, u32[]{:S(2)}, u32[]{:S(2)}) collective-permute-start(bf16[96,768]{1,0:T(8,128)(2,1)S(1)} %shard_map.106.refs_1_), channel_id=1, source_target_pairs={{0,16},{2,17},{12,18},{14,19},{4,20},{6,21},{8,22},{10,23},{9,24},... | collective-permute-start | bytes 442376 | tf_op jit(solution)/shard_map/ppermute | solution.py:67
  78.9 1.8 shard_map.108
  80.7 5.0 %collective-permute-start.9 = (bf16[96,768]{1,0:T(8,128)(2,1)S(1)}, bf16[96,768]{1,0:T(8,128)(2,1)S(1)}, u32[]{:S(2)}, u32[]{:S(2)}) collective-permute-start(bf16[96,768]{1,0:T(8,128)(2,1)S(1)} %get-tuple-element.75), channel_id=1, source_target_pairs={{16,0},{17,2},{18,12},{19,14},{20,4},{21,6},{22,8},{23,10},{24,9},... | collective-permute-start | bytes 442376 | tf_op jit(solution)/shard_map/ppermute | solution.py:58
  87.1 4.1 %collective-permute-done.9.refs_0_ = bf16[96,768]{1,0:T(8,128)(2,1)S(1)} collective-permute-done((bf16[96,768]{1,0:T(8,128)(2,1)S(1)}, bf16[96,768]{1,0:T(8,128)(2,1)S(1)}, u32[]{:S(2)}, u32[]{:S(2)}) %collective-permute-start.9) | collective-permute-done | bytes 147488 | tf_op jit(solution)/shard_map/ppermute | solution.py:58
  91.3 1.9 collective-permute-start.10
  95.5 17.6 %all_to_all.27.got = bf16[4,96,1280]{2,1,0:T(8,128)(2,1)S(1)} all-to-all(bf16[4,96,1280]{2,1,0:T(8,128)(2,1)S(1)} %get-tuple-element.79), channel_id=1, replica_groups={{0,4,8,12},{2,6,10,14},{1,5,9,13},{3,7,11,15},{16,20,24,28},{18,22,26,3..., dimensions={0} | all-to-all | bytes 1966080 | tf_op jit(solution)/shard_map/all_to_all | solution.py:76
  113.7 3.4 %collective-permute-start.11 = (bf16[96,2048]{1,0:T(8,128)(2,1)S(1)}, bf16[96,2048]{1,0:T(8,128)(2,1)S(1)}, u32[]{:S(2)}, u32[]{:S(2)}) collective-permute-start(bf16[96,2048]{1,0:T(8,128)(2,1)S(1)} %get-tuple-element.80.mine), channel_id=1, source_target_pairs={{0,2},{2,0},{4,6},{6,4},{8,10},{10,8},{12,14},{14,12},{1,3},{3,1},... | collective-permute-start | bytes 1179656 | tf_op jit(solution)/shard_map/ppermute | solution.py:71
  118.5 7.7 %collective-permute-start.12 = (bf16[96,768]{1,0:T(8,128)(2,1)S(1)}, bf16[96,768]{1,0:T(8,128)(2,1)S(1)}, u32[]{:S(2)}, u32[]{:S(2)}) collective-permute-start(bf16[96,768]{1,0:T(8,128)(2,1)S(1)} %shard_map.112.refs_1_), channel_id=1, source_target_pairs={{0,16},{2,17},{12,18},{14,19},{4,20},{6,21},{8,22},{10,23},{9,24},... | collective-permute-start | bytes 442376 | tf_op jit(solution)/shard_map/ppermute | solution.py:67
  126.2 1.8 shard_map.114
  128.1 2.6 %collective-permute-start.13 = (bf16[96,768]{1,0:T(8,128)(2,1)S(1)}, bf16[96,768]{1,0:T(8,128)(2,1)S(1)}, u32[]{:S(2)}, u32[]{:S(2)}) collective-permute-start(bf16[96,768]{1,0:T(8,128)(2,1)S(1)} %get-tuple-element.85), channel_id=1, source_target_pairs={{16,0},{17,2},{18,12},{19,14},{20,4},{21,6},{22,8},{23,10},{24,9},... | collective-permute-start | bytes 442376 | tf_op jit(solution)/shard_map/ppermute | solution.py:58
  132.0 5.3 %collective-permute-done.13.refs_0_ = bf16[96,768]{1,0:T(8,128)(2,1)S(1)} collective-permute-done((bf16[96,768]{1,0:T(8,128)(2,1)S(1)}, bf16[96,768]{1,0:T(8,128)(2,1)S(1)}, u32[]{:S(2)}, u32[]{:S(2)}) %collective-permute-start.13) | collective-permute-done | bytes 147488 | tf_op jit(solution)/shard_map/ppermute | solution.py:58
  137.4 1.9 collective-permute-start.14
  141.6 18.9 %all_to_all.28.got = bf16[4,96,1280]{2,1,0:T(8,128)(2,1)S(1)} all-to-all(bf16[4,96,1280]{2,1,0:T(8,128)(2,1)S(1)} %get-tuple-element.89), channel_id=1, replica_groups={{0,4,8,12},{2,6,10,14},{1,5,9,13},{3,7,11,15},{16,20,24,28},{18,22,26,3..., dimensions={0} | all-to-all | bytes 1966080 | tf_op jit(solution)/shard_map/all_to_all | solution.py:76
  161.1 3.4 %collective-permute-start.15 = (bf16[96,2048]{1,0:T(8,128)(2,1)S(1)}, bf16[96,2048]{1,0:T(8,128)(2,1)S(1)}, u32[]{:S(2)}, u32[]{:S(2)}) collective-permute-start(bf16[96,2048]{1,0:T(8,128)(2,1)S(1)} %get-tuple-element.90.mine), channel_id=1, source_target_pairs={{0,2},{2,0},{4,6},{6,4},{8,10},{10,8},{12,14},{14,12},{1,3},{3,1},... | collective-permute-start | bytes 1179656 | tf_op jit(solution)/shard_map/ppermute | solution.py:71
  165.9 1.8 shard_map.118
  167.7 1.9 collective-permute-start.16
  171.7 2.0 %collective-permute-start.18 = (f32[16,768]{1,0:T(8,128)S(1)}, f32[16,768]{1,0:T(8,128)S(1)}, u32[]{:S(2)}, u32[]{:S(2)}) collective-permute-start(f32[16,768]{1,0:T(8,128)S(1)} %get-tuple-element.101.mine), channel_id=1, source_target_pairs={{0,1},{1,0},{2,3},{3,2},{4,5},{5,4},{6,7},{7,6},{8,9},{9,8},{10,11... | collective-permute-start | bytes 147464 | tf_op jit(solution)/shard_map/ppermute | solution.py:560
  173.7 5.2 %collective-permute-done.18.after.theirs = f32[16,768]{1,0:T(8,128)S(1)} collective-permute-done((f32[16,768]{1,0:T(8,128)S(1)}, f32[16,768]{1,0:T(8,128)S(1)}, u32[]{:S(2)}, u32[]{:S(2)}) %collective-permute-start.18) | collective-permute-done | bytes 49184 | tf_op jit(solution)/shard_map/ppermute | solution.py:560
  179.9 3.8 %all-to-all-start.4 = ((bf16[16,16,640]{2,1,0:T(8,128)(2,1)}), bf16[16,16,640]{2,1,0:T(8,128)(2,1)S(1)}, u32[]{:S(2)}, u32[]{:S(2)}) async-start(bf16[16,16,640]{2,1,0:T(8,128)(2,1)} %get-tuple-element.102), calls=%async_computation.4 | async-start | bytes 655360 | tf_op jit(solution)/shard_map/all_to_all | solution.py:574
  183.7 3.3 %collective-permute-start.19 = (bf16[16,768]{1,0:T(8,128)(2,1)S(1)}, bf16[16,768]{1,0:T(8,128)(2,1)S(1)}, u32[]{:S(2)}, u32[]{:S(2)}) collective-permute-start(bf16[16,768]{1,0:T(8,128)(2,1)S(1)} %get-tuple-element.103.up_mine), channel_id=1, source_target_pairs={{0,1},{1,0},{2,3},{3,2},{4,5},{5,4},{6,7},{7,6},{8,9},{9,8},{10,11... | collective-permute-start | bytes 73736 | tf_op jit(solution)/shard_map/ppermute | solution.py:585
  188.6 3.7 %all-to-all-done.4.got = bf16[16,16,640]{2,1,0:T(8,128)(2,1)S(1)} async-done(((bf16[16,16,640]{2,1,0:T(8,128)(2,1)}), bf16[16,16,640]{2,1,0:T(8,128)(2,1)S(1)}, u32[]{:S(2)}, u32[]{:S(2)}) %all-to-all-start.4) | async-done | bytes 327712 | tf_op jit(solution)/shard_map/all_to_all | solution.py:574
  (63 shorter events, 29.5 us)
Async XLA Ops:
  0.6 6.4 %copy-start.1 = (f32[1,768]{1,0:T(1,128)S(1)}, f32[1,768]{1,0:T(1,128)}, u32[]{:S(2)}) copy-start(f32[1,768]{1,0:T(1,128)} %gains.9) | copy-start | bytes 9220
  0.6 6.4 %collective-permute-start = (bf16[48,768]{1,0:T(8,128)(2,1)}, bf16[48,768]{1,0:T(8,128)(2,1)S(1)}, u32[]{:S(2)}, u32[]{:S(2)}) collective-permute-start(bf16[48,768]{1,0:T(8,128)(2,1)} %bitcast.28), channel_id=1, source_target_pairs={{0,1},{1,0},{2,3},{3,2},{4,5},{5,4},{6,7},{7,6},{8,9},{9,8},{10,11... | collective-permute-start | bytes 221192 | tf_op jit(solution)/shard_map/ppermute | solution.py:433
  3.9 2.3 %copy-start = (bf16[1,768,3072]{2,1,0:T(8,128)(2,1)S(1)}, bf16[1,768,3072]{2,1,0:T(8,128)(2,1)}, u32[]{:S(2)}) copy-start(bf16[1,768,3072]{2,1,0:T(8,128)(2,1)} %param.9) | copy-start | bytes 14155780
  6.2 0.7 copy-start.6
  6.9 0.9 copy-start.5
  6.9 2.4 %copy-start.2 = (bf16[1,16,768]{2,1,0:T(8,128)(2,1)S(1)}, bf16[1,16,768]{2,1,0:T(8,128)(2,1)}, u32[]{:S(2)}) copy-start(bf16[1,16,768]{2,1,0:T(8,128)(2,1)} %param.11) | copy-start | bytes 73732
  6.9 39.4 %slice-start = ((s8[4718592]{0:T(1024)(128)(4,1)}), s8[4194304]{0:T(1024)(128)(4,1)S(1)}, s32[]{:S(2)}) async-start(s8[4718592]{0:T(1024)(128)(4,1)} %bitcast.15), calls=%async_computation.5 | async-start | bytes 8388608
  7.0 26.9 %copy-start.3 = (bf16[1,1,2,48,768]{4,3,2,1,0:T(8,128)(2,1)S(1)}, bf16[1,1,2,48,768]{4,3,2,1,0:T(8,128)(2,1)}, u32[]{:S(2)}) copy-start(bf16[1,1,2,48,768]{4,3,2,1,0:T(8,128)(2,1)} %param.13) | copy-start | bytes 442372
  7.0 26.9 %copy-start.4 = (bf16[1,48,768]{2,1,0:T(8,128)(2,1)S(1)}, bf16[1,48,768]{2,1,0:T(8,128)(2,1)}, u32[]{:S(2)}) copy-start(bf16[1,48,768]{2,1,0:T(8,128)(2,1)} %param.15) | copy-start | bytes 221188
  7.0 26.9 %copy-start.7 = (s32[1,1,4]{2,1,0:T(1,128)S(1)}, s32[1,1,4]{2,1,0:T(1,128)}, u32[]{:S(2)}) copy-start(s32[1,1,4]{2,1,0:T(1,128)} %param.16) | copy-start | bytes 52
  7.0 39.3 %slice-start.1 = ((s8[4718592]{0:T(1024)(128)(4,1)}), s8[524288]{0:T(1024)(128)(4,1)S(1)}, s32[]{:S(2)}) async-start(s8[4718592]{0:T(1024)(128)(4,1)} %bitcast.15), calls=%async_computation.6 | async-start | bytes 1048576
  9.4 4.3 %collective-permute-start.1 = (bf16[112,2048]{1,0:T(8,128)(2,1)S(1)}, bf16[112,2048]{1,0:T(8,128)(2,1)S(1)}, u32[]{:S(2)}, u32[]{:S(2)}) collective-permute-start(bf16[112,2048]{1,0:T(8,128)(2,1)S(1)} %shard_map.97), channel_id=1, source_target_pairs={{0,2},{2,0},{4,6},{6,4},{8,10},{10,8},{12,14},{14,12},{1,3},{3,1},... | collective-permute-start | bytes 1376264 | tf_op jit(solution)/shard_map/ppermute | solution.py:71
  30.4 4.7 %collective-permute-start.2 = (bf16[96,384]{1,0:T(8,128)(2,1)S(1)}, bf16[96,384]{1,0:T(8,128)(2,1)S(1)}, u32[]{:S(2)}, u32[]{:S(2)}) collective-permute-start(bf16[96,384]{1,0:T(8,128)(2,1)S(1)} %get-tuple-element.57.mine.after), channel_id=1, source_target_pairs={{0,2},{2,0},{4,6},{6,4},{8,10},{10,8},{12,14},{14,12},{1,3},{3,1},... | collective-permute-start | bytes 221192 | tf_op jit(solution)/shard_map/ppermute | solution.py:71
  34.5 11.8 %collective-permute-start.4 = (bf16[3,48,768]{2,1,0:T(8,128)(2,1)S(1)}, bf16[3,48,768]{2,1,0:T(8,128)(2,1)S(1)}, u32[]{:S(2)}, u32[]{:S(2)}) collective-permute-start(bf16[3,48,768]{2,1,0:T(8,128)(2,1)S(1)} %get-tuple-element.58.refs_1_), channel_id=1, source_target_pairs={{0,1},{1,0},{2,3},{3,2},{4,5},{5,4},{6,7},{7,6},{8,9},{9,8},{10,11... | collective-permute-start | bytes 663560 | tf_op jit(solution)/shard_map/ppermute | solution.py:524
  35.2 11.1 %collective-permute-start.3 = (bf16[96,768]{1,0:T(8,128)(2,1)S(1)}, bf16[96,768]{1,0:T(8,128)(2,1)S(1)}, u32[]{:S(2)}, u32[]{:S(2)}) collective-permute-start(bf16[96,768]{1,0:T(8,128)(2,1)S(1)} %shard_map.100.refs_1_), channel_id=1, source_target_pairs={{0,16},{2,17},{12,18},{14,19},{4,20},{6,21},{8,22},{10,23},{9,24},... | collective-permute-start | bytes 442376 | tf_op jit(solution)/shard_map/ppermute | solution.py:67
  38.9 8.8 %collective-permute-start.5 = (bf16[48,768]{1,0:T(8,128)(2,1)S(1)}, bf16[48,768]{1,0:T(8,128)(2,1)S(1)}, u32[]{:S(2)}, u32[]{:S(2)}) collective-permute-start(bf16[48,768]{1,0:T(8,128)(2,1)S(1)} %get-tuple-element.62), channel_id=1, source_target_pairs={{0,0},{1,2},{2,12},{3,14},{4,4},{5,6},{6,8},{7,10},{8,9},{9,11},{1... | collective-permute-start | bytes 221192 | tf_op jit(solution)/shard_map/ppermute | solution.py:58
  47.8 3.7 %collective-permute-start.6 = (bf16[96,2432]{1,0:T(8,128)(2,1)S(1)}, bf16[96,2432]{1,0:T(8,128)(2,1)S(1)}, u32[]{:S(2)}, u32[]{:S(2)}) collective-permute-start(bf16[96,2432]{1,0:T(8,128)(2,1)S(1)} %get-tuple-element.63), channel_id=1, source_target_pairs={{0,2},{2,0},{4,6},{6,4},{8,10},{10,8},{12,14},{14,12},{1,3},{3,1},... | collective-permute-start | bytes 1400840 | tf_op jit(solution)/shard_map/ppermute | solution.py:71
  69.0 4.8 %collective-permute-start.7 = (bf16[96,2048]{1,0:T(8,128)(2,1)S(1)}, bf16[96,2048]{1,0:T(8,128)(2,1)S(1)}, u32[]{:S(2)}, u32[]{:S(2)}) collective-permute-start(bf16[96,2048]{1,0:T(8,128)(2,1)S(1)} %get-tuple-element.70.mine), channel_id=1, source_target_pairs={{0,2},{2,0},{4,6},{6,4},{8,10},{10,8},{12,14},{14,12},{1,3},{3,1},... | collective-permute-start | bytes 1179656 | tf_op jit(solution)/shard_map/ppermute | solution.py:71
  73.8 11.9 %collective-permute-start.8 = (bf16[96,768]{1,0:T(8,128)(2,1)S(1)}, bf16[96,768]{1,0:T(8,128)(2,1)S(1)}, u32[]{:S(2)}, u32[]{:S(2)}) collective-permute-start(bf16[96,768]{1,0:T(8,128)(2,1)S(1)} %shard_map.106.refs_1_), channel_id=1, source_target_pairs={{0,16},{2,17},{12,18},{14,19},{4,20},{6,21},{8,22},{10,23},{9,24},... | collective-permute-start | bytes 442376 | tf_op jit(solution)/shard_map/ppermute | solution.py:67
  80.7 10.5 %collective-permute-start.9 = (bf16[96,768]{1,0:T(8,128)(2,1)S(1)}, bf16[96,768]{1,0:T(8,128)(2,1)S(1)}, u32[]{:S(2)}, u32[]{:S(2)}) collective-permute-start(bf16[96,768]{1,0:T(8,128)(2,1)S(1)} %get-tuple-element.75), channel_id=1, source_target_pairs={{16,0},{17,2},{18,12},{19,14},{20,4},{21,6},{22,8},{23,10},{24,9},... | collective-permute-start | bytes 442376 | tf_op jit(solution)/shard_map/ppermute | solution.py:58
  91.3 3.7 %collective-permute-start.10 = (bf16[96,2432]{1,0:T(8,128)(2,1)S(1)}, bf16[96,2432]{1,0:T(8,128)(2,1)S(1)}, u32[]{:S(2)}, u32[]{:S(2)}) collective-permute-start(bf16[96,2432]{1,0:T(8,128)(2,1)S(1)} %get-tuple-element.76), channel_id=1, source_target_pairs={{0,2},{2,0},{4,6},{6,4},{8,10},{10,8},{12,14},{14,12},{1,3},{3,1},... | collective-permute-start | bytes 1400840 | tf_op jit(solution)/shard_map/ppermute | solution.py:71
  113.7 4.8 %collective-permute-start.11 = (bf16[96,2048]{1,0:T(8,128)(2,1)S(1)}, bf16[96,2048]{1,0:T(8,128)(2,1)S(1)}, u32[]{:S(2)}, u32[]{:S(2)}) collective-permute-start(bf16[96,2048]{1,0:T(8,128)(2,1)S(1)} %get-tuple-element.80.mine), channel_id=1, source_target_pairs={{0,2},{2,0},{4,6},{6,4},{8,10},{10,8},{12,14},{14,12},{1,3},{3,1},... | collective-permute-start | bytes 1179656 | tf_op jit(solution)/shard_map/ppermute | solution.py:71
  118.5 12.1 %collective-permute-start.12 = (bf16[96,768]{1,0:T(8,128)(2,1)S(1)}, bf16[96,768]{1,0:T(8,128)(2,1)S(1)}, u32[]{:S(2)}, u32[]{:S(2)}) collective-permute-start(bf16[96,768]{1,0:T(8,128)(2,1)S(1)} %shard_map.112.refs_1_), channel_id=1, source_target_pairs={{0,16},{2,17},{12,18},{14,19},{4,20},{6,21},{8,22},{10,23},{9,24},... | collective-permute-start | bytes 442376 | tf_op jit(solution)/shard_map/ppermute | solution.py:67
  128.1 9.3 %collective-permute-start.13 = (bf16[96,768]{1,0:T(8,128)(2,1)S(1)}, bf16[96,768]{1,0:T(8,128)(2,1)S(1)}, u32[]{:S(2)}, u32[]{:S(2)}) collective-permute-start(bf16[96,768]{1,0:T(8,128)(2,1)S(1)} %get-tuple-element.85), channel_id=1, source_target_pairs={{16,0},{17,2},{18,12},{19,14},{20,4},{21,6},{22,8},{23,10},{24,9},... | collective-permute-start | bytes 442376 | tf_op jit(solution)/shard_map/ppermute | solution.py:58
  137.4 3.7 %collective-permute-start.14 = (bf16[96,2432]{1,0:T(8,128)(2,1)S(1)}, bf16[96,2432]{1,0:T(8,128)(2,1)S(1)}, u32[]{:S(2)}, u32[]{:S(2)}) collective-permute-start(bf16[96,2432]{1,0:T(8,128)(2,1)S(1)} %get-tuple-element.86), channel_id=1, source_target_pairs={{0,2},{2,0},{4,6},{6,4},{8,10},{10,8},{12,14},{14,12},{1,3},{3,1},... | collective-permute-start | bytes 1400840 | tf_op jit(solution)/shard_map/ppermute | solution.py:71
  161.1 4.8 %collective-permute-start.15 = (bf16[96,2048]{1,0:T(8,128)(2,1)S(1)}, bf16[96,2048]{1,0:T(8,128)(2,1)S(1)}, u32[]{:S(2)}, u32[]{:S(2)}) collective-permute-start(bf16[96,2048]{1,0:T(8,128)(2,1)S(1)} %get-tuple-element.90.mine), channel_id=1, source_target_pairs={{0,2},{2,0},{4,6},{6,4},{8,10},{10,8},{12,14},{14,12},{1,3},{3,1},... | collective-permute-start | bytes 1179656 | tf_op jit(solution)/shard_map/ppermute | solution.py:71
  167.7 11.3 %collective-permute-start.16 = (bf16[96,768]{1,0:T(8,128)(2,1)S(1)}, bf16[96,768]{1,0:T(8,128)(2,1)S(1)}, u32[]{:S(2)}, u32[]{:S(2)}) collective-permute-start(bf16[96,768]{1,0:T(8,128)(2,1)S(1)} %get-tuple-element.92.after), channel_id=1, source_target_pairs={{16,0},{32,16},{48,32},{64,48},{80,64},{96,80},{112,96},{128,112},... | collective-permute-start | bytes 442376 | tf_op jit(solution)/shard_map/ppermute | solution.py:404
  169.7 9.3 %collective-permute-start.17 = (bf16[96,768]{1,0:T(8,128)(2,1)S(1)}, bf16[96,768]{1,0:T(8,128)(2,1)S(1)}, u32[]{:S(2)}, u32[]{:S(2)}) collective-permute-start(bf16[96,768]{1,0:T(8,128)(2,1)S(1)} %shard_map.119), channel_id=1, source_target_pairs={{496,496},{508,498},{500,500},{504,502},{505,504},{501,506},{509,5... | collective-permute-start | bytes 442376 | tf_op jit(solution)/shard_map/ppermute | solution.py:410
  171.7 7.3 %collective-permute-start.18 = (f32[16,768]{1,0:T(8,128)S(1)}, f32[16,768]{1,0:T(8,128)S(1)}, u32[]{:S(2)}, u32[]{:S(2)}) collective-permute-start(f32[16,768]{1,0:T(8,128)S(1)} %get-tuple-element.101.mine), channel_id=1, source_target_pairs={{0,1},{1,0},{2,3},{3,2},{4,5},{5,4},{6,7},{7,6},{8,9},{9,8},{10,11... | collective-permute-start | bytes 147464 | tf_op jit(solution)/shard_map/ppermute | solution.py:560
  179.9 12.4 %all-to-all-start.4 = ((bf16[16,16,640]{2,1,0:T(8,128)(2,1)}), bf16[16,16,640]{2,1,0:T(8,128)(2,1)S(1)}, u32[]{:S(2)}, u32[]{:S(2)}) async-start(bf16[16,16,640]{2,1,0:T(8,128)(2,1)} %get-tuple-element.102), calls=%async_computation.4 | async-start | bytes 655360 | tf_op jit(solution)/shard_map/all_to_all | solution.py:574
  183.7 4.9 %collective-permute-start.19 = (bf16[16,768]{1,0:T(8,128)(2,1)S(1)}, bf16[16,768]{1,0:T(8,128)(2,1)S(1)}, u32[]{:S(2)}, u32[]{:S(2)}) collective-permute-start(bf16[16,768]{1,0:T(8,128)(2,1)S(1)} %get-tuple-element.103.up_mine), channel_id=1, source_target_pairs={{0,1},{1,0},{2,3},{3,2},{4,5},{5,4},{6,7},{7,6},{8,9},{9,8},{10,11... | collective-permute-start | bytes 73736 | tf_op jit(solution)/shard_map/ppermute | solution.py:585

commit v10 on v9

--- a/solution.py
+++ b/solution.py
@@ -314,7 +314,8 @@
             out[:, at : at + width] = got[j, :, feats + LANES :]
 
 
-def whole_kernel(mine, theirs, output):
+def whole_kernel(mine, theirs, *refs):
+    output = refs[-1]
     width = output.shape[1] // 2
     output[...] = both_halves(mine[:, :width], theirs[:, :width])
 
@@ -508,9 +509,6 @@
             own, stats, *mixed = call(kernel, out, got, up, gain_w, gain_low)
             mixed = mixed[0] if mixed else None
         other = swap_cores(own)
-        output = call(whole_kernel, block, own, other)
-        if tick < TICKS - 1:
-            arrived = to_next(output, sections)
         if start:
             chosen, grads_out = call(
                 prepare_kernel,
@@ -544,6 +542,9 @@
                 grad_arrived = to_owner(grad_x, sections, 1)
             else:
                 grad_arrived = to_same(grad_x, sections)
+        output = call(whole_kernel, block, own, other, *([] if start else [grad_x]))
+        if tick < TICKS - 1:
+            arrived = to_next(output, sections)
         xs.append(x)
         all_stats.append(stats)
 

time: 194 us -> 195 us (level)
  transfers between devices with their start and end apart: 21 -> 21, of which waited for: 13 -> 15; matrix products, arithmetic and copies ran while one was open for 0% -> 0% of each run, Pallas kernels for 5% -> 3%
where the time goes in v10:
time: 195 us; the launch traced here: 194 us
  blocking collectives  68.6 us (35%)
  starting transfers between devices  67.4 us (35%)
  waiting for transfers between devices  33.5 us (17%)
  Pallas kernels  19.6 us (10%)
  local copies, waits for them, and re-layouts  3.89 us (2%)
    all_to_all x4, blocking collectives, over_chips(): return lax.all_to_all(array, 'tensor', 0, 0, axis_index_groups=groups)  68.6 us
    ppermute x8, starting transfers between devices, swap_cores(): return lax.ppermute(array, 'tensor', [(i, i ^ 1) for i in range(2 * CHIPS)])  22.4 us
    pallas_call x28, Pallas kernels, call(): pl.pallas_call(kernel, out_shape=out, in_specs=[pl.BlockSpec(memory_space...  19.6 us
    ppermute x3, starting transfers between devices, to_next(): return lax.ppermute(array, AXES, route)  16.5 us
    ppermute x3, starting transfers between devices, to_owner(): return lax.ppermute(array, AXES, route)  13 us
    ppermute x8, waiting for transfers between devices, swap_cores(): return lax.ppermute(array, 'tensor', [(i, i ^ 1) for i in range(2 * CHIPS)])  10.8 us
    ppermute x3, waiting for transfers between devices, to_owner(): return lax.ppermute(array, AXES, route)  7.9 us
    ppermute x1, waiting for transfers between devices, on_device(): acc_other = lax.ppermute(acc_down, 'dp', [(0, 1), (1, 0)])  5.97 us
  transfers between devices with their start and end apart: 21, of which 15 were waited for; matrix products, arithmetic and copies ran while one was open for 0% of the time, Pallas kernels for 3%

profile of v10, /device:TPU:225, one launch (start us, length us, event | category | flops | bytes accessed | tf_op | source)
XLA Modules:
  0.0 194.0 jit_solution(712945883134033979)
XLA Ops:
  0.6 3.2 %collective-permute-start = (bf16[48,768]{1,0:T(8,128)(2,1)}, bf16[48,768]{1,0:T(8,128)(2,1)S(1)}, u32[]{:S(2)}, u32[]{:S(2)}) collective-permute-start(bf16[48,768]{1,0:T(8,128)(2,1)} %bitcast.28), channel_id=1, source_target_pairs={{0,1},{1,0},{2,3},{3,2},{4,5},{5,4},{6,7},{7,6},{8,9},{9,8},{10,11... | collective-permute-start | bytes 221192 | tf_op jit(solution)/shard_map/ppermute | solution.py:434
  3.9 2.3 %copy-done = bf16[1,768,3072]{2,1,0:T(8,128)(2,1)S(1)} copy-done((bf16[1,768,3072]{2,1,0:T(8,128)(2,1)S(1)}, bf16[1,768,3072]{2,1,0:T(8,128)(2,1)}, u32[]{:S(2)}) %copy-start) | copy-done | bytes 4718616
  9.4 2.9 %collective-permute-start.1 = (bf16[112,2048]{1,0:T(8,128)(2,1)S(1)}, bf16[112,2048]{1,0:T(8,128)(2,1)S(1)}, u32[]{:S(2)}, u32[]{:S(2)}) collective-permute-start(bf16[112,2048]{1,0:T(8,128)(2,1)S(1)} %shard_map.97), channel_id=1, source_target_pairs={{0,2},{2,0},{4,6},{6,4},{8,10},{10,8},{12,14},{14,12},{1,3},{3,1},... | collective-permute-start | bytes 1376264 | tf_op jit(solution)/shard_map/ppermute | solution.py:71
  14.1 15.7 %all_to_all.25.got = bf16[4,112,896]{2,1,0:T(8,128)(2,1)S(1)} all-to-all(bf16[4,112,896]{2,1,0:T(8,128)(2,1)S(1)} %shard_map.98), channel_id=1, replica_groups={{0,4,8,12},{2,6,10,14},{1,5,9,13},{3,7,11,15},{16,20,24,28},{18,22,26,3..., dimensions={0} | all-to-all | bytes 1605632 | tf_op jit(solution)/shard_map/all_to_all | solution.py:76
  30.4 3.4 %collective-permute-start.2 = (bf16[96,384]{1,0:T(8,128)(2,1)S(1)}, bf16[96,384]{1,0:T(8,128)(2,1)S(1)}, u32[]{:S(2)}, u32[]{:S(2)}) collective-permute-start(bf16[96,384]{1,0:T(8,128)(2,1)S(1)} %get-tuple-element.57.mine.after), channel_id=1, source_target_pairs={{0,2},{2,0},{4,6},{6,4},{8,10},{10,8},{12,14},{14,12},{1,3},{3,1},... | collective-permute-start | bytes 221192 | tf_op jit(solution)/shard_map/ppermute | solution.py:71
  35.2 3.7 %collective-permute-start.3 = (bf16[96,768]{1,0:T(8,128)(2,1)S(1)}, bf16[96,768]{1,0:T(8,128)(2,1)S(1)}, u32[]{:S(2)}, u32[]{:S(2)}) collective-permute-start(bf16[96,768]{1,0:T(8,128)(2,1)S(1)} %shard_map.100.refs_1_), channel_id=1, source_target_pairs={{0,16},{2,17},{12,18},{14,19},{4,20},{6,21},{8,22},{10,23},{9,24},... | collective-permute-start | bytes 442376 | tf_op jit(solution)/shard_map/ppermute | solution.py:67
  38.9 5.4 %collective-permute-start.5 = (bf16[48,768]{1,0:T(8,128)(2,1)S(1)}, bf16[48,768]{1,0:T(8,128)(2,1)S(1)}, u32[]{:S(2)}, u32[]{:S(2)}) collective-permute-start(bf16[48,768]{1,0:T(8,128)(2,1)S(1)} %get-tuple-element.62), channel_id=1, source_target_pairs={{0,0},{1,2},{2,12},{3,14},{4,4},{5,6},{6,8},{7,10},{8,9},{9,11},{1... | collective-permute-start | bytes 221192 | tf_op jit(solution)/shard_map/ppermute | solution.py:58
  44.3 2.0 %collective-permute-done.3.refs_0_ = bf16[96,768]{1,0:T(8,128)(2,1)S(1)} collective-permute-done((bf16[96,768]{1,0:T(8,128)(2,1)S(1)}, bf16[96,768]{1,0:T(8,128)(2,1)S(1)}, u32[]{:S(2)}, u32[]{:S(2)}) %collective-permute-start.3) | collective-permute-done | bytes 147488 | tf_op jit(solution)/shard_map/ppermute | solution.py:67
  47.8 1.9 collective-permute-start.6
  52.0 16.4 %all_to_all.26.got = bf16[4,96,1280]{2,1,0:T(8,128)(2,1)S(1)} all-to-all(bf16[4,96,1280]{2,1,0:T(8,128)(2,1)S(1)} %get-tuple-element.68), channel_id=1, replica_groups={{0,4,8,12},{2,6,10,14},{1,5,9,13},{3,7,11,15},{16,20,24,28},{18,22,26,3..., dimensions={0} | all-to-all | bytes 1966080 | tf_op jit(solution)/shard_map/all_to_all | solution.py:76
  69.0 3.5 %collective-permute-start.7 = (bf16[96,2048]{1,0:T(8,128)(2,1)S(1)}, bf16[96,2048]{1,0:T(8,128)(2,1)S(1)}, u32[]{:S(2)}, u32[]{:S(2)}) collective-permute-start(bf16[96,2048]{1,0:T(8,128)(2,1)S(1)} %get-tuple-element.70.mine), channel_id=1, source_target_pairs={{0,2},{2,0},{4,6},{6,4},{8,10},{10,8},{12,14},{14,12},{1,3},{3,1},... | collective-permute-start | bytes 1179656 | tf_op jit(solution)/shard_map/ppermute | solution.py:71
  73.8 1.8 shard_map.106
  75.6 5.1 %collective-permute-start.8 = (bf16[96,768]{1,0:T(8,128)(2,1)S(1)}, bf16[96,768]{1,0:T(8,128)(2,1)S(1)}, u32[]{:S(2)}, u32[]{:S(2)}) collective-permute-start(bf16[96,768]{1,0:T(8,128)(2,1)S(1)} %shard_map.107.refs_1_), channel_id=1, source_target_pairs={{0,16},{2,17},{12,18},{14,19},{4,20},{6,21},{8,22},{10,23},{9,24},... | collective-permute-start | bytes 442376 | tf_op jit(solution)/shard_map/ppermute | solution.py:67
  80.7 5.0 %collective-permute-start.9 = (bf16[96,768]{1,0:T(8,128)(2,1)S(1)}, bf16[96,768]{1,0:T(8,128)(2,1)S(1)}, u32[]{:S(2)}, u32[]{:S(2)}) collective-permute-start(bf16[96,768]{1,0:T(8,128)(2,1)S(1)} %get-tuple-element.72.refs_0_), channel_id=1, source_target_pairs={{16,0},{17,2},{18,12},{19,14},{20,4},{21,6},{22,8},{23,10},{24,9},... | collective-permute-start | bytes 442376 | tf_op jit(solution)/shard_map/ppermute | solution.py:58
  87.9 3.3 %collective-permute-done.9.refs_0_ = bf16[96,768]{1,0:T(8,128)(2,1)S(1)} collective-permute-done((bf16[96,768]{1,0:T(8,128)(2,1)S(1)}, bf16[96,768]{1,0:T(8,128)(2,1)S(1)}, u32[]{:S(2)}, u32[]{:S(2)}) %collective-permute-start.9) | collective-permute-done | bytes 147488 | tf_op jit(solution)/shard_map/ppermute | solution.py:58
  91.3 1.9 collective-permute-start.10
  95.5 17.6 %all_to_all.27.got = bf16[4,96,1280]{2,1,0:T(8,128)(2,1)S(1)} all-to-all(bf16[4,96,1280]{2,1,0:T(8,128)(2,1)S(1)} %get-tuple-element.79), channel_id=1, replica_groups={{0,4,8,12},{2,6,10,14},{1,5,9,13},{3,7,11,15},{16,20,24,28},{18,22,26,3..., dimensions={0} | all-to-all | bytes 1966080 | tf_op jit(solution)/shard_map/all_to_all | solution.py:76
  113.8 3.4 %collective-permute-start.11 = (bf16[96,2048]{1,0:T(8,128)(2,1)S(1)}, bf16[96,2048]{1,0:T(8,128)(2,1)S(1)}, u32[]{:S(2)}, u32[]{:S(2)}) collective-permute-start(bf16[96,2048]{1,0:T(8,128)(2,1)S(1)} %get-tuple-element.80.mine), channel_id=1, source_target_pairs={{0,2},{2,0},{4,6},{6,4},{8,10},{10,8},{12,14},{14,12},{1,3},{3,1},... | collective-permute-start | bytes 1179656 | tf_op jit(solution)/shard_map/ppermute | solution.py:71
  118.5 1.8 shard_map.112
  120.4 7.7 %collective-permute-start.12 = (bf16[96,768]{1,0:T(8,128)(2,1)S(1)}, bf16[96,768]{1,0:T(8,128)(2,1)S(1)}, u32[]{:S(2)}, u32[]{:S(2)}) collective-permute-start(bf16[96,768]{1,0:T(8,128)(2,1)S(1)} %shard_map.113.refs_1_), channel_id=1, source_target_pairs={{0,16},{2,17},{12,18},{14,19},{4,20},{6,21},{8,22},{10,23},{9,24},... | collective-permute-start | bytes 442376 | tf_op jit(solution)/shard_map/ppermute | solution.py:67
  128.1 2.6 %collective-permute-start.13 = (bf16[96,768]{1,0:T(8,128)(2,1)S(1)}, bf16[96,768]{1,0:T(8,128)(2,1)S(1)}, u32[]{:S(2)}, u32[]{:S(2)}) collective-permute-start(bf16[96,768]{1,0:T(8,128)(2,1)S(1)} %get-tuple-element.82.refs_0_), channel_id=1, source_target_pairs={{16,0},{17,2},{18,12},{19,14},{20,4},{21,6},{22,8},{23,10},{24,9},... | collective-permute-start | bytes 442376 | tf_op jit(solution)/shard_map/ppermute | solution.py:58
  132.7 4.6 %collective-permute-done.13.refs_0_ = bf16[96,768]{1,0:T(8,128)(2,1)S(1)} collective-permute-done((bf16[96,768]{1,0:T(8,128)(2,1)S(1)}, bf16[96,768]{1,0:T(8,128)(2,1)S(1)}, u32[]{:S(2)}, u32[]{:S(2)}) %collective-permute-start.13) | collective-permute-done | bytes 147488 | tf_op jit(solution)/shard_map/ppermute | solution.py:58
  137.4 1.9 collective-permute-start.14
  141.6 18.9 %all_to_all.28.got = bf16[4,96,1280]{2,1,0:T(8,128)(2,1)S(1)} all-to-all(bf16[4,96,1280]{2,1,0:T(8,128)(2,1)S(1)} %get-tuple-element.89), channel_id=1, replica_groups={{0,4,8,12},{2,6,10,14},{1,5,9,13},{3,7,11,15},{16,20,24,28},{18,22,26,3..., dimensions={0} | all-to-all | bytes 1966080 | tf_op jit(solution)/shard_map/all_to_all | solution.py:76
  161.1 3.4 %collective-permute-start.15 = (bf16[96,2048]{1,0:T(8,128)(2,1)S(1)}, bf16[96,2048]{1,0:T(8,128)(2,1)S(1)}, u32[]{:S(2)}, u32[]{:S(2)}) collective-permute-start(bf16[96,2048]{1,0:T(8,128)(2,1)S(1)} %get-tuple-element.90.mine), channel_id=1, source_target_pairs={{0,2},{2,0},{4,6},{6,4},{8,10},{10,8},{12,14},{14,12},{1,3},{3,1},... | collective-permute-start | bytes 1179656 | tf_op jit(solution)/shard_map/ppermute | solution.py:71
  165.9 1.8 shard_map.118
  168.4 1.9 collective-permute-start.16
  171.7 2.0 %collective-permute-start.18 = (f32[16,768]{1,0:T(8,128)S(1)}, f32[16,768]{1,0:T(8,128)S(1)}, u32[]{:S(2)}, u32[]{:S(2)}) collective-permute-start(f32[16,768]{1,0:T(8,128)S(1)} %get-tuple-element.101.mine), channel_id=1, source_target_pairs={{0,1},{1,0},{2,3},{3,2},{4,5},{5,4},{6,7},{7,6},{8,9},{9,8},{10,11... | collective-permute-start | bytes 147464 | tf_op jit(solution)/shard_map/ppermute | solution.py:561
  173.7 6.0 %collective-permute-done.18.after.theirs = f32[16,768]{1,0:T(8,128)S(1)} collective-permute-done((f32[16,768]{1,0:T(8,128)S(1)}, f32[16,768]{1,0:T(8,128)S(1)}, u32[]{:S(2)}, u32[]{:S(2)}) %collective-permute-start.18) | collective-permute-done | bytes 49184 | tf_op jit(solution)/shard_map/ppermute | solution.py:561
  180.7 3.8 %all-to-all-start.4 = ((bf16[16,16,640]{2,1,0:T(8,128)(2,1)}), bf16[16,16,640]{2,1,0:T(8,128)(2,1)S(1)}, u32[]{:S(2)}, u32[]{:S(2)}) async-start(bf16[16,16,640]{2,1,0:T(8,128)(2,1)} %get-tuple-element.102), calls=%async_computation.4 | async-start | bytes 655360 | tf_op jit(solution)/shard_map/all_to_all | solution.py:575
  184.5 3.3 %collective-permute-start.19 = (bf16[16,768]{1,0:T(8,128)(2,1)S(1)}, bf16[16,768]{1,0:T(8,128)(2,1)S(1)}, u32[]{:S(2)}, u32[]{:S(2)}) collective-permute-start(bf16[16,768]{1,0:T(8,128)(2,1)S(1)} %get-tuple-element.103.up_mine), channel_id=1, source_target_pairs={{0,1},{1,0},{2,3},{3,2},{4,5},{5,4},{6,7},{7,6},{8,9},{9,8},{10,11... | collective-permute-start | bytes 73736 | tf_op jit(solution)/shard_map/ppermute | solution.py:586
  189.3 3.7 %all-to-all-done.4.got = bf16[16,16,640]{2,1,0:T(8,128)(2,1)S(1)} async-done(((bf16[16,16,640]{2,1,0:T(8,128)(2,1)}), bf16[16,16,640]{2,1,0:T(8,128)(2,1)S(1)}, u32[]{:S(2)}, u32[]{:S(2)}) %all-to-all-start.4) | async-done | bytes 327712 | tf_op jit(solution)/shard_map/all_to_all | solution.py:575
  (63 shorter events, 31.1 us)
Async XLA Ops:
  0.6 6.4 %copy-start.1 = (f32[1,768]{1,0:T(1,128)S(1)}, f32[1,768]{1,0:T(1,128)}, u32[]{:S(2)}) copy-start(f32[1,768]{1,0:T(1,128)} %gains.9) | copy-start | bytes 9220
  0.6 6.4 %collective-permute-start = (bf16[48,768]{1,0:T(8,128)(2,1)}, bf16[48,768]{1,0:T(8,128)(2,1)S(1)}, u32[]{:S(2)}, u32[]{:S(2)}) collective-permute-start(bf16[48,768]{1,0:T(8,128)(2,1)} %bitcast.28), channel_id=1, source_target_pairs={{0,1},{1,0},{2,3},{3,2},{4,5},{5,4},{6,7},{7,6},{8,9},{9,8},{10,11... | collective-permute-start | bytes 221192 | tf_op jit(solution)/shard_map/ppermute | solution.py:434
  3.9 2.3 %copy-start = (bf16[1,768,3072]{2,1,0:T(8,128)(2,1)S(1)}, bf16[1,768,3072]{2,1,0:T(8,128)(2,1)}, u32[]{:S(2)}) copy-start(bf16[1,768,3072]{2,1,0:T(8,128)(2,1)} %param.9) | copy-start | bytes 14155780
  6.2 0.7 copy-start.6
  6.9 0.9 copy-start.5
  6.9 2.4 %copy-start.2 = (bf16[1,16,768]{2,1,0:T(8,128)(2,1)S(1)}, bf16[1,16,768]{2,1,0:T(8,128)(2,1)}, u32[]{:S(2)}) copy-start(bf16[1,16,768]{2,1,0:T(8,128)(2,1)} %param.11) | copy-start | bytes 73732
  6.9 39.4 %slice-start = ((s8[4718592]{0:T(1024)(128)(4,1)}), s8[4194304]{0:T(1024)(128)(4,1)S(1)}, s32[]{:S(2)}) async-start(s8[4718592]{0:T(1024)(128)(4,1)} %bitcast.15), calls=%async_computation.5 | async-start | bytes 8388608
  7.0 26.9 %copy-start.3 = (bf16[1,1,2,48,768]{4,3,2,1,0:T(8,128)(2,1)S(1)}, bf16[1,1,2,48,768]{4,3,2,1,0:T(8,128)(2,1)}, u32[]{:S(2)}) copy-start(bf16[1,1,2,48,768]{4,3,2,1,0:T(8,128)(2,1)} %param.13) | copy-start | bytes 442372
  7.0 26.9 %copy-start.4 = (bf16[1,48,768]{2,1,0:T(8,128)(2,1)S(1)}, bf16[1,48,768]{2,1,0:T(8,128)(2,1)}, u32[]{:S(2)}) copy-start(bf16[1,48,768]{2,1,0:T(8,128)(2,1)} %param.15) | copy-start | bytes 221188
  7.0 26.9 %copy-start.7 = (s32[1,1,4]{2,1,0:T(1,128)S(1)}, s32[1,1,4]{2,1,0:T(1,128)}, u32[]{:S(2)}) copy-start(s32[1,1,4]{2,1,0:T(1,128)} %param.16) | copy-start | bytes 52
  7.0 39.3 %slice-start.1 = ((s8[4718592]{0:T(1024)(128)(4,1)}), s8[524288]{0:T(1024)(128)(4,1)S(1)}, s32[]{:S(2)}) async-start(s8[4718592]{0:T(1024)(128)(4,1)} %bitcast.15), calls=%async_computation.6 | async-start | bytes 1048576
  9.4 4.3 %collective-permute-start.1 = (bf16[112,2048]{1,0:T(8,128)(2,1)S(1)}, bf16[112,2048]{1,0:T(8,128)(2,1)S(1)}, u32[]{:S(2)}, u32[]{:S(2)}) collective-permute-start(bf16[112,2048]{1,0:T(8,128)(2,1)S(1)} %shard_map.97), channel_id=1, source_target_pairs={{0,2},{2,0},{4,6},{6,4},{8,10},{10,8},{12,14},{14,12},{1,3},{3,1},... | collective-permute-start | bytes 1376264 | tf_op jit(solution)/shard_map/ppermute | solution.py:71
  30.4 4.7 %collective-permute-start.2 = (bf16[96,384]{1,0:T(8,128)(2,1)S(1)}, bf16[96,384]{1,0:T(8,128)(2,1)S(1)}, u32[]{:S(2)}, u32[]{:S(2)}) collective-permute-start(bf16[96,384]{1,0:T(8,128)(2,1)S(1)} %get-tuple-element.57.mine.after), channel_id=1, source_target_pairs={{0,2},{2,0},{4,6},{6,4},{8,10},{10,8},{12,14},{14,12},{1,3},{3,1},... | collective-permute-start | bytes 221192 | tf_op jit(solution)/shard_map/ppermute | solution.py:71
  34.5 11.8 %collective-permute-start.4 = (bf16[3,48,768]{2,1,0:T(8,128)(2,1)S(1)}, bf16[3,48,768]{2,1,0:T(8,128)(2,1)S(1)}, u32[]{:S(2)}, u32[]{:S(2)}) collective-permute-start(bf16[3,48,768]{2,1,0:T(8,128)(2,1)S(1)} %get-tuple-element.58.refs_1_), channel_id=1, source_target_pairs={{0,1},{1,0},{2,3},{3,2},{4,5},{5,4},{6,7},{7,6},{8,9},{9,8},{10,11... | collective-permute-start | bytes 663560 | tf_op jit(solution)/shard_map/ppermute | solution.py:522
  35.2 11.1 %collective-permute-start.3 = (bf16[96,768]{1,0:T(8,128)(2,1)S(1)}, bf16[96,768]{1,0:T(8,128)(2,1)S(1)}, u32[]{:S(2)}, u32[]{:S(2)}) collective-permute-start(bf16[96,768]{1,0:T(8,128)(2,1)S(1)} %shard_map.100.refs_1_), channel_id=1, source_target_pairs={{0,16},{2,17},{12,18},{14,19},{4,20},{6,21},{8,22},{10,23},{9,24},... | collective-permute-start | bytes 442376 | tf_op jit(solution)/shard_map/ppermute | solution.py:67
  38.9 8.8 %collective-permute-start.5 = (bf16[48,768]{1,0:T(8,128)(2,1)S(1)}, bf16[48,768]{1,0:T(8,128)(2,1)S(1)}, u32[]{:S(2)}, u32[]{:S(2)}) collective-permute-start(bf16[48,768]{1,0:T(8,128)(2,1)S(1)} %get-tuple-element.62), channel_id=1, source_target_pairs={{0,0},{1,2},{2,12},{3,14},{4,4},{5,6},{6,8},{7,10},{8,9},{9,11},{1... | collective-permute-start | bytes 221192 | tf_op jit(solution)/shard_map/ppermute | solution.py:58
  47.8 3.7 %collective-permute-start.6 = (bf16[96,2432]{1,0:T(8,128)(2,1)S(1)}, bf16[96,2432]{1,0:T(8,128)(2,1)S(1)}, u32[]{:S(2)}, u32[]{:S(2)}) collective-permute-start(bf16[96,2432]{1,0:T(8,128)(2,1)S(1)} %get-tuple-element.63), channel_id=1, source_target_pairs={{0,2},{2,0},{4,6},{6,4},{8,10},{10,8},{12,14},{14,12},{1,3},{3,1},... | collective-permute-start | bytes 1400840 | tf_op jit(solution)/shard_map/ppermute | solution.py:71
  69.0 4.8 %collective-permute-start.7 = (bf16[96,2048]{1,0:T(8,128)(2,1)S(1)}, bf16[96,2048]{1,0:T(8,128)(2,1)S(1)}, u32[]{:S(2)}, u32[]{:S(2)}) collective-permute-start(bf16[96,2048]{1,0:T(8,128)(2,1)S(1)} %get-tuple-element.70.mine), channel_id=1, source_target_pairs={{0,2},{2,0},{4,6},{6,4},{8,10},{10,8},{12,14},{14,12},{1,3},{3,1},... | collective-permute-start | bytes 1179656 | tf_op jit(solution)/shard_map/ppermute | solution.py:71
  75.6 11.0 %collective-permute-start.8 = (bf16[96,768]{1,0:T(8,128)(2,1)S(1)}, bf16[96,768]{1,0:T(8,128)(2,1)S(1)}, u32[]{:S(2)}, u32[]{:S(2)}) collective-permute-start(bf16[96,768]{1,0:T(8,128)(2,1)S(1)} %shard_map.107.refs_1_), channel_id=1, source_target_pairs={{0,16},{2,17},{12,18},{14,19},{4,20},{6,21},{8,22},{10,23},{9,24},... | collective-permute-start | bytes 442376 | tf_op jit(solution)/shard_map/ppermute | solution.py:67
  80.7 10.5 %collective-permute-start.9 = (bf16[96,768]{1,0:T(8,128)(2,1)S(1)}, bf16[96,768]{1,0:T(8,128)(2,1)S(1)}, u32[]{:S(2)}, u32[]{:S(2)}) collective-permute-start(bf16[96,768]{1,0:T(8,128)(2,1)S(1)} %get-tuple-element.72.refs_0_), channel_id=1, source_target_pairs={{16,0},{17,2},{18,12},{19,14},{20,4},{21,6},{22,8},{23,10},{24,9},... | collective-permute-start | bytes 442376 | tf_op jit(solution)/shard_map/ppermute | solution.py:58
  91.3 3.7 %collective-permute-start.10 = (bf16[96,2432]{1,0:T(8,128)(2,1)S(1)}, bf16[96,2432]{1,0:T(8,128)(2,1)S(1)}, u32[]{:S(2)}, u32[]{:S(2)}) collective-permute-start(bf16[96,2432]{1,0:T(8,128)(2,1)S(1)} %get-tuple-element.76), channel_id=1, source_target_pairs={{0,2},{2,0},{4,6},{6,4},{8,10},{10,8},{12,14},{14,12},{1,3},{3,1},... | collective-permute-start | bytes 1400840 | tf_op jit(solution)/shard_map/ppermute | solution.py:71
  113.8 4.8 %collective-permute-start.11 = (bf16[96,2048]{1,0:T(8,128)(2,1)S(1)}, bf16[96,2048]{1,0:T(8,128)(2,1)S(1)}, u32[]{:S(2)}, u32[]{:S(2)}) collective-permute-start(bf16[96,2048]{1,0:T(8,128)(2,1)S(1)} %get-tuple-element.80.mine), channel_id=1, source_target_pairs={{0,2},{2,0},{4,6},{6,4},{8,10},{10,8},{12,14},{14,12},{1,3},{3,1},... | collective-permute-start | bytes 1179656 | tf_op jit(solution)/shard_map/ppermute | solution.py:71
  120.4 11.0 %collective-permute-start.12 = (bf16[96,768]{1,0:T(8,128)(2,1)S(1)}, bf16[96,768]{1,0:T(8,128)(2,1)S(1)}, u32[]{:S(2)}, u32[]{:S(2)}) collective-permute-start(bf16[96,768]{1,0:T(8,128)(2,1)S(1)} %shard_map.113.refs_1_), channel_id=1, source_target_pairs={{0,16},{2,17},{12,18},{14,19},{4,20},{6,21},{8,22},{10,23},{9,24},... | collective-permute-start | bytes 442376 | tf_op jit(solution)/shard_map/ppermute | solution.py:67
  128.1 9.3 %collective-permute-start.13 = (bf16[96,768]{1,0:T(8,128)(2,1)S(1)}, bf16[96,768]{1,0:T(8,128)(2,1)S(1)}, u32[]{:S(2)}, u32[]{:S(2)}) collective-permute-start(bf16[96,768]{1,0:T(8,128)(2,1)S(1)} %get-tuple-element.82.refs_0_), channel_id=1, source_target_pairs={{16,0},{17,2},{18,12},{19,14},{20,4},{21,6},{22,8},{23,10},{24,9},... | collective-permute-start | bytes 442376 | tf_op jit(solution)/shard_map/ppermute | solution.py:58
  137.4 3.7 %collective-permute-start.14 = (bf16[96,2432]{1,0:T(8,128)(2,1)S(1)}, bf16[96,2432]{1,0:T(8,128)(2,1)S(1)}, u32[]{:S(2)}, u32[]{:S(2)}) collective-permute-start(bf16[96,2432]{1,0:T(8,128)(2,1)S(1)} %get-tuple-element.86), channel_id=1, source_target_pairs={{0,2},{2,0},{4,6},{6,4},{8,10},{10,8},{12,14},{14,12},{1,3},{3,1},... | collective-permute-start | bytes 1400840 | tf_op jit(solution)/shard_map/ppermute | solution.py:71
  161.1 4.8 %collective-permute-start.15 = (bf16[96,2048]{1,0:T(8,128)(2,1)S(1)}, bf16[96,2048]{1,0:T(8,128)(2,1)S(1)}, u32[]{:S(2)}, u32[]{:S(2)}) collective-permute-start(bf16[96,2048]{1,0:T(8,128)(2,1)S(1)} %get-tuple-element.90.mine), channel_id=1, source_target_pairs={{0,2},{2,0},{4,6},{6,4},{8,10},{10,8},{12,14},{14,12},{1,3},{3,1},... | collective-permute-start | bytes 1179656 | tf_op jit(solution)/shard_map/ppermute | solution.py:71
  167.7 12.0 %collective-permute-start.17 = (bf16[96,768]{1,0:T(8,128)(2,1)S(1)}, bf16[96,768]{1,0:T(8,128)(2,1)S(1)}, u32[]{:S(2)}, u32[]{:S(2)}) collective-permute-start(bf16[96,768]{1,0:T(8,128)(2,1)S(1)} %shard_map.119), channel_id=1, source_target_pairs={{496,496},{508,498},{500,500},{504,502},{505,504},{501,506},{509,5... | collective-permute-start | bytes 442376 | tf_op jit(solution)/shard_map/ppermute | solution.py:411
  168.4 11.3 %collective-permute-start.16 = (bf16[96,768]{1,0:T(8,128)(2,1)S(1)}, bf16[96,768]{1,0:T(8,128)(2,1)S(1)}, u32[]{:S(2)}, u32[]{:S(2)}) collective-permute-start(bf16[96,768]{1,0:T(8,128)(2,1)S(1)} %get-tuple-element.92.refs_0_.after), channel_id=1, source_target_pairs={{16,0},{32,16},{48,32},{64,48},{80,64},{96,80},{112,96},{128,112},... | collective-permute-start | bytes 442376 | tf_op jit(solution)/shard_map/ppermute | solution.py:405
  171.7 8.0 %collective-permute-start.18 = (f32[16,768]{1,0:T(8,128)S(1)}, f32[16,768]{1,0:T(8,128)S(1)}, u32[]{:S(2)}, u32[]{:S(2)}) collective-permute-start(f32[16,768]{1,0:T(8,128)S(1)} %get-tuple-element.101.mine), channel_id=1, source_target_pairs={{0,1},{1,0},{2,3},{3,2},{4,5},{5,4},{6,7},{7,6},{8,9},{9,8},{10,11... | collective-permute-start | bytes 147464 | tf_op jit(solution)/shard_map/ppermute | solution.py:561
  180.7 12.4 %all-to-all-start.4 = ((bf16[16,16,640]{2,1,0:T(8,128)(2,1)}), bf16[16,16,640]{2,1,0:T(8,128)(2,1)S(1)}, u32[]{:S(2)}, u32[]{:S(2)}) async-start(bf16[16,16,640]{2,1,0:T(8,128)(2,1)} %get-tuple-element.102), calls=%async_computation.4 | async-start | bytes 655360 | tf_op jit(solution)/shard_map/all_to_all | solution.py:575
  184.5 4.9 %collective-permute-start.19 = (bf16[16,768]{1,0:T(8,128)(2,1)S(1)}, bf16[16,768]{1,0:T(8,128)(2,1)S(1)}, u32[]{:S(2)}, u32[]{:S(2)}) collective-permute-start(bf16[16,768]{1,0:T(8,128)(2,1)S(1)} %get-tuple-element.103.up_mine), channel_id=1, source_target_pairs={{0,1},{1,0},{2,3},{3,2},{4,5},{5,4},{6,7},{7,6},{8,9},{9,8},{10,11... | collective-permute-start | bytes 73736 | tf_op jit(solution)/shard_map/ppermute | solution.py:586
